TPU v7x, 256 devices: a whole 4x4x8 slice. The times are simulated.
256 devices in a mesh: pipe: 8 (over z), expert: 16 (over y, x), dp: 2 (over core).
Axes of the slice: x: 4, y: 4, z: 8, core: 2. Of those that a mesh axis runs over, the one named last changes fastest.
Arguments:
- sent_down: bfloat16 [8, 512, 3584], P('pipe', 'expert'), may hold values from -6 to 6
- sent_up: bfloat16 [8, 512, 3584], P('pipe', 'expert'), may hold values from -6 to 6
- expert_ids: int32 [2, 8, 512, 2], P(None, 'pipe', 'expert'), may hold values from 0 to 7, all different within a row; in each aligned block of 32 rows (0 to 31, 32 to 63, ..., all dimensions but the last counted through in order) at most 16 rows name the same one
- router_logits: float32 [2, 8, 512, 2], P(None, 'pipe', 'expert'), may hold values from -6 to 6
- saved_gate_up: bfloat16 [2, 8, 16, 2, 256, 512], P(None, 'pipe', 'expert', None, None, 'dp'), may hold values from -6 to 6
- down_weight: bfloat16 [8, 16, 512, 3584], P('pipe', 'expert', 'dp'), may hold values from -0.09375 to 0.09375
Outputs:
- grad_gate_up: bfloat16 [2, 8, 16, 2, 256, 512], P(None, 'pipe', 'expert', None, None, 'dp')
- grad_down: bfloat16 [8, 16, 512, 3584], P('pipe', 'expert', 'dp')
- grad_logits: float32 [2, 8, 512, 2], P(None, 'pipe', 'expert')
Inputs may be any that keep to these rules, and one draw needn't show every extreme that they name: `expert_ids`: in each aligned block of 32 tokens of a span and segment no expert is named by more than 16 tokens, a bound that some block reaches.
All inputs are finite; a program needn't handle non-finite values.
Results may differ from a plain program's by a relative error of at most 0.015.
Values may be sent and summed in bfloat16 or wider, within the bound.
No kernel may reach another device: no remote copies, remote signals or barrier semaphores. Data moves between devices by JAX's collectives and lax.ppermute only.
A program may use at most 64 MiB of HBM per device.

v0:
```python
import jax
import jax.numpy as jnp
from jax import lax
from jax.sharding import PartitionSpec as P

route_scale = 2.5


def shifted(value, axis, steps):
    count = lax.axis_size(axis)
    leading, last = (max(0, -steps), min(count, count - steps))
    return lax.ppermute(value, axis, [(source, source + steps) for source in range(leading, last)])


def slot_table(expert_list, experts, capacity):
    flat_ids = expert_list.reshape(-1)
    marks = (flat_ids[:, None] == jnp.arange(experts, dtype=jnp.int32)[None, :]).astype(jnp.int32)
    before = jnp.cumsum(marks, axis=0) - marks
    place = jnp.sum(before * marks, axis=1)
    slot_index = flat_ids * capacity + place
    filler = flat_ids.shape[0]
    owner = (
        jnp.full((experts * capacity,), filler, jnp.int32)
        .at[slot_index]
        .set(jnp.arange(filler, dtype=jnp.int32))
    )
    return (slot_index, owner)


def local(sent_down, sent_up, expert_ids, router_logits, saved_gate_up, down_weight):
    blocks = lax.axis_size("expert")
    group_size = max(1, blocks // 8)
    experts = blocks // group_size
    from_above = shifted(sent_down, "pipe", -1)
    from_below = shifted(sent_up, "pipe", 1)
    incoming = jnp.stack([from_above[0], from_below[0]])
    tok_rows = incoming.shape[1]
    width = incoming.shape[2]
    expert_list = expert_ids[:, 0]
    top_count = expert_list.shape[2]
    saved = saved_gate_up[:, 0, 0]
    weight = down_weight[0, 0]
    rows_all = saved.shape[2]
    capacity = rows_all // blocks
    scores = jax.nn.sigmoid(router_logits[:, 0])
    total = jnp.sum(scores, axis=-1, keepdims=True)
    combine = (route_scale * scores / total).astype(jnp.bfloat16)
    slot_index, owner = jax.vmap(lambda block_ids: slot_table(block_ids, experts, capacity))(
        expert_list
    )
    padded_rows = jnp.concatenate([incoming, jnp.zeros((2, 1, width), jnp.bfloat16)], axis=1)
    send_rows = jax.vmap(lambda table, index: table[index])(padded_rows, owner // top_count)
    send_rows = jnp.repeat(send_rows.reshape(2, experts, capacity, width), group_size, axis=1)
    padded_weights = jnp.concatenate(
        [combine.reshape(2, -1), jnp.zeros((2, 1), jnp.bfloat16)], axis=1
    )
    send_weights = jnp.take_along_axis(padded_weights, owner, axis=1).reshape(2, experts, capacity)
    send_weights = jnp.repeat(send_weights, group_size, axis=1)
    recv_rows, recv_weights = (
        lax.all_to_all(send_rows, "expert", split_axis=1, concat_axis=1, tiled=True),
        lax.all_to_all(send_weights, "expert", split_axis=1, concat_axis=1, tiled=True),
    )
    slot_rows = recv_rows.reshape(2, rows_all, width)
    slot_weight = recv_weights.reshape(2, rows_all).astype(jnp.float32)[..., None]
    gate_pre = saved[:, 0].astype(jnp.float32)
    up_pre = saved[:, 1].astype(jnp.float32)
    sigma = jax.nn.sigmoid(gate_pre)
    silu_val = gate_pre * sigma
    hidden_f = (silu_val * up_pre).astype(jnp.bfloat16).astype(jnp.float32)
    raw_grad = jnp.einsum("crd,hd->crh", slot_rows, weight, preferred_element_type=jnp.float32)
    partial_dot = jnp.sum(hidden_f * raw_grad, axis=-1).reshape(2, blocks, capacity)
    hidden_grad = slot_weight * raw_grad
    gate_grad = hidden_grad * up_pre * sigma * (1.0 + gate_pre * (1.0 - sigma))
    up_grad = hidden_grad * silu_val
    pair_grads = jnp.stack([gate_grad, up_grad], axis=1).astype(jnp.bfloat16)
    scaled = (slot_weight * hidden_f).astype(jnp.bfloat16)
    weight_grad = jnp.einsum(
        "crh,crd->hd", scaled, slot_rows, preferred_element_type=jnp.float32
    ).astype(jnp.bfloat16)
    summed = lax.psum(partial_dot, "dp")
    returned = lax.all_to_all(summed, "expert", split_axis=1, concat_axis=1, tiled=True)
    returned = jnp.sum(returned.reshape(2, experts, group_size, capacity), axis=2)
    route_grad = jnp.take_along_axis(returned.reshape(2, experts * capacity), slot_index, axis=1)
    route_grad = route_grad.reshape(2, tok_rows, top_count)
    score_grad = (
        route_scale
        / total
        * (route_grad - jnp.sum(route_grad * scores, axis=-1, keepdims=True) / total)
    )
    logit_grads = score_grad * scores * (1.0 - scores)
    return (pair_grads[:, None, None], weight_grad[None, None], logit_grads[:, None])


def solution(mesh):
    placed = (
        P("pipe", "expert", None),
        P("pipe", "expert", None),
        P(None, "pipe", "expert", None),
        P(None, "pipe", "expert", None),
        P(None, "pipe", "expert", None, None, "dp"),
        P("pipe", "expert", "dp", None),
    )
    return jax.shard_map(
        local,
        mesh=mesh,
        in_specs=placed,
        out_specs=(
            P(None, "pipe", "expert", None, None, "dp"),
            P("pipe", "expert", "dp", None),
            P(None, "pipe", "expert", None),
        ),
        check_vma=False,
    )
```

profile of v0, /device:TPU:1, one launch (start us, length us, event | category | flops | bytes accessed | tf_op | source)
XLA Modules:
  0.0 127.0 jit_solution(9308327470401320413)
XLA Ops:
  0.6 0.0 copy-start
  0.6 0.0 copy-start.2
  0.7 1.4 %copy.88 = bf16[1,32,3584]{2,0,1:T(2,128)(2,1)S(1)} copy(bf16[1,32,3584]{2,1,0:T(8,128)(2,1)} %param.6) | data formatting | bytes 458752 | tf_op args[0]
  2.1 1.3 %collective-permute-start = (bf16[1,32,3584]{2,0,1:T(2,128)(2,1)S(1)}, bf16[1,32,3584]{2,0,1:T(2,128)(2,1)S(1)}, u32[]{:S(2)}, u32[]{:S(2)}) collective-permute-start(bf16[1,32,3584]{2,0,1:T(2,128)(2,1)S(1)} %copy.88), channel_id=1, source_target_pairs={{32,0},{64,32},{96,64},{128,96},{160,128},{192,160},{224,192},{33,... | collective-permute-start | bytes 688136 | tf_op jit(solution)/shard_map/ppermute | solution.py:12
  3.4 1.3 %copy.89 = bf16[1,32,3584]{2,0,1:T(2,128)(2,1)S(1)} copy(bf16[1,32,3584]{2,1,0:T(8,128)(2,1)} %param.7) | data formatting | bytes 458752 | tf_op args[1]
  4.7 5.8 %collective-permute-start.1 = (bf16[1,32,3584]{2,0,1:T(2,128)(2,1)S(1)}, bf16[1,32,3584]{2,0,1:T(2,128)(2,1)}, u32[]{:S(2)}, u32[]{:S(2)}) collective-permute-start(bf16[1,32,3584]{2,0,1:T(2,128)(2,1)S(1)} %copy.89), channel_id=1, source_target_pairs={{0,32},{32,64},{64,96},{96,128},{128,160},{160,192},{192,224},{1,3... | collective-permute-start | bytes 688136 | tf_op jit(solution)/shard_map/ppermute | solution.py:12
  10.5 0.8 copy.83
  11.2 0.1 eq.15
  11.4 0.1 fusion.33
  11.4 0.1 reduce_window_sum.11
  11.5 0.2 select_reduce_fusion
  11.7 0.1 mul.102
  11.9 0.1 reshape.190
  11.9 0.1 reshape.192
  12.0 6.4 %scatter_fusion = s32[2,128]{1,0:T(2,128)S(1)} fusion(s32[2,128]{1,0:T(2,128)S(1)} %broadcast_in_dim.36, s32[128]{0:T(128)S(1)} %reshape.190, s32[128]{0:T(128)S(1)} %reshape.192), kind=kCustom, calls=%fused_computation.3 | custom fusion | bytes 2560 | tf_op jit(solution)/shard_map/vmap()/scatter | solution.py:25
  18.5 0.0 copy-done.2
  18.5 0.1 copy.85
  18.6 0.1 fusion.45
  18.7 0.1 reshape.168
  18.8 0.1 div.59
  18.9 0.1 div.60
  19.0 2.3 %gather_fusion = bf16[256]{0:T(256)(128)(2,1)S(1)} fusion(bf16[2,65]{1,0:T(2,128)(2,1)S(1)} %concatenate.14, s32[256]{0:T(256)S(1)} %get-tuple-element.30), kind=kCustom, calls=%fused_computation | custom fusion | bytes 3072 | tf_op jit(solution)/shard_map/jit(take_along_axis)/gather | solution.py:57
  21.4 0.1 select_n.51
  21.5 0.6 broadcast_in_dim.39
  22.1 6.8 %all-to-all-start = ((bf16[2,16,16]{2,0,1:T(2,128)(2,1)}), bf16[2,16,16]{2,0,1:T(2,128)(2,1)S(1)}, u32[]{:S(2)}, u32[]{:S(2)}) async-start(bf16[2,16,16]{2,0,1:T(2,128)(2,1)} %bitcast.4), calls=%async_computation | async-start | bytes 16384 | tf_op jit(solution)/shard_map/all_to_all | solution.py:61
  28.8 0.0 collective-permute-done
  28.9 0.0 collective-permute-done.1
  28.9 2.1 %fusion.23 = bf16[2,33,3584]{2,0,1:T(2,128)(2,1)S(1)} fusion(bf16[1,32,3584]{2,0,1:T(2,128)(2,1)} %collective-permute-done.1, bf16[1,32,3584]{2,0,1:T(2,128)(2,1)S(1)} %collective-permute-done), kind=kLoop, calls=%fused_computation.38 | loop fusion | flops 1655808 | bytes 931840 | tf_op jit(solution)/shard_map/stack | solution.py:36
  30.9 5.3 %gather_fusion.1 = bf16[256,3584]{1,0:T(8,128)(2,1)} fusion(bf16[2,33,3584]{2,0,1:T(2,128)(2,1)S(1)} %fusion.23, s32[256]{0:T(256)S(1)} %get-tuple-element.31), kind=kCustom, calls=%fused_computation.1 | custom fusion | bytes 3672064 | tf_op jit(solution)/shard_map/vmap()/gather | solution.py:52
  36.3 2.9 %copy.90 = bf16[2,8,16,3584]{3,2,0,1:T(8,128)(2,1)} copy(bf16[2,8,16,3584]{3,2,1,0:T(8,128)(2,1)} %bitcast.130) | data formatting | bytes 3670016 | tf_op jit(solution)/shard_map/reshape | solution.py:53
  39.1 0.0 all-to-all-done
  39.1 3.7 %broadcast_in_dim.41 = bf16[2,8,2,16,3584]{4,3,0,2,1:T(8,128)(2,1)} broadcast(bf16[2,8,16,3584]{3,2,0,1:T(8,128)(2,1)} %copy.90), dimensions={0,1,3,4} | broadcast | bytes 5505024 | tf_op jit(solution)/shard_map/broadcast_in_dim | solution.py:53
  42.8 0.0 copy-start.1
  42.9 6.8 %all-to-all-start.1 = ((bf16[2,16,16,3584]{3,2,0,1:T(8,128)(2,1)}), bf16[2,16,16,3584]{3,2,0,1:T(8,128)(2,1)}, u32[]{:S(2)}, u32[]{:S(2)}) async-start(bf16[2,16,16,3584]{3,2,0,1:T(8,128)(2,1)} %bitcast.129), calls=%async_computation.1 | async-start | bytes 7340032 | tf_op jit(solution)/shard_map/all_to_all | solution.py:60
  49.7 0.1 reduce_sum.57
  49.8 0.1 copy.98
  49.9 0.1 copy.95
  50.0 0.1 reduce_sum.54
  50.1 0.0 copy-done.1
  50.1 0.2 copy.92
  50.3 0.1 reshape.184
  50.4 0.1 copy.96
  50.5 0.1 reshape.169
  50.6 51.1 %all-to-all-done.1 = bf16[2,16,16,3584]{3,2,0,1:T(8,128)(2,1)} async-done(((bf16[2,16,16,3584]{3,2,0,1:T(8,128)(2,1)}), bf16[2,16,16,3584]{3,2,0,1:T(8,128)(2,1)}, u32[]{:S(2)}, u32[]{:S(2)}) %all-to-all-start.1) | async-done | bytes 3670048 | tf_op jit(solution)/shard_map/all_to_all | solution.py:60
  101.6 2.3 %copy.91 = bf16[2,16,16,3584]{3,2,1,0:T(8,128)(2,1)S(1)} copy(bf16[2,16,16,3584]{3,2,0,1:T(8,128)(2,1)} %all-to-all-done.1) | data formatting | bytes 7340032 | tf_op jit(solution)/shard_map/all_to_all | solution.py:60
  103.9 2.4 %fusion.1 = bf16[1,1,256,3584]{3,2,1,0:T(8,128)(2,1)} fusion(bf16[2,256,3584]{2,1,0:T(8,128)(2,1)S(1)} %bitcast.131, f32[2,256]{1,0:T(2,128)S(1)} %reshape.169, bf16[2,2,256,256]{2,3,0,1:T(8,128)(2,1)S(1)} %bitcast.133), kind=kOutput, calls=%fused_computation.6 | convolution fusion | flops 941883392 | bytes 6031360 | tf_op jit(solution)/shard_map/crh,crd->hd/dot_general | solution.py:77
  106.3 0.0 copy-done
  106.3 1.4 %fusion.30 = (bf16[2,1,1,1,256,256]{4,5,0,3,2,1:T(8,128)(2,1)S(1)}, bf16[2,1,1,1,256,256]{4,5,0,3,2,1:T(8,128)(2,1)S(1)}, f32[2,256]{1,0:T(2,128)S(1)}) fusion(f32[2,256]{1,0:T(2,128)S(1)} %reshape.169, bf16[2,2,256,256]{2,3,0,1:T(8,128)(2,1)S(1)} %bitcast.134, bf16[2,256,3584]{2,1,0:T(8,128)(2,1)S(1)} %bitcast.132, bf16[1,1,256,3584]{3,2,1,0:T(8,128)(2,1)S(1)} %copy-done), kind=kOutput, calls=%fused_computation.43 | convolution fusion | flops 942276096 | bytes 6557696 | tf_op jit(solution)/shard_map/crd,hd->crh/dot_general | solution.py:70
  107.7 0.1 reshape.164
  107.8 6.0 %psum.7 = f32[2,16,16]{2,1,0:T(8,128)S(1)} all-reduce(f32[2,16,16]{2,1,0:T(8,128)S(1)} %reshape.164), channel_id=1, replica_groups=mesh['pipe'=8,'expert'=16,'dp'=2] {'dp'}, use_global_device_ids=true, to_apply=%region_5.6 | all-reduce | flops 512 | bytes 4096 | tf_op jit(solution)/shard_map/psum | solution.py:80
  113.7 0.6 copy.93
  114.3 3.5 %all-to-all-start.2 = ((f32[2,16,16]{2,0,1:T(2,128)}), f32[2,16,16]{2,0,1:T(2,128)S(1)}, u32[]{:S(2)}, u32[]{:S(2)}) async-start(f32[2,16,16]{2,0,1:T(2,128)} %copy.93), calls=%async_computation.2 | async-start | bytes 32768 | tf_op jit(solution)/shard_map/all_to_all | solution.py:81
  117.8 0.1 pad_maximum_fusion
  117.9 1.0 copy.99
  118.9 5.3 %all-to-all-done.2 = f32[2,16,16]{2,0,1:T(2,128)S(1)} async-done(((f32[2,16,16]{2,0,1:T(2,128)}), f32[2,16,16]{2,0,1:T(2,128)S(1)}, u32[]{:S(2)}, u32[]{:S(2)}) %all-to-all-start.2) | async-done | bytes 2080 | tf_op jit(solution)/shard_map/all_to_all | solution.py:81
  124.2 0.1 reshape.166
  124.3 1.5 %gather_fusion.2 = f32[128]{0:T(128)S(1)} fusion(f32[2,128]{1,0:T(2,128)S(1)} %reshape.166, s32[128]{0:T(128)S(1)} %reshape.184), kind=kCustom, calls=%fused_computation.2 | custom fusion | bytes 2048 | tf_op jit(solution)/shard_map/jit(take_along_axis)/gather | solution.py:83
  125.8 0.1 gather.19
  126.0 0.1 gather.18
  126.1 0.1 copy.97
  126.2 0.1 subtract_multiply_fusion
  126.3 0.7 copy.100
  (15 shorter events, 0.1 us)
Async XLA Ops:
  0.6 105.7 %copy-start = (bf16[1,1,256,3584]{3,2,1,0:T(8,128)(2,1)S(1)}, bf16[1,1,256,3584]{3,2,1,0:T(8,128)(2,1)}, u32[]{:S(2)}) copy-start(bf16[1,1,256,3584]{3,2,1,0:T(8,128)(2,1)} %param.11) | copy-start | bytes 5505028
  0.6 17.8 %copy-start.2 = (f32[2,1,32,2]{2,3,1,0:T(2,128)S(1)}, f32[2,1,32,2]{2,3,1,0:T(2,128)}, u32[]{:S(2)}) copy-start(f32[2,1,32,2]{2,3,1,0:T(2,128)} %param.9) | copy-start | bytes 1540
  2.1 26.8 %collective-permute-start = (bf16[1,32,3584]{2,0,1:T(2,128)(2,1)S(1)}, bf16[1,32,3584]{2,0,1:T(2,128)(2,1)S(1)}, u32[]{:S(2)}, u32[]{:S(2)}) collective-permute-start(bf16[1,32,3584]{2,0,1:T(2,128)(2,1)S(1)} %copy.88), channel_id=1, source_target_pairs={{32,0},{64,32},{96,64},{128,96},{160,128},{192,160},{224,192},{33,... | collective-permute-start | bytes 688136 | tf_op jit(solution)/shard_map/ppermute | solution.py:12
  4.7 24.2 %collective-permute-start.1 = (bf16[1,32,3584]{2,0,1:T(2,128)(2,1)S(1)}, bf16[1,32,3584]{2,0,1:T(2,128)(2,1)}, u32[]{:S(2)}, u32[]{:S(2)}) collective-permute-start(bf16[1,32,3584]{2,0,1:T(2,128)(2,1)S(1)} %copy.89), channel_id=1, source_target_pairs={{0,32},{32,64},{64,96},{96,128},{128,160},{160,192},{192,224},{1,3... | collective-permute-start | bytes 688136 | tf_op jit(solution)/shard_map/ppermute | solution.py:12
  22.1 17.1 %all-to-all-start = ((bf16[2,16,16]{2,0,1:T(2,128)(2,1)}), bf16[2,16,16]{2,0,1:T(2,128)(2,1)S(1)}, u32[]{:S(2)}, u32[]{:S(2)}) async-start(bf16[2,16,16]{2,0,1:T(2,128)(2,1)} %bitcast.4), calls=%async_computation | async-start | bytes 16384 | tf_op jit(solution)/shard_map/all_to_all | solution.py:61
  42.8 7.2 %copy-start.1 = (bf16[2,1,1,2,256,256]{5,4,3,2,1,0:T(8,128)(2,1)S(1)}, bf16[2,1,1,2,256,256]{5,4,3,2,1,0:T(8,128)(2,1)}, u32[]{:S(2)}) copy-start(bf16[2,1,1,2,256,256]{5,4,3,2,1,0:T(8,128)(2,1)} %param.10) | copy-start | bytes 1572868
  42.9 58.8 %all-to-all-start.1 = ((bf16[2,16,16,3584]{3,2,0,1:T(8,128)(2,1)}), bf16[2,16,16,3584]{3,2,0,1:T(8,128)(2,1)}, u32[]{:S(2)}, u32[]{:S(2)}) async-start(bf16[2,16,16,3584]{3,2,0,1:T(8,128)(2,1)} %bitcast.129), calls=%async_computation.1 | async-start | bytes 7340032 | tf_op jit(solution)/shard_map/all_to_all | solution.py:60
  114.3 9.9 %all-to-all-start.2 = ((f32[2,16,16]{2,0,1:T(2,128)}), f32[2,16,16]{2,0,1:T(2,128)S(1)}, u32[]{:S(2)}, u32[]{:S(2)}) async-start(f32[2,16,16]{2,0,1:T(2,128)} %copy.93), calls=%async_computation.2 | async-start | bytes 32768 | tf_op jit(solution)/shard_map/all_to_all | solution.py:81
where the time goes:
time: 128 us; the launch traced here: 127 us
  waiting for transfers between devices  56.4 us (44%)
  local copies, waits for them, and re-layouts  33 us (26%)
  starting transfers between devices  24.1 us (19%)
  blocking collectives  5.96 us (5%)
  matrix products  3.79 us (3%)
  other arithmetic  2.77 us (2%)
    all_to_all x1, waiting for transfers between devices, local(): lax.all_to_all(send_rows, 'expert', split_axis=1, concat_axis=1, tiled=True)  51.1 us
    ppermute x2, starting transfers between devices, shifted(): lax.ppermute(value, axis, [(source, source + steps) for source in range(l...  7.07 us
    all_to_all x1, starting transfers between devices, local(): lax.all_to_all(send_rows, 'expert', split_axis=1, concat_axis=1, tiled=True)  6.83 us
    all_to_all x1, starting transfers between devices, local(): lax.all_to_all(send_weights, 'expert', split_axis=1, concat_axis=1, tiled...  6.75 us
    scatter x3, local copies, waits for them, and re-layouts, slot_table(): owner = jnp.full((experts * capacity,), filler, jnp.int32).at[slot_index]...  6.6 us
    psum x1, blocking collectives, local(): summed = lax.psum(partial_dot, 'dp')  5.96 us
    unnamed x13, local copies, waits for them, and re-layouts  5.47 us
    gather x1, local copies, waits for them, and re-layouts, local(): table[index]  5.33 us
  transfers between devices with their start and end apart: 5, of which 2 were waited for; matrix products, arithmetic and copies ran while one was open for 20% of the time, Pallas kernels for 0%

commit v1 on v0

v1 whole, which is shorter than its diff:
```python
import functools

import jax
import jax.numpy as jnp
from jax import lax
from jax.experimental import pallas as pl
from jax.experimental.pallas import tpu as pltpu
from jax.sharding import PartitionSpec as P

route_scale = 2.5
side = 4
shifts = (1, -1, 2)
extra = 128
bf16, f32 = jnp.bfloat16, jnp.float32
params = pltpu.CompilerParams(vmem_limit_bytes=48 * 2**20)
whole = pl.BlockSpec(memory_space=pltpu.VMEM)
scalars = pl.BlockSpec(memory_space=pltpu.SMEM)


def moved(place, step, along_x):
    y, x = place // side, place % side
    return y * side + (x + step) % side if along_x else (y + step) % side * side + x


def plane_shift(value, step, first_along_x):
    pairs = [
        (place * 2 + core, moved(place, step, first_along_x == (core == 0)) * 2 + core)
        for place in range(side * side)
        for core in range(2)
    ]
    return lax.ppermute(value, ("expert", "dp"), pairs)


def swapped(value):
    return lax.ppermute(value, "dp", [(0, 1), (1, 0)])


def select_kernel(info, *refs):
    blocks, outs = refs[:4], refs[4:]
    tokens, width = blocks[0].shape
    width -= extra
    slots = outs[0].shape[0] // 4
    rows, columns = 4 * tokens, 4 * outs[0].shape[0]

    def pick(index, base):
        return jnp.where(
            index < 2,
            jnp.where(index == 0, info[base], info[base + 1]),
            jnp.where(index == 2, info[base + 2], info[base + 3]),
        )

    notes = jnp.concatenate([ref[:, width:] for ref in blocks], axis=0).astype(f32)
    id0, id1 = notes[:, 0:1], notes[:, 1:2]
    row = lax.broadcasted_iota(jnp.int32, (rows, columns), 0)
    column = lax.broadcasted_iota(jnp.int32, (rows, columns), 1)
    expert = pick(column // (4 * slots), 4).astype(f32)
    same = pick(row // tokens, 0) == column // slots % 4
    named0 = same & (id0 == expert)
    named = named0 | (same & (id1 == expert))
    i = lax.broadcasted_iota(jnp.int32, (rows, rows), 0)
    j = lax.broadcasted_iota(jnp.int32, (rows, rows), 1)
    earlier = ((j < i) & (i // tokens == j // tokens)).astype(f32).astype(bf16)
    place = jnp.dot(earlier, named.astype(f32).astype(bf16), preferred_element_type=f32)
    taken = jnp.where(named & (place == (column % slots).astype(f32)), 1.0, 0.0)
    weights = (taken * jnp.where(named0, notes[:, 2:3], notes[:, 3:4])).astype(bf16)
    taken = taken.astype(bf16)
    across = (((0,), (0,)), ((), ()))

    def put(start, size, value):
        for out_index, out in enumerate(outs):
            out[:, start : start + size] = value[
                out_index * 4 * slots : (out_index + 1) * 4 * slots
            ].astype(bf16)

    put(
        width,
        extra,
        lax.dot_general(
            weights, jnp.ones((rows, extra), bf16), across, preferred_element_type=f32
        ),
    )
    step = 512 if width % 512 == 0 else width
    for start in range(0, width, step):
        chunk = jnp.concatenate([ref[:, start : start + step] for ref in blocks], axis=0)
        put(start, step, lax.dot_general(taken, chunk, across, preferred_element_type=f32))


def select_rows(info, blocks, slots):
    shape = jax.ShapeDtypeStruct((4 * slots, blocks[0].shape[1]), bf16)
    return pl.pallas_call(
        select_kernel,
        out_shape=(shape,) * 4,
        in_specs=[scalars] + [whole] * 4,
        out_specs=(whole,) * 4,
        compiler_params=params,
        name="select_rows",
    )(info, *blocks)


def hidden_of(saved, block):
    gate, up = saved[0, block, :].astype(f32), saved[1, block, :].astype(f32)
    sigma = jax.nn.sigmoid(gate)
    silu = gate * sigma
    return gate, up, sigma, silu, (silu * up).astype(bf16).astype(f32)


def raw_kernel(order, rows, mine, other, saved_mine, saved_other, g_mine, g_other, dots):
    count = rows.shape[0]
    width = rows.shape[1] - extra
    slots = count // 16
    slot_weight = rows[:, width : width + 1].astype(f32)
    total = jnp.zeros((count, 1), f32)
    for weight, saved, out in ((other, saved_other, g_other), (mine, saved_mine, g_mine)):
        raw = lax.dot_general(
            rows[:, :width], weight[...], (((1,), (1,)), ((), ())), preferred_element_type=f32
        )
        for chunk in range(16):
            at = pl.ds(pl.multiple_of(order[chunk] * slots, slots), slots)
            gate, up, sigma, silu, hidden = hidden_of(saved, at)
            raw_chunk = raw[chunk * slots : (chunk + 1) * slots]
            lane = lax.broadcasted_iota(jnp.int32, (slots, 128), 1)
            row = lax.broadcasted_iota(jnp.int32, (slots, 128), 0)
            dot = jnp.sum(hidden * raw_chunk, axis=1, keepdims=True)
            dot = jnp.sum(jnp.where(lane == row, dot, 0.0), axis=0, keepdims=True)
            spot = pl.ds(order[chunk] * 2, 1)
            if weight is other:
                dots[spot, :] = dot
            else:
                dot = dots[spot, :] + dot
                dots[spot, :] = dot
                dots[pl.ds(order[chunk] * 2 + 1, 1), :] = dot
            grad = slot_weight[chunk * slots : (chunk + 1) * slots] * raw_chunk
            out[0, at, :] = (grad * up * sigma * (1.0 + gate * (1.0 - sigma))).astype(bf16)
            out[1, at, :] = (grad * silu).astype(bf16)


def raw_grads(order, rows, mine, other, saved_mine, saved_other):
    return pl.pallas_call(
        raw_kernel,
        out_shape=(
            jax.ShapeDtypeStruct(saved_mine.shape, bf16),
            jax.ShapeDtypeStruct(saved_mine.shape, bf16),
            jax.ShapeDtypeStruct((32, 128), f32),
        ),
        in_specs=[scalars] + [whole] * 5,
        out_specs=(whole,) * 3,
        compiler_params=params,
        name="raw_grads",
    )(order, rows, mine, other, saved_mine, saved_other)


def down_kernel(order, rows, saved, *refs):
    out, scaled = refs[-2:]
    count = rows.shape[0]
    width = rows.shape[1] - extra
    slots = count // 16
    for chunk in range(16):
        at = pl.ds(pl.multiple_of(order[chunk] * slots, slots), slots)
        here = slice(chunk * slots, (chunk + 1) * slots)
        weight = rows[here, width : width + 1].astype(f32)
        scaled[here, :] = (weight * hidden_of(saved, at)[4]).astype(bf16)
    step = 512 if width % 512 == 0 else width
    for start in range(0, width, step):
        here = slice(start, start + step)
        value = lax.dot_general(
            scaled[...], rows[:, here], (((0,), (0,)), ((), ())), preferred_element_type=f32
        )
        if len(refs) == 3:
            value = value + refs[0][:, here].astype(f32)
        out[:, here] = value.astype(bf16)


def down_grads(order, rows, saved, *added):
    hidden_units = saved.shape[2]
    return pl.pallas_call(
        down_kernel,
        out_shape=jax.ShapeDtypeStruct((hidden_units, rows.shape[1] - extra), bf16),
        in_specs=[scalars] + [whole] * (2 + len(added)),
        out_specs=whole,
        scratch_shapes=[pltpu.VMEM((rows.shape[0], hidden_units), bf16)],
        compiler_params=params,
        name="down_grads",
    )(order, rows, saved, *added)


def logit_kernel(returned, experts, places, scores, out):
    half = scores.shape[0]
    spread = jnp.dot(
        experts[...], returned[...], preferred_element_type=f32, precision=lax.Precision.HIGHEST
    )
    route = jnp.sum(spread * places[...], axis=1, keepdims=True)
    route0, route1 = route[:half], route[half:]
    score0, score1 = scores[:, 0:1], scores[:, 1:2]
    total = score0 + score1
    mean = (route0 * score0 + route1 * score1) / total
    scale = route_scale / total
    grad0 = scale * (route0 - mean) * score0 * (1.0 - score0)
    grad1 = scale * (route1 - mean) * score1 * (1.0 - score1)
    lane = lax.broadcasted_iota(jnp.int32, (half, 2), 1)
    out[...] = jnp.where(lane == 0, grad0, grad1)


def local(sent_down, sent_up, expert_ids, router_logits, saved_gate_up, down_weight):
    core = lax.axis_index("dp")
    spot = lax.axis_index("expert")
    y, x = spot >> 2, spot & 3
    first = core == 0
    segments = lax.axis_size("pipe")
    ids = expert_ids[:, 0]
    scores = jax.nn.sigmoid(router_logits[:, 0])
    saved = saved_gate_up[:, 0, 0]
    mine = down_weight[0, 0]
    slots = saved.shape[2] // 16
    tokens, top = ids.shape[1:]

    pairs = [(2 * z, 2 * (z - 1)) for z in range(1, segments)]
    pairs += [(2 * z + 1, 2 * (z + 1) + 1) for z in range(segments - 1)]
    incoming = lax.ppermute(
        jnp.where(first, sent_down[0], sent_up[0]), ("pipe", "dp"), pairs
    )
    other = swapped(mine)
    saved_mine = jnp.where(first, saved[0], saved[1])
    saved_other = swapped(jnp.where(first, saved[1], saved[0]))

    combine = (route_scale * scores / jnp.sum(scores, axis=-1, keepdims=True)).astype(bf16)
    my_ids = jnp.where(first, ids[0], ids[1]).astype(bf16)
    my_combine = jnp.where(first, combine[0], combine[1])
    notes = jnp.concatenate(
        [my_ids, my_combine, jnp.zeros((tokens, extra - 2 * top), bf16)], axis=1
    )
    block = jnp.concatenate([incoming, notes], axis=1)

    near, far = jnp.where(first, x, y), jnp.where(first, y, x)
    blocks = [block] + [plane_shift(block, step, True) for step in shifts]
    held = [near] + [(near + side - step) & 3 for step in shifts]
    targets = [far] + [(far + side + step) & 3 for step in shifts]
    wanted = [jnp.where(first, t * 2 + (x >> 1), y * 2 + (t >> 1)) for t in targets]
    pieces = select_rows(jnp.stack(held + wanted).astype(jnp.int32), blocks, slots)
    pieces = [pieces[0]] + [
        plane_shift(piece, step, False) for piece, step in zip(pieces[1:], shifts, strict=True)
    ]
    rows = jnp.zeros((16 * slots, pieces[0].shape[1]), bf16)
    for piece, step in zip(pieces, (0,) + shifts, strict=True):
        rows = lax.dynamic_update_slice(
            rows, piece, (((far + side - step) & 3) * (4 * slots), jnp.int32(0))
        )
    number = jnp.arange(16, dtype=jnp.int32)
    order = jnp.where(first, number, (number & 3) * 4 + (number >> 2))

    g_mine, g_other, dots = raw_grads(order, rows, mine, other, saved_mine, saved_other)
    returned = lax.all_to_all(dots, ("expert", "dp"), split_axis=0, concat_axis=0, tiled=True)
    g_other = swapped(g_other)
    down_other = swapped(down_grads(order, rows, saved_other))
    weight_grad = down_grads(order, rows, saved_mine, down_other)
    pair_grads = jnp.where(
        first, jnp.stack([g_mine, g_other]), jnp.stack([g_other, g_mine])
    )

    marks = jnp.sum(
        (ids[..., None] == jnp.arange(8, dtype=jnp.int32)).astype(jnp.int32), axis=2
    )
    before = jnp.cumsum(marks, axis=1) - marks
    span = jnp.arange(2, dtype=jnp.int32)[:, None]
    source = jnp.arange(32, dtype=jnp.int32)
    lanes = jnp.arange(128, dtype=jnp.int32)
    experts, places = [], []
    for k in range(top):
        own = ids[..., k]
        experts.append(
            (source // 4 == own[..., None]) & (source % 2 == span[..., None])
        )
        place = jnp.sum(
            jnp.where(own[..., None] == jnp.arange(8, dtype=jnp.int32), before, 0), axis=-1
        )
        places.append(lanes == place[..., None])
    logit_grads = pl.pallas_call(
        logit_kernel,
        out_shape=jax.ShapeDtypeStruct((2 * tokens, top), f32),
        in_specs=[whole] * 4,
        out_specs=whole,
        compiler_params=params,
        name="logit_grads",
    )(
        returned,
        jnp.stack(experts).astype(f32).reshape(2 * top * tokens, 32),
        jnp.stack(places).astype(f32).reshape(2 * top * tokens, 128),
        scores.reshape(2 * tokens, top),
    )
    return (
        pair_grads[:, None, None],
        weight_grad[None, None],
        logit_grads.reshape(2, 1, tokens, top),
    )


def solution(mesh):
    placed = (
        P("pipe", "expert", None),
        P("pipe", "expert", None),
        P(None, "pipe", "expert", None),
        P(None, "pipe", "expert", None),
        P(None, "pipe", "expert", None, None, "dp"),
        P("pipe", "expert", "dp", None),
    )
    return jax.shard_map(
        local,
        mesh=mesh,
        in_specs=placed,
        out_specs=(
            P(None, "pipe", "expert", None, None, "dp"),
            P("pipe", "expert", "dp", None),
            P(None, "pipe", "expert", None),
        ),
        check_vma=False,
    )
```

time: 128 us -> 70.1 us (0.55)
  waiting for transfers between devices: 56.4 us -> 18.8 us
  local copies, waits for them, and re-layouts: 33 us -> 4.07 us
  Pallas kernels: 0 us -> 13.2 us
  blocking collectives: 5.96 us -> 0 us
  matrix products: 3.79 us -> 0 us
  starting transfers between devices: 24.1 us -> 27.3 us
  other arithmetic: 2.77 us -> 5.54 us
    all_to_all x3 -> x1, waiting for transfers between devices: 56.4 us -> 6.75 us  [local(): lax.all_to_all(dots, ('expert', 'dp'), split_axis=0, concat_axis=0, tiled...]
    ppermute x2 -> x11, starting transfers between devices: 7.07 us -> 21.6 us  [the longest x6 8.66 us: plane_shift(): return lax.ppermute(value, ('expert', 'dp'), pairs)]
    pallas_call x0 -> x5, Pallas kernels: none -> 13.2 us  [the longest x2 6.02 us: down_grads(): pl.pallas_call(down_kernel, out_shape=jax.ShapeDtypeStruct((hidden_units,...]
    ppermute x2 -> x11, waiting for transfers between devices: 0.01 us -> 12.1 us  [the longest x6 11 us: plane_shift(): return lax.ppermute(value, ('expert', 'dp'), pairs)]
    all_to_all x3 -> x1, starting transfers between devices: 17.1 us -> 5.68 us  [local(): lax.all_to_all(dots, ('expert', 'dp'), split_axis=0, concat_axis=0, tiled...]
    gather x6 -> x0, local copies, waits for them, and re-layouts: 9.49 us -> none  [the longest x1 5.33 us: local(): table[index]]
    scatter x3 -> x0, local copies, waits for them, and re-layouts: 6.6 us -> none  [slot_table(): owner = jnp.full((experts * capacity,), filler, jnp.int32).at[slot_index]...]
    psum x1 -> x0, blocking collectives: 5.96 us -> none  [local(): summed = lax.psum(partial_dot, 'dp')]
  transfers between devices with their start and end apart: 5 -> 12, of which waited for: 2 -> 6; matrix products, arithmetic and copies ran while one was open for 20% -> 10% of each run, Pallas kernels for 0% -> 14%
where the time goes in v1:
time: 70.1 us; the launch traced here: 69.7 us
  starting transfers between devices  27.3 us (39%)
  waiting for transfers between devices  18.8 us (27%)
  Pallas kernels  13.2 us (19%)
  other arithmetic  5.54 us (8%)
  local copies, waits for them, and re-layouts  4.07 us (6%)
  between operations  0.81 us (1%)
    ppermute x6, waiting for transfers between devices, plane_shift(): return lax.ppermute(value, ('expert', 'dp'), pairs)  11 us
    ppermute x6, starting transfers between devices, plane_shift(): return lax.ppermute(value, ('expert', 'dp'), pairs)  8.66 us
    ppermute x4, starting transfers between devices, swapped(): return lax.ppermute(value, 'dp', [(0, 1), (1, 0)])  8.55 us
    all_to_all x1, waiting for transfers between devices, local(): lax.all_to_all(dots, ('expert', 'dp'), split_axis=0, concat_axis=0, tiled...  6.75 us
    pallas_call x2, Pallas kernels, down_grads(): pl.pallas_call(down_kernel, out_shape=jax.ShapeDtypeStruct((hidden_units,...  6.02 us
    all_to_all x1, starting transfers between devices, local(): lax.all_to_all(dots, ('expert', 'dp'), split_axis=0, concat_axis=0, tiled...  5.68 us
    ppermute x1, starting transfers between devices, local(): lax.ppermute(jnp.where(first, sent_down[0], sent_up[0]), ('pipe', 'dp'),...  4.38 us
    pallas_call x1, Pallas kernels, raw_grads(): pl.pallas_call(raw_kernel, out_shape=(jax.ShapeDtypeStruct(saved_mine.sha...  4.35 us
  transfers between devices with their start and end apart: 12, of which 6 were waited for; matrix products, arithmetic and copies ran while one was open for 10% of the time, Pallas kernels for 14%

profile of v1, /device:TPU:1, one launch (start us, length us, event | category | flops | bytes accessed | tf_op | source)
XLA Modules:
  0.0 69.7 jit_solution(6384072333655436809)
XLA Ops:
  0.6 1.0 %select_bitcast_fusion.2 = bf16[32,3584]{1,0:T(8,128)(2,1)S(1)} fusion(bf16[1,32,3584]{2,1,0:T(8,128)(2,1)} %param.6, bf16[1,32,3584]{2,1,0:T(8,128)(2,1)} %param.7, pred[]{:T(512)S(6)} %eq.160), kind=kLoop, calls=%fused_computation.3 | loop fusion | flops 114688 | bytes 688129 | tf_op jit(solution)/shard_map/jit(_where)/select_n | solution.py:219
  1.6 4.4 %collective-permute-start = (bf16[32,3584]{1,0:T(8,128)(2,1)S(1)}, bf16[32,3584]{1,0:T(8,128)(2,1)S(1)}, u32[]{:S(2)}, u32[]{:S(2)}) collective-permute-start(bf16[32,3584]{1,0:T(8,128)(2,1)S(1)} %select_bitcast_fusion.2), channel_id=1, source_target_pairs={{32,0},{64,32},{96,64},{128,96},{160,128},{192,160},{224,192},{1,3... | collective-permute-start | bytes 688136 | tf_op jit(solution)/shard_map/ppermute | solution.py:218
  6.0 0.2 collective-permute-start.7
  6.2 0.7 %fusion.5 = (f32[2,32]{1,0:T(2,128)S(1)}, f32[2,1,32,2]{2,3,1,0:T(2,128)S(1)}) fusion(f32[2,1,32,2]{2,3,1,0:T(2,128)} %param.9), kind=kLoop, calls=%fused_computation.38 | loop fusion | flops 448 | bytes 1280 | tf_op jit(solution)/shard_map/reduce_sum | solution.py:225
  7.0 0.7 %fusion.4 = bf16[32,2]{0,1:T(2,128)(2,1)S(1)} fusion(s32[2,1,32,2]{2,3,1,0:T(2,128)} %param.8, pred[]{:T(512)S(6)} %eq.160), kind=kLoop, calls=%fused_computation.37 | loop fusion | flops 128 | bytes 641 | tf_op jit(solution)/shard_map/convert_element_type | solution.py:226
  7.7 0.1 copy.24
  7.8 0.1 copy.25
  7.9 1.1 %collective-permute-done = bf16[32,3584]{1,0:T(8,128)(2,1)S(1)} collective-permute-done((bf16[32,3584]{1,0:T(8,128)(2,1)S(1)}, bf16[32,3584]{1,0:T(8,128)(2,1)S(1)}, u32[]{:S(2)}, u32[]{:S(2)}) %collective-permute-start) | collective-permute-done | bytes 229408 | tf_op jit(solution)/shard_map/ppermute | solution.py:218
  8.9 0.1 concatenate.17.refs_0_
  9.0 1.4 %collective-permute-start.1 = (bf16[32,3712]{1,0:T(8,128)(2,1)S(1)}, bf16[32,3712]{1,0:T(8,128)(2,1)S(1)}, u32[]{:S(2)}, u32[]{:S(2)}) collective-permute-start(bf16[32,3712]{1,0:T(8,128)(2,1)S(1)} %concatenate.17.refs_0_), channel_id=1, source_target_pairs={{0,2},{1,9},{2,4},{3,11},{4,6},{5,13},{6,0},{7,15},{8,10},{9,17},{... | collective-permute-start | bytes 712712 | tf_op jit(solution)/shard_map/ppermute | solution.py:31
  10.4 1.5 %collective-permute-start.2 = (bf16[32,3712]{1,0:T(8,128)(2,1)S(1)}, bf16[32,3712]{1,0:T(8,128)(2,1)S(1)}, u32[]{:S(2)}, u32[]{:S(2)}) collective-permute-start(bf16[32,3712]{1,0:T(8,128)(2,1)S(1)} %concatenate.17.refs_0_), channel_id=1, source_target_pairs={{0,6},{1,25},{2,0},{3,27},{4,2},{5,29},{6,4},{7,31},{8,14},{9,1},{... | collective-permute-start | bytes 712712 | tf_op jit(solution)/shard_map/ppermute | solution.py:31
  11.9 1.6 %collective-permute-start.3 = (bf16[32,3712]{1,0:T(8,128)(2,1)S(1)}, bf16[32,3712]{1,0:T(8,128)(2,1)S(1)}, u32[]{:S(2)}, u32[]{:S(2)}) collective-permute-start(bf16[32,3712]{1,0:T(8,128)(2,1)S(1)} %concatenate.17.refs_0_), channel_id=1, source_target_pairs={{0,4},{1,17},{2,6},{3,19},{4,0},{5,21},{6,2},{7,23},{8,12},{9,25},... | collective-permute-start | bytes 712712 | tf_op jit(solution)/shard_map/ppermute | solution.py:31
  13.5 1.8 %select_bitcast_fusion = (bf16[2,256,256]{2,1,0:T(8,128)(2,1)}, bf16[2,256,256]{2,1,0:T(8,128)(2,1)S(1)}) fusion(pred[]{:T(512)S(6)} %eq.160, bf16[2,1,1,2,256,256]{5,4,3,2,1,0:T(8,128)(2,1)} %param.10), kind=kLoop, calls=%fused_computation.1 | loop fusion | flops 262144 | bytes 1048577 | tf_op jit(solution)/shard_map/jit(_where)/select_n | solution.py:223
  15.3 2.8 %collective-permute-start.8 = (bf16[2,256,256]{2,1,0:T(8,128)(2,1)}, bf16[2,256,256]{2,1,0:T(8,128)(2,1)S(1)}, u32[]{:S(2)}, u32[]{:S(2)}) collective-permute-start(bf16[2,256,256]{2,1,0:T(8,128)(2,1)} %get-tuple-element.30), channel_id=1, source_target_pairs={{0,1},{1,0},{2,3},{3,2},{4,5},{5,4},{6,7},{7,6},{8,9},{9,8},{10,11... | collective-permute-start | bytes 786440 | tf_op jit(solution)/shard_map/ppermute | solution.py:35
  18.0 0.1 stack.59.info
  18.1 0.0 collective-permute-done.1.refs_1_
  18.1 0.0 collective-permute-done.2.refs_2_
  18.1 0.9 %collective-permute-done.3.refs_3_ = bf16[32,3712]{1,0:T(8,128)(2,1)S(1)} collective-permute-done((bf16[32,3712]{1,0:T(8,128)(2,1)S(1)}, bf16[32,3712]{1,0:T(8,128)(2,1)S(1)}, u32[]{:S(2)}, u32[]{:S(2)}) %collective-permute-start.3) | collective-permute-done | bytes 237600 | tf_op jit(solution)/shard_map/ppermute | solution.py:31
  19.1 2.4 %select_rows.1 = (bf16[64,3712]{1,0:T(8,128)(2,1)S(1)}, bf16[64,3712]{1,0:T(8,128)(2,1)}, bf16[64,3712]{1,0:T(8,128)(2,1)}, bf16[64,3712]{1,0:T(8,128)(2,1)S(1)}) custom-call(s32[8]{0:T(128)S(1)} %stack.59.info, bf16[32,3712]{1,0:T(8,128)(2,1)S(1)} %concatenate.17.refs_0_, bf16[32,3712]{1,0:T(8,128)(2,1)S(1)} %collective-permute-done.1.refs_1_, ...), custom_call_target="tpu_custom_call" | custom-call | tf_op jit(solution)/shard_map/select_rows/pallas_call | solution.py:90
  21.5 1.2 %collective-permute-start.4 = (bf16[64,3712]{1,0:T(8,128)(2,1)}, bf16[64,3712]{1,0:T(8,128)(2,1)}, u32[]{:S(2)}, u32[]{:S(2)}) collective-permute-start(bf16[64,3712]{1,0:T(8,128)(2,1)} %get-tuple-element.11), channel_id=1, source_target_pairs={{0,8},{1,3},{2,10},{3,5},{4,12},{5,7},{6,14},{7,1},{8,16},{9,11},{... | collective-permute-start | bytes 1425416 | tf_op jit(solution)/shard_map/ppermute | solution.py:31
  22.7 1.6 %collective-permute-start.5 = (bf16[64,3712]{1,0:T(8,128)(2,1)}, bf16[64,3712]{1,0:T(8,128)(2,1)S(1)}, u32[]{:S(2)}, u32[]{:S(2)}) collective-permute-start(bf16[64,3712]{1,0:T(8,128)(2,1)} %get-tuple-element.12), channel_id=1, source_target_pairs={{0,24},{1,7},{2,26},{3,1},{4,28},{5,3},{6,30},{7,5},{8,0},{9,15},{... | collective-permute-start | bytes 1425416 | tf_op jit(solution)/shard_map/ppermute | solution.py:31
  24.3 1.3 %collective-permute-start.6 = (bf16[64,3712]{1,0:T(8,128)(2,1)S(1)}, bf16[64,3712]{1,0:T(8,128)(2,1)S(1)}, u32[]{:S(2)}, u32[]{:S(2)}) collective-permute-start(bf16[64,3712]{1,0:T(8,128)(2,1)S(1)} %get-tuple-element.13), channel_id=1, source_target_pairs={{0,16},{1,5},{2,18},{3,7},{4,20},{5,1},{6,22},{7,3},{8,24},{9,13},... | collective-permute-start | bytes 1425416 | tf_op jit(solution)/shard_map/ppermute | solution.py:31
  25.7 0.1 broadcast_in_dim.11
  25.9 5.0 %collective-permute-done.4 = bf16[64,3712]{1,0:T(8,128)(2,1)} collective-permute-done((bf16[64,3712]{1,0:T(8,128)(2,1)}, bf16[64,3712]{1,0:T(8,128)(2,1)}, u32[]{:S(2)}, u32[]{:S(2)}) %collective-permute-start.4) | collective-permute-done | bytes 475168 | tf_op jit(solution)/shard_map/ppermute | solution.py:31
  30.9 1.1 %constant_dynamic-update-slice_fusion.2 = bf16[256,3712]{1,0:T(8,128)(2,1)S(1)} fusion(bf16[256,3712]{1,0:T(8,128)(2,1)S(1)} %constant_dynamic-update-slice_fusion.3, bf16[64,3712]{1,0:T(8,128)(2,1)} %collective-permute-done.4, s32[]{:T(128)S(6)} %select_n.153), kind=kLoop, calls=%fused_computation.28 | loop fusion | bytes 950276 | tf_op jit(solution)/shard_map/dynamic_update_slice | solution.py:244
  32.0 3.4 %collective-permute-done.5 = bf16[64,3712]{1,0:T(8,128)(2,1)S(1)} collective-permute-done((bf16[64,3712]{1,0:T(8,128)(2,1)}, bf16[64,3712]{1,0:T(8,128)(2,1)S(1)}, u32[]{:S(2)}, u32[]{:S(2)}) %collective-permute-start.5) | collective-permute-done | bytes 475168 | tf_op jit(solution)/shard_map/ppermute | solution.py:31
  35.4 1.6 %collective-permute-done.6 = bf16[64,3712]{1,0:T(8,128)(2,1)S(1)} collective-permute-done((bf16[64,3712]{1,0:T(8,128)(2,1)S(1)}, bf16[64,3712]{1,0:T(8,128)(2,1)S(1)}, u32[]{:S(2)}, u32[]{:S(2)}) %collective-permute-start.6) | collective-permute-done | bytes 475168 | tf_op jit(solution)/shard_map/ppermute | solution.py:31
  37.1 0.0 copy-start
  37.1 0.0 copy-start.3
  37.1 0.0 collective-permute-done.8.saved_other.saved
  37.1 2.5 %down_grads.2 = bf16[256,3584]{1,0:T(8,128)(2,1)} custom-call(s32[16]{0:T(128)S(1)} %broadcast_select_fusion.1.order, bf16[256,3712]{1,0:T(8,128)(2,1)S(1)} %constant_dynamic-update-slice_fusion.rows, bf16[2,256,256]{2,1,0:T(8,128)(2,1)S(1)} %collective-permute-done.8.saved_other.saved), custom_call_target="tpu_custom_call" | custom-call | tf_op jit(solution)/shard_map/down_grads/pallas_call | solution.py:175
  39.7 0.0 copy-done
  39.7 5.6 %collective-permute-start.10 = (bf16[256,3584]{1,0:T(8,128)(2,1)}, bf16[256,3584]{1,0:T(8,128)(2,1)}, u32[]{:S(2)}, u32[]{:S(2)}) collective-permute-start(bf16[256,3584]{1,0:T(8,128)(2,1)} %down_grads.2), channel_id=1, source_target_pairs={{0,1},{1,0},{2,3},{3,2},{4,5},{5,4},{6,7},{7,6},{8,9},{9,8},{10,11... | collective-permute-start | bytes 5505032 | tf_op jit(solution)/shard_map/ppermute | solution.py:35
  45.2 0.0 copy-done.3
  45.2 0.1 copy.27
  45.3 0.1 reduce_window_sum.11
  45.4 0.2 select_reduce_fusion.1
  45.6 0.1 compare_and_fusion.1
  45.7 0.0 collective-permute-done.7.other
  45.7 0.0 copy-start.2
  45.8 1.5 %copy-done.2 = bf16[1,1,256,3584]{3,2,1,0:T(8,128)(2,1)S(1)} copy-done((bf16[1,1,256,3584]{3,2,1,0:T(8,128)(2,1)S(1)}, bf16[1,1,256,3584]{3,2,1,0:T(8,128)(2,1)}, u32[]{:S(2)}) %copy-start.2) | copy-done | bytes 1835032
  47.2 0.0 copy-start.1
  47.2 4.4 %raw_grads.1 = (bf16[2,256,256]{2,1,0:T(8,128)(2,1)S(1)}, bf16[2,256,256]{2,1,0:T(8,128)(2,1)S(1)}, f32[32,128]{1,0:T(8,128)}) custom-call(s32[16]{0:T(128)S(1)} %broadcast_select_fusion.1.order, bf16[256,3712]{1,0:T(8,128)(2,1)} %copy-done, bf16[256,3584]{1,0:T(8,128)(2,1)S(1)} %bitcast.38, bf16[256,3584]{1,0:T(8,128)(2,1)} %collective-permute-done.7.other, ...), custom_call_target="tpu_custom_call" | custom-call | tf_op jit(solution)/shard_map/raw_grads/pallas_call | solution.py:138
  51.6 0.0 collective-permute-start.9
  51.6 0.1 iota_compare_fusion.1
  51.7 5.7 %all-to-all-start = ((f32[32,1,128]{2,1,0:T(1,128)}), f32[32,1,128]{2,1,0:T(1,128)S(1)}, u32[]{:S(2)}, u32[]{:S(2)}) async-start(f32[32,1,128]{2,1,0:T(1,128)} %bitcast.19), calls=%async_computation | async-start | bytes 32768 | tf_op jit(solution)/shard_map/all_to_all | solution.py:251
  57.4 0.1 copy.33
  57.5 6.8 %all-to-all-done = f32[32,1,128]{2,1,0:T(1,128)S(1)} async-done(((f32[32,1,128]{2,1,0:T(1,128)}), f32[32,1,128]{2,1,0:T(1,128)S(1)}, u32[]{:S(2)}, u32[]{:S(2)}) %all-to-all-start) | async-done | bytes 16416 | tf_op jit(solution)/shard_map/all_to_all | solution.py:251
  64.3 0.4 logit_grads.1
  64.7 0.7 copy.32
  65.4 0.0 collective-permute-done.9
  65.4 0.9 %maximum_select_fusion = bf16[2,1,1,2,256,256]{5,4,3,2,1,0:T(8,128)(2,1)} fusion(bf16[1,1,1,2,256,256]{5,4,3,2,1,0:T(8,128)(2,1)S(1)} %bitcast.46, bf16[1,1,1,2,256,256]{5,4,3,2,1,0:T(8,128)(2,1)S(1)} %bitcast.41, pred[]{:T(512)S(6)} %eq.160), kind=kLoop, calls=%fused_computation | loop fusion | flops 786432 | bytes 1048577 | tf_op jit(solution)/shard_map/jit(_where)/select_n | solution.py:255
  66.2 0.0 collective-permute-done.10.refs_0_
  66.2 0.0 copy-done.1
  66.3 3.5 %down_grads.3 = bf16[256,3584]{1,0:T(8,128)(2,1)} custom-call(s32[16]{0:T(128)S(1)} %broadcast_select_fusion.1.order, bf16[256,3712]{1,0:T(8,128)(2,1)S(1)} %copy-done.1, bf16[2,256,256]{2,1,0:T(8,128)(2,1)S(1)} %get-tuple-element.31.saved_mine.saved, bf16[256,3584]{1,0:T(8,128)(2,1)} %collective-permute-done.10.refs_0_), custom_call_target="tpu_custom_call" | custom-call | tf_op jit(solution)/shard_map/down_grads/pallas_call | solution.py:175
  (13 shorter events, 0.2 us)
Async XLA Ops:
  1.6 7.3 %collective-permute-start = (bf16[32,3584]{1,0:T(8,128)(2,1)S(1)}, bf16[32,3584]{1,0:T(8,128)(2,1)S(1)}, u32[]{:S(2)}, u32[]{:S(2)}) collective-permute-start(bf16[32,3584]{1,0:T(8,128)(2,1)S(1)} %select_bitcast_fusion.2), channel_id=1, source_target_pairs={{32,0},{64,32},{96,64},{128,96},{160,128},{192,160},{224,192},{1,3... | collective-permute-start | bytes 688136 | tf_op jit(solution)/shard_map/ppermute | solution.py:218
  6.0 39.7 %collective-permute-start.7 = (bf16[256,3584]{1,0:T(8,128)(2,1)}, bf16[256,3584]{1,0:T(8,128)(2,1)}, u32[]{:S(2)}, u32[]{:S(2)}) collective-permute-start(bf16[256,3584]{1,0:T(8,128)(2,1)} %bitcast.37), channel_id=1, source_target_pairs={{0,1},{1,0},{2,3},{3,2},{4,5},{5,4},{6,7},{7,6},{8,9},{9,8},{10,11... | collective-permute-start | bytes 5505032 | tf_op jit(solution)/shard_map/ppermute | solution.py:35
  9.0 9.1 %collective-permute-start.1 = (bf16[32,3712]{1,0:T(8,128)(2,1)S(1)}, bf16[32,3712]{1,0:T(8,128)(2,1)S(1)}, u32[]{:S(2)}, u32[]{:S(2)}) collective-permute-start(bf16[32,3712]{1,0:T(8,128)(2,1)S(1)} %concatenate.17.refs_0_), channel_id=1, source_target_pairs={{0,2},{1,9},{2,4},{3,11},{4,6},{5,13},{6,0},{7,15},{8,10},{9,17},{... | collective-permute-start | bytes 712712 | tf_op jit(solution)/shard_map/ppermute | solution.py:31
  10.4 7.7 %collective-permute-start.2 = (bf16[32,3712]{1,0:T(8,128)(2,1)S(1)}, bf16[32,3712]{1,0:T(8,128)(2,1)S(1)}, u32[]{:S(2)}, u32[]{:S(2)}) collective-permute-start(bf16[32,3712]{1,0:T(8,128)(2,1)S(1)} %concatenate.17.refs_0_), channel_id=1, source_target_pairs={{0,6},{1,25},{2,0},{3,27},{4,2},{5,29},{6,4},{7,31},{8,14},{9,1},{... | collective-permute-start | bytes 712712 | tf_op jit(solution)/shard_map/ppermute | solution.py:31
  11.9 7.1 %collective-permute-start.3 = (bf16[32,3712]{1,0:T(8,128)(2,1)S(1)}, bf16[32,3712]{1,0:T(8,128)(2,1)S(1)}, u32[]{:S(2)}, u32[]{:S(2)}) collective-permute-start(bf16[32,3712]{1,0:T(8,128)(2,1)S(1)} %concatenate.17.refs_0_), channel_id=1, source_target_pairs={{0,4},{1,17},{2,6},{3,19},{4,0},{5,21},{6,2},{7,23},{8,12},{9,25},... | collective-permute-start | bytes 712712 | tf_op jit(solution)/shard_map/ppermute | solution.py:31
  15.3 21.9 %collective-permute-start.8 = (bf16[2,256,256]{2,1,0:T(8,128)(2,1)}, bf16[2,256,256]{2,1,0:T(8,128)(2,1)S(1)}, u32[]{:S(2)}, u32[]{:S(2)}) collective-permute-start(bf16[2,256,256]{2,1,0:T(8,128)(2,1)} %get-tuple-element.30), channel_id=1, source_target_pairs={{0,1},{1,0},{2,3},{3,2},{4,5},{5,4},{6,7},{7,6},{8,9},{9,8},{10,11... | collective-permute-start | bytes 786440 | tf_op jit(solution)/shard_map/ppermute | solution.py:35
  21.5 9.4 %collective-permute-start.4 = (bf16[64,3712]{1,0:T(8,128)(2,1)}, bf16[64,3712]{1,0:T(8,128)(2,1)}, u32[]{:S(2)}, u32[]{:S(2)}) collective-permute-start(bf16[64,3712]{1,0:T(8,128)(2,1)} %get-tuple-element.11), channel_id=1, source_target_pairs={{0,8},{1,3},{2,10},{3,5},{4,12},{5,7},{6,14},{7,1},{8,16},{9,11},{... | collective-permute-start | bytes 1425416 | tf_op jit(solution)/shard_map/ppermute | solution.py:31
  22.7 12.7 %collective-permute-start.5 = (bf16[64,3712]{1,0:T(8,128)(2,1)}, bf16[64,3712]{1,0:T(8,128)(2,1)S(1)}, u32[]{:S(2)}, u32[]{:S(2)}) collective-permute-start(bf16[64,3712]{1,0:T(8,128)(2,1)} %get-tuple-element.12), channel_id=1, source_target_pairs={{0,24},{1,7},{2,26},{3,1},{4,28},{5,3},{6,30},{7,5},{8,0},{9,15},{... | collective-permute-start | bytes 1425416 | tf_op jit(solution)/shard_map/ppermute | solution.py:31
  24.3 12.7 %collective-permute-start.6 = (bf16[64,3712]{1,0:T(8,128)(2,1)S(1)}, bf16[64,3712]{1,0:T(8,128)(2,1)S(1)}, u32[]{:S(2)}, u32[]{:S(2)}) collective-permute-start(bf16[64,3712]{1,0:T(8,128)(2,1)S(1)} %get-tuple-element.13), channel_id=1, source_target_pairs={{0,16},{1,5},{2,18},{3,7},{4,20},{5,1},{6,22},{7,3},{8,24},{9,13},... | collective-permute-start | bytes 1425416 | tf_op jit(solution)/shard_map/ppermute | solution.py:31
  37.1 2.6 %copy-start = (bf16[256,3712]{1,0:T(8,128)(2,1)}, bf16[256,3712]{1,0:T(8,128)(2,1)S(1)}, u32[]{:S(2)}) copy-start(bf16[256,3712]{1,0:T(8,128)(2,1)S(1)} %constant_dynamic-update-slice_fusion.rows) | copy-start | bytes 5701636
  37.1 8.1 %copy-start.3 = (s32[2,1,32,2]{2,3,1,0:T(2,128)S(1)}, s32[2,1,32,2]{2,3,1,0:T(2,128)}, u32[]{:S(2)}) copy-start(s32[2,1,32,2]{2,3,1,0:T(2,128)} %param.8) | copy-start | bytes 1540
  39.7 26.6 %collective-permute-start.10 = (bf16[256,3584]{1,0:T(8,128)(2,1)}, bf16[256,3584]{1,0:T(8,128)(2,1)}, u32[]{:S(2)}, u32[]{:S(2)}) collective-permute-start(bf16[256,3584]{1,0:T(8,128)(2,1)} %down_grads.2), channel_id=1, source_target_pairs={{0,1},{1,0},{2,3},{3,2},{4,5},{5,4},{6,7},{7,6},{8,9},{9,8},{10,11... | collective-permute-start | bytes 5505032 | tf_op jit(solution)/shard_map/ppermute | solution.py:35
  45.7 1.5 %copy-start.2 = (bf16[1,1,256,3584]{3,2,1,0:T(8,128)(2,1)S(1)}, bf16[1,1,256,3584]{3,2,1,0:T(8,128)(2,1)}, u32[]{:S(2)}) copy-start(bf16[1,1,256,3584]{3,2,1,0:T(8,128)(2,1)} %param.11) | copy-start | bytes 5505028
  47.2 19.0 %copy-start.1 = (bf16[256,3712]{1,0:T(8,128)(2,1)S(1)}, bf16[256,3712]{1,0:T(8,128)(2,1)}, u32[]{:S(2)}) copy-start(bf16[256,3712]{1,0:T(8,128)(2,1)} %copy-done) | copy-start | bytes 5701636
  51.6 13.8 %collective-permute-start.9 = (bf16[2,256,256]{2,1,0:T(8,128)(2,1)S(1)}, bf16[2,256,256]{2,1,0:T(8,128)(2,1)S(1)}, u32[]{:S(2)}, u32[]{:S(2)}) collective-permute-start(bf16[2,256,256]{2,1,0:T(8,128)(2,1)S(1)} %get-tuple-element.15), channel_id=1, source_target_pairs={{0,1},{1,0},{2,3},{3,2},{4,5},{5,4},{6,7},{7,6},{8,9},{9,8},{10,11... | collective-permute-start | bytes 786440 | tf_op jit(solution)/shard_map/ppermute | solution.py:35
  51.7 12.6 %all-to-all-start = ((f32[32,1,128]{2,1,0:T(1,128)}), f32[32,1,128]{2,1,0:T(1,128)S(1)}, u32[]{:S(2)}, u32[]{:S(2)}) async-start(f32[32,1,128]{2,1,0:T(1,128)} %bitcast.19), calls=%async_computation | async-start | bytes 32768 | tf_op jit(solution)/shard_map/all_to_all | solution.py:251

commit v2 on v1

v2 whole, which is shorter than its diff:
```python
import jax
import jax.numpy as jnp
from jax import lax
from jax.experimental import pallas as pl
from jax.experimental.pallas import tpu as pltpu
from jax.sharding import PartitionSpec as P

route_scale = 2.5
side = 4
shifts = (2, 1, -1)
extra = 128
bf16, f32 = jnp.bfloat16, jnp.float32
params = pltpu.CompilerParams(vmem_limit_bytes=16 * 2**20)
whole = pl.BlockSpec(memory_space=pltpu.VMEM)
scalars = pl.BlockSpec(memory_space=pltpu.SMEM)


def moved(place, step, along_x):
    y, x = place // side, place % side
    return y * side + (x + step) % side if along_x else (y + step) % side * side + x


def plane_shift(value, step, first_along_x):
    pairs = [
        (place * 2 + core, moved(place, step, first_along_x == (core == 0)) * 2 + core)
        for place in range(side * side)
        for core in range(2)
    ]
    return lax.ppermute(value, ("expert", "dp"), pairs)


def swapped(value):
    return lax.ppermute(value, "dp", [(0, 1), (1, 0)])


def select_kernel(info, *refs):
    blocks, outs = refs[:4], refs[4:]
    tokens, width = blocks[0].shape
    width -= extra
    slots = outs[0].shape[0] // 4
    rows, columns = 4 * outs[0].shape[0], 4 * tokens

    def pick(index, base):
        return jnp.where(
            index < 2,
            jnp.where(index == 0, info[base], info[base + 1]),
            jnp.where(index == 2, info[base + 2], info[base + 3]),
        )

    notes = jnp.concatenate([ref[:, width:] for ref in blocks], axis=0).astype(f32).T
    row = lax.broadcasted_iota(jnp.int32, (rows, 1), 0)
    column = lax.broadcasted_iota(jnp.int32, (1, columns), 1)
    expert = pick(row >> 6, 4).astype(f32)
    same = ((row >> 4) & 3) == pick(column >> 5, 0)
    named0 = same & (notes[0:1] == expert)
    named = named0 | (same & (notes[1:2] == expert))
    i = lax.broadcasted_iota(jnp.int32, (columns, columns), 0)
    j = lax.broadcasted_iota(jnp.int32, (columns, columns), 1)
    earlier = jnp.where((i < j) & ((i >> 5) == (j >> 5)), 1.0, 0.0).astype(bf16)
    marked = jnp.where(named, 1.0, 0.0).astype(bf16)
    place = jnp.dot(marked, earlier, preferred_element_type=f32)
    taken = jnp.where(named & (place == (row & 15).astype(f32)), 1.0, 0.0)
    weight = jnp.sum(
        taken * jnp.where(named0, notes[2:3], notes[3:4]), axis=1, keepdims=True
    )
    taken = taken.astype(bf16)

    def put(start, size, value):
        for index, out in enumerate(outs):
            out[:, start : start + size] = value[index * 4 * slots : (index + 1) * 4 * slots]

    put(width, extra, jnp.broadcast_to(weight, (rows, extra)).astype(bf16))
    step = 512 if width % 512 == 0 else width
    for start in range(0, width, step):
        chunk = jnp.concatenate([ref[:, start : start + step] for ref in blocks], axis=0)
        put(start, step, jnp.dot(taken, chunk, preferred_element_type=f32).astype(bf16))


def select_rows(info, blocks, slots):
    shape = jax.ShapeDtypeStruct((4 * slots, blocks[0].shape[1]), bf16)
    return pl.pallas_call(
        select_kernel,
        out_shape=(shape,) * 4,
        in_specs=[scalars] + [whole] * 4,
        out_specs=(whole,) * 4,
        compiler_params=params,
        name="select_rows",
    )(info, *blocks)


def factor_kernel(order, saved, swapped_saved, factors):
    slots = saved.shape[2] // 16
    span = order[16]
    for index, ref in enumerate((swapped_saved, saved)):
        for chunk in range(16):
            at = pl.ds(pl.multiple_of(order[chunk] * slots, slots), slots)
            here = slice(chunk * slots, (chunk + 1) * slots)
            gate, up = ref[span, 0, at, :].astype(f32), ref[span, 1, at, :].astype(f32)
            sigma = jax.nn.sigmoid(gate)
            silu = gate * sigma
            factors[index, 0, here, :] = (silu * up).astype(bf16).astype(f32)
            factors[index, 1, here, :] = up * sigma * (1.0 + gate * (1.0 - sigma))
            factors[index, 2, here, :] = silu


def saved_factors(order, saved, swapped_saved):
    return pl.pallas_call(
        factor_kernel,
        out_shape=jax.ShapeDtypeStruct((2, 3) + saved.shape[2:], f32),
        in_specs=[scalars] + [whole] * 2,
        out_specs=whole,
        compiler_params=params,
        name="saved_factors",
    )(order, saved, swapped_saved)


def down_product(scaled, rows, out, added=None):
    width = out.shape[1]
    step = 512 if width % 512 == 0 else width
    for start in range(0, width, step):
        here = slice(start, start + step)
        value = lax.dot_general(
            scaled, rows[:, here], (((0,), (0,)), ((), ())), preferred_element_type=f32
        )
        if added is not None:
            value = value + added[:, here].astype(f32)
        out[:, here] = value.astype(bf16)


def slot_weights(rows, like):
    weights = rows[:, rows.shape[1] - extra :].astype(f32)
    return jnp.concatenate([weights] * (like.shape[-1] // extra), axis=1)


def raw_kernel(order, rows, mine, other, factors, g_mine, g_other, dots, down_other):
    count = rows.shape[0]
    width = rows.shape[1] - extra
    slots = count // 16
    weights = slot_weights(rows, factors)
    dot = jnp.zeros((count, 1), f32)
    for index, (weight, out) in enumerate(((other, g_other), (mine, g_mine))):
        raw = lax.dot_general(
            rows[:, :width], weight[...], (((1,), (1,)), ((), ())), preferred_element_type=f32
        )
        dot = dot + jnp.sum(factors[index, 0] * raw, axis=1, keepdims=True)
        grad = weights * raw
        for part in range(2):
            value = (grad * factors[index, part + 1]).astype(bf16)
            for chunk in range(16):
                at = pl.ds(pl.multiple_of(order[chunk] * slots, slots), slots)
                out[part, at, :] = value[chunk * slots : (chunk + 1) * slots]
    lane = lax.broadcasted_iota(jnp.int32, (count, 128), 1)
    row = lax.broadcasted_iota(jnp.int32, (count, 128), 0)
    spread = jnp.where(lane == (row & 15), dot, 0.0)
    for chunk in range(16):
        line = jnp.sum(spread[chunk * slots : (chunk + 1) * slots], axis=0, keepdims=True)
        for core in range(2):
            dots[pl.ds(order[chunk] * 2 + core, 1), :] = line
    down_product((weights * factors[0, 0]).astype(bf16), rows, down_other)


def raw_grads(order, rows, mine, other, factors):
    grads = jax.ShapeDtypeStruct((2,) + factors.shape[2:], bf16)
    return pl.pallas_call(
        raw_kernel,
        out_shape=(
            grads,
            grads,
            jax.ShapeDtypeStruct((32, 128), f32),
            jax.ShapeDtypeStruct(mine.shape, bf16),
        ),
        in_specs=[scalars] + [whole] * 4,
        out_specs=(whole,) * 4,
        compiler_params=params,
        name="raw_grads",
    )(order, rows, mine, other, factors)


def finish_kernel(order, rows, factors, g_mine, g_other, down_other, pair_grads, weight_grad):
    span = order[16]
    pair_grads[span] = g_mine[...]
    pair_grads[1 - span] = g_other[...]
    scaled = (slot_weights(rows, factors) * factors[1, 0]).astype(bf16)
    down_product(scaled, rows, weight_grad, down_other)


def finished(order, rows, factors, g_mine, g_other, down_other):
    return pl.pallas_call(
        finish_kernel,
        out_shape=(
            jax.ShapeDtypeStruct((2,) + g_mine.shape, bf16),
            jax.ShapeDtypeStruct(down_other.shape, bf16),
        ),
        in_specs=[scalars] + [whole] * 5,
        out_specs=(whole,) * 2,
        compiler_params=params,
        name="finished",
    )(order, rows, factors, g_mine, g_other, down_other)


def logit_kernel(returned, experts, places, scores, out):
    tokens = scores.shape[1]
    spread = lax.dot_general(
        returned[...],
        experts[...],
        (((0,), (0,)), ((), ())),
        preferred_element_type=f32,
        precision=lax.Precision.HIGHEST,
    )
    route = jnp.sum(spread * places[...], axis=0, keepdims=True)
    for span in range(2):
        first, second = 2 * span, 2 * span + 1
        route0 = route[:, first * tokens : (first + 1) * tokens]
        route1 = route[:, second * tokens : (second + 1) * tokens]
        score0, score1 = scores[first : first + 1], scores[second : second + 1]
        total = score0 + score1
        mean = (route0 * score0 + route1 * score1) / total
        scale = route_scale / total
        out[first : first + 1] = scale * (route0 - mean) * score0 * (1.0 - score0)
        out[second : second + 1] = scale * (route1 - mean) * score1 * (1.0 - score1)


def note_kernel(ids, logits, notes, experts, places, scores):
    tokens = ids.shape[1]
    score = jax.nn.sigmoid(logits[...])
    scores[...] = score
    number = ids[...]
    line = jnp.concatenate([number[row : row + 1] for row in range(4)], axis=1)
    lane = lax.broadcasted_iota(jnp.int32, (1, 4 * tokens), 1)
    source = lax.broadcasted_iota(jnp.int32, (32, 4 * tokens), 0)
    span = lane >> 6
    experts[...] = jnp.where(((source >> 2) == line) & ((source & 1) == span), 1.0, 0.0)
    expert = lax.broadcasted_iota(jnp.int32, (8, 4 * tokens), 0)
    marked = jnp.where(expert == line, 1.0, 0.0)
    i = lax.broadcasted_iota(jnp.int32, (4 * tokens, 4 * tokens), 0)
    j = lax.broadcasted_iota(jnp.int32, (4 * tokens, 4 * tokens), 1)
    earlier = jnp.where(((i >> 6) == (j >> 6)) & ((i & 31) < (j & 31)), 1.0, 0.0)
    before = jnp.dot(marked.astype(bf16), earlier.astype(bf16), preferred_element_type=f32)
    place = jnp.sum(before * marked, axis=0, keepdims=True)
    slot = lax.broadcasted_iota(jnp.int32, (128, 4 * tokens), 0).astype(f32)
    places[...] = jnp.where(slot == place, 1.0, 0.0)
    for span in range(2):
        pair = score[2 * span : 2 * span + 2]
        combine = route_scale * pair / (pair[0:1] + pair[1:2])
        lines = [
            number[2 * span : 2 * span + 2].astype(f32),
            combine,
            jnp.zeros((extra - 4, tokens), f32),
        ]
        table = jnp.concatenate(lines, axis=0)
        table = jnp.concatenate([table, jnp.zeros((extra, extra - tokens), f32)], axis=1)
        notes[span] = table.T[:tokens].astype(bf16)


def slot_notes(ids, logits):
    tokens = ids.shape[1]
    return pl.pallas_call(
        note_kernel,
        out_shape=(
            jax.ShapeDtypeStruct((2, tokens, extra), bf16),
            jax.ShapeDtypeStruct((32, 4 * tokens), f32),
            jax.ShapeDtypeStruct((128, 4 * tokens), f32),
            jax.ShapeDtypeStruct((4, tokens), f32),
        ),
        in_specs=[whole] * 2,
        out_specs=(whole,) * 4,
        compiler_params=params,
        name="slot_notes",
    )(ids, logits)


def local(sent_down, sent_up, expert_ids, router_logits, saved_gate_up, down_weight):
    core = lax.axis_index("dp")
    spot = lax.axis_index("expert")
    y, x = spot >> 2, spot & 3
    first = core == 0
    segments = lax.axis_size("pipe")
    saved = saved_gate_up[:, 0, 0]
    mine = down_weight[0, 0]
    slots = saved.shape[2] // 16
    tokens, top = expert_ids.shape[2:]

    def by_slot(value):
        return jnp.swapaxes(value[:, 0], 1, 2).reshape(2 * top, tokens)

    pairs = [(2 * z, 2 * (z - 1)) for z in range(1, segments)]
    pairs += [(2 * z + 1, 2 * (z + 1) + 1) for z in range(segments - 1)]
    incoming = lax.ppermute(
        jnp.where(first, sent_down[0], sent_up[0]), ("pipe", "dp"), pairs
    )
    other = swapped(mine)
    swapped_saved = swapped(saved)
    notes, experts, places, scores = slot_notes(by_slot(expert_ids), by_slot(router_logits))
    block = jnp.concatenate([incoming, jnp.where(first, notes[0], notes[1])], axis=1)

    near, far = jnp.where(first, x, y), jnp.where(first, y, x)
    blocks = [block] + [plane_shift(block, step, True) for step in shifts]
    held = [near] + [(near + side - step) & 3 for step in shifts]
    targets = [far] + [(far + side + step) & 3 for step in shifts]
    wanted = [jnp.where(first, t * 2 + (x >> 1), y * 2 + (t >> 1)) for t in targets]
    pieces = select_rows(jnp.stack(held + wanted).astype(jnp.int32), blocks, slots)
    pieces = [pieces[0]] + [
        plane_shift(piece, step, False) for piece, step in zip(pieces[1:], shifts, strict=True)
    ]
    rows = jnp.zeros((16 * slots, pieces[0].shape[1]), bf16)
    for piece, step in zip(pieces, (0,) + shifts, strict=True):
        rows = lax.dynamic_update_slice(
            rows, piece, (((far + side - step) & 3) * (4 * slots), jnp.int32(0))
        )
    number = jnp.arange(16, dtype=jnp.int32)
    order = jnp.where(first, number, (number & 3) * 4 + (number >> 2))
    order = jnp.concatenate([order, core[None].astype(jnp.int32)])

    factors = saved_factors(order, saved, swapped_saved)
    g_mine, g_other, dots, down_other = raw_grads(order, rows, mine, other, factors)
    returned = lax.all_to_all(dots, ("expert", "dp"), split_axis=0, concat_axis=0, tiled=True)
    pair_grads, weight_grad = finished(
        order, rows, factors, g_mine, swapped(g_other), swapped(down_other)
    )
    returned, pair_grads, weight_grad = lax.optimization_barrier(
        (returned, pair_grads, weight_grad)
    )
    logit_grads = pl.pallas_call(
        logit_kernel,
        out_shape=jax.ShapeDtypeStruct((2 * top, tokens), f32),
        in_specs=[whole] * 4,
        out_specs=whole,
        compiler_params=params,
        name="logit_grads",
    )(returned, experts, places, scores)
    return (
        pair_grads[:, None, None],
        weight_grad[None, None],
        jnp.swapaxes(logit_grads.reshape(2, 1, top, tokens), 2, 3),
    )


def solution(mesh):
    placed = (
        P("pipe", "expert", None),
        P("pipe", "expert", None),
        P(None, "pipe", "expert", None),
        P(None, "pipe", "expert", None),
        P(None, "pipe", "expert", None, None, "dp"),
        P("pipe", "expert", "dp", None),
    )
    return jax.shard_map(
        local,
        mesh=mesh,
        in_specs=placed,
        out_specs=(
            P(None, "pipe", "expert", None, None, "dp"),
            P("pipe", "expert", "dp", None),
            P(None, "pipe", "expert", None),
        ),
        check_vma=False,
    )
```

time: 70.1 us -> 62.7 us (0.89)
  waiting for transfers between devices: 18.8 us -> 8.2 us
  local copies, waits for them, and re-layouts: 4.07 us -> 9.5 us
  other arithmetic: 5.54 us -> 1.08 us
  starting transfers between devices: 27.3 us -> 29.6 us
    ppermute x6, waiting for transfers between devices: 11 us -> 5.2 us  [plane_shift(): return lax.ppermute(value, ('expert', 'dp'), pairs)]
    unnamed x9 -> x30, local copies, waits for them, and re-layouts: 2.18 us -> 7.95 us
    all_to_all x1, waiting for transfers between devices: 6.75 us -> 1.66 us  [local(): lax.all_to_all(dots, ('expert', 'dp'), split_axis=0, concat_axis=0, tiled...]
    select_n x4 -> x1, other arithmetic: 2.66 us -> 0.01 us  [local(): jnp.where(first, notes[0], notes[1])]
    ppermute x6, starting transfers between devices: 8.66 us -> 11.1 us  [plane_shift(): return lax.ppermute(value, ('expert', 'dp'), pairs)]
    reduce_sum x3 -> x0, other arithmetic: 0.93 us -> none  [the longest x1 0.7 us: local(): jnp.sum(scores, axis=-1, keepdims=True)]
    convert_element_type x4 -> x0, other arithmetic: 0.73 us -> none  [the longest x1 0.7 us: local(): my_ids = jnp.where(first, ids[0], ids[1]).astype(bf16)]
    pallas_call x4 -> x5, Pallas kernels: 10.8 us -> 10.1 us  [the longest x1 4.46 us: raw_grads(): pl.pallas_call(raw_kernel, out_shape=(grads, grads, jax.ShapeDtypeStruct(...]
  transfers between devices with their start and end apart: 12 -> 12, of which waited for: 6 -> 7; matrix products, arithmetic and copies ran while one was open for 10% -> 3% of each run, Pallas kernels for 14% -> 11%
where the time goes in v2:
time: 62.7 us; the launch traced here: 61.8 us
  starting transfers between devices  29.6 us (47%)
  Pallas kernels  12.6 us (20%)
  local copies, waits for them, and re-layouts  9.5 us (15%)
  waiting for transfers between devices  8.2 us (13%)
  other arithmetic  1.08 us (2%)
  between operations  0.82 us (1%)
    ppermute x6, starting transfers between devices, plane_shift(): return lax.ppermute(value, ('expert', 'dp'), pairs)  11.1 us
    ppermute x4, starting transfers between devices, swapped(): return lax.ppermute(value, 'dp', [(0, 1), (1, 0)])  7.98 us
    unnamed x30, local copies, waits for them, and re-layouts  7.95 us
    all_to_all x1, starting transfers between devices, local(): lax.all_to_all(dots, ('expert', 'dp'), split_axis=0, concat_axis=0, tiled...  6.09 us
    ppermute x6, waiting for transfers between devices, plane_shift(): return lax.ppermute(value, ('expert', 'dp'), pairs)  5.2 us
    pallas_call x1, Pallas kernels, raw_grads(): pl.pallas_call(raw_kernel, out_shape=(grads, grads, jax.ShapeDtypeStruct(...  4.46 us
    ppermute x1, starting transfers between devices, local(): lax.ppermute(jnp.where(first, sent_down[0], sent_up[0]), ('pipe', 'dp'),...  4.38 us
    pallas_call x1, Pallas kernels, finished(): pl.pallas_call(finish_kernel, out_shape=(jax.ShapeDtypeStruct((2,) + g_mi...  3.65 us
  transfers between devices with their start and end apart: 12, of which 7 were waited for; matrix products, arithmetic and copies ran while one was open for 3% of the time, Pallas kernels for 11%

profile of v2, /device:TPU:1, one launch (start us, length us, event | category | flops | bytes accessed | tf_op | source)
XLA Modules:
  0.0 61.8 jit_solution(9648871595309143069)
XLA Ops:
  0.6 1.0 %select_bitcast_fusion = bf16[32,3584]{1,0:T(8,128)(2,1)S(1)} fusion(bf16[1,32,3584]{2,1,0:T(8,128)(2,1)} %param.6, bf16[1,32,3584]{2,1,0:T(8,128)(2,1)} %param.7, pred[]{:T(512)S(6)} %eq.3), kind=kLoop, calls=%fused_computation.1 | loop fusion | flops 114688 | bytes 688129 | tf_op jit(solution)/shard_map/jit(_where)/select_n | solution.py:289
  1.6 4.4 %collective-permute-start = (bf16[32,3584]{1,0:T(8,128)(2,1)S(1)}, bf16[32,3584]{1,0:T(8,128)(2,1)S(1)}, u32[]{:S(2)}, u32[]{:S(2)}) collective-permute-start(bf16[32,3584]{1,0:T(8,128)(2,1)S(1)} %select_bitcast_fusion), channel_id=1, source_target_pairs={{32,0},{64,32},{96,64},{128,96},{160,128},{192,160},{224,192},{1,3... | collective-permute-start | bytes 688136 | tf_op jit(solution)/shard_map/ppermute | solution.py:288
  6.0 0.0 copy-start.13
  6.0 0.7 %copy-done.13 = s32[2,1,32,2]{2,3,1,0:T(2,128)S(1)} copy-done((s32[2,1,32,2]{2,3,1,0:T(2,128)S(1)}, s32[2,1,32,2]{2,3,1,0:T(2,128)}, u32[]{:S(2)}) %copy-start.13) | copy-done | bytes 536
  6.7 0.0 copy-start.14
  6.7 0.7 %copy-done.14 = f32[2,1,32,2]{2,3,1,0:T(2,128)S(1)} copy-done((f32[2,1,32,2]{2,3,1,0:T(2,128)S(1)}, f32[2,1,32,2]{2,3,1,0:T(2,128)}, u32[]{:S(2)}) %copy-start.14) | copy-done | bytes 536
  7.4 0.2 slot_notes.1
  7.6 0.0 copy-start.6
  7.6 0.0 copy-start.11
  7.6 1.3 %collective-permute-done = bf16[32,3584]{1,0:T(8,128)(2,1)S(1)} collective-permute-done((bf16[32,3584]{1,0:T(8,128)(2,1)S(1)}, bf16[32,3584]{1,0:T(8,128)(2,1)S(1)}, u32[]{:S(2)}, u32[]{:S(2)}) %collective-permute-start) | collective-permute-done | bytes 229408 | tf_op jit(solution)/shard_map/ppermute | solution.py:288
  9.0 3.0 %collective-permute-start.1 = (bf16[32,3712]{1,0:T(8,128)(2,1)S(1)}, bf16[32,3712]{1,0:T(8,128)(2,1)S(1)}, u32[]{:S(2)}, u32[]{:S(2)}) collective-permute-start(bf16[32,3712]{1,0:T(8,128)(2,1)S(1)} %pad_maximum_fusion.refs_0_), channel_id=1, source_target_pairs={{0,4},{1,17},{2,6},{3,19},{4,0},{5,21},{6,2},{7,23},{8,12},{9,25},... | collective-permute-start | bytes 712712 | tf_op jit(solution)/shard_map/ppermute | solution.py:29
  12.0 0.4 collective-permute-start.2
  12.4 2.3 %collective-permute-start.3 = (bf16[32,3712]{1,0:T(8,128)(2,1)S(1)}, bf16[32,3712]{1,0:T(8,128)(2,1)S(1)}, u32[]{:S(2)}, u32[]{:S(2)}) collective-permute-start(bf16[32,3712]{1,0:T(8,128)(2,1)S(1)} %pad_maximum_fusion.refs_0_), channel_id=1, source_target_pairs={{0,6},{1,25},{2,0},{3,27},{4,2},{5,29},{6,4},{7,31},{8,14},{9,1},{... | collective-permute-start | bytes 712712 | tf_op jit(solution)/shard_map/ppermute | solution.py:29
  14.6 2.8 %collective-permute-start.7 = (bf16[256,3584]{1,0:T(8,128)(2,1)}, bf16[256,3584]{1,0:T(8,128)(2,1)}, u32[]{:S(2)}, u32[]{:S(2)}) collective-permute-start(bf16[256,3584]{1,0:T(8,128)(2,1)} %bitcast.38), channel_id=1, source_target_pairs={{0,1},{1,0},{2,3},{3,2},{4,5},{5,4},{6,7},{7,6},{8,9},{9,8},{10,11... | collective-permute-start | bytes 5505032 | tf_op jit(solution)/shard_map/ppermute | solution.py:33
  17.4 0.0 copy-done.6
  17.4 0.0 copy-done.11
  17.4 0.1 collective-permute-start.8
  17.5 0.1 stack.35.info
  17.6 0.0 collective-permute-done.1.refs_1_
  17.6 0.8 %collective-permute-done.2.refs_2_ = bf16[32,3712]{1,0:T(8,128)(2,1)S(1)} collective-permute-done((bf16[32,3712]{1,0:T(8,128)(2,1)S(1)}, bf16[32,3712]{1,0:T(8,128)(2,1)S(1)}, u32[]{:S(2)}, u32[]{:S(2)}) %collective-permute-start.2) | collective-permute-done | bytes 237600 | tf_op jit(solution)/shard_map/ppermute | solution.py:29
  18.4 0.3 collective-permute-done.3.refs_3_
  18.7 2.5 %select_rows.1 = (bf16[64,3712]{1,0:T(8,128)(2,1)S(1)}, bf16[64,3712]{1,0:T(8,128)(2,1)}, bf16[64,3712]{1,0:T(8,128)(2,1)}, bf16[64,3712]{1,0:T(8,128)(2,1)}) custom-call(s32[8]{0:T(128)S(1)} %stack.35.info, bf16[32,3712]{1,0:T(8,128)(2,1)S(1)} %pad_maximum_fusion.refs_0_, bf16[32,3712]{1,0:T(8,128)(2,1)S(1)} %collective-permute-done.1.refs_1_, ...), custom_call_target="tpu_custom_call" | custom-call | tf_op jit(solution)/shard_map/select_rows/pallas_call | solution.py:81
  21.2 2.7 %collective-permute-start.4 = (bf16[64,3712]{1,0:T(8,128)(2,1)}, bf16[64,3712]{1,0:T(8,128)(2,1)}, u32[]{:S(2)}, u32[]{:S(2)}) collective-permute-start(bf16[64,3712]{1,0:T(8,128)(2,1)} %get-tuple-element.22), channel_id=1, source_target_pairs={{0,16},{1,5},{2,18},{3,7},{4,20},{5,1},{6,22},{7,3},{8,24},{9,13},... | collective-permute-start | bytes 1425416 | tf_op jit(solution)/shard_map/ppermute | solution.py:29
  23.9 0.1 pad_add_fusion.order
  24.0 0.0 copy-start.9
  24.0 0.3 collective-permute-start.5
  24.3 2.4 %collective-permute-start.6 = (bf16[64,3712]{1,0:T(8,128)(2,1)}, bf16[64,3712]{1,0:T(8,128)(2,1)S(1)}, u32[]{:S(2)}, u32[]{:S(2)}) collective-permute-start(bf16[64,3712]{1,0:T(8,128)(2,1)} %get-tuple-element.24), channel_id=1, source_target_pairs={{0,24},{1,7},{2,26},{3,1},{4,28},{5,3},{6,30},{7,5},{8,0},{9,15},{... | collective-permute-start | bytes 1425416 | tf_op jit(solution)/shard_map/ppermute | solution.py:29
  26.7 0.1 broadcast_in_dim.13
  26.9 0.0 collective-permute-done.8.swapped_saved
  26.9 0.0 copy-start.2
  26.9 0.8 %copy-done.2 = bf16[2,2,256,256]{3,2,1,0:T(8,128)(2,1)} copy-done((bf16[2,2,256,256]{3,2,1,0:T(8,128)(2,1)}, bf16[2,2,256,256]{3,2,1,0:T(8,128)(2,1)S(1)}, u32[]{:S(2)}) %copy-start.2) | copy-done | bytes 524312
  27.7 0.0 copy-start.1
  27.7 1.0 %copy-done.1 = bf16[2,1,1,2,256,256]{5,4,3,2,1,0:T(8,128)(2,1)S(1)} copy-done((bf16[2,1,1,2,256,256]{5,4,3,2,1,0:T(8,128)(2,1)S(1)}, bf16[2,1,1,2,256,256]{5,4,3,2,1,0:T(8,128)(2,1)}, u32[]{:S(2)}) %copy-start.1) | copy-done | bytes 524312
  28.7 0.0 copy-start.3
  28.7 1.0 %copy-done.3 = bf16[2,2,256,256]{3,2,1,0:T(8,128)(2,1)S(1)} copy-done((bf16[2,2,256,256]{3,2,1,0:T(8,128)(2,1)S(1)}, bf16[2,2,256,256]{3,2,1,0:T(8,128)(2,1)}, u32[]{:S(2)}) %copy-start.3) | copy-done | bytes 524312
  29.8 0.8 %saved_factors.1.factors = f32[2,3,256,256]{3,2,1,0:T(8,128)S(1)} custom-call(s32[17]{0:T(128)S(1)} %pad_add_fusion.order, bf16[2,2,256,256]{3,2,1,0:T(8,128)(2,1)S(1)} %bitcast.41, bf16[2,2,256,256]{3,2,1,0:T(8,128)(2,1)S(1)} %copy-done.3), custom_call_target="tpu_custom_call" | custom-call | tf_op jit(solution)/shard_map/saved_factors/pallas_call | solution.py:107
  30.5 0.0 copy-start
  30.5 0.3 collective-permute-done.4
  30.8 1.2 %constant_dynamic-update-slice_fusion.2 = bf16[256,3712]{1,0:T(8,128)(2,1)S(1)} fusion(bf16[256,3712]{1,0:T(8,128)(2,1)S(1)} %constant_dynamic-update-slice_fusion.3, bf16[64,3712]{1,0:T(8,128)(2,1)} %collective-permute-done.4, s32[]{:T(128)S(6)} %select_n.76), kind=kLoop, calls=%fused_computation.5 | loop fusion | bytes 950276 | tf_op jit(solution)/shard_map/dynamic_update_slice | solution.py:307
  32.0 3.7 %collective-permute-done.5 = bf16[64,3712]{1,0:T(8,128)(2,1)S(1)} collective-permute-done((bf16[64,3712]{1,0:T(8,128)(2,1)}, bf16[64,3712]{1,0:T(8,128)(2,1)S(1)}, u32[]{:S(2)}, u32[]{:S(2)}) %collective-permute-start.5) | collective-permute-done | bytes 475168 | tf_op jit(solution)/shard_map/ppermute | solution.py:29
  35.8 0.1 collective-permute-done.6
  35.9 0.0 collective-permute-done.7.other
  36.0 0.0 copy-done.9
  36.0 0.0 copy-done
  36.0 4.5 %raw_grads.1 = (bf16[2,256,256]{2,1,0:T(8,128)(2,1)S(1)}, bf16[2,256,256]{2,1,0:T(8,128)(2,1)}, f32[32,128]{1,0:T(8,128)S(1)}, bf16[256,3584]{1,0:T(8,128)(2,1)}) custom-call(s32[17]{0:T(128)S(1)} %pad_add_fusion.order, bf16[256,3712]{1,0:T(8,128)(2,1)S(1)} %constant_dynamic-update-slice_fusion.rows, bf16[256,3584]{1,0:T(8,128)(2,1)S(1)} %bitcast.39, ...), custom_call_target="tpu_custom_call" | custom-call | tf_op jit(solution)/shard_map/raw_grads/pallas_call | solution.py:164
  40.4 0.0 copy-start.4
  40.4 0.7 %copy-done.4 = bf16[2,256,256]{2,1,0:T(8,128)(2,1)} copy-done((bf16[2,256,256]{2,1,0:T(8,128)(2,1)}, bf16[2,256,256]{2,1,0:T(8,128)(2,1)S(1)}, u32[]{:S(2)}) %copy-start.4) | copy-done | bytes 262168
  41.1 0.0 copy-start.8
  41.1 5.1 %collective-permute-start.10 = (bf16[256,3584]{1,0:T(8,128)(2,1)}, bf16[256,3584]{1,0:T(8,128)(2,1)}, u32[]{:S(2)}, u32[]{:S(2)}) collective-permute-start(bf16[256,3584]{1,0:T(8,128)(2,1)} %get-tuple-element.28), channel_id=1, source_target_pairs={{0,1},{1,0},{2,3},{3,2},{4,5},{5,4},{6,7},{7,6},{8,9},{9,8},{10,11... | collective-permute-start | bytes 5505032 | tf_op jit(solution)/shard_map/ppermute | solution.py:33
  46.3 0.0 collective-permute-start.9
  46.3 0.0 copy-done.8
  46.3 6.1 %all-to-all-start = ((f32[32,1,128]{2,1,0:T(1,128)}), f32[32,1,128]{2,1,0:T(1,128)S(1)}, u32[]{:S(2)}, u32[]{:S(2)}) async-start(f32[32,1,128]{2,1,0:T(1,128)} %bitcast.43), calls=%async_computation | async-start | bytes 32768 | tf_op jit(solution)/shard_map/all_to_all | solution.py:316
  52.4 0.0 collective-permute-done.9.g_other
  52.4 0.0 collective-permute-done.10.down_other
  52.4 0.0 copy-start.5
  52.4 0.9 %copy-done.5 = bf16[2,256,256]{2,1,0:T(8,128)(2,1)S(1)} copy-done((bf16[2,256,256]{2,1,0:T(8,128)(2,1)S(1)}, bf16[2,256,256]{2,1,0:T(8,128)(2,1)}, u32[]{:S(2)}) %copy-start.5) | copy-done | bytes 262168
  53.3 0.0 copy-start.10
  53.3 0.7 %copy-done.10 = s32[17]{0:T(128)S(1)} copy-done((s32[17]{0:T(128)S(1)}, s32[17]{0:T(128)}, u32[]{:S(2)}) %copy-start.10) | copy-done | bytes 92
  54.0 3.6 %finished.1 = (bf16[2,2,256,256]{3,2,1,0:T(8,128)(2,1)}, bf16[256,3584]{1,0:T(8,128)(2,1)}) custom-call(s32[17]{0:T(128)S(1)} %copy-done.10, bf16[256,3712]{1,0:T(8,128)(2,1)S(1)} %constant_dynamic-update-slice_fusion.rows, f32[2,3,256,256]{3,2,1,0:T(8,128)S(1)} %saved_factors.1.factors, bf16[2,256,256]{2,1,0:T(8,128)(2,1)S(1)} %copy-done.5, ...), custom_call_target="tpu_custom_call" | custom-call | tf_op jit(solution)/shard_map/finished/pallas_call | solution.py:188
  57.6 1.7 %all-to-all-done = f32[32,1,128]{2,1,0:T(1,128)S(1)} async-done(((f32[32,1,128]{2,1,0:T(1,128)}), f32[32,1,128]{2,1,0:T(1,128)S(1)}, u32[]{:S(2)}, u32[]{:S(2)}) %all-to-all-start) | async-done | bytes 16416 | tf_op jit(solution)/shard_map/all_to_all | solution.py:316
  59.3 0.0 copy-start.7
  59.3 0.7 %copy-done.7 = f32[32,128]{1,0:T(8,128)S(1)} copy-done((f32[32,128]{1,0:T(8,128)S(1)}, f32[32,128]{1,0:T(8,128)}, u32[]{:S(2)}) %copy-start.7) | copy-done | bytes 16408
  60.0 0.7 %copy-done.12 = f32[4,32]{1,0:T(4,128)S(1)} copy-done((f32[4,32]{1,0:T(4,128)S(1)}, f32[4,32]{1,0:T(4,128)}, u32[]{:S(2)}) %copy-start.12) | copy-done | bytes 536
  60.7 1.1 %logit_grads.1 = f32[4,32]{1,0:T(4,128)} custom-call(f32[32,128]{1,0:T(8,128)S(1)} %bitcast.42, f32[32,128]{1,0:T(8,128)S(1)} %copy-done.7, f32[128,128]{1,0:T(8,128)S(1)} %get-tuple-element.35.places, f32[4,32]{1,0:T(4,128)S(1)} %copy-done.12), custom_call_target="tpu_custom_call" | custom-call | tf_op jit(solution)/shard_map/logit_grads/pallas_call | solution.py:323
  (7 shorter events, 0.2 us)
Async XLA Ops:
  1.6 7.3 %collective-permute-start = (bf16[32,3584]{1,0:T(8,128)(2,1)S(1)}, bf16[32,3584]{1,0:T(8,128)(2,1)S(1)}, u32[]{:S(2)}, u32[]{:S(2)}) collective-permute-start(bf16[32,3584]{1,0:T(8,128)(2,1)S(1)} %select_bitcast_fusion), channel_id=1, source_target_pairs={{32,0},{64,32},{96,64},{128,96},{160,128},{192,160},{224,192},{1,3... | collective-permute-start | bytes 688136 | tf_op jit(solution)/shard_map/ppermute | solution.py:288
  6.0 0.7 %copy-start.13 = (s32[2,1,32,2]{2,3,1,0:T(2,128)S(1)}, s32[2,1,32,2]{2,3,1,0:T(2,128)}, u32[]{:S(2)}) copy-start(s32[2,1,32,2]{2,3,1,0:T(2,128)} %param.8) | copy-start | bytes 1540
  6.7 0.7 %copy-start.14 = (f32[2,1,32,2]{2,3,1,0:T(2,128)S(1)}, f32[2,1,32,2]{2,3,1,0:T(2,128)}, u32[]{:S(2)}) copy-start(f32[2,1,32,2]{2,3,1,0:T(2,128)} %param.9) | copy-start | bytes 1540
  7.6 9.8 %copy-start.6 = (f32[32,128]{1,0:T(8,128)}, f32[32,128]{1,0:T(8,128)S(1)}, u32[]{:S(2)}) copy-start(f32[32,128]{1,0:T(8,128)S(1)} %get-tuple-element.34.experts) | copy-start | bytes 49156
  7.6 9.8 %copy-start.11 = (f32[4,32]{1,0:T(4,128)}, f32[4,32]{1,0:T(4,128)S(1)}, u32[]{:S(2)}) copy-start(f32[4,32]{1,0:T(4,128)S(1)} %get-tuple-element.36.scores) | copy-start | bytes 1540
  9.0 8.6 %collective-permute-start.1 = (bf16[32,3712]{1,0:T(8,128)(2,1)S(1)}, bf16[32,3712]{1,0:T(8,128)(2,1)S(1)}, u32[]{:S(2)}, u32[]{:S(2)}) collective-permute-start(bf16[32,3712]{1,0:T(8,128)(2,1)S(1)} %pad_maximum_fusion.refs_0_), channel_id=1, source_target_pairs={{0,4},{1,17},{2,6},{3,19},{4,0},{5,21},{6,2},{7,23},{8,12},{9,25},... | collective-permute-start | bytes 712712 | tf_op jit(solution)/shard_map/ppermute | solution.py:29
  12.0 6.5 %collective-permute-start.2 = (bf16[32,3712]{1,0:T(8,128)(2,1)S(1)}, bf16[32,3712]{1,0:T(8,128)(2,1)S(1)}, u32[]{:S(2)}, u32[]{:S(2)}) collective-permute-start(bf16[32,3712]{1,0:T(8,128)(2,1)S(1)} %pad_maximum_fusion.refs_0_), channel_id=1, source_target_pairs={{0,2},{1,9},{2,4},{3,11},{4,6},{5,13},{6,0},{7,15},{8,10},{9,17},{... | collective-permute-start | bytes 712712 | tf_op jit(solution)/shard_map/ppermute | solution.py:29
  12.4 6.3 %collective-permute-start.3 = (bf16[32,3712]{1,0:T(8,128)(2,1)S(1)}, bf16[32,3712]{1,0:T(8,128)(2,1)S(1)}, u32[]{:S(2)}, u32[]{:S(2)}) collective-permute-start(bf16[32,3712]{1,0:T(8,128)(2,1)S(1)} %pad_maximum_fusion.refs_0_), channel_id=1, source_target_pairs={{0,6},{1,25},{2,0},{3,27},{4,2},{5,29},{6,4},{7,31},{8,14},{9,1},{... | collective-permute-start | bytes 712712 | tf_op jit(solution)/shard_map/ppermute | solution.py:29
  14.6 21.3 %collective-permute-start.7 = (bf16[256,3584]{1,0:T(8,128)(2,1)}, bf16[256,3584]{1,0:T(8,128)(2,1)}, u32[]{:S(2)}, u32[]{:S(2)}) collective-permute-start(bf16[256,3584]{1,0:T(8,128)(2,1)} %bitcast.38), channel_id=1, source_target_pairs={{0,1},{1,0},{2,3},{3,2},{4,5},{5,4},{6,7},{7,6},{8,9},{9,8},{10,11... | collective-permute-start | bytes 5505032 | tf_op jit(solution)/shard_map/ppermute | solution.py:33
  17.4 9.5 %collective-permute-start.8 = (bf16[2,2,256,256]{3,2,1,0:T(8,128)(2,1)}, bf16[2,2,256,256]{3,2,1,0:T(8,128)(2,1)S(1)}, u32[]{:S(2)}, u32[]{:S(2)}) collective-permute-start(bf16[2,2,256,256]{3,2,1,0:T(8,128)(2,1)} %bitcast.40), channel_id=1, source_target_pairs={{0,1},{1,0},{2,3},{3,2},{4,5},{5,4},{6,7},{7,6},{8,9},{9,8},{10,11... | collective-permute-start | bytes 1572872 | tf_op jit(solution)/shard_map/ppermute | solution.py:33
  21.2 9.7 %collective-permute-start.4 = (bf16[64,3712]{1,0:T(8,128)(2,1)}, bf16[64,3712]{1,0:T(8,128)(2,1)}, u32[]{:S(2)}, u32[]{:S(2)}) collective-permute-start(bf16[64,3712]{1,0:T(8,128)(2,1)} %get-tuple-element.22), channel_id=1, source_target_pairs={{0,16},{1,5},{2,18},{3,7},{4,20},{5,1},{6,22},{7,3},{8,24},{9,13},... | collective-permute-start | bytes 1425416 | tf_op jit(solution)/shard_map/ppermute | solution.py:29
  24.0 12.0 %copy-start.9 = (s32[17]{0:T(128)}, s32[17]{0:T(128)S(1)}, u32[]{:S(2)}) copy-start(s32[17]{0:T(128)S(1)} %pad_add_fusion.order) | copy-start | bytes 208
  24.0 11.8 %collective-permute-start.5 = (bf16[64,3712]{1,0:T(8,128)(2,1)}, bf16[64,3712]{1,0:T(8,128)(2,1)S(1)}, u32[]{:S(2)}, u32[]{:S(2)}) collective-permute-start(bf16[64,3712]{1,0:T(8,128)(2,1)} %get-tuple-element.23), channel_id=1, source_target_pairs={{0,8},{1,3},{2,10},{3,5},{4,12},{5,7},{6,14},{7,1},{8,16},{9,11},{... | collective-permute-start | bytes 1425416 | tf_op jit(solution)/shard_map/ppermute | solution.py:29
  24.3 11.6 %collective-permute-start.6 = (bf16[64,3712]{1,0:T(8,128)(2,1)}, bf16[64,3712]{1,0:T(8,128)(2,1)S(1)}, u32[]{:S(2)}, u32[]{:S(2)}) collective-permute-start(bf16[64,3712]{1,0:T(8,128)(2,1)} %get-tuple-element.24), channel_id=1, source_target_pairs={{0,24},{1,7},{2,26},{3,1},{4,28},{5,3},{6,30},{7,5},{8,0},{9,15},{... | collective-permute-start | bytes 1425416 | tf_op jit(solution)/shard_map/ppermute | solution.py:29
  26.9 0.8 %copy-start.2 = (bf16[2,2,256,256]{3,2,1,0:T(8,128)(2,1)}, bf16[2,2,256,256]{3,2,1,0:T(8,128)(2,1)S(1)}, u32[]{:S(2)}) copy-start(bf16[2,2,256,256]{3,2,1,0:T(8,128)(2,1)S(1)} %collective-permute-done.8.swapped_saved) | copy-start | bytes 1572868
  27.7 1.0 %copy-start.1 = (bf16[2,1,1,2,256,256]{5,4,3,2,1,0:T(8,128)(2,1)S(1)}, bf16[2,1,1,2,256,256]{5,4,3,2,1,0:T(8,128)(2,1)}, u32[]{:S(2)}) copy-start(bf16[2,1,1,2,256,256]{5,4,3,2,1,0:T(8,128)(2,1)} %param.10) | copy-start | bytes 1572868
  28.7 1.0 %copy-start.3 = (bf16[2,2,256,256]{3,2,1,0:T(8,128)(2,1)S(1)}, bf16[2,2,256,256]{3,2,1,0:T(8,128)(2,1)}, u32[]{:S(2)}) copy-start(bf16[2,2,256,256]{3,2,1,0:T(8,128)(2,1)} %copy-done.2) | copy-start | bytes 1572868
  30.5 5.4 %copy-start = (bf16[1,1,256,3584]{3,2,1,0:T(8,128)(2,1)S(1)}, bf16[1,1,256,3584]{3,2,1,0:T(8,128)(2,1)}, u32[]{:S(2)}) copy-start(bf16[1,1,256,3584]{3,2,1,0:T(8,128)(2,1)} %param.11) | copy-start | bytes 5505028
  40.4 0.7 %copy-start.4 = (bf16[2,256,256]{2,1,0:T(8,128)(2,1)}, bf16[2,256,256]{2,1,0:T(8,128)(2,1)S(1)}, u32[]{:S(2)}) copy-start(bf16[2,256,256]{2,1,0:T(8,128)(2,1)S(1)} %get-tuple-element.26.g_mine) | copy-start | bytes 786436
  41.1 5.1 %copy-start.8 = (f32[32,128]{1,0:T(8,128)}, f32[32,128]{1,0:T(8,128)S(1)}, u32[]{:S(2)}) copy-start(f32[32,128]{1,0:T(8,128)S(1)} %get-tuple-element.25) | copy-start | bytes 49156
  41.1 11.2 %collective-permute-start.10 = (bf16[256,3584]{1,0:T(8,128)(2,1)}, bf16[256,3584]{1,0:T(8,128)(2,1)}, u32[]{:S(2)}, u32[]{:S(2)}) collective-permute-start(bf16[256,3584]{1,0:T(8,128)(2,1)} %get-tuple-element.28), channel_id=1, source_target_pairs={{0,1},{1,0},{2,3},{3,2},{4,5},{5,4},{6,7},{7,6},{8,9},{9,8},{10,11... | collective-permute-start | bytes 5505032 | tf_op jit(solution)/shard_map/ppermute | solution.py:33
  46.3 6.1 %collective-permute-start.9 = (bf16[2,256,256]{2,1,0:T(8,128)(2,1)}, bf16[2,256,256]{2,1,0:T(8,128)(2,1)}, u32[]{:S(2)}, u32[]{:S(2)}) collective-permute-start(bf16[2,256,256]{2,1,0:T(8,128)(2,1)} %get-tuple-element.27), channel_id=1, source_target_pairs={{0,1},{1,0},{2,3},{3,2},{4,5},{5,4},{6,7},{7,6},{8,9},{9,8},{10,11... | collective-permute-start | bytes 786440 | tf_op jit(solution)/shard_map/ppermute | solution.py:33
  46.3 13.0 %all-to-all-start = ((f32[32,1,128]{2,1,0:T(1,128)}), f32[32,1,128]{2,1,0:T(1,128)S(1)}, u32[]{:S(2)}, u32[]{:S(2)}) async-start(f32[32,1,128]{2,1,0:T(1,128)} %bitcast.43), calls=%async_computation | async-start | bytes 32768 | tf_op jit(solution)/shard_map/all_to_all | solution.py:316
  52.4 1.0 %copy-start.5 = (bf16[2,256,256]{2,1,0:T(8,128)(2,1)S(1)}, bf16[2,256,256]{2,1,0:T(8,128)(2,1)}, u32[]{:S(2)}) copy-start(bf16[2,256,256]{2,1,0:T(8,128)(2,1)} %copy-done.4) | copy-start | bytes 786436
  53.3 0.7 %copy-start.10 = (s32[17]{0:T(128)S(1)}, s32[17]{0:T(128)}, u32[]{:S(2)}) copy-start(s32[17]{0:T(128)} %copy-done.9) | copy-start | bytes 208
  59.3 0.7 %copy-start.7 = (f32[32,128]{1,0:T(8,128)S(1)}, f32[32,128]{1,0:T(8,128)}, u32[]{:S(2)}) copy-start(f32[32,128]{1,0:T(8,128)} %copy-done.6) | copy-start | bytes 49156
  60.0 0.7 %copy-start.12 = (f32[4,32]{1,0:T(4,128)S(1)}, f32[4,32]{1,0:T(4,128)}, u32[]{:S(2)}) copy-start(f32[4,32]{1,0:T(4,128)} %copy-done.11) | copy-start | bytes 1540

commit v3 on v2

v3 whole, which is shorter than its diff:
```python
import jax
import jax.numpy as jnp
from jax import lax
from jax.experimental import pallas as pl
from jax.experimental.pallas import tpu as pltpu
from jax.sharding import PartitionSpec as P

route_scale = 2.5
side = 4
shifts = (2, 1, -1)
extra = 128
bf16, f32 = jnp.bfloat16, jnp.float32
params = pltpu.CompilerParams(vmem_limit_bytes=16 * 2**20)
whole = pl.BlockSpec(memory_space=pltpu.VMEM)


def moved(place, step, along_x):
    y, x = place // side, place % side
    return y * side + (x + step) % side if along_x else (y + step) % side * side + x


def plane_shift(value, step, first_along_x):
    pairs = [
        (place * 2 + core, moved(place, step, first_along_x == (core == 0)) * 2 + core)
        for place in range(side * side)
        for core in range(2)
    ]
    return lax.ppermute(value, ("expert", "dp"), pairs)


def swapped(value):
    return lax.ppermute(value, "dp", [(0, 1), (1, 0)])


def position():
    core, spot = lax.axis_index("dp"), lax.axis_index("expert")
    y, x = spot >> 2, spot & 3
    return core, jnp.where(core == 0, x, y), jnp.where(core == 0, y, x)


def token_blocks(core, far):
    places = [(far + side - step) & 3 for step in (0,) + shifts]
    return [
        jnp.where(core == 0, place * 4 + chunk, chunk * 4 + place)
        for place in places
        for chunk in range(side)
    ]


def select_kernel(*refs):
    blocks, outs = refs[:4], refs[4:]
    core, near, far = position()
    held = [(near + side - step) & 3 for step in (0,) + shifts]
    targets = [(far + side + step) & 3 for step in (0,) + shifts]
    wanted = [jnp.where(core == 0, t * 2 + (near >> 1), near * 2 + (t >> 1)) for t in targets]
    tokens, width = blocks[0].shape
    width -= extra
    slots = outs[0].shape[0] // 4
    rows, columns = 4 * outs[0].shape[0], 4 * tokens

    def pick(index, values):
        return jnp.where(
            index < 2,
            jnp.where(index == 0, values[0], values[1]),
            jnp.where(index == 2, values[2], values[3]),
        )

    notes = jnp.concatenate([ref[:, width:] for ref in blocks], axis=0).astype(f32).T
    row = lax.broadcasted_iota(jnp.int32, (rows, 1), 0)
    column = lax.broadcasted_iota(jnp.int32, (1, columns), 1)
    expert = pick(row >> 6, wanted).astype(f32)
    same = ((row >> 4) & 3) == pick(column >> 5, held)
    named0 = same & (notes[0:1] == expert)
    named = named0 | (same & (notes[1:2] == expert))
    i = lax.broadcasted_iota(jnp.int32, (columns, columns), 0)
    j = lax.broadcasted_iota(jnp.int32, (columns, columns), 1)
    earlier = jnp.where((i < j) & ((i >> 5) == (j >> 5)), 1.0, 0.0).astype(bf16)
    marked = jnp.where(named, 1.0, 0.0).astype(bf16)
    place = jnp.dot(marked, earlier, preferred_element_type=f32)
    taken = jnp.where(named & (place == (row & 15).astype(f32)), 1.0, 0.0)
    weight = jnp.sum(
        taken * jnp.where(named0, notes[2:3], notes[3:4]), axis=1, keepdims=True
    )
    taken = taken.astype(bf16)

    def put(start, size, value):
        for index, out in enumerate(outs):
            out[:, start : start + size] = value[index * 4 * slots : (index + 1) * 4 * slots]

    put(width, extra, jnp.broadcast_to(weight, (rows, extra)).astype(bf16))
    step = 512 if width % 512 == 0 else width
    for start in range(0, width, step):
        chunk = jnp.concatenate([ref[:, start : start + step] for ref in blocks], axis=0)
        put(start, step, jnp.dot(taken, chunk, preferred_element_type=f32).astype(bf16))


def select_rows(blocks, slots):
    shape = jax.ShapeDtypeStruct((4 * slots, blocks[0].shape[1]), bf16)
    return pl.pallas_call(
        select_kernel,
        out_shape=(shape,) * 4,
        in_specs=[whole] * 4,
        out_specs=(whole,) * 4,
        compiler_params=params,
        name="select_rows",
    )(*blocks)


def factor_kernel(saved, swapped_saved, mine, factors, hidden, kept, arrived):
    fetch = pltpu.make_async_copy(mine, kept, arrived)
    fetch.start()
    slots = saved.shape[2] // 16
    span, near, far = position()
    order = token_blocks(span, far) + token_blocks(1 - span, near)

    def at(chunk):
        return pl.ds(pl.multiple_of(order[chunk] * slots, slots), slots)

    for chunk in range(16):
        here = slice(chunk * slots, (chunk + 1) * slots)
        for index, ref in enumerate((swapped_saved, saved)):
            gate = ref[span, 0, at(chunk), :].astype(f32)
            up = ref[span, 1, at(chunk), :].astype(f32)
            sigma = jax.nn.sigmoid(gate)
            silu = gate * sigma
            product = (silu * up).astype(bf16)
            factors[index, 0, here, :] = product.astype(f32)
            factors[index, 1, here, :] = up * sigma * (1.0 + gate * (1.0 - sigma))
            factors[index, 2, here, :] = silu
        hidden[0, here, :] = product
        gate = saved[1 - span, 0, at(16 + chunk), :].astype(f32)
        up = saved[1 - span, 1, at(16 + chunk), :].astype(f32)
        hidden[1, here, :] = (gate * jax.nn.sigmoid(gate) * up).astype(bf16)
    fetch.wait()


def saved_factors(saved, swapped_saved, mine):
    return pl.pallas_call(
        factor_kernel,
        out_shape=(
            jax.ShapeDtypeStruct((2, 3) + saved.shape[2:], f32),
            jax.ShapeDtypeStruct((2,) + saved.shape[2:], bf16),
            jax.ShapeDtypeStruct(mine.shape, bf16),
        ),
        in_specs=[whole, whole, pl.BlockSpec(memory_space=pl.ANY)],
        out_specs=(whole,) * 3,
        scratch_shapes=[pltpu.SemaphoreType.DMA],
        compiler_params=params,
        name="saved_factors",
    )(saved, swapped_saved, mine)


def slot_weights(notes, wide):
    return jnp.concatenate([notes.astype(f32)] * (wide // extra), axis=1)


def raw_kernel(rows, mine, other, factors, g_mine, g_other, dots):
    count = rows.shape[0]
    width = rows.shape[1] - extra
    slots = count // 16
    core, _, far = position()
    order = token_blocks(core, far)
    weights = slot_weights(rows[:, width:], factors.shape[3])
    dot = jnp.zeros((count, 1), f32)
    for index, (weight, out) in ((1, (mine, g_mine)), (0, (other, g_other))):
        raw = lax.dot_general(
            rows[:, :width], weight[...], (((1,), (1,)), ((), ())), preferred_element_type=f32
        )
        dot = dot + jnp.sum(factors[index, 0] * raw, axis=1, keepdims=True)
        grad = weights * raw
        for part in range(2):
            value = (grad * factors[index, part + 1]).astype(bf16)
            for chunk in range(16):
                at = pl.ds(pl.multiple_of(order[chunk] * slots, slots), slots)
                out[part, at, :] = value[chunk * slots : (chunk + 1) * slots]
    lane = lax.broadcasted_iota(jnp.int32, (count, 128), 1)
    row = lax.broadcasted_iota(jnp.int32, (count, 128), 0)
    spread = jnp.where(lane == (row & 15), dot, 0.0)
    for chunk in range(16):
        line = jnp.sum(spread[chunk * slots : (chunk + 1) * slots], axis=0, keepdims=True)
        for core in range(2):
            dots[pl.ds(order[chunk] * 2 + core, 1), :] = line


def raw_grads(rows, mine, other, factors):
    grads = jax.ShapeDtypeStruct((2,) + factors.shape[2:], bf16)
    return pl.pallas_call(
        raw_kernel,
        out_shape=(grads, grads, jax.ShapeDtypeStruct((32, 128), f32)),
        in_specs=[whole] * 4,
        out_specs=(whole,) * 3,
        compiler_params=params,
        name="raw_grads",
    )(rows, mine, other, factors)


def finish_kernel(
    rows, notes, rows_other, notes_other, hidden, g_mine, g_other, *refs
):
    tables, (pair_grads, weight_grad), passed, scaled = refs[:3], refs[3:5], refs[5:8], refs[8]
    count, wide = hidden.shape[1:]

    @pl.when(pl.program_id(0) == 0)
    def _():
        span = lax.axis_index("dp")
        pair_grads[span] = g_mine[...]
        pair_grads[1 - span] = g_other[...]
        for table, out in zip(tables, passed, strict=True):
            out[...] = table[...]
        for index, ref in enumerate((notes, notes_other)):
            value = slot_weights(ref[...], wide) * hidden[index].astype(f32)
            scaled[:, index * count : (index + 1) * count] = value.T.astype(bf16)

    total = jnp.dot(scaled[:, :count], rows[...], preferred_element_type=f32)
    total = total + jnp.dot(scaled[:, count:], rows_other[...], preferred_element_type=f32)
    weight_grad[...] = total.astype(bf16)


def finished(rows, rows_other, hidden, g_mine, g_other, tables):
    count, wide = hidden.shape[1:]
    width = rows.shape[1] - extra
    step = 512 if width % 512 == 0 else width

    def kept(shape):
        return pl.BlockSpec(shape, lambda i: (0,) * len(shape))

    block = pl.BlockSpec((count, step), lambda i: (0, i))
    note = pl.BlockSpec((count, extra), lambda i: (0, width // extra))
    return pl.pallas_call(
        finish_kernel,
        grid=(width // step,),
        out_shape=(
            jax.ShapeDtypeStruct((2,) + g_mine.shape, bf16),
            jax.ShapeDtypeStruct((wide, width), bf16),
            *(jax.ShapeDtypeStruct(table.shape, table.dtype) for table in tables),
        ),
        in_specs=[
            block,
            note,
            block,
            note,
            kept(hidden.shape),
            kept(g_mine.shape),
            kept(g_other.shape),
            *(kept(table.shape) for table in tables),
        ],
        out_specs=(
            kept((2,) + g_mine.shape),
            pl.BlockSpec((wide, step), lambda i: (0, i)),
            *(kept(table.shape) for table in tables),
        ),
        scratch_shapes=[pltpu.VMEM((wide, 2 * count), bf16)],
        compiler_params=params,
        name="finished",
    )(rows, rows, rows_other, rows_other, hidden, g_mine, g_other, *tables)


def logit_kernel(returned, experts, places, scores, out):
    tokens = scores.shape[1]
    spread = lax.dot_general(
        returned[...],
        experts[...],
        (((0,), (0,)), ((), ())),
        preferred_element_type=f32,
        precision=lax.Precision.HIGHEST,
    )
    route = jnp.sum(spread * places[...], axis=0, keepdims=True)
    for span in range(2):
        first, second = 2 * span, 2 * span + 1
        route0 = route[:, first * tokens : (first + 1) * tokens]
        route1 = route[:, second * tokens : (second + 1) * tokens]
        score0, score1 = scores[first : first + 1], scores[second : second + 1]
        total = score0 + score1
        mean = (route0 * score0 + route1 * score1) / total
        scale = route_scale / total
        out[first : first + 1] = scale * (route0 - mean) * score0 * (1.0 - score0)
        out[second : second + 1] = scale * (route1 - mean) * score1 * (1.0 - score1)


def note_kernel(ids, logits, notes, experts, places, scores):
    tokens = ids.shape[1]
    score = jax.nn.sigmoid(logits[...])
    scores[...] = score
    number = ids[...]
    line = jnp.concatenate([number[row : row + 1] for row in range(4)], axis=1)
    lane = lax.broadcasted_iota(jnp.int32, (1, 4 * tokens), 1)
    source = lax.broadcasted_iota(jnp.int32, (32, 4 * tokens), 0)
    span = lane >> 6
    experts[...] = jnp.where(((source >> 2) == line) & ((source & 1) == span), 1.0, 0.0)
    expert = lax.broadcasted_iota(jnp.int32, (8, 4 * tokens), 0)
    marked = jnp.where(expert == line, 1.0, 0.0)
    i = lax.broadcasted_iota(jnp.int32, (4 * tokens, 4 * tokens), 0)
    j = lax.broadcasted_iota(jnp.int32, (4 * tokens, 4 * tokens), 1)
    earlier = jnp.where(((i >> 6) == (j >> 6)) & ((i & 31) < (j & 31)), 1.0, 0.0)
    before = jnp.dot(marked.astype(bf16), earlier.astype(bf16), preferred_element_type=f32)
    place = jnp.sum(before * marked, axis=0, keepdims=True)
    slot = lax.broadcasted_iota(jnp.int32, (128, 4 * tokens), 0).astype(f32)
    places[...] = jnp.where(slot == place, 1.0, 0.0)
    first = lax.axis_index("dp") == 0
    pair = jnp.where(first, score[0:2], score[2:4])
    lines = [
        jnp.where(first, number[0:2], number[2:4]).astype(f32),
        route_scale * pair / (pair[0:1] + pair[1:2]),
        jnp.zeros((extra - 4, tokens), f32),
    ]
    table = jnp.concatenate(lines, axis=0)
    table = jnp.concatenate([table, jnp.zeros((extra, extra - tokens), f32)], axis=1)
    notes[...] = table.T[:tokens].astype(bf16)


def slot_notes(ids, logits):
    tokens = ids.shape[1]
    return pl.pallas_call(
        note_kernel,
        out_shape=(
            jax.ShapeDtypeStruct((tokens, extra), bf16),
            jax.ShapeDtypeStruct((32, 4 * tokens), f32),
            jax.ShapeDtypeStruct((128, 4 * tokens), f32),
            jax.ShapeDtypeStruct((4, tokens), f32),
        ),
        in_specs=[whole] * 2,
        out_specs=(whole,) * 4,
        compiler_params=params,
        name="slot_notes",
    )(ids, logits)


def local(sent_down, sent_up, expert_ids, router_logits, saved_gate_up, down_weight):
    first = lax.axis_index("dp") == 0
    segments = lax.axis_size("pipe")
    saved = saved_gate_up[:, 0, 0]
    mine = down_weight[0, 0]
    slots = saved.shape[2] // 16
    tokens, top = expert_ids.shape[2:]

    def by_slot(value):
        return jnp.swapaxes(value[:, 0], 1, 2).reshape(2 * top, tokens)

    pairs = [(2 * z, 2 * (z - 1)) for z in range(1, segments)]
    pairs += [(2 * z + 1, 2 * (z + 1) + 1) for z in range(segments - 1)]
    outgoing, expert_ids, router_logits = lax.optimization_barrier(
        (jnp.where(first, sent_down[0], sent_up[0]), expert_ids, router_logits)
    )
    incoming = lax.ppermute(outgoing, ("pipe", "dp"), pairs)
    notes, experts, places, scores = slot_notes(by_slot(expert_ids), by_slot(router_logits))
    block = jnp.concatenate([incoming, notes], axis=1)
    swapped_saved = swapped(saved)
    block, held, swapped_saved = lax.optimization_barrier((block, mine, swapped_saved))
    other = swapped(held)

    blocks = [block] + [plane_shift(block, step, True) for step in shifts]
    factors, hidden, mine = saved_factors(saved, swapped_saved, mine)
    blocks[1], other, mine, factors, hidden = lax.optimization_barrier(
        (blocks[1], other, mine, factors, hidden)
    )
    pieces = select_rows(blocks, slots)
    pieces = [pieces[0]] + [
        plane_shift(piece, step, False) for piece, step in zip(pieces[1:], shifts, strict=True)
    ]
    rows = jnp.zeros((16 * slots, pieces[0].shape[1]), bf16)
    for index, piece in enumerate(pieces):
        rows = lax.dynamic_update_slice(rows, piece, (index * 4 * slots, 0))
    g_mine, g_other, dots = raw_grads(rows, mine, other, factors)
    returned = lax.all_to_all(dots, ("expert", "dp"), split_axis=0, concat_axis=0, tiled=True)
    pair_grads, weight_grad, experts, places, scores = finished(
        rows, swapped(rows), hidden, g_mine, swapped(g_other), (experts, places, scores)
    )
    returned, pair_grads, weight_grad = lax.optimization_barrier(
        (returned, pair_grads, weight_grad)
    )
    logit_grads = pl.pallas_call(
        logit_kernel,
        out_shape=jax.ShapeDtypeStruct((2 * top, tokens), f32),
        in_specs=[whole] * 4,
        out_specs=whole,
        compiler_params=params,
        name="logit_grads",
    )(returned, experts, places, scores)
    return (
        pair_grads[:, None, None],
        weight_grad[None, None],
        jnp.swapaxes(logit_grads.reshape(2, 1, top, tokens), 2, 3),
    )


def solution(mesh):
    placed = (
        P("pipe", "expert", None),
        P("pipe", "expert", None),
        P(None, "pipe", "expert", None),
        P(None, "pipe", "expert", None),
        P(None, "pipe", "expert", None, None, "dp"),
        P("pipe", "expert", "dp", None),
    )
    return jax.shard_map(
        local,
        mesh=mesh,
        in_specs=placed,
        out_specs=(
            P(None, "pipe", "expert", None, None, "dp"),
            P("pipe", "expert", "dp", None),
            P(None, "pipe", "expert", None),
        ),
        check_vma=False,
    )
```

time: 62.7 us -> 55.8 us (0.89)
  waiting for transfers between devices: 8.2 us -> 15.4 us
  starting transfers between devices: 29.6 us -> 23 us
  local copies, waits for them, and re-layouts: 9.5 us -> 4.15 us
  Pallas kernels: 12.6 us -> 10.7 us
    ppermute x6, waiting for transfers between devices: 5.2 us -> 13.7 us  [plane_shift(): return lax.ppermute(value, ('expert', 'dp'), pairs)]
    ppermute x6, starting transfers between devices: 11.1 us -> 6.97 us  [plane_shift(): return lax.ppermute(value, ('expert', 'dp'), pairs)]
    unnamed x30 -> x8, local copies, waits for them, and re-layouts: 7.95 us -> 3.9 us
    pallas_call x1, Pallas kernels: 4.46 us -> 1.86 us  [raw_grads(): pl.pallas_call(raw_kernel, out_shape=(grads, grads, jax.ShapeDtypeStruct(...]
    ppermute x4, starting transfers between devices: 7.98 us -> 6.06 us  [swapped(): return lax.ppermute(value, 'dp', [(0, 1), (1, 0)])]
    dynamic_update_slice x4, local copies, waits for them, and re-layouts: 1.33 us -> 0.25 us  [local(): rows = lax.dynamic_update_slice(rows, piece, (index * 4 * slots, 0))]
    all_to_all x1, waiting for transfers between devices: 1.66 us -> 0.62 us  [local(): lax.all_to_all(dots, ('expert', 'dp'), split_axis=0, concat_axis=0, tiled...]
    pallas_call x4, Pallas kernels: 7.08 us -> 7.76 us  [the longest x1 6.3 us: finished(): pl.pallas_call(finish_kernel, grid=(width // step,), out_shape=(jax.Shape...]
  transfers between devices with their start and end apart: 12 -> 12, of which waited for: 7 -> 7; matrix products, arithmetic and copies ran while one was open for 3% -> 0% of each run, Pallas kernels for 11% -> 16%
where the time goes in v3:
time: 55.8 us; the launch traced here: 55 us
  starting transfers between devices  23 us (41%)
  waiting for transfers between devices  15.4 us (28%)
  Pallas kernels  10.7 us (19%)
  local copies, waits for them, and re-layouts  4.15 us (7%)
  other arithmetic  0.99 us (2%)
  between operations  0.75 us (1%)
    ppermute x6, waiting for transfers between devices, plane_shift(): return lax.ppermute(value, ('expert', 'dp'), pairs)  13.7 us
    ppermute x6, starting transfers between devices, plane_shift(): return lax.ppermute(value, ('expert', 'dp'), pairs)  6.97 us
    pallas_call x1, Pallas kernels, finished(): pl.pallas_call(finish_kernel, grid=(width // step,), out_shape=(jax.Shape...  6.3 us
    ppermute x4, starting transfers between devices, swapped(): return lax.ppermute(value, 'dp', [(0, 1), (1, 0)])  6.06 us
    all_to_all x1, starting transfers between devices, local(): lax.all_to_all(dots, ('expert', 'dp'), split_axis=0, concat_axis=0, tiled...  5.6 us
    ppermute x1, starting transfers between devices, local(): incoming = lax.ppermute(outgoing, ('pipe', 'dp'), pairs)  4.38 us
    unnamed x8, local copies, waits for them, and re-layouts  3.9 us
    pallas_call x1, Pallas kernels, raw_grads(): pl.pallas_call(raw_kernel, out_shape=(grads, grads, jax.ShapeDtypeStruct(...  1.86 us
  transfers between devices with their start and end apart: 12, of which 7 were waited for; matrix products, arithmetic and copies ran while one was open for 0% of the time, Pallas kernels for 16%

profile of v3, /device:TPU:1, one launch (start us, length us, event | category | flops | bytes accessed | tf_op | source)
XLA Modules:
  0.0 55.0 jit_solution(12622176421180681945)
XLA Ops:
  0.6 1.0 %select_bitcast_fusion = bf16[32,3584]{1,0:T(8,128)(2,1)S(1)} fusion(bf16[1,32,3584]{2,1,0:T(8,128)(2,1)} %param.6, bf16[1,32,3584]{2,1,0:T(8,128)(2,1)} %param.7, pred[]{:T(512)S(6)} %eq.3), kind=kLoop, calls=%fused_computation.1 | loop fusion | flops 114688 | bytes 688129 | tf_op jit(solution)/shard_map/jit(_where)/select_n | solution.py:342
  1.6 4.4 %collective-permute-start = (bf16[32,3584]{1,0:T(8,128)(2,1)S(1)}, bf16[32,3584]{1,0:T(8,128)(2,1)S(1)}, u32[]{:S(2)}, u32[]{:S(2)}) collective-permute-start(bf16[32,3584]{1,0:T(8,128)(2,1)S(1)} %select_bitcast_fusion), channel_id=1, source_target_pairs={{32,0},{64,32},{96,64},{128,96},{160,128},{192,160},{224,192},{1,3... | collective-permute-start | bytes 688136 | tf_op jit(solution)/shard_map/ppermute | solution.py:344
  6.0 0.2 collective-permute-start.1
  6.2 0.0 copy-start.2
  6.2 0.7 %copy-done.2 = s32[2,1,32,2]{2,3,1,0:T(2,128)S(1)} copy-done((s32[2,1,32,2]{2,3,1,0:T(2,128)S(1)}, s32[2,1,32,2]{2,3,1,0:T(2,128)}, u32[]{:S(2)}) %copy-start.2) | copy-done | bytes 536
  6.9 0.0 copy-start.3
  6.9 0.7 %copy-done.3 = f32[2,1,32,2]{2,3,1,0:T(2,128)S(1)} copy-done((f32[2,1,32,2]{2,3,1,0:T(2,128)S(1)}, f32[2,1,32,2]{2,3,1,0:T(2,128)}, u32[]{:S(2)}) %copy-start.3) | copy-done | bytes 536
  7.6 0.2 slot_notes.1
  7.8 1.1 %collective-permute-done = bf16[32,3584]{1,0:T(8,128)(2,1)S(1)} collective-permute-done((bf16[32,3584]{1,0:T(8,128)(2,1)S(1)}, bf16[32,3584]{1,0:T(8,128)(2,1)S(1)}, u32[]{:S(2)}, u32[]{:S(2)}) %collective-permute-start) | collective-permute-done | bytes 229408 | tf_op jit(solution)/shard_map/ppermute | solution.py:344
  9.0 0.0 collective-permute-done.1.swapped_saved
  9.0 3.9 %collective-permute-start.3 = (bf16[256,3584]{1,0:T(8,128)(2,1)}, bf16[256,3584]{1,0:T(8,128)(2,1)S(1)}, u32[]{:S(2)}, u32[]{:S(2)}) collective-permute-start(bf16[256,3584]{1,0:T(8,128)(2,1)} %bitcast.27), channel_id=1, source_target_pairs={{0,1},{1,0},{2,3},{3,2},{4,5},{5,4},{6,7},{7,6},{8,9},{9,8},{10,11... | collective-permute-start | bytes 5505032 | tf_op jit(solution)/shard_map/ppermute | solution.py:32
  12.9 1.2 %collective-permute-start.2 = (bf16[32,3712]{1,0:T(8,128)(2,1)S(1)}, bf16[32,3712]{1,0:T(8,128)(2,1)S(1)}, u32[]{:S(2)}, u32[]{:S(2)}) collective-permute-start(bf16[32,3712]{1,0:T(8,128)(2,1)S(1)} %pad_maximum_fusion.refs_0_), channel_id=1, source_target_pairs={{0,4},{1,17},{2,6},{3,19},{4,0},{5,21},{6,2},{7,23},{8,12},{9,25},... | collective-permute-start | bytes 712712 | tf_op jit(solution)/shard_map/ppermute | solution.py:28
  14.1 0.8 %collective-permute-start.5 = (bf16[32,3712]{1,0:T(8,128)(2,1)S(1)}, bf16[32,3712]{1,0:T(8,128)(2,1)S(1)}, u32[]{:S(2)}, u32[]{:S(2)}) collective-permute-start(bf16[32,3712]{1,0:T(8,128)(2,1)S(1)} %pad_maximum_fusion.refs_0_), channel_id=1, source_target_pairs={{0,6},{1,25},{2,0},{3,27},{4,2},{5,29},{6,4},{7,31},{8,14},{9,1},{... | collective-permute-start | bytes 712712 | tf_op jit(solution)/shard_map/ppermute | solution.py:28
  14.8 0.7 %collective-permute-start.4 = (bf16[32,3712]{1,0:T(8,128)(2,1)S(1)}, bf16[32,3712]{1,0:T(8,128)(2,1)S(1)}, u32[]{:S(2)}, u32[]{:S(2)}) collective-permute-start(bf16[32,3712]{1,0:T(8,128)(2,1)S(1)} %pad_maximum_fusion.refs_0_), channel_id=1, source_target_pairs={{0,2},{1,9},{2,4},{3,11},{4,6},{5,13},{6,0},{7,15},{8,10},{9,17},{... | collective-permute-start | bytes 712712 | tf_op jit(solution)/shard_map/ppermute | solution.py:28
  15.5 0.0 copy-start
  15.5 1.5 %copy-done = bf16[1,1,256,3584]{3,2,1,0:T(8,128)(2,1)S(1)} copy-done((bf16[1,1,256,3584]{3,2,1,0:T(8,128)(2,1)S(1)}, bf16[1,1,256,3584]{3,2,1,0:T(8,128)(2,1)}, u32[]{:S(2)}) %copy-start) | copy-done | bytes 1835032
  17.0 0.0 copy-start.1
  17.0 1.0 %copy-done.1 = bf16[2,1,1,2,256,256]{5,4,3,2,1,0:T(8,128)(2,1)S(1)} copy-done((bf16[2,1,1,2,256,256]{5,4,3,2,1,0:T(8,128)(2,1)S(1)}, bf16[2,1,1,2,256,256]{5,4,3,2,1,0:T(8,128)(2,1)}, u32[]{:S(2)}) %copy-start.1) | copy-done | bytes 524312
  18.1 0.4 saved_factors.1
  18.5 1.1 %collective-permute-done.2.refs_1_ = bf16[32,3712]{1,0:T(8,128)(2,1)S(1)} collective-permute-done((bf16[32,3712]{1,0:T(8,128)(2,1)S(1)}, bf16[32,3712]{1,0:T(8,128)(2,1)S(1)}, u32[]{:S(2)}, u32[]{:S(2)}) %collective-permute-start.2) | collective-permute-done | bytes 237600 | tf_op jit(solution)/shard_map/ppermute | solution.py:28
  19.6 0.0 collective-permute-done.3.other
  19.6 1.2 %collective-permute-done.5.refs_3_ = bf16[32,3712]{1,0:T(8,128)(2,1)S(1)} collective-permute-done((bf16[32,3712]{1,0:T(8,128)(2,1)S(1)}, bf16[32,3712]{1,0:T(8,128)(2,1)S(1)}, u32[]{:S(2)}, u32[]{:S(2)}) %collective-permute-start.5) | collective-permute-done | bytes 237600 | tf_op jit(solution)/shard_map/ppermute | solution.py:28
  20.8 1.4 %collective-permute-done.4.refs_2_ = bf16[32,3712]{1,0:T(8,128)(2,1)S(1)} collective-permute-done((bf16[32,3712]{1,0:T(8,128)(2,1)S(1)}, bf16[32,3712]{1,0:T(8,128)(2,1)S(1)}, u32[]{:S(2)}, u32[]{:S(2)}) %collective-permute-start.4) | collective-permute-done | bytes 237600 | tf_op jit(solution)/shard_map/ppermute | solution.py:28
  22.2 0.8 %select_rows.1 = (bf16[64,3712]{1,0:T(8,128)(2,1)S(1)}, bf16[64,3712]{1,0:T(8,128)(2,1)S(1)}, bf16[64,3712]{1,0:T(8,128)(2,1)S(1)}, bf16[64,3712]{1,0:T(8,128)(2,1)S(1)}) custom-call(bf16[32,3712]{1,0:T(8,128)(2,1)S(1)} %pad_maximum_fusion.refs_0_, bf16[32,3712]{1,0:T(8,128)(2,1)S(1)} %collective-permute-done.2.refs_1_, ...), custom_call_target="tpu_custom_call" | custom-call | tf_op jit(solution)/shard_map/select_rows/pallas_call | solution.py:99
  23.0 1.7 %collective-permute-start.6 = (bf16[64,3712]{1,0:T(8,128)(2,1)S(1)}, bf16[64,3712]{1,0:T(8,128)(2,1)S(1)}, u32[]{:S(2)}, u32[]{:S(2)}) collective-permute-start(bf16[64,3712]{1,0:T(8,128)(2,1)S(1)} %get-tuple-element.48), channel_id=1, source_target_pairs={{0,16},{1,5},{2,18},{3,7},{4,20},{5,1},{6,22},{7,3},{8,24},{9,13},... | collective-permute-start | bytes 1425416 | tf_op jit(solution)/shard_map/ppermute | solution.py:28
  24.7 0.3 collective-permute-start.7
  25.0 2.4 %collective-permute-start.8 = (bf16[64,3712]{1,0:T(8,128)(2,1)S(1)}, bf16[64,3712]{1,0:T(8,128)(2,1)S(1)}, u32[]{:S(2)}, u32[]{:S(2)}) collective-permute-start(bf16[64,3712]{1,0:T(8,128)(2,1)S(1)} %get-tuple-element.50), channel_id=1, source_target_pairs={{0,24},{1,7},{2,26},{3,1},{4,28},{5,3},{6,30},{7,5},{8,0},{9,15},{... | collective-permute-start | bytes 1425416 | tf_op jit(solution)/shard_map/ppermute | solution.py:28
  27.4 0.1 dynamic_update_slice.12
  27.5 5.0 %collective-permute-done.6 = bf16[64,3712]{1,0:T(8,128)(2,1)S(1)} collective-permute-done((bf16[64,3712]{1,0:T(8,128)(2,1)S(1)}, bf16[64,3712]{1,0:T(8,128)(2,1)S(1)}, u32[]{:S(2)}, u32[]{:S(2)}) %collective-permute-start.6) | collective-permute-done | bytes 475168 | tf_op jit(solution)/shard_map/ppermute | solution.py:28
  32.5 5.0 %collective-permute-done.7 = bf16[64,3712]{1,0:T(8,128)(2,1)S(1)} collective-permute-done((bf16[64,3712]{1,0:T(8,128)(2,1)S(1)}, bf16[64,3712]{1,0:T(8,128)(2,1)S(1)}, u32[]{:S(2)}, u32[]{:S(2)}) %collective-permute-start.7) | collective-permute-done | bytes 475168 | tf_op jit(solution)/shard_map/ppermute | solution.py:28
  37.6 0.0 collective-permute-done.8
  37.6 1.9 %collective-permute-start.9 = (bf16[256,3712]{1,0:T(8,128)(2,1)S(1)}, bf16[256,3712]{1,0:T(8,128)(2,1)}, u32[]{:S(2)}, u32[]{:S(2)}) collective-permute-start(bf16[256,3712]{1,0:T(8,128)(2,1)S(1)} %constant_dynamic-update-slice_fusion.rows.notes), channel_id=1, source_target_pairs={{0,1},{1,0},{2,3},{3,2},{4,5},{5,4},{6,7},{7,6},{8,9},{9,8},{10,11... | collective-permute-start | bytes 5701640 | tf_op jit(solution)/shard_map/ppermute | solution.py:32
  39.5 1.9 %raw_grads.1 = (bf16[2,256,256]{2,1,0:T(8,128)(2,1)S(1)}, bf16[2,256,256]{2,1,0:T(8,128)(2,1)S(1)}, f32[32,128]{1,0:T(8,128)}) custom-call(bf16[256,3712]{1,0:T(8,128)(2,1)S(1)} %constant_dynamic-update-slice_fusion.rows.notes, bf16[256,3584]{1,0:T(8,128)(2,1)S(1)} %get-tuple-element.51.mine, bf16[256,3584]{1,0:T(8,128)(2,1)S(1)} %collective-permute-done.3.other, ...), custom_call_target="tpu_custom_call" | custom-call | tf_op jit(solution)/shard_map/raw_grads/pallas_call | solution.py:187
  41.4 0.0 collective-permute-start.10
  41.4 5.6 %all-to-all-start = ((f32[32,1,128]{2,1,0:T(1,128)}), f32[32,1,128]{2,1,0:T(1,128)S(1)}, u32[]{:S(2)}, u32[]{:S(2)}) async-start(f32[32,1,128]{2,1,0:T(1,128)} %bitcast.10), calls=%async_computation | async-start | bytes 32768 | tf_op jit(solution)/shard_map/all_to_all | solution.py:364
  47.0 0.0 collective-permute-done.10.g_other
  47.0 0.0 collective-permute-done.9.rows_other.notes_other
  47.0 6.3 %finished.1 = (bf16[2,2,256,256]{3,2,1,0:T(8,128)(2,1)}, bf16[256,3584]{1,0:T(8,128)(2,1)}, f32[32,128]{1,0:T(8,128)S(1)}, f32[128,128]{1,0:T(8,128)S(1)}, f32[4,32]{1,0:T(4,128)S(1)}) custom-call(bf16[256,3712]{1,0:T(8,128)(2,1)S(1)} %constant_dynamic-update-slice_fusion.rows.notes, bf16[256,3712]{1,0:T(8,128)(2,1)S(1)} %constant_dynamic-update-slice_fusion.rows.notes, ...), custom_call_target="tpu_custom_call" | custom-call | tf_op jit(solution)/shard_map/finished/pallas_call | solution.py:229
  53.3 0.6 %all-to-all-done = f32[32,1,128]{2,1,0:T(1,128)S(1)} async-done(((f32[32,1,128]{2,1,0:T(1,128)}), f32[32,1,128]{2,1,0:T(1,128)S(1)}, u32[]{:S(2)}, u32[]{:S(2)}) %all-to-all-start) | async-done | bytes 16416 | tf_op jit(solution)/shard_map/all_to_all | solution.py:364
  54.0 1.1 %logit_grads.1 = f32[4,32]{1,0:T(4,128)} custom-call(f32[32,128]{1,0:T(8,128)S(1)} %bitcast.31, f32[32,128]{1,0:T(8,128)S(1)} %get-tuple-element.66.experts, f32[128,128]{1,0:T(8,128)S(1)} %get-tuple-element.67.places, f32[4,32]{1,0:T(4,128)S(1)} %get-tuple-element.68.scores), custom_call_target="tpu_custom_call" | custom-call | tf_op jit(solution)/shard_map/logit_grads/pallas_call | solution.py:371
  (4 shorter events, 0.1 us)
Async XLA Ops:
  1.6 7.3 %collective-permute-start = (bf16[32,3584]{1,0:T(8,128)(2,1)S(1)}, bf16[32,3584]{1,0:T(8,128)(2,1)S(1)}, u32[]{:S(2)}, u32[]{:S(2)}) collective-permute-start(bf16[32,3584]{1,0:T(8,128)(2,1)S(1)} %select_bitcast_fusion), channel_id=1, source_target_pairs={{32,0},{64,32},{96,64},{128,96},{160,128},{192,160},{224,192},{1,3... | collective-permute-start | bytes 688136 | tf_op jit(solution)/shard_map/ppermute | solution.py:344
  6.0 3.0 %collective-permute-start.1 = (bf16[2,2,256,256]{3,2,1,0:T(8,128)(2,1)}, bf16[2,2,256,256]{3,2,1,0:T(8,128)(2,1)S(1)}, u32[]{:S(2)}, u32[]{:S(2)}) collective-permute-start(bf16[2,2,256,256]{3,2,1,0:T(8,128)(2,1)} %bitcast.29), channel_id=1, source_target_pairs={{0,1},{1,0},{2,3},{3,2},{4,5},{5,4},{6,7},{7,6},{8,9},{9,8},{10,11... | collective-permute-start | bytes 1572872 | tf_op jit(solution)/shard_map/ppermute | solution.py:32
  6.2 0.7 %copy-start.2 = (s32[2,1,32,2]{2,3,1,0:T(2,128)S(1)}, s32[2,1,32,2]{2,3,1,0:T(2,128)}, u32[]{:S(2)}) copy-start(s32[2,1,32,2]{2,3,1,0:T(2,128)} %param.8) | copy-start | bytes 1540
  6.9 0.7 %copy-start.3 = (f32[2,1,32,2]{2,3,1,0:T(2,128)S(1)}, f32[2,1,32,2]{2,3,1,0:T(2,128)}, u32[]{:S(2)}) copy-start(f32[2,1,32,2]{2,3,1,0:T(2,128)} %param.9) | copy-start | bytes 1540
  9.0 10.7 %collective-permute-start.3 = (bf16[256,3584]{1,0:T(8,128)(2,1)}, bf16[256,3584]{1,0:T(8,128)(2,1)S(1)}, u32[]{:S(2)}, u32[]{:S(2)}) collective-permute-start(bf16[256,3584]{1,0:T(8,128)(2,1)} %bitcast.27), channel_id=1, source_target_pairs={{0,1},{1,0},{2,3},{3,2},{4,5},{5,4},{6,7},{7,6},{8,9},{9,8},{10,11... | collective-permute-start | bytes 5505032 | tf_op jit(solution)/shard_map/ppermute | solution.py:32
  12.9 6.8 %collective-permute-start.2 = (bf16[32,3712]{1,0:T(8,128)(2,1)S(1)}, bf16[32,3712]{1,0:T(8,128)(2,1)S(1)}, u32[]{:S(2)}, u32[]{:S(2)}) collective-permute-start(bf16[32,3712]{1,0:T(8,128)(2,1)S(1)} %pad_maximum_fusion.refs_0_), channel_id=1, source_target_pairs={{0,4},{1,17},{2,6},{3,19},{4,0},{5,21},{6,2},{7,23},{8,12},{9,25},... | collective-permute-start | bytes 712712 | tf_op jit(solution)/shard_map/ppermute | solution.py:28
  14.1 6.8 %collective-permute-start.5 = (bf16[32,3712]{1,0:T(8,128)(2,1)S(1)}, bf16[32,3712]{1,0:T(8,128)(2,1)S(1)}, u32[]{:S(2)}, u32[]{:S(2)}) collective-permute-start(bf16[32,3712]{1,0:T(8,128)(2,1)S(1)} %pad_maximum_fusion.refs_0_), channel_id=1, source_target_pairs={{0,6},{1,25},{2,0},{3,27},{4,2},{5,29},{6,4},{7,31},{8,14},{9,1},{... | collective-permute-start | bytes 712712 | tf_op jit(solution)/shard_map/ppermute | solution.py:28
  14.8 7.3 %collective-permute-start.4 = (bf16[32,3712]{1,0:T(8,128)(2,1)S(1)}, bf16[32,3712]{1,0:T(8,128)(2,1)S(1)}, u32[]{:S(2)}, u32[]{:S(2)}) collective-permute-start(bf16[32,3712]{1,0:T(8,128)(2,1)S(1)} %pad_maximum_fusion.refs_0_), channel_id=1, source_target_pairs={{0,2},{1,9},{2,4},{3,11},{4,6},{5,13},{6,0},{7,15},{8,10},{9,17},{... | collective-permute-start | bytes 712712 | tf_op jit(solution)/shard_map/ppermute | solution.py:28
  15.5 1.5 %copy-start = (bf16[1,1,256,3584]{3,2,1,0:T(8,128)(2,1)S(1)}, bf16[1,1,256,3584]{3,2,1,0:T(8,128)(2,1)}, u32[]{:S(2)}) copy-start(bf16[1,1,256,3584]{3,2,1,0:T(8,128)(2,1)} %param.11) | copy-start | bytes 5505028
  17.0 1.0 %copy-start.1 = (bf16[2,1,1,2,256,256]{5,4,3,2,1,0:T(8,128)(2,1)S(1)}, bf16[2,1,1,2,256,256]{5,4,3,2,1,0:T(8,128)(2,1)}, u32[]{:S(2)}) copy-start(bf16[2,1,1,2,256,256]{5,4,3,2,1,0:T(8,128)(2,1)} %param.10) | copy-start | bytes 1572868
  23.0 9.4 %collective-permute-start.6 = (bf16[64,3712]{1,0:T(8,128)(2,1)S(1)}, bf16[64,3712]{1,0:T(8,128)(2,1)S(1)}, u32[]{:S(2)}, u32[]{:S(2)}) collective-permute-start(bf16[64,3712]{1,0:T(8,128)(2,1)S(1)} %get-tuple-element.48), channel_id=1, source_target_pairs={{0,16},{1,5},{2,18},{3,7},{4,20},{5,1},{6,22},{7,3},{8,24},{9,13},... | collective-permute-start | bytes 1425416 | tf_op jit(solution)/shard_map/ppermute | solution.py:28
  24.7 12.8 %collective-permute-start.7 = (bf16[64,3712]{1,0:T(8,128)(2,1)S(1)}, bf16[64,3712]{1,0:T(8,128)(2,1)S(1)}, u32[]{:S(2)}, u32[]{:S(2)}) collective-permute-start(bf16[64,3712]{1,0:T(8,128)(2,1)S(1)} %get-tuple-element.49), channel_id=1, source_target_pairs={{0,8},{1,3},{2,10},{3,5},{4,12},{5,7},{6,14},{7,1},{8,16},{9,11},{... | collective-permute-start | bytes 1425416 | tf_op jit(solution)/shard_map/ppermute | solution.py:28
  25.0 12.6 %collective-permute-start.8 = (bf16[64,3712]{1,0:T(8,128)(2,1)S(1)}, bf16[64,3712]{1,0:T(8,128)(2,1)S(1)}, u32[]{:S(2)}, u32[]{:S(2)}) collective-permute-start(bf16[64,3712]{1,0:T(8,128)(2,1)S(1)} %get-tuple-element.50), channel_id=1, source_target_pairs={{0,24},{1,7},{2,26},{3,1},{4,28},{5,3},{6,30},{7,5},{8,0},{9,15},{... | collective-permute-start | bytes 1425416 | tf_op jit(solution)/shard_map/ppermute | solution.py:28
  37.6 9.4 %collective-permute-start.9 = (bf16[256,3712]{1,0:T(8,128)(2,1)S(1)}, bf16[256,3712]{1,0:T(8,128)(2,1)}, u32[]{:S(2)}, u32[]{:S(2)}) collective-permute-start(bf16[256,3712]{1,0:T(8,128)(2,1)S(1)} %constant_dynamic-update-slice_fusion.rows.notes), channel_id=1, source_target_pairs={{0,1},{1,0},{2,3},{3,2},{4,5},{5,4},{6,7},{7,6},{8,9},{9,8},{10,11... | collective-permute-start | bytes 5701640 | tf_op jit(solution)/shard_map/ppermute | solution.py:32
  41.4 5.6 %collective-permute-start.10 = (bf16[2,256,256]{2,1,0:T(8,128)(2,1)S(1)}, bf16[2,256,256]{2,1,0:T(8,128)(2,1)S(1)}, u32[]{:S(2)}, u32[]{:S(2)}) collective-permute-start(bf16[2,256,256]{2,1,0:T(8,128)(2,1)S(1)} %get-tuple-element.57), channel_id=1, source_target_pairs={{0,1},{1,0},{2,3},{3,2},{4,5},{5,4},{6,7},{7,6},{8,9},{9,8},{10,11... | collective-permute-start | bytes 786440 | tf_op jit(solution)/shard_map/ppermute | solution.py:32
  41.4 12.5 %all-to-all-start = ((f32[32,1,128]{2,1,0:T(1,128)}), f32[32,1,128]{2,1,0:T(1,128)S(1)}, u32[]{:S(2)}, u32[]{:S(2)}) async-start(f32[32,1,128]{2,1,0:T(1,128)} %bitcast.10), calls=%async_computation | async-start | bytes 32768 | tf_op jit(solution)/shard_map/all_to_all | solution.py:364

commit v4 on v3

--- a/solution.py
+++ b/solution.py
@@ -12,6 +12,7 @@
 bf16, f32 = jnp.bfloat16, jnp.float32
 params = pltpu.CompilerParams(vmem_limit_bytes=16 * 2**20)
 whole = pl.BlockSpec(memory_space=pltpu.VMEM)
+in_hbm = pl.BlockSpec(memory_space=pltpu.HBM)
 
 
 def moved(place, step, along_x):
@@ -106,44 +107,46 @@
     )(*blocks)
 
 
-def factor_kernel(saved, swapped_saved, mine, factors, hidden, kept, arrived):
+def factor_kernel(saved, swapped_saved, mine, factors, later, hidden, kept, arrived):
     fetch = pltpu.make_async_copy(mine, kept, arrived)
     fetch.start()
     slots = saved.shape[2] // 16
     span, near, far = position()
-    order = token_blocks(span, far) + token_blocks(1 - span, near)
-
-    def at(chunk):
-        return pl.ds(pl.multiple_of(order[chunk] * slots, slots), slots)
+    order, order_other = token_blocks(span, far), token_blocks(1 - span, near)
+
+    def loaded(ref, which, block):
+        at = pl.ds(pl.multiple_of(block * slots, slots), slots)
+        gate, up = ref[which, 0, at, :].astype(f32), ref[which, 1, at, :].astype(f32)
+        sigma = jax.nn.sigmoid(gate)
+        silu = gate * sigma
+        return up * sigma * (1.0 + gate * (1.0 - sigma)), silu, (silu * up).astype(bf16)
 
     for chunk in range(16):
         here = slice(chunk * slots, (chunk + 1) * slots)
-        for index, ref in enumerate((swapped_saved, saved)):
-            gate = ref[span, 0, at(chunk), :].astype(f32)
-            up = ref[span, 1, at(chunk), :].astype(f32)
-            sigma = jax.nn.sigmoid(gate)
-            silu = gate * sigma
-            product = (silu * up).astype(bf16)
-            factors[index, 0, here, :] = product.astype(f32)
-            factors[index, 1, here, :] = up * sigma * (1.0 + gate * (1.0 - sigma))
-            factors[index, 2, here, :] = silu
+        factors[0, here, :] = loaded(swapped_saved, span, order[chunk])[2].astype(f32)
+        gate, up, product = loaded(saved, span, order[chunk])
+        factors[1, here, :] = product.astype(f32)
+        factors[2, here, :] = gate
+        factors[3, here, :] = up
         hidden[0, here, :] = product
-        gate = saved[1 - span, 0, at(16 + chunk), :].astype(f32)
-        up = saved[1 - span, 1, at(16 + chunk), :].astype(f32)
-        hidden[1, here, :] = (gate * jax.nn.sigmoid(gate) * up).astype(bf16)
+        later[0, here, :], later[1, here, :], hidden[1, here, :] = loaded(
+            saved, 1 - span, order_other[chunk]
+        )
     fetch.wait()
 
 
 def saved_factors(saved, swapped_saved, mine):
+    shape = saved.shape[2:]
     return pl.pallas_call(
         factor_kernel,
         out_shape=(
-            jax.ShapeDtypeStruct((2, 3) + saved.shape[2:], f32),
-            jax.ShapeDtypeStruct((2,) + saved.shape[2:], bf16),
+            jax.ShapeDtypeStruct((4,) + shape, f32),
+            jax.ShapeDtypeStruct((2,) + shape, f32),
+            jax.ShapeDtypeStruct((2,) + shape, bf16),
             jax.ShapeDtypeStruct(mine.shape, bf16),
         ),
-        in_specs=[whole, whole, pl.BlockSpec(memory_space=pl.ANY)],
-        out_specs=(whole,) * 3,
+        in_specs=[whole, whole, in_hbm],
+        out_specs=(whole,) * 4,
         scratch_shapes=[pltpu.SemaphoreType.DMA],
         compiler_params=params,
         name="saved_factors",
@@ -154,105 +157,124 @@
     return jnp.concatenate([notes.astype(f32)] * (wide // extra), axis=1)
 
 
-def raw_kernel(rows, mine, other, factors, g_mine, g_other, dots):
+def product_with(rows, weight):
+    return lax.dot_general(
+        rows, weight, (((1,), (1,)), ((), ())), preferred_element_type=f32
+    )
+
+
+def store_grads(out, raw, weights, gate, up, order):
+    slots = raw.shape[0] // 16
+    grad = weights * raw
+    for part, factor in enumerate((gate, up)):
+        value = (grad * factor).astype(bf16)
+        for chunk in range(16):
+            at = pl.ds(pl.multiple_of(order[chunk] * slots, slots), slots)
+            out[part, at, :] = value[chunk * slots : (chunk + 1) * slots]
+
+
+def raw_kernel(rows, mine, other, factors, grads, dots):
     count = rows.shape[0]
     width = rows.shape[1] - extra
     slots = count // 16
     core, _, far = position()
     order = token_blocks(core, far)
-    weights = slot_weights(rows[:, width:], factors.shape[3])
-    dot = jnp.zeros((count, 1), f32)
-    for index, (weight, out) in ((1, (mine, g_mine)), (0, (other, g_other))):
-        raw = lax.dot_general(
-            rows[:, :width], weight[...], (((1,), (1,)), ((), ())), preferred_element_type=f32
-        )
-        dot = dot + jnp.sum(factors[index, 0] * raw, axis=1, keepdims=True)
-        grad = weights * raw
-        for part in range(2):
-            value = (grad * factors[index, part + 1]).astype(bf16)
-            for chunk in range(16):
-                at = pl.ds(pl.multiple_of(order[chunk] * slots, slots), slots)
-                out[part, at, :] = value[chunk * slots : (chunk + 1) * slots]
+    raw_other = product_with(rows[:, :width], other[...])
+    raw = product_with(rows[:, :width], mine[...])
+    dot = jnp.sum(factors[0] * raw_other + factors[1] * raw, axis=1, keepdims=True)
     lane = lax.broadcasted_iota(jnp.int32, (count, 128), 1)
     row = lax.broadcasted_iota(jnp.int32, (count, 128), 0)
     spread = jnp.where(lane == (row & 15), dot, 0.0)
     for chunk in range(16):
         line = jnp.sum(spread[chunk * slots : (chunk + 1) * slots], axis=0, keepdims=True)
-        for core in range(2):
-            dots[pl.ds(order[chunk] * 2 + core, 1), :] = line
+        for target in range(2):
+            dots[pl.ds(order[chunk] * 2 + target, 1), :] = line
+    weights = slot_weights(rows[:, width:], raw.shape[1])
+    store_grads(grads, raw, weights, factors[2], factors[3], order)
 
 
 def raw_grads(rows, mine, other, factors):
-    grads = jax.ShapeDtypeStruct((2,) + factors.shape[2:], bf16)
     return pl.pallas_call(
         raw_kernel,
-        out_shape=(grads, grads, jax.ShapeDtypeStruct((32, 128), f32)),
+        out_shape=(
+            jax.ShapeDtypeStruct((2,) + factors.shape[1:], bf16),
+            jax.ShapeDtypeStruct((32, 128), f32),
+        ),
         in_specs=[whole] * 4,
-        out_specs=(whole,) * 3,
+        out_specs=(whole,) * 2,
         compiler_params=params,
         name="raw_grads",
     )(rows, mine, other, factors)
 
 
 def finish_kernel(
-    rows, notes, rows_other, notes_other, hidden, g_mine, g_other, *refs
+    rows, notes, rows_other, notes_other, mine, hidden, later, grads, *refs
 ):
-    tables, (pair_grads, weight_grad), passed, scaled = refs[:3], refs[3:5], refs[5:8], refs[8]
+    tables, (pair_grads, weight_grad), passed = refs[:3], refs[3:5], refs[5:8]
+    scaled, raw = refs[8:]
     count, wide = hidden.shape[1:]
-
-    @pl.when(pl.program_id(0) == 0)
+    step = pl.program_id(0)
+    span, near, _ = position()
+
+    @pl.when(step == 0)
     def _():
-        span = lax.axis_index("dp")
-        pair_grads[span] = g_mine[...]
-        pair_grads[1 - span] = g_other[...]
+        pair_grads[span] = grads[...]
         for table, out in zip(tables, passed, strict=True):
             out[...] = table[...]
         for index, ref in enumerate((notes, notes_other)):
             value = slot_weights(ref[...], wide) * hidden[index].astype(f32)
             scaled[:, index * count : (index + 1) * count] = value.T.astype(bf16)
+        raw[...] = jnp.zeros_like(raw)
 
     total = jnp.dot(scaled[:, :count], rows[...], preferred_element_type=f32)
     total = total + jnp.dot(scaled[:, count:], rows_other[...], preferred_element_type=f32)
     weight_grad[...] = total.astype(bf16)
-
-
-def finished(rows, rows_other, hidden, g_mine, g_other, tables):
+    columns = rows.shape[1]
+    here = pl.ds(pl.multiple_of(step * columns, 128), columns)
+    raw[...] += product_with(rows_other[...], mine[:, here])
+
+    @pl.when(step == pl.num_programs(0) - 1)
+    def _():
+        store_grads(
+            pair_grads.at[1 - span],
+            raw[...],
+            slot_weights(notes_other[...], wide),
+            later[0],
+            later[1],
+            token_blocks(1 - span, near),
+        )
+
+
+def finished(rows, rows_other, mine, hidden, later, grads, tables):
     count, wide = hidden.shape[1:]
     width = rows.shape[1] - extra
-    step = 512 if width % 512 == 0 else width
-
-    def kept(shape):
-        return pl.BlockSpec(shape, lambda i: (0,) * len(shape))
+    step = width // 2 if width % 256 == 0 else width
+
+    def kept(value):
+        return pl.BlockSpec(value.shape, lambda i: (0,) * len(value.shape))
 
     block = pl.BlockSpec((count, step), lambda i: (0, i))
     note = pl.BlockSpec((count, extra), lambda i: (0, width // extra))
+    weight = pl.BlockSpec((wide, step), lambda i: (0, i))
+    shapes = (
+        jax.ShapeDtypeStruct((2,) + grads.shape, bf16),
+        jax.ShapeDtypeStruct((wide, width), bf16),
+        *(jax.ShapeDtypeStruct(table.shape, table.dtype) for table in tables),
+    )
+    inputs = (hidden, later, grads, *tables)
     return pl.pallas_call(
         finish_kernel,
         grid=(width // step,),
-        out_shape=(
-            jax.ShapeDtypeStruct((2,) + g_mine.shape, bf16),
-            jax.ShapeDtypeStruct((wide, width), bf16),
-            *(jax.ShapeDtypeStruct(table.shape, table.dtype) for table in tables),
-        ),
-        in_specs=[
-            block,
-            note,
-            block,
-            note,
-            kept(hidden.shape),
-            kept(g_mine.shape),
-            kept(g_other.shape),
-            *(kept(table.shape) for table in tables),
+        out_shape=shapes,
+        in_specs=[block, note, block, note, whole, *(kept(value) for value in inputs)],
+        out_specs=(kept(shapes[0]), weight, *(kept(value) for value in shapes[2:])),
+        scratch_shapes=[
+            pltpu.VMEM((wide, 2 * count), bf16),
+            pltpu.VMEM((count, wide), f32),
         ],
-        out_specs=(
-            kept((2,) + g_mine.shape),
-            pl.BlockSpec((wide, step), lambda i: (0, i)),
-            *(kept(table.shape) for table in tables),
-        ),
-        scratch_shapes=[pltpu.VMEM((wide, 2 * count), bf16)],
         compiler_params=params,
         name="finished",
-    )(rows, rows, rows_other, rows_other, hidden, g_mine, g_other, *tables)
+    )(rows, rows, rows_other, rows_other, mine, *inputs)
 
 
 def logit_kernel(returned, experts, places, scores, out):
@@ -277,7 +299,7 @@
         out[second : second + 1] = scale * (route1 - mean) * score1 * (1.0 - score1)
 
 
-def note_kernel(ids, logits, notes, experts, places, scores):
+def note_kernel(ids, logits, notes, core, experts, places, scores):
     tokens = ids.shape[1]
     score = jax.nn.sigmoid(logits[...])
     scores[...] = score
@@ -296,6 +318,7 @@
     place = jnp.sum(before * marked, axis=0, keepdims=True)
     slot = lax.broadcasted_iota(jnp.int32, (128, 4 * tokens), 0).astype(f32)
     places[...] = jnp.where(slot == place, 1.0, 0.0)
+    core[...] = jnp.broadcast_to(lax.axis_index("dp"), core.shape)
     first = lax.axis_index("dp") == 0
     pair = jnp.where(first, score[0:2], score[2:4])
     lines = [
@@ -314,20 +337,19 @@
         note_kernel,
         out_shape=(
             jax.ShapeDtypeStruct((tokens, extra), bf16),
+            jax.ShapeDtypeStruct((tokens, 1), jnp.int32),
             jax.ShapeDtypeStruct((32, 4 * tokens), f32),
             jax.ShapeDtypeStruct((128, 4 * tokens), f32),
             jax.ShapeDtypeStruct((4, tokens), f32),
         ),
         in_specs=[whole] * 2,
-        out_specs=(whole,) * 4,
+        out_specs=(whole,) * 5,
         compiler_params=params,
         name="slot_notes",
     )(ids, logits)
 
 
 def local(sent_down, sent_up, expert_ids, router_logits, saved_gate_up, down_weight):
-    first = lax.axis_index("dp") == 0
-    segments = lax.axis_size("pipe")
     saved = saved_gate_up[:, 0, 0]
     mine = down_weight[0, 0]
     slots = saved.shape[2] // 16
@@ -336,22 +358,27 @@
     def by_slot(value):
         return jnp.swapaxes(value[:, 0], 1, 2).reshape(2 * top, tokens)
 
-    pairs = [(2 * z, 2 * (z - 1)) for z in range(1, segments)]
-    pairs += [(2 * z + 1, 2 * (z + 1) + 1) for z in range(segments - 1)]
-    outgoing, expert_ids, router_logits = lax.optimization_barrier(
-        (jnp.where(first, sent_down[0], sent_up[0]), expert_ids, router_logits)
-    )
-    incoming = lax.ppermute(outgoing, ("pipe", "dp"), pairs)
-    notes, experts, places, scores = slot_notes(by_slot(expert_ids), by_slot(router_logits))
+    count = lax.axis_size("pipe")
+    from_above = lax.ppermute(
+        sent_down[0], ("pipe", "dp"), [(2 * z, 2 * z - 2) for z in range(1, count)]
+    )
+    from_below = lax.ppermute(
+        sent_up[0], ("pipe", "dp"), [(2 * z + 1, 2 * z + 3) for z in range(count - 1)]
+    )
+    notes, core, experts, places, scores = slot_notes(
+        by_slot(expert_ids), by_slot(router_logits)
+    )
+    incoming = jnp.where(core == 0, from_above, from_below)
     block = jnp.concatenate([incoming, notes], axis=1)
     swapped_saved = swapped(saved)
-    block, held, swapped_saved = lax.optimization_barrier((block, mine, swapped_saved))
+    held, swapped_saved = lax.optimization_barrier((mine, swapped_saved))
     other = swapped(held)
+    block, swapped_saved = lax.optimization_barrier((block, swapped_saved))
 
     blocks = [block] + [plane_shift(block, step, True) for step in shifts]
-    factors, hidden, mine = saved_factors(saved, swapped_saved, mine)
-    blocks[1], other, mine, factors, hidden = lax.optimization_barrier(
-        (blocks[1], other, mine, factors, hidden)
+    factors, later, hidden, kept = saved_factors(saved, swapped_saved, mine)
+    blocks[1], other, kept, factors, later, hidden = lax.optimization_barrier(
+        (blocks[1], other, kept, factors, later, hidden)
     )
     pieces = select_rows(blocks, slots)
     pieces = [pieces[0]] + [
@@ -360,10 +387,10 @@
     rows = jnp.zeros((16 * slots, pieces[0].shape[1]), bf16)
     for index, piece in enumerate(pieces):
         rows = lax.dynamic_update_slice(rows, piece, (index * 4 * slots, 0))
-    g_mine, g_other, dots = raw_grads(rows, mine, other, factors)
+    grads, dots = raw_grads(rows, kept, other, factors)
     returned = lax.all_to_all(dots, ("expert", "dp"), split_axis=0, concat_axis=0, tiled=True)
     pair_grads, weight_grad, experts, places, scores = finished(
-        rows, swapped(rows), hidden, g_mine, swapped(g_other), (experts, places, scores)
+        rows, swapped(rows), mine, hidden, later, grads, (experts, places, scores)
     )
     returned, pair_grads, weight_grad = lax.optimization_barrier(
         (returned, pair_grads, weight_grad)

time: 55.8 us -> 54.6 us (0.978)
  Pallas kernels: 10.7 us -> 8.74 us
  local copies, waits for them, and re-layouts: 4.15 us -> 5.64 us
  starting transfers between devices: 23 us -> 24.1 us
  waiting for transfers between devices: 15.4 us -> 14.4 us
  other arithmetic: 0.99 us -> 0.22 us
    ppermute x6, starting transfers between devices: 6.97 us -> 9.69 us  [plane_shift(): return lax.ppermute(value, ('expert', 'dp'), pairs)]
    pallas_call x3, Pallas kernels: 8.58 us -> 6.65 us  [the longest x1 4.39 us: finished(): pl.pallas_call(finish_kernel, grid=(width // step,), out_shape=shapes, in...]
    ppermute x1 -> x2, starting transfers between devices: 4.38 us -> 2.48 us  [the longest x1 1.82 us: local(): lax.ppermute(sent_up[0], ('pipe', 'dp'), [(2 * z + 1, 2 * z + 3) for z in...]
    ppermute x6, waiting for transfers between devices: 13.7 us -> 12 us  [plane_shift(): return lax.ppermute(value, ('expert', 'dp'), pairs)]
    unnamed x8 -> x10, local copies, waits for them, and re-layouts: 3.9 us -> 5.39 us
    select_n x1, other arithmetic: 0.98 us -> 0.09 us  [local(): incoming = jnp.where(core == 0, from_above, from_below)]
    ppermute x4 -> x3, starting transfers between devices: 6.06 us -> 6.7 us  [swapped(): return lax.ppermute(value, 'dp', [(0, 1), (1, 0)])]
    ppermute x1 -> x2, waiting for transfers between devices: 1.13 us -> 1.45 us  [the longest x1 1.45 us: local(): lax.ppermute(sent_up[0], ('pipe', 'dp'), [(2 * z + 1, 2 * z + 3) for z in...]
  transfers between devices with their start and end apart: 12 -> 12, of which waited for: 7 -> 7; matrix products, arithmetic and copies ran while one was open for 0% -> 1% of each run, Pallas kernels for 16% -> 13%
where the time goes in v4:
time: 54.6 us; the launch traced here: 53.9 us
  starting transfers between devices  24.1 us (44%)
  waiting for transfers between devices  14.4 us (26%)
  Pallas kernels  8.74 us (16%)
  local copies, waits for them, and re-layouts  5.64 us (10%)
  between operations  0.78 us (1%)
    ppermute x6, waiting for transfers between devices, plane_shift(): return lax.ppermute(value, ('expert', 'dp'), pairs)  12 us
    ppermute x6, starting transfers between devices, plane_shift(): return lax.ppermute(value, ('expert', 'dp'), pairs)  9.69 us
    ppermute x3, starting transfers between devices, swapped(): return lax.ppermute(value, 'dp', [(0, 1), (1, 0)])  6.7 us
    unnamed x10, local copies, waits for them, and re-layouts  5.39 us
    all_to_all x1, starting transfers between devices, local(): lax.all_to_all(dots, ('expert', 'dp'), split_axis=0, concat_axis=0, tiled...  5.23 us
    pallas_call x1, Pallas kernels, finished(): pl.pallas_call(finish_kernel, grid=(width // step,), out_shape=shapes, in...  4.39 us
    pallas_call x1, Pallas kernels, raw_grads(): pl.pallas_call(raw_kernel, out_shape=(jax.ShapeDtypeStruct((2,) + factors...  1.83 us
    ppermute x1, starting transfers between devices, local(): lax.ppermute(sent_up[0], ('pipe', 'dp'), [(2 * z + 1, 2 * z + 3) for z in...  1.82 us
  transfers between devices with their start and end apart: 12, of which 7 were waited for; matrix products, arithmetic and copies ran while one was open for 1% of the time, Pallas kernels for 13%

profile of v4, /device:TPU:1, one launch (start us, length us, event | category | flops | bytes accessed | tf_op | source)
XLA Modules:
  0.0 53.9 jit_solution(2589676128288869189)
XLA Ops:
  0.6 3.3 %collective-permute-start.2 = (bf16[2,2,256,256]{3,2,1,0:T(8,128)(2,1)}, bf16[2,2,256,256]{3,2,1,0:T(8,128)(2,1)S(1)}, u32[]{:S(2)}, u32[]{:S(2)}) collective-permute-start(bf16[2,2,256,256]{3,2,1,0:T(8,128)(2,1)} %bitcast.30), channel_id=1, source_target_pairs={{0,1},{1,0},{2,3},{3,2},{4,5},{5,4},{6,7},{7,6},{8,9},{9,8},{10,11... | collective-permute-start | bytes 1572872 | tf_op jit(solution)/shard_map/ppermute | solution.py:33
  4.0 0.7 %collective-permute-start = (bf16[32,3584]{1,0:T(8,128)(2,1)}, bf16[32,3584]{1,0:T(8,128)(2,1)S(1)}, u32[]{:S(2)}, u32[]{:S(2)}) collective-permute-start(bf16[32,3584]{1,0:T(8,128)(2,1)} %bitcast.38), channel_id=1, source_target_pairs={{32,0},{64,32},{96,64},{128,96},{160,128},{192,160},{224,192},{34,... | collective-permute-start | bytes 688136 | tf_op jit(solution)/shard_map/ppermute | solution.py:362
  4.6 1.8 %collective-permute-start.1 = (bf16[32,3584]{1,0:T(8,128)(2,1)}, bf16[32,3584]{1,0:T(8,128)(2,1)S(1)}, u32[]{:S(2)}, u32[]{:S(2)}) collective-permute-start(bf16[32,3584]{1,0:T(8,128)(2,1)} %bitcast.39), channel_id=1, source_target_pairs={{1,33},{33,65},{65,97},{97,129},{129,161},{161,193},{193,225},{3,3... | collective-permute-start | bytes 688136 | tf_op jit(solution)/shard_map/ppermute | solution.py:365
  6.5 0.0 collective-permute-done.2.swapped_saved
  6.5 0.1 collective-permute-start.4
  6.6 0.0 copy-start.3
  6.6 0.7 %copy-done.3 = s32[2,1,32,2]{2,3,1,0:T(2,128)S(1)} copy-done((s32[2,1,32,2]{2,3,1,0:T(2,128)S(1)}, s32[2,1,32,2]{2,3,1,0:T(2,128)}, u32[]{:S(2)}) %copy-start.3) | copy-done | bytes 536
  7.3 0.0 copy-start.4
  7.3 0.7 %copy-done.4 = f32[2,1,32,2]{2,3,1,0:T(2,128)S(1)} copy-done((f32[2,1,32,2]{2,3,1,0:T(2,128)S(1)}, f32[2,1,32,2]{2,3,1,0:T(2,128)}, u32[]{:S(2)}) %copy-start.4) | copy-done | bytes 536
  7.9 0.2 slot_notes.1
  8.1 0.1 compare_reduce_fusion
  8.3 0.0 collective-permute-done
  8.3 1.4 %collective-permute-done.1 = bf16[32,3584]{1,0:T(8,128)(2,1)S(1)} collective-permute-done((bf16[32,3584]{1,0:T(8,128)(2,1)}, bf16[32,3584]{1,0:T(8,128)(2,1)S(1)}, u32[]{:S(2)}, u32[]{:S(2)}) %collective-permute-start.1) | collective-permute-done | bytes 229408 | tf_op jit(solution)/shard_map/ppermute | solution.py:365
  9.7 0.1 broadcast_select_fusion
  9.8 3.0 %collective-permute-start.3 = (bf16[32,3712]{1,0:T(8,128)(2,1)S(1)}, bf16[32,3712]{1,0:T(8,128)(2,1)S(1)}, u32[]{:S(2)}, u32[]{:S(2)}) collective-permute-start(bf16[32,3712]{1,0:T(8,128)(2,1)S(1)} %pad_maximum_fusion.refs_0_), channel_id=1, source_target_pairs={{0,4},{1,17},{2,6},{3,19},{4,0},{5,21},{6,2},{7,23},{8,12},{9,25},... | collective-permute-start | bytes 712712 | tf_op jit(solution)/shard_map/ppermute | solution.py:29
  12.8 0.8 %collective-permute-start.6 = (bf16[32,3712]{1,0:T(8,128)(2,1)S(1)}, bf16[32,3712]{1,0:T(8,128)(2,1)S(1)}, u32[]{:S(2)}, u32[]{:S(2)}) collective-permute-start(bf16[32,3712]{1,0:T(8,128)(2,1)S(1)} %pad_maximum_fusion.refs_0_), channel_id=1, source_target_pairs={{0,6},{1,25},{2,0},{3,27},{4,2},{5,29},{6,4},{7,31},{8,14},{9,1},{... | collective-permute-start | bytes 712712 | tf_op jit(solution)/shard_map/ppermute | solution.py:29
  13.6 0.7 %collective-permute-start.5 = (bf16[32,3712]{1,0:T(8,128)(2,1)S(1)}, bf16[32,3712]{1,0:T(8,128)(2,1)S(1)}, u32[]{:S(2)}, u32[]{:S(2)}) collective-permute-start(bf16[32,3712]{1,0:T(8,128)(2,1)S(1)} %pad_maximum_fusion.refs_0_), channel_id=1, source_target_pairs={{0,2},{1,9},{2,4},{3,11},{4,6},{5,13},{6,0},{7,15},{8,10},{9,17},{... | collective-permute-start | bytes 712712 | tf_op jit(solution)/shard_map/ppermute | solution.py:29
  14.3 0.0 copy-start
  14.3 1.5 %copy-done = bf16[1,1,256,3584]{3,2,1,0:T(8,128)(2,1)S(1)} copy-done((bf16[1,1,256,3584]{3,2,1,0:T(8,128)(2,1)S(1)}, bf16[1,1,256,3584]{3,2,1,0:T(8,128)(2,1)}, u32[]{:S(2)}) %copy-start) | copy-done | bytes 1835032
  15.8 0.0 copy-start.2
  15.8 1.0 %copy-done.2 = bf16[2,1,1,2,256,256]{5,4,3,2,1,0:T(8,128)(2,1)S(1)} copy-done((bf16[2,1,1,2,256,256]{5,4,3,2,1,0:T(8,128)(2,1)S(1)}, bf16[2,1,1,2,256,256]{5,4,3,2,1,0:T(8,128)(2,1)}, u32[]{:S(2)}) %copy-start.2) | copy-done | bytes 524312
  16.8 0.4 saved_factors.1
  17.3 0.0 collective-permute-done.3.refs_1_
  17.3 0.0 collective-permute-done.4.other
  17.3 2.3 %collective-permute-done.6.refs_3_ = bf16[32,3712]{1,0:T(8,128)(2,1)S(1)} collective-permute-done((bf16[32,3712]{1,0:T(8,128)(2,1)S(1)}, bf16[32,3712]{1,0:T(8,128)(2,1)S(1)}, u32[]{:S(2)}, u32[]{:S(2)}) %collective-permute-start.6) | collective-permute-done | bytes 237600 | tf_op jit(solution)/shard_map/ppermute | solution.py:29
  19.6 0.5 collective-permute-done.5.refs_2_
  20.1 0.8 %select_rows.1 = (bf16[64,3712]{1,0:T(8,128)(2,1)S(1)}, bf16[64,3712]{1,0:T(8,128)(2,1)S(1)}, bf16[64,3712]{1,0:T(8,128)(2,1)S(1)}, bf16[64,3712]{1,0:T(8,128)(2,1)S(1)}) custom-call(bf16[32,3712]{1,0:T(8,128)(2,1)S(1)} %pad_maximum_fusion.refs_0_, bf16[32,3712]{1,0:T(8,128)(2,1)S(1)} %collective-permute-done.3.refs_1_, ...), custom_call_target="tpu_custom_call" | custom-call | tf_op jit(solution)/shard_map/select_rows/pallas_call | solution.py:100
  20.9 2.5 %collective-permute-start.7 = (bf16[64,3712]{1,0:T(8,128)(2,1)S(1)}, bf16[64,3712]{1,0:T(8,128)(2,1)S(1)}, u32[]{:S(2)}, u32[]{:S(2)}) collective-permute-start(bf16[64,3712]{1,0:T(8,128)(2,1)S(1)} %get-tuple-element.48), channel_id=1, source_target_pairs={{0,16},{1,5},{2,18},{3,7},{4,20},{5,1},{6,22},{7,3},{8,24},{9,13},... | collective-permute-start | bytes 1425416 | tf_op jit(solution)/shard_map/ppermute | solution.py:29
  23.5 0.6 %collective-permute-start.8 = (bf16[64,3712]{1,0:T(8,128)(2,1)S(1)}, bf16[64,3712]{1,0:T(8,128)(2,1)S(1)}, u32[]{:S(2)}, u32[]{:S(2)}) collective-permute-start(bf16[64,3712]{1,0:T(8,128)(2,1)S(1)} %get-tuple-element.49), channel_id=1, source_target_pairs={{0,8},{1,3},{2,10},{3,5},{4,12},{5,7},{6,14},{7,1},{8,16},{9,11},{... | collective-permute-start | bytes 1425416 | tf_op jit(solution)/shard_map/ppermute | solution.py:29
  24.1 2.1 %collective-permute-start.9 = (bf16[64,3712]{1,0:T(8,128)(2,1)S(1)}, bf16[64,3712]{1,0:T(8,128)(2,1)S(1)}, u32[]{:S(2)}, u32[]{:S(2)}) collective-permute-start(bf16[64,3712]{1,0:T(8,128)(2,1)S(1)} %get-tuple-element.50), channel_id=1, source_target_pairs={{0,24},{1,7},{2,26},{3,1},{4,28},{5,3},{6,30},{7,5},{8,0},{9,15},{... | collective-permute-start | bytes 1425416 | tf_op jit(solution)/shard_map/ppermute | solution.py:29
  26.1 0.1 dynamic_update_slice.12
  26.3 4.1 %collective-permute-done.7 = bf16[64,3712]{1,0:T(8,128)(2,1)S(1)} collective-permute-done((bf16[64,3712]{1,0:T(8,128)(2,1)S(1)}, bf16[64,3712]{1,0:T(8,128)(2,1)S(1)}, u32[]{:S(2)}, u32[]{:S(2)}) %collective-permute-start.7) | collective-permute-done | bytes 475168 | tf_op jit(solution)/shard_map/ppermute | solution.py:29
  30.4 5.0 %collective-permute-done.8 = bf16[64,3712]{1,0:T(8,128)(2,1)S(1)} collective-permute-done((bf16[64,3712]{1,0:T(8,128)(2,1)S(1)}, bf16[64,3712]{1,0:T(8,128)(2,1)S(1)}, u32[]{:S(2)}, u32[]{:S(2)}) %collective-permute-start.8) | collective-permute-done | bytes 475168 | tf_op jit(solution)/shard_map/ppermute | solution.py:29
  35.4 0.1 collective-permute-done.9
  35.6 3.3 %collective-permute-start.10 = (bf16[256,3712]{1,0:T(8,128)(2,1)S(1)}, bf16[256,3712]{1,0:T(8,128)(2,1)}, u32[]{:S(2)}, u32[]{:S(2)}) collective-permute-start(bf16[256,3712]{1,0:T(8,128)(2,1)S(1)} %constant_dynamic-update-slice_fusion.rows.notes), channel_id=1, source_target_pairs={{0,1},{1,0},{2,3},{3,2},{4,5},{5,4},{6,7},{7,6},{8,9},{9,8},{10,11... | collective-permute-start | bytes 5701640 | tf_op jit(solution)/shard_map/ppermute | solution.py:33
  38.9 1.8 %raw_grads.1 = (bf16[2,256,256]{2,1,0:T(8,128)(2,1)S(1)}, f32[32,128]{1,0:T(8,128)}) custom-call(bf16[256,3712]{1,0:T(8,128)(2,1)S(1)} %constant_dynamic-update-slice_fusion.rows.notes, bf16[256,3584]{1,0:T(8,128)(2,1)S(1)} %get-tuple-element.51.mine, bf16[256,3584]{1,0:T(8,128)(2,1)S(1)} %collective-permute-done.4.other, ...), custom_call_target="tpu_custom_call" | custom-call | tf_op jit(solution)/shard_map/raw_grads/pallas_call | solution.py:197
  40.7 5.2 %all-to-all-start = ((f32[32,1,128]{2,1,0:T(1,128)}), f32[32,1,128]{2,1,0:T(1,128)S(1)}, u32[]{:S(2)}, u32[]{:S(2)}) async-start(f32[32,1,128]{2,1,0:T(1,128)} %bitcast.11), calls=%async_computation | async-start | bytes 32768 | tf_op jit(solution)/shard_map/all_to_all | solution.py:391
  45.9 0.0 collective-permute-done.10.rows_other.notes_other
  45.9 0.0 copy-start.1
  45.9 1.5 %copy-done.1 = bf16[1,1,256,3584]{3,2,1,0:T(8,128)(2,1)S(1)} copy-done((bf16[1,1,256,3584]{3,2,1,0:T(8,128)(2,1)S(1)}, bf16[1,1,256,3584]{3,2,1,0:T(8,128)(2,1)}, u32[]{:S(2)}) %copy-start.1) | copy-done | bytes 1835032
  47.4 4.4 %finished.1 = (bf16[2,2,256,256]{3,2,1,0:T(8,128)(2,1)}, bf16[256,3584]{1,0:T(8,128)(2,1)}, f32[32,128]{1,0:T(8,128)S(1)}, f32[128,128]{1,0:T(8,128)S(1)}, f32[4,32]{1,0:T(4,128)S(1)}) custom-call(bf16[256,3712]{1,0:T(8,128)(2,1)S(1)} %constant_dynamic-update-slice_fusion.rows.notes, bf16[256,3712]{1,0:T(8,128)(2,1)S(1)} %constant_dynamic-update-slice_fusion.rows.notes, ...), custom_call_target="tpu_custom_call" | custom-call | tf_op jit(solution)/shard_map/finished/pallas_call | solution.py:265
  51.8 1.0 %all-to-all-done = f32[32,1,128]{2,1,0:T(1,128)S(1)} async-done(((f32[32,1,128]{2,1,0:T(1,128)}), f32[32,1,128]{2,1,0:T(1,128)S(1)}, u32[]{:S(2)}, u32[]{:S(2)}) %all-to-all-start) | async-done | bytes 16416 | tf_op jit(solution)/shard_map/all_to_all | solution.py:391
  52.9 1.1 %logit_grads.1 = f32[4,32]{1,0:T(4,128)} custom-call(f32[32,128]{1,0:T(8,128)S(1)} %bitcast.32, f32[32,128]{1,0:T(8,128)S(1)} %get-tuple-element.66.experts, f32[128,128]{1,0:T(8,128)S(1)} %get-tuple-element.67.places, f32[4,32]{1,0:T(4,128)S(1)} %get-tuple-element.68.scores), custom_call_target="tpu_custom_call" | custom-call | tf_op jit(solution)/shard_map/logit_grads/pallas_call | solution.py:398
  (4 shorter events, 0.1 us)
Async XLA Ops:
  0.6 5.8 %collective-permute-start.2 = (bf16[2,2,256,256]{3,2,1,0:T(8,128)(2,1)}, bf16[2,2,256,256]{3,2,1,0:T(8,128)(2,1)S(1)}, u32[]{:S(2)}, u32[]{:S(2)}) collective-permute-start(bf16[2,2,256,256]{3,2,1,0:T(8,128)(2,1)} %bitcast.30), channel_id=1, source_target_pairs={{0,1},{1,0},{2,3},{3,2},{4,5},{5,4},{6,7},{7,6},{8,9},{9,8},{10,11... | collective-permute-start | bytes 1572872 | tf_op jit(solution)/shard_map/ppermute | solution.py:33
  4.0 4.3 %collective-permute-start = (bf16[32,3584]{1,0:T(8,128)(2,1)}, bf16[32,3584]{1,0:T(8,128)(2,1)S(1)}, u32[]{:S(2)}, u32[]{:S(2)}) collective-permute-start(bf16[32,3584]{1,0:T(8,128)(2,1)} %bitcast.38), channel_id=1, source_target_pairs={{32,0},{64,32},{96,64},{128,96},{160,128},{192,160},{224,192},{34,... | collective-permute-start | bytes 688136 | tf_op jit(solution)/shard_map/ppermute | solution.py:362
  4.6 5.1 %collective-permute-start.1 = (bf16[32,3584]{1,0:T(8,128)(2,1)}, bf16[32,3584]{1,0:T(8,128)(2,1)S(1)}, u32[]{:S(2)}, u32[]{:S(2)}) collective-permute-start(bf16[32,3584]{1,0:T(8,128)(2,1)} %bitcast.39), channel_id=1, source_target_pairs={{1,33},{33,65},{65,97},{97,129},{129,161},{161,193},{193,225},{3,3... | collective-permute-start | bytes 688136 | tf_op jit(solution)/shard_map/ppermute | solution.py:365
  6.5 10.8 %collective-permute-start.4 = (bf16[256,3584]{1,0:T(8,128)(2,1)}, bf16[256,3584]{1,0:T(8,128)(2,1)S(1)}, u32[]{:S(2)}, u32[]{:S(2)}) collective-permute-start(bf16[256,3584]{1,0:T(8,128)(2,1)} %bitcast.27), channel_id=1, source_target_pairs={{0,1},{1,0},{2,3},{3,2},{4,5},{5,4},{6,7},{7,6},{8,9},{9,8},{10,11... | collective-permute-start | bytes 5505032 | tf_op jit(solution)/shard_map/ppermute | solution.py:33
  6.6 0.7 %copy-start.3 = (s32[2,1,32,2]{2,3,1,0:T(2,128)S(1)}, s32[2,1,32,2]{2,3,1,0:T(2,128)}, u32[]{:S(2)}) copy-start(s32[2,1,32,2]{2,3,1,0:T(2,128)} %param.8) | copy-start | bytes 1540
  7.3 0.7 %copy-start.4 = (f32[2,1,32,2]{2,3,1,0:T(2,128)S(1)}, f32[2,1,32,2]{2,3,1,0:T(2,128)}, u32[]{:S(2)}) copy-start(f32[2,1,32,2]{2,3,1,0:T(2,128)} %param.9) | copy-start | bytes 1540
  9.8 7.4 %collective-permute-start.3 = (bf16[32,3712]{1,0:T(8,128)(2,1)S(1)}, bf16[32,3712]{1,0:T(8,128)(2,1)S(1)}, u32[]{:S(2)}, u32[]{:S(2)}) collective-permute-start(bf16[32,3712]{1,0:T(8,128)(2,1)S(1)} %pad_maximum_fusion.refs_0_), channel_id=1, source_target_pairs={{0,4},{1,17},{2,6},{3,19},{4,0},{5,21},{6,2},{7,23},{8,12},{9,25},... | collective-permute-start | bytes 712712 | tf_op jit(solution)/shard_map/ppermute | solution.py:29
  12.8 6.8 %collective-permute-start.6 = (bf16[32,3712]{1,0:T(8,128)(2,1)S(1)}, bf16[32,3712]{1,0:T(8,128)(2,1)S(1)}, u32[]{:S(2)}, u32[]{:S(2)}) collective-permute-start(bf16[32,3712]{1,0:T(8,128)(2,1)S(1)} %pad_maximum_fusion.refs_0_), channel_id=1, source_target_pairs={{0,6},{1,25},{2,0},{3,27},{4,2},{5,29},{6,4},{7,31},{8,14},{9,1},{... | collective-permute-start | bytes 712712 | tf_op jit(solution)/shard_map/ppermute | solution.py:29
  13.6 6.5 %collective-permute-start.5 = (bf16[32,3712]{1,0:T(8,128)(2,1)S(1)}, bf16[32,3712]{1,0:T(8,128)(2,1)S(1)}, u32[]{:S(2)}, u32[]{:S(2)}) collective-permute-start(bf16[32,3712]{1,0:T(8,128)(2,1)S(1)} %pad_maximum_fusion.refs_0_), channel_id=1, source_target_pairs={{0,2},{1,9},{2,4},{3,11},{4,6},{5,13},{6,0},{7,15},{8,10},{9,17},{... | collective-permute-start | bytes 712712 | tf_op jit(solution)/shard_map/ppermute | solution.py:29
  14.3 1.5 %copy-start = (bf16[1,1,256,3584]{3,2,1,0:T(8,128)(2,1)S(1)}, bf16[1,1,256,3584]{3,2,1,0:T(8,128)(2,1)}, u32[]{:S(2)}) copy-start(bf16[1,1,256,3584]{3,2,1,0:T(8,128)(2,1)} %param.11) | copy-start | bytes 5505028
  15.8 1.0 %copy-start.2 = (bf16[2,1,1,2,256,256]{5,4,3,2,1,0:T(8,128)(2,1)S(1)}, bf16[2,1,1,2,256,256]{5,4,3,2,1,0:T(8,128)(2,1)}, u32[]{:S(2)}) copy-start(bf16[2,1,1,2,256,256]{5,4,3,2,1,0:T(8,128)(2,1)} %param.10) | copy-start | bytes 1572868
  20.9 9.4 %collective-permute-start.7 = (bf16[64,3712]{1,0:T(8,128)(2,1)S(1)}, bf16[64,3712]{1,0:T(8,128)(2,1)S(1)}, u32[]{:S(2)}, u32[]{:S(2)}) collective-permute-start(bf16[64,3712]{1,0:T(8,128)(2,1)S(1)} %get-tuple-element.48), channel_id=1, source_target_pairs={{0,16},{1,5},{2,18},{3,7},{4,20},{5,1},{6,22},{7,3},{8,24},{9,13},... | collective-permute-start | bytes 1425416 | tf_op jit(solution)/shard_map/ppermute | solution.py:29
  23.5 11.9 %collective-permute-start.8 = (bf16[64,3712]{1,0:T(8,128)(2,1)S(1)}, bf16[64,3712]{1,0:T(8,128)(2,1)S(1)}, u32[]{:S(2)}, u32[]{:S(2)}) collective-permute-start(bf16[64,3712]{1,0:T(8,128)(2,1)S(1)} %get-tuple-element.49), channel_id=1, source_target_pairs={{0,8},{1,3},{2,10},{3,5},{4,12},{5,7},{6,14},{7,1},{8,16},{9,11},{... | collective-permute-start | bytes 1425416 | tf_op jit(solution)/shard_map/ppermute | solution.py:29
  24.1 11.5 %collective-permute-start.9 = (bf16[64,3712]{1,0:T(8,128)(2,1)S(1)}, bf16[64,3712]{1,0:T(8,128)(2,1)S(1)}, u32[]{:S(2)}, u32[]{:S(2)}) collective-permute-start(bf16[64,3712]{1,0:T(8,128)(2,1)S(1)} %get-tuple-element.50), channel_id=1, source_target_pairs={{0,24},{1,7},{2,26},{3,1},{4,28},{5,3},{6,30},{7,5},{8,0},{9,15},{... | collective-permute-start | bytes 1425416 | tf_op jit(solution)/shard_map/ppermute | solution.py:29
  35.6 10.4 %collective-permute-start.10 = (bf16[256,3712]{1,0:T(8,128)(2,1)S(1)}, bf16[256,3712]{1,0:T(8,128)(2,1)}, u32[]{:S(2)}, u32[]{:S(2)}) collective-permute-start(bf16[256,3712]{1,0:T(8,128)(2,1)S(1)} %constant_dynamic-update-slice_fusion.rows.notes), channel_id=1, source_target_pairs={{0,1},{1,0},{2,3},{3,2},{4,5},{5,4},{6,7},{7,6},{8,9},{9,8},{10,11... | collective-permute-start | bytes 5701640 | tf_op jit(solution)/shard_map/ppermute | solution.py:33
  40.7 12.2 %all-to-all-start = ((f32[32,1,128]{2,1,0:T(1,128)}), f32[32,1,128]{2,1,0:T(1,128)S(1)}, u32[]{:S(2)}, u32[]{:S(2)}) async-start(f32[32,1,128]{2,1,0:T(1,128)} %bitcast.11), calls=%async_computation | async-start | bytes 32768 | tf_op jit(solution)/shard_map/all_to_all | solution.py:391
  45.9 1.5 %copy-start.1 = (bf16[1,1,256,3584]{3,2,1,0:T(8,128)(2,1)S(1)}, bf16[1,1,256,3584]{3,2,1,0:T(8,128)(2,1)}, u32[]{:S(2)}) copy-start(bf16[1,1,256,3584]{3,2,1,0:T(8,128)(2,1)} %param.11) | copy-start | bytes 5505028

commit v5 on v4

--- a/solution.py
+++ b/solution.py
@@ -107,7 +107,7 @@
     )(*blocks)
 
 
-def factor_kernel(saved, swapped_saved, mine, factors, later, hidden, kept, arrived):
+def factor_kernel(saved, swapped_saved, mine, factors, hidden, kept, arrived):
     fetch = pltpu.make_async_copy(mine, kept, arrived)
     fetch.start()
     slots = saved.shape[2] // 16
@@ -119,19 +119,17 @@
         gate, up = ref[which, 0, at, :].astype(f32), ref[which, 1, at, :].astype(f32)
         sigma = jax.nn.sigmoid(gate)
         silu = gate * sigma
-        return up * sigma * (1.0 + gate * (1.0 - sigma)), silu, (silu * up).astype(bf16)
+        return (silu * up).astype(bf16), up * sigma * (1.0 + gate * (1.0 - sigma)), silu
 
     for chunk in range(16):
         here = slice(chunk * slots, (chunk + 1) * slots)
-        factors[0, here, :] = loaded(swapped_saved, span, order[chunk])[2].astype(f32)
-        gate, up, product = loaded(saved, span, order[chunk])
-        factors[1, here, :] = product.astype(f32)
-        factors[2, here, :] = gate
-        factors[3, here, :] = up
+        for base, ref in ((0, swapped_saved), (3, saved)):
+            product, gate, up = loaded(ref, span, order[chunk])
+            factors[base, here, :] = product.astype(f32)
+            factors[base + 1, here, :] = gate
+            factors[base + 2, here, :] = up
         hidden[0, here, :] = product
-        later[0, here, :], later[1, here, :], hidden[1, here, :] = loaded(
-            saved, 1 - span, order_other[chunk]
-        )
+        hidden[1, here, :] = loaded(saved, 1 - span, order_other[chunk])[0]
     fetch.wait()
 
 
@@ -140,13 +138,12 @@
     return pl.pallas_call(
         factor_kernel,
         out_shape=(
-            jax.ShapeDtypeStruct((4,) + shape, f32),
-            jax.ShapeDtypeStruct((2,) + shape, f32),
+            jax.ShapeDtypeStruct((6,) + shape, f32),
             jax.ShapeDtypeStruct((2,) + shape, bf16),
             jax.ShapeDtypeStruct(mine.shape, bf16),
         ),
         in_specs=[whole, whole, in_hbm],
-        out_specs=(whole,) * 4,
+        out_specs=(whole,) * 3,
         scratch_shapes=[pltpu.SemaphoreType.DMA],
         compiler_params=params,
         name="saved_factors",
@@ -157,95 +154,113 @@
     return jnp.concatenate([notes.astype(f32)] * (wide // extra), axis=1)
 
 
-def product_with(rows, weight):
-    return lax.dot_general(
-        rows, weight, (((1,), (1,)), ((), ())), preferred_element_type=f32
-    )
-
-
-def store_grads(out, raw, weights, gate, up, order):
-    slots = raw.shape[0] // 16
-    grad = weights * raw
-    for part, factor in enumerate((gate, up)):
-        value = (grad * factor).astype(bf16)
-        for chunk in range(16):
-            at = pl.ds(pl.multiple_of(order[chunk] * slots, slots), slots)
-            out[part, at, :] = value[chunk * slots : (chunk + 1) * slots]
-
-
-def raw_kernel(rows, mine, other, factors, grads, dots):
+def raw_values(pieces, mine, other, factors, start):
+    width = pieces[0].shape[1] - extra
+    rows = jnp.concatenate([piece[:, :width] for piece in pieces], axis=0)
+    notes = jnp.concatenate([piece[:, width:] for piece in pieces], axis=0)
     count = rows.shape[0]
-    width = rows.shape[1] - extra
-    slots = count // 16
-    core, _, far = position()
-    order = token_blocks(core, far)
-    raw_other = product_with(rows[:, :width], other[...])
-    raw = product_with(rows[:, :width], mine[...])
-    dot = jnp.sum(factors[0] * raw_other + factors[1] * raw, axis=1, keepdims=True)
+    here = slice(start, start + count)
+    weights = slot_weights(notes, factors.shape[2])
+    dot = jnp.zeros((count, 1), f32)
+    values = []
+    for base, weight in ((3, mine), (0, other)):
+        raw = lax.dot_general(
+            rows, weight[...], (((1,), (1,)), ((), ())), preferred_element_type=f32
+        )
+        dot = dot + jnp.sum(factors[base, here, :] * raw, axis=1, keepdims=True)
+        grad = weights * raw
+        for part in range(1, 3):
+            values.append((grad * factors[base + part, here, :]).astype(bf16))
     lane = lax.broadcasted_iota(jnp.int32, (count, 128), 1)
     row = lax.broadcasted_iota(jnp.int32, (count, 128), 0)
     spread = jnp.where(lane == (row & 15), dot, 0.0)
+    lines = [
+        jnp.sum(spread[chunk : chunk + 16], axis=0, keepdims=True)
+        for chunk in range(0, count, 16)
+    ]
+    return values, lines
+
+
+def first_kernel(piece0, piece1, mine, other, factors, values, lines):
+    results, sums = raw_values((piece0, piece1), mine, other, factors, 0)
+    for index, value in enumerate(results):
+        values[index] = value
+    for index, line in enumerate(sums):
+        lines[index : index + 1] = line
+
+
+def first_grads(pieces, mine, other, factors):
+    count = 2 * pieces[0].shape[0]
+    return pl.pallas_call(
+        first_kernel,
+        out_shape=(
+            jax.ShapeDtypeStruct((4, count, factors.shape[2]), bf16),
+            jax.ShapeDtypeStruct((count // 16, 128), f32),
+        ),
+        in_specs=[whole] * 5,
+        out_specs=(whole,) * 2,
+        compiler_params=params,
+        name="first_grads",
+    )(*pieces, mine, other, factors)
+
+
+def last_kernel(
+    piece0, piece1, mine, other, factors, values, lines, g_mine, g_other, dots
+):
+    half = values.shape[1]
+    core, _, far = position()
+    order = token_blocks(core, far)
+    results, sums = raw_values((piece0, piece1), mine, other, factors, half)
     for chunk in range(16):
-        line = jnp.sum(spread[chunk * slots : (chunk + 1) * slots], axis=0, keepdims=True)
+        line = lines[chunk : chunk + 1] if chunk < 8 else sums[chunk - 8]
         for target in range(2):
             dots[pl.ds(order[chunk] * 2 + target, 1), :] = line
-    weights = slot_weights(rows[:, width:], raw.shape[1])
-    store_grads(grads, raw, weights, factors[2], factors[3], order)
-
-
-def raw_grads(rows, mine, other, factors):
-    return pl.pallas_call(
-        raw_kernel,
-        out_shape=(
-            jax.ShapeDtypeStruct((2,) + factors.shape[1:], bf16),
-            jax.ShapeDtypeStruct((32, 128), f32),
-        ),
-        in_specs=[whole] * 4,
-        out_specs=(whole,) * 2,
-        compiler_params=params,
-        name="raw_grads",
-    )(rows, mine, other, factors)
+    for chunk in range(16):
+        at = pl.ds(pl.multiple_of(order[chunk] * 16, 16), 16)
+        start = chunk % 8 * 16
+        for index in range(4):
+            out = g_mine if index < 2 else g_other
+            if chunk < 8:
+                out[index % 2, at, :] = values[index, start : start + 16]
+            else:
+                out[index % 2, at, :] = results[index][start : start + 16]
+
+
+def last_grads(pieces, mine, other, factors, values, lines):
+    grads = jax.ShapeDtypeStruct((2,) + factors.shape[1:], bf16)
+    return pl.pallas_call(
+        last_kernel,
+        out_shape=(grads, grads, jax.ShapeDtypeStruct((32, 128), f32)),
+        in_specs=[whole] * 7,
+        out_specs=(whole,) * 3,
+        compiler_params=params,
+        name="last_grads",
+    )(*pieces, mine, other, factors, values, lines)
 
 
 def finish_kernel(
-    rows, notes, rows_other, notes_other, mine, hidden, later, grads, *refs
+    rows, notes, rows_other, notes_other, hidden, g_mine, g_other, *refs
 ):
-    tables, (pair_grads, weight_grad), passed = refs[:3], refs[3:5], refs[5:8]
-    scaled, raw = refs[8:]
+    tables, (pair_grads, weight_grad), passed, scaled = refs[:3], refs[3:5], refs[5:8], refs[8]
     count, wide = hidden.shape[1:]
-    step = pl.program_id(0)
-    span, near, _ = position()
-
-    @pl.when(step == 0)
+
+    @pl.when(pl.program_id(0) == 0)
     def _():
-        pair_grads[span] = grads[...]
+        span = lax.axis_index("dp")
+        pair_grads[span] = g_mine[...]
+        pair_grads[1 - span] = g_other[...]
         for table, out in zip(tables, passed, strict=True):
             out[...] = table[...]
         for index, ref in enumerate((notes, notes_other)):
             value = slot_weights(ref[...], wide) * hidden[index].astype(f32)
             scaled[:, index * count : (index + 1) * count] = value.T.astype(bf16)
-        raw[...] = jnp.zeros_like(raw)
 
     total = jnp.dot(scaled[:, :count], rows[...], preferred_element_type=f32)
     total = total + jnp.dot(scaled[:, count:], rows_other[...], preferred_element_type=f32)
     weight_grad[...] = total.astype(bf16)
-    columns = rows.shape[1]
-    here = pl.ds(pl.multiple_of(step * columns, 128), columns)
-    raw[...] += product_with(rows_other[...], mine[:, here])
-
-    @pl.when(step == pl.num_programs(0) - 1)
-    def _():
-        store_grads(
-            pair_grads.at[1 - span],
-            raw[...],
-            slot_weights(notes_other[...], wide),
-            later[0],
-            later[1],
-            token_blocks(1 - span, near),
-        )
-
-
-def finished(rows, rows_other, mine, hidden, later, grads, tables):
+
+
+def finished(rows, rows_other, hidden, g_mine, g_other, tables):
     count, wide = hidden.shape[1:]
     width = rows.shape[1] - extra
     step = width // 2 if width % 256 == 0 else width
@@ -255,38 +270,42 @@
 
     block = pl.BlockSpec((count, step), lambda i: (0, i))
     note = pl.BlockSpec((count, extra), lambda i: (0, width // extra))
-    weight = pl.BlockSpec((wide, step), lambda i: (0, i))
     shapes = (
-        jax.ShapeDtypeStruct((2,) + grads.shape, bf16),
+        jax.ShapeDtypeStruct((2,) + g_mine.shape, bf16),
         jax.ShapeDtypeStruct((wide, width), bf16),
         *(jax.ShapeDtypeStruct(table.shape, table.dtype) for table in tables),
     )
-    inputs = (hidden, later, grads, *tables)
+    inputs = (hidden, g_mine, g_other, *tables)
     return pl.pallas_call(
         finish_kernel,
         grid=(width // step,),
         out_shape=shapes,
-        in_specs=[block, note, block, note, whole, *(kept(value) for value in inputs)],
-        out_specs=(kept(shapes[0]), weight, *(kept(value) for value in shapes[2:])),
-        scratch_shapes=[
-            pltpu.VMEM((wide, 2 * count), bf16),
-            pltpu.VMEM((count, wide), f32),
-        ],
+        in_specs=[block, note, block, note, *(kept(value) for value in inputs)],
+        out_specs=(
+            kept(shapes[0]),
+            pl.BlockSpec((wide, step), lambda i: (0, i)),
+            *(kept(value) for value in shapes[2:]),
+        ),
+        scratch_shapes=[pltpu.VMEM((wide, 2 * count), bf16)],
         compiler_params=params,
         name="finished",
-    )(rows, rows, rows_other, rows_other, mine, *inputs)
+    )(rows, rows, rows_other, rows_other, *inputs)
 
 
 def logit_kernel(returned, experts, places, scores, out):
     tokens = scores.shape[1]
+    left, parts = returned[...], []
+    for _ in range(3):
+        parts.append(left.astype(bf16))
+        left = left - parts[-1].astype(f32)
     spread = lax.dot_general(
-        returned[...],
+        jnp.concatenate(parts, axis=0),
         experts[...],
         (((0,), (0,)), ((), ())),
         preferred_element_type=f32,
-        precision=lax.Precision.HIGHEST,
-    )
-    route = jnp.sum(spread * places[...], axis=0, keepdims=True)
+    )
+    slots = places.shape[0]
+    route = jnp.sum(spread[:slots] * places[...], axis=0, keepdims=True)
     for span in range(2):
         first, second = 2 * span, 2 * span + 1
         route0 = route[:, first * tokens : (first + 1) * tokens]
@@ -308,7 +327,8 @@
     lane = lax.broadcasted_iota(jnp.int32, (1, 4 * tokens), 1)
     source = lax.broadcasted_iota(jnp.int32, (32, 4 * tokens), 0)
     span = lane >> 6
-    experts[...] = jnp.where(((source >> 2) == line) & ((source & 1) == span), 1.0, 0.0)
+    table = jnp.where(((source >> 2) == line) & ((source & 1) == span), 1.0, 0.0)
+    experts[...] = jnp.concatenate([table] * 3, axis=0).astype(bf16)
     expert = lax.broadcasted_iota(jnp.int32, (8, 4 * tokens), 0)
     marked = jnp.where(expert == line, 1.0, 0.0)
     i = lax.broadcasted_iota(jnp.int32, (4 * tokens, 4 * tokens), 0)
@@ -316,7 +336,7 @@
     earlier = jnp.where(((i >> 6) == (j >> 6)) & ((i & 31) < (j & 31)), 1.0, 0.0)
     before = jnp.dot(marked.astype(bf16), earlier.astype(bf16), preferred_element_type=f32)
     place = jnp.sum(before * marked, axis=0, keepdims=True)
-    slot = lax.broadcasted_iota(jnp.int32, (128, 4 * tokens), 0).astype(f32)
+    slot = lax.broadcasted_iota(jnp.int32, places.shape, 0).astype(f32)
     places[...] = jnp.where(slot == place, 1.0, 0.0)
     core[...] = jnp.broadcast_to(lax.axis_index("dp"), core.shape)
     first = lax.axis_index("dp") == 0
@@ -338,8 +358,8 @@
         out_shape=(
             jax.ShapeDtypeStruct((tokens, extra), bf16),
             jax.ShapeDtypeStruct((tokens, 1), jnp.int32),
-            jax.ShapeDtypeStruct((32, 4 * tokens), f32),
-            jax.ShapeDtypeStruct((128, 4 * tokens), f32),
+            jax.ShapeDtypeStruct((96, 4 * tokens), bf16),
+            jax.ShapeDtypeStruct((16, 4 * tokens), f32),
             jax.ShapeDtypeStruct((4, tokens), f32),
         ),
         in_specs=[whole] * 2,
@@ -376,21 +396,23 @@
     block, swapped_saved = lax.optimization_barrier((block, swapped_saved))
 
     blocks = [block] + [plane_shift(block, step, True) for step in shifts]
-    factors, later, hidden, kept = saved_factors(saved, swapped_saved, mine)
-    blocks[1], other, kept, factors, later, hidden = lax.optimization_barrier(
-        (blocks[1], other, kept, factors, later, hidden)
+    factors, hidden, kept = saved_factors(saved, swapped_saved, mine)
+    blocks[1], other, kept, factors, hidden = lax.optimization_barrier(
+        (blocks[1], other, kept, factors, hidden)
     )
     pieces = select_rows(blocks, slots)
     pieces = [pieces[0]] + [
         plane_shift(piece, step, False) for piece, step in zip(pieces[1:], shifts, strict=True)
     ]
+    values, lines = first_grads(pieces[:2], kept, other, factors)
+    pieces[2], values, lines = lax.optimization_barrier((pieces[2], values, lines))
     rows = jnp.zeros((16 * slots, pieces[0].shape[1]), bf16)
     for index, piece in enumerate(pieces):
         rows = lax.dynamic_update_slice(rows, piece, (index * 4 * slots, 0))
-    grads, dots = raw_grads(rows, kept, other, factors)
+    g_mine, g_other, dots = last_grads(pieces[2:], kept, other, factors, values, lines)
     returned = lax.all_to_all(dots, ("expert", "dp"), split_axis=0, concat_axis=0, tiled=True)
     pair_grads, weight_grad, experts, places, scores = finished(
-        rows, swapped(rows), mine, hidden, later, grads, (experts, places, scores)
+        rows, swapped(rows), hidden, g_mine, swapped(g_other), (experts, places, scores)
     )
     returned, pair_grads, weight_grad = lax.optimization_barrier(
         (returned, pair_grads, weight_grad)

time: 54.6 us -> 55.1 us (level)
  local copies, waits for them, and re-layouts: 5.64 us -> 4.14 us
  Pallas kernels: 8.74 us -> 9.56 us
  waiting for transfers between devices: 14.4 us -> 15.2 us
    all_to_all x1, waiting for transfers between devices: 1.03 us -> 3.23 us  [local(): lax.all_to_all(dots, ('expert', 'dp'), split_axis=0, concat_axis=0, tiled...]
    pallas_call x2 -> x3, Pallas kernels: 2.25 us -> 3.86 us  [the longest x1 2.01 us: last_grads(): pl.pallas_call(last_kernel, out_shape=(grads, grads, jax.ShapeDtypeStruct...]
    unnamed x10 -> x8, local copies, waits for them, and re-layouts: 5.39 us -> 3.9 us
    ppermute x6, waiting for transfers between devices: 12 us -> 10.5 us  [plane_shift(): return lax.ppermute(value, ('expert', 'dp'), pairs)]
    pallas_call x1, Pallas kernels: 4.39 us -> 3.69 us  [finished(): pl.pallas_call(finish_kernel, grid=(width // step,), out_shape=shapes, in...]
    ppermute x3 -> x4, starting transfers between devices: 6.7 us -> 6.72 us  [swapped(): return lax.ppermute(value, 'dp', [(0, 1), (1, 0)])]
  transfers between devices with their start and end apart: 12 -> 13, of which waited for: 7 -> 7; matrix products, arithmetic and copies ran while one was open for 1% -> 1% of each run, Pallas kernels for 13% -> 14%
where the time goes in v5:
time: 55.1 us; the launch traced here: 54.4 us
  starting transfers between devices  24.5 us (44%)
  waiting for transfers between devices  15.2 us (28%)
  Pallas kernels  9.56 us (17%)
  local copies, waits for them, and re-layouts  4.14 us (8%)
  between operations  0.78 us (1%)
    ppermute x6, waiting for transfers between devices, plane_shift(): return lax.ppermute(value, ('expert', 'dp'), pairs)  10.5 us
    ppermute x6, starting transfers between devices, plane_shift(): return lax.ppermute(value, ('expert', 'dp'), pairs)  9.68 us
    ppermute x4, starting transfers between devices, swapped(): return lax.ppermute(value, 'dp', [(0, 1), (1, 0)])  6.72 us
    all_to_all x1, starting transfers between devices, local(): lax.all_to_all(dots, ('expert', 'dp'), split_axis=0, concat_axis=0, tiled...  5.61 us
    unnamed x8, local copies, waits for them, and re-layouts  3.9 us
    pallas_call x1, Pallas kernels, finished(): pl.pallas_call(finish_kernel, grid=(width // step,), out_shape=shapes, in...  3.69 us
    all_to_all x1, waiting for transfers between devices, local(): lax.all_to_all(dots, ('expert', 'dp'), split_axis=0, concat_axis=0, tiled...  3.23 us
    pallas_call x1, Pallas kernels, last_grads(): pl.pallas_call(last_kernel, out_shape=(grads, grads, jax.ShapeDtypeStruct...  2.01 us
  transfers between devices with their start and end apart: 13, of which 7 were waited for; matrix products, arithmetic and copies ran while one was open for 1% of the time, Pallas kernels for 14%

profile of v5, /device:TPU:1, one launch (start us, length us, event | category | flops | bytes accessed | tf_op | source)
XLA Modules:
  0.0 54.4 jit_solution(9180107814987050349)
XLA Ops:
  0.6 3.3 %collective-permute-start.2 = (bf16[2,2,256,256]{3,2,1,0:T(8,128)(2,1)}, bf16[2,2,256,256]{3,2,1,0:T(8,128)(2,1)S(1)}, u32[]{:S(2)}, u32[]{:S(2)}) collective-permute-start(bf16[2,2,256,256]{3,2,1,0:T(8,128)(2,1)} %bitcast.29), channel_id=1, source_target_pairs={{0,1},{1,0},{2,3},{3,2},{4,5},{5,4},{6,7},{7,6},{8,9},{9,8},{10,11... | collective-permute-start | bytes 1572872 | tf_op jit(solution)/shard_map/ppermute | solution.py:33
  4.0 0.7 %collective-permute-start = (bf16[32,3584]{1,0:T(8,128)(2,1)}, bf16[32,3584]{1,0:T(8,128)(2,1)S(1)}, u32[]{:S(2)}, u32[]{:S(2)}) collective-permute-start(bf16[32,3584]{1,0:T(8,128)(2,1)} %bitcast.37), channel_id=1, source_target_pairs={{32,0},{64,32},{96,64},{128,96},{160,128},{192,160},{224,192},{34,... | collective-permute-start | bytes 688136 | tf_op jit(solution)/shard_map/ppermute | solution.py:382
  4.6 1.8 %collective-permute-start.1 = (bf16[32,3584]{1,0:T(8,128)(2,1)}, bf16[32,3584]{1,0:T(8,128)(2,1)S(1)}, u32[]{:S(2)}, u32[]{:S(2)}) collective-permute-start(bf16[32,3584]{1,0:T(8,128)(2,1)} %bitcast.38), channel_id=1, source_target_pairs={{1,33},{33,65},{65,97},{97,129},{129,161},{161,193},{193,225},{3,3... | collective-permute-start | bytes 688136 | tf_op jit(solution)/shard_map/ppermute | solution.py:385
  6.5 0.0 collective-permute-done.2.swapped_saved
  6.5 0.1 collective-permute-start.4
  6.6 0.0 copy-start.2
  6.6 0.7 %copy-done.2 = s32[2,1,32,2]{2,3,1,0:T(2,128)S(1)} copy-done((s32[2,1,32,2]{2,3,1,0:T(2,128)S(1)}, s32[2,1,32,2]{2,3,1,0:T(2,128)}, u32[]{:S(2)}) %copy-start.2) | copy-done | bytes 536
  7.3 0.0 copy-start.3
  7.3 0.7 %copy-done.3 = f32[2,1,32,2]{2,3,1,0:T(2,128)S(1)} copy-done((f32[2,1,32,2]{2,3,1,0:T(2,128)S(1)}, f32[2,1,32,2]{2,3,1,0:T(2,128)}, u32[]{:S(2)}) %copy-start.3) | copy-done | bytes 536
  7.9 0.2 slot_notes.1
  8.1 0.1 compare_reduce_fusion
  8.2 0.0 collective-permute-done
  8.3 1.5 %collective-permute-done.1 = bf16[32,3584]{1,0:T(8,128)(2,1)S(1)} collective-permute-done((bf16[32,3584]{1,0:T(8,128)(2,1)}, bf16[32,3584]{1,0:T(8,128)(2,1)S(1)}, u32[]{:S(2)}, u32[]{:S(2)}) %collective-permute-start.1) | collective-permute-done | bytes 229408 | tf_op jit(solution)/shard_map/ppermute | solution.py:385
  9.7 0.1 broadcast_select_fusion
  9.8 3.0 %collective-permute-start.3 = (bf16[32,3712]{1,0:T(8,128)(2,1)S(1)}, bf16[32,3712]{1,0:T(8,128)(2,1)S(1)}, u32[]{:S(2)}, u32[]{:S(2)}) collective-permute-start(bf16[32,3712]{1,0:T(8,128)(2,1)S(1)} %pad_maximum_fusion.refs_0_), channel_id=1, source_target_pairs={{0,4},{1,17},{2,6},{3,19},{4,0},{5,21},{6,2},{7,23},{8,12},{9,25},... | collective-permute-start | bytes 712712 | tf_op jit(solution)/shard_map/ppermute | solution.py:29
  12.8 0.8 %collective-permute-start.6 = (bf16[32,3712]{1,0:T(8,128)(2,1)S(1)}, bf16[32,3712]{1,0:T(8,128)(2,1)S(1)}, u32[]{:S(2)}, u32[]{:S(2)}) collective-permute-start(bf16[32,3712]{1,0:T(8,128)(2,1)S(1)} %pad_maximum_fusion.refs_0_), channel_id=1, source_target_pairs={{0,6},{1,25},{2,0},{3,27},{4,2},{5,29},{6,4},{7,31},{8,14},{9,1},{... | collective-permute-start | bytes 712712 | tf_op jit(solution)/shard_map/ppermute | solution.py:29
  13.6 0.7 %collective-permute-start.5 = (bf16[32,3712]{1,0:T(8,128)(2,1)S(1)}, bf16[32,3712]{1,0:T(8,128)(2,1)S(1)}, u32[]{:S(2)}, u32[]{:S(2)}) collective-permute-start(bf16[32,3712]{1,0:T(8,128)(2,1)S(1)} %pad_maximum_fusion.refs_0_), channel_id=1, source_target_pairs={{0,2},{1,9},{2,4},{3,11},{4,6},{5,13},{6,0},{7,15},{8,10},{9,17},{... | collective-permute-start | bytes 712712 | tf_op jit(solution)/shard_map/ppermute | solution.py:29
  14.3 0.0 copy-start
  14.3 1.5 %copy-done = bf16[1,1,256,3584]{3,2,1,0:T(8,128)(2,1)S(1)} copy-done((bf16[1,1,256,3584]{3,2,1,0:T(8,128)(2,1)S(1)}, bf16[1,1,256,3584]{3,2,1,0:T(8,128)(2,1)}, u32[]{:S(2)}) %copy-start) | copy-done | bytes 1835032
  15.8 0.0 copy-start.1
  15.8 1.0 %copy-done.1 = bf16[2,1,1,2,256,256]{5,4,3,2,1,0:T(8,128)(2,1)S(1)} copy-done((bf16[2,1,1,2,256,256]{5,4,3,2,1,0:T(8,128)(2,1)S(1)}, bf16[2,1,1,2,256,256]{5,4,3,2,1,0:T(8,128)(2,1)}, u32[]{:S(2)}) %copy-start.1) | copy-done | bytes 524312
  16.8 0.4 saved_factors.1
  17.3 0.0 collective-permute-done.3.refs_1_
  17.3 0.0 collective-permute-done.4.other
  17.3 2.3 %collective-permute-done.6.refs_3_ = bf16[32,3712]{1,0:T(8,128)(2,1)S(1)} collective-permute-done((bf16[32,3712]{1,0:T(8,128)(2,1)S(1)}, bf16[32,3712]{1,0:T(8,128)(2,1)S(1)}, u32[]{:S(2)}, u32[]{:S(2)}) %collective-permute-start.6) | collective-permute-done | bytes 237600 | tf_op jit(solution)/shard_map/ppermute | solution.py:29
  19.6 0.5 collective-permute-done.5.refs_2_
  20.1 0.8 %select_rows.1 = (bf16[64,3712]{1,0:T(8,128)(2,1)S(1)}, bf16[64,3712]{1,0:T(8,128)(2,1)S(1)}, bf16[64,3712]{1,0:T(8,128)(2,1)S(1)}, bf16[64,3712]{1,0:T(8,128)(2,1)S(1)}) custom-call(bf16[32,3712]{1,0:T(8,128)(2,1)S(1)} %pad_maximum_fusion.refs_0_, bf16[32,3712]{1,0:T(8,128)(2,1)S(1)} %collective-permute-done.3.refs_1_, ...), custom_call_target="tpu_custom_call" | custom-call | tf_op jit(solution)/shard_map/select_rows/pallas_call | solution.py:100
  20.9 2.5 %collective-permute-start.8 = (bf16[64,3712]{1,0:T(8,128)(2,1)S(1)}, bf16[64,3712]{1,0:T(8,128)(2,1)S(1)}, u32[]{:S(2)}, u32[]{:S(2)}) collective-permute-start(bf16[64,3712]{1,0:T(8,128)(2,1)S(1)} %get-tuple-element.52), channel_id=1, source_target_pairs={{0,16},{1,5},{2,18},{3,7},{4,20},{5,1},{6,22},{7,3},{8,24},{9,13},... | collective-permute-start | bytes 1425416 | tf_op jit(solution)/shard_map/ppermute | solution.py:29
  23.5 0.6 %collective-permute-start.7 = (bf16[64,3712]{1,0:T(8,128)(2,1)S(1)}, bf16[64,3712]{1,0:T(8,128)(2,1)S(1)}, u32[]{:S(2)}, u32[]{:S(2)}) collective-permute-start(bf16[64,3712]{1,0:T(8,128)(2,1)S(1)} %get-tuple-element.50), channel_id=1, source_target_pairs={{0,8},{1,3},{2,10},{3,5},{4,12},{5,7},{6,14},{7,1},{8,16},{9,11},{... | collective-permute-start | bytes 1425416 | tf_op jit(solution)/shard_map/ppermute | solution.py:29
  24.1 2.1 %collective-permute-start.9 = (bf16[64,3712]{1,0:T(8,128)(2,1)S(1)}, bf16[64,3712]{1,0:T(8,128)(2,1)S(1)}, u32[]{:S(2)}, u32[]{:S(2)}) collective-permute-start(bf16[64,3712]{1,0:T(8,128)(2,1)S(1)} %get-tuple-element.59), channel_id=1, source_target_pairs={{0,24},{1,7},{2,26},{3,1},{4,28},{5,3},{6,30},{7,5},{8,0},{9,15},{... | collective-permute-start | bytes 1425416 | tf_op jit(solution)/shard_map/ppermute | solution.py:29
  26.1 0.1 dynamic_update_slice.12
  26.3 4.1 %collective-permute-done.8.piece1 = bf16[64,3712]{1,0:T(8,128)(2,1)S(1)} collective-permute-done((bf16[64,3712]{1,0:T(8,128)(2,1)S(1)}, bf16[64,3712]{1,0:T(8,128)(2,1)S(1)}, u32[]{:S(2)}, u32[]{:S(2)}) %collective-permute-start.8) | collective-permute-done | bytes 475168 | tf_op jit(solution)/shard_map/ppermute | solution.py:29
  30.4 1.4 %first_grads.1 = (bf16[4,128,256]{2,1,0:T(8,128)(2,1)S(1)}, f32[8,128]{1,0:T(8,128)S(1)}) custom-call(bf16[64,3712]{1,0:T(8,128)(2,1)S(1)} %get-tuple-element.51.piece0, bf16[64,3712]{1,0:T(8,128)(2,1)S(1)} %collective-permute-done.8.piece1, bf16[256,3584]{1,0:T(8,128)(2,1)S(1)} %get-tuple-element.53.mine, ...), custom_call_target="tpu_custom_call" | custom-call | tf_op jit(solution)/shard_map/first_grads/pallas_call | solution.py:194
  31.8 3.6 %collective-permute-done.7.piece0 = bf16[64,3712]{1,0:T(8,128)(2,1)S(1)} collective-permute-done((bf16[64,3712]{1,0:T(8,128)(2,1)S(1)}, bf16[64,3712]{1,0:T(8,128)(2,1)S(1)}, u32[]{:S(2)}, u32[]{:S(2)}) %collective-permute-start.7) | collective-permute-done | bytes 475168 | tf_op jit(solution)/shard_map/ppermute | solution.py:29
  35.4 0.1 collective-permute-done.9.piece1
  35.6 3.3 %collective-permute-start.10 = (bf16[256,3712]{1,0:T(8,128)(2,1)S(1)}, bf16[256,3712]{1,0:T(8,128)(2,1)}, u32[]{:S(2)}, u32[]{:S(2)}) collective-permute-start(bf16[256,3712]{1,0:T(8,128)(2,1)S(1)} %constant_dynamic-update-slice_fusion.rows.notes), channel_id=1, source_target_pairs={{0,1},{1,0},{2,3},{3,2},{4,5},{5,4},{6,7},{7,6},{8,9},{9,8},{10,11... | collective-permute-start | bytes 5701640 | tf_op jit(solution)/shard_map/ppermute | solution.py:33
  38.9 2.0 %last_grads.1 = (bf16[2,256,256]{2,1,0:T(8,128)(2,1)S(1)}, bf16[2,256,256]{2,1,0:T(8,128)(2,1)S(1)}, f32[32,128]{1,0:T(8,128)}) custom-call(bf16[64,3712]{1,0:T(8,128)(2,1)S(1)} %collective-permute-done.7.piece0, bf16[64,3712]{1,0:T(8,128)(2,1)S(1)} %collective-permute-done.9.piece1, bf16[256,3584]{1,0:T(8,128)(2,1)S(1)} %get-tuple-element.53.mine, ...), custom_call_target="tpu_custom_call" | custom-call | tf_op jit(solution)/shard_map/last_grads/pallas_call | solution.py:231
  40.9 0.0 collective-permute-start.11
  40.9 5.6 %all-to-all-start = ((f32[32,1,128]{2,1,0:T(1,128)}), f32[32,1,128]{2,1,0:T(1,128)S(1)}, u32[]{:S(2)}, u32[]{:S(2)}) async-start(f32[32,1,128]{2,1,0:T(1,128)} %bitcast.11), calls=%async_computation | async-start | bytes 32768 | tf_op jit(solution)/shard_map/all_to_all | solution.py:413
  46.5 0.0 collective-permute-done.11.g_other
  46.5 0.0 collective-permute-done.10.rows_other.notes_other
  46.5 3.7 %finished.1 = (bf16[2,2,256,256]{3,2,1,0:T(8,128)(2,1)}, bf16[256,3584]{1,0:T(8,128)(2,1)}, bf16[96,128]{1,0:T(8,128)(2,1)S(1)}, f32[16,128]{1,0:T(8,128)S(1)}, f32[4,32]{1,0:T(4,128)S(1)}) custom-call(bf16[256,3712]{1,0:T(8,128)(2,1)S(1)} %constant_dynamic-update-slice_fusion.rows.notes, bf16[256,3712]{1,0:T(8,128)(2,1)S(1)} %constant_dynamic-update-slice_fusion.rows.notes, ...), custom_call_target="tpu_custom_call" | custom-call | tf_op jit(solution)/shard_map/finished/pallas_call | solution.py:279
  50.2 3.2 %all-to-all-done = f32[32,1,128]{2,1,0:T(1,128)S(1)} async-done(((f32[32,1,128]{2,1,0:T(1,128)}), f32[32,1,128]{2,1,0:T(1,128)S(1)}, u32[]{:S(2)}, u32[]{:S(2)}) %all-to-all-start) | async-done | bytes 16416 | tf_op jit(solution)/shard_map/all_to_all | solution.py:413
  53.4 1.0 %logit_grads.1 = f32[4,32]{1,0:T(4,128)} custom-call(f32[32,128]{1,0:T(8,128)S(1)} %bitcast.31, bf16[96,128]{1,0:T(8,128)(2,1)S(1)} %get-tuple-element.74.experts, f32[16,128]{1,0:T(8,128)S(1)} %get-tuple-element.75.places, f32[4,32]{1,0:T(4,128)S(1)} %get-tuple-element.76.scores), custom_call_target="tpu_custom_call" | custom-call | tf_op jit(solution)/shard_map/logit_grads/pallas_call | solution.py:420
  (4 shorter events, 0.1 us)
Async XLA Ops:
  0.6 5.8 %collective-permute-start.2 = (bf16[2,2,256,256]{3,2,1,0:T(8,128)(2,1)}, bf16[2,2,256,256]{3,2,1,0:T(8,128)(2,1)S(1)}, u32[]{:S(2)}, u32[]{:S(2)}) collective-permute-start(bf16[2,2,256,256]{3,2,1,0:T(8,128)(2,1)} %bitcast.29), channel_id=1, source_target_pairs={{0,1},{1,0},{2,3},{3,2},{4,5},{5,4},{6,7},{7,6},{8,9},{9,8},{10,11... | collective-permute-start | bytes 1572872 | tf_op jit(solution)/shard_map/ppermute | solution.py:33
  4.0 4.3 %collective-permute-start = (bf16[32,3584]{1,0:T(8,128)(2,1)}, bf16[32,3584]{1,0:T(8,128)(2,1)S(1)}, u32[]{:S(2)}, u32[]{:S(2)}) collective-permute-start(bf16[32,3584]{1,0:T(8,128)(2,1)} %bitcast.37), channel_id=1, source_target_pairs={{32,0},{64,32},{96,64},{128,96},{160,128},{192,160},{224,192},{34,... | collective-permute-start | bytes 688136 | tf_op jit(solution)/shard_map/ppermute | solution.py:382
  4.6 5.1 %collective-permute-start.1 = (bf16[32,3584]{1,0:T(8,128)(2,1)}, bf16[32,3584]{1,0:T(8,128)(2,1)S(1)}, u32[]{:S(2)}, u32[]{:S(2)}) collective-permute-start(bf16[32,3584]{1,0:T(8,128)(2,1)} %bitcast.38), channel_id=1, source_target_pairs={{1,33},{33,65},{65,97},{97,129},{129,161},{161,193},{193,225},{3,3... | collective-permute-start | bytes 688136 | tf_op jit(solution)/shard_map/ppermute | solution.py:385
  6.5 10.8 %collective-permute-start.4 = (bf16[256,3584]{1,0:T(8,128)(2,1)}, bf16[256,3584]{1,0:T(8,128)(2,1)S(1)}, u32[]{:S(2)}, u32[]{:S(2)}) collective-permute-start(bf16[256,3584]{1,0:T(8,128)(2,1)} %bitcast.27), channel_id=1, source_target_pairs={{0,1},{1,0},{2,3},{3,2},{4,5},{5,4},{6,7},{7,6},{8,9},{9,8},{10,11... | collective-permute-start | bytes 5505032 | tf_op jit(solution)/shard_map/ppermute | solution.py:33
  6.6 0.7 %copy-start.2 = (s32[2,1,32,2]{2,3,1,0:T(2,128)S(1)}, s32[2,1,32,2]{2,3,1,0:T(2,128)}, u32[]{:S(2)}) copy-start(s32[2,1,32,2]{2,3,1,0:T(2,128)} %param.8) | copy-start | bytes 1540
  7.3 0.7 %copy-start.3 = (f32[2,1,32,2]{2,3,1,0:T(2,128)S(1)}, f32[2,1,32,2]{2,3,1,0:T(2,128)}, u32[]{:S(2)}) copy-start(f32[2,1,32,2]{2,3,1,0:T(2,128)} %param.9) | copy-start | bytes 1540
  9.8 7.4 %collective-permute-start.3 = (bf16[32,3712]{1,0:T(8,128)(2,1)S(1)}, bf16[32,3712]{1,0:T(8,128)(2,1)S(1)}, u32[]{:S(2)}, u32[]{:S(2)}) collective-permute-start(bf16[32,3712]{1,0:T(8,128)(2,1)S(1)} %pad_maximum_fusion.refs_0_), channel_id=1, source_target_pairs={{0,4},{1,17},{2,6},{3,19},{4,0},{5,21},{6,2},{7,23},{8,12},{9,25},... | collective-permute-start | bytes 712712 | tf_op jit(solution)/shard_map/ppermute | solution.py:29
  12.8 6.8 %collective-permute-start.6 = (bf16[32,3712]{1,0:T(8,128)(2,1)S(1)}, bf16[32,3712]{1,0:T(8,128)(2,1)S(1)}, u32[]{:S(2)}, u32[]{:S(2)}) collective-permute-start(bf16[32,3712]{1,0:T(8,128)(2,1)S(1)} %pad_maximum_fusion.refs_0_), channel_id=1, source_target_pairs={{0,6},{1,25},{2,0},{3,27},{4,2},{5,29},{6,4},{7,31},{8,14},{9,1},{... | collective-permute-start | bytes 712712 | tf_op jit(solution)/shard_map/ppermute | solution.py:29
  13.6 6.5 %collective-permute-start.5 = (bf16[32,3712]{1,0:T(8,128)(2,1)S(1)}, bf16[32,3712]{1,0:T(8,128)(2,1)S(1)}, u32[]{:S(2)}, u32[]{:S(2)}) collective-permute-start(bf16[32,3712]{1,0:T(8,128)(2,1)S(1)} %pad_maximum_fusion.refs_0_), channel_id=1, source_target_pairs={{0,2},{1,9},{2,4},{3,11},{4,6},{5,13},{6,0},{7,15},{8,10},{9,17},{... | collective-permute-start | bytes 712712 | tf_op jit(solution)/shard_map/ppermute | solution.py:29
  14.3 1.5 %copy-start = (bf16[1,1,256,3584]{3,2,1,0:T(8,128)(2,1)S(1)}, bf16[1,1,256,3584]{3,2,1,0:T(8,128)(2,1)}, u32[]{:S(2)}) copy-start(bf16[1,1,256,3584]{3,2,1,0:T(8,128)(2,1)} %param.11) | copy-start | bytes 5505028
  15.8 1.0 %copy-start.1 = (bf16[2,1,1,2,256,256]{5,4,3,2,1,0:T(8,128)(2,1)S(1)}, bf16[2,1,1,2,256,256]{5,4,3,2,1,0:T(8,128)(2,1)}, u32[]{:S(2)}) copy-start(bf16[2,1,1,2,256,256]{5,4,3,2,1,0:T(8,128)(2,1)} %param.10) | copy-start | bytes 1572868
  20.9 9.4 %collective-permute-start.8 = (bf16[64,3712]{1,0:T(8,128)(2,1)S(1)}, bf16[64,3712]{1,0:T(8,128)(2,1)S(1)}, u32[]{:S(2)}, u32[]{:S(2)}) collective-permute-start(bf16[64,3712]{1,0:T(8,128)(2,1)S(1)} %get-tuple-element.52), channel_id=1, source_target_pairs={{0,16},{1,5},{2,18},{3,7},{4,20},{5,1},{6,22},{7,3},{8,24},{9,13},... | collective-permute-start | bytes 1425416 | tf_op jit(solution)/shard_map/ppermute | solution.py:29
  23.5 11.9 %collective-permute-start.7 = (bf16[64,3712]{1,0:T(8,128)(2,1)S(1)}, bf16[64,3712]{1,0:T(8,128)(2,1)S(1)}, u32[]{:S(2)}, u32[]{:S(2)}) collective-permute-start(bf16[64,3712]{1,0:T(8,128)(2,1)S(1)} %get-tuple-element.50), channel_id=1, source_target_pairs={{0,8},{1,3},{2,10},{3,5},{4,12},{5,7},{6,14},{7,1},{8,16},{9,11},{... | collective-permute-start | bytes 1425416 | tf_op jit(solution)/shard_map/ppermute | solution.py:29
  24.1 11.5 %collective-permute-start.9 = (bf16[64,3712]{1,0:T(8,128)(2,1)S(1)}, bf16[64,3712]{1,0:T(8,128)(2,1)S(1)}, u32[]{:S(2)}, u32[]{:S(2)}) collective-permute-start(bf16[64,3712]{1,0:T(8,128)(2,1)S(1)} %get-tuple-element.59), channel_id=1, source_target_pairs={{0,24},{1,7},{2,26},{3,1},{4,28},{5,3},{6,30},{7,5},{8,0},{9,15},{... | collective-permute-start | bytes 1425416 | tf_op jit(solution)/shard_map/ppermute | solution.py:29
  35.6 10.9 %collective-permute-start.10 = (bf16[256,3712]{1,0:T(8,128)(2,1)S(1)}, bf16[256,3712]{1,0:T(8,128)(2,1)}, u32[]{:S(2)}, u32[]{:S(2)}) collective-permute-start(bf16[256,3712]{1,0:T(8,128)(2,1)S(1)} %constant_dynamic-update-slice_fusion.rows.notes), channel_id=1, source_target_pairs={{0,1},{1,0},{2,3},{3,2},{4,5},{5,4},{6,7},{7,6},{8,9},{9,8},{10,11... | collective-permute-start | bytes 5701640 | tf_op jit(solution)/shard_map/ppermute | solution.py:33
  40.9 5.6 %collective-permute-start.11 = (bf16[2,256,256]{2,1,0:T(8,128)(2,1)S(1)}, bf16[2,256,256]{2,1,0:T(8,128)(2,1)S(1)}, u32[]{:S(2)}, u32[]{:S(2)}) collective-permute-start(bf16[2,256,256]{2,1,0:T(8,128)(2,1)S(1)} %get-tuple-element.65), channel_id=1, source_target_pairs={{0,1},{1,0},{2,3},{3,2},{4,5},{5,4},{6,7},{7,6},{8,9},{9,8},{10,11... | collective-permute-start | bytes 786440 | tf_op jit(solution)/shard_map/ppermute | solution.py:33
  40.9 12.6 %all-to-all-start = ((f32[32,1,128]{2,1,0:T(1,128)}), f32[32,1,128]{2,1,0:T(1,128)S(1)}, u32[]{:S(2)}, u32[]{:S(2)}) async-start(f32[32,1,128]{2,1,0:T(1,128)} %bitcast.11), calls=%async_computation | async-start | bytes 32768 | tf_op jit(solution)/shard_map/all_to_all | solution.py:413

commit v6 on v5

--- a/solution.py
+++ b/solution.py
@@ -181,74 +181,72 @@
     return values, lines
 
 
-def first_kernel(piece0, piece1, mine, other, factors, values, lines):
+def first_kernel(piece0, piece1, mine, other, factors, g_mine, g_other, lines):
     results, sums = raw_values((piece0, piece1), mine, other, factors, 0)
-    for index, value in enumerate(results):
-        values[index] = value
+    g_mine[0], g_mine[1], g_other[0], g_other[1] = results
     for index, line in enumerate(sums):
         lines[index : index + 1] = line
 
 
 def first_grads(pieces, mine, other, factors):
     count = 2 * pieces[0].shape[0]
+    grads = jax.ShapeDtypeStruct((2, count, factors.shape[2]), bf16)
     return pl.pallas_call(
         first_kernel,
-        out_shape=(
-            jax.ShapeDtypeStruct((4, count, factors.shape[2]), bf16),
-            jax.ShapeDtypeStruct((count // 16, 128), f32),
-        ),
+        out_shape=(grads, grads, jax.ShapeDtypeStruct((count // 16, 128), f32)),
         in_specs=[whole] * 5,
-        out_specs=(whole,) * 2,
+        out_specs=(whole,) * 3,
         compiler_params=params,
         name="first_grads",
     )(*pieces, mine, other, factors)
 
 
-def last_kernel(
-    piece0, piece1, mine, other, factors, values, lines, g_mine, g_other, dots
-):
-    half = values.shape[1]
+def last_kernel(piece0, piece1, mine, other, factors, lines, g_mine, g_other, dots):
     core, _, far = position()
     order = token_blocks(core, far)
-    results, sums = raw_values((piece0, piece1), mine, other, factors, half)
-    for chunk in range(16):
-        line = lines[chunk : chunk + 1] if chunk < 8 else sums[chunk - 8]
+    for chunk in range(8):
         for target in range(2):
-            dots[pl.ds(order[chunk] * 2 + target, 1), :] = line
-    for chunk in range(16):
-        at = pl.ds(pl.multiple_of(order[chunk] * 16, 16), 16)
-        start = chunk % 8 * 16
-        for index in range(4):
-            out = g_mine if index < 2 else g_other
-            if chunk < 8:
-                out[index % 2, at, :] = values[index, start : start + 16]
-            else:
-                out[index % 2, at, :] = results[index][start : start + 16]
-
-
-def last_grads(pieces, mine, other, factors, values, lines):
-    grads = jax.ShapeDtypeStruct((2,) + factors.shape[1:], bf16)
+            dots[pl.ds(order[chunk] * 2 + target, 1), :] = lines[chunk : chunk + 1]
+    start = 2 * piece0.shape[0]
+    results, sums = raw_values((piece0, piece1), mine, other, factors, start)
+    for chunk in range(8):
+        for target in range(2):
+            dots[pl.ds(order[8 + chunk] * 2 + target, 1), :] = sums[chunk]
+    g_mine[0], g_mine[1], g_other[0], g_other[1] = results
+
+
+def last_grads(pieces, mine, other, factors, lines):
+    count = 2 * pieces[0].shape[0]
+    grads = jax.ShapeDtypeStruct((2, count, factors.shape[2]), bf16)
     return pl.pallas_call(
         last_kernel,
         out_shape=(grads, grads, jax.ShapeDtypeStruct((32, 128), f32)),
-        in_specs=[whole] * 7,
+        in_specs=[whole] * 6,
         out_specs=(whole,) * 3,
         compiler_params=params,
         name="last_grads",
-    )(*pieces, mine, other, factors, values, lines)
+    )(*pieces, mine, other, factors, lines)
 
 
 def finish_kernel(
-    rows, notes, rows_other, notes_other, hidden, g_mine, g_other, *refs
+    rows, notes, rows_other, notes_other, hidden, mine0, mine1, other0, other1, *refs
 ):
     tables, (pair_grads, weight_grad), passed, scaled = refs[:3], refs[3:5], refs[5:8], refs[8]
     count, wide = hidden.shape[1:]
 
     @pl.when(pl.program_id(0) == 0)
     def _():
-        span = lax.axis_index("dp")
-        pair_grads[span] = g_mine[...]
-        pair_grads[1 - span] = g_other[...]
+        span, near, far = position()
+        for which, order, halves in (
+            (span, token_blocks(span, far), (mine0, mine1)),
+            (1 - span, token_blocks(1 - span, near), (other0, other1)),
+        ):
+            for chunk in range(16):
+                at = pl.ds(pl.multiple_of(order[chunk] * 16, 16), 16)
+                start = chunk % 8 * 16
+                for part in range(2):
+                    value = halves[chunk // 8][part, start : start + 16, :]
+                    pair_grads[which, part, at, :] = value
         for table, out in zip(tables, passed, strict=True):
             out[...] = table[...]
         for index, ref in enumerate((notes, notes_other)):
@@ -260,7 +258,7 @@
     weight_grad[...] = total.astype(bf16)
 
 
-def finished(rows, rows_other, hidden, g_mine, g_other, tables):
+def finished(rows, rows_other, hidden, grads, tables):
     count, wide = hidden.shape[1:]
     width = rows.shape[1] - extra
     step = width // 2 if width % 256 == 0 else width
@@ -271,11 +269,11 @@
     block = pl.BlockSpec((count, step), lambda i: (0, i))
     note = pl.BlockSpec((count, extra), lambda i: (0, width // extra))
     shapes = (
-        jax.ShapeDtypeStruct((2,) + g_mine.shape, bf16),
+        jax.ShapeDtypeStruct((2, 2, count, wide), bf16),
         jax.ShapeDtypeStruct((wide, width), bf16),
         *(jax.ShapeDtypeStruct(table.shape, table.dtype) for table in tables),
     )
-    inputs = (hidden, g_mine, g_other, *tables)
+    inputs = (hidden, *grads, *tables)
     return pl.pallas_call(
         finish_kernel,
         grid=(width // step,),
@@ -388,31 +386,36 @@
     notes, core, experts, places, scores = slot_notes(
         by_slot(expert_ids), by_slot(router_logits)
     )
+    notes, held = lax.optimization_barrier((notes, mine))
+    other = swapped(held)
     incoming = jnp.where(core == 0, from_above, from_below)
     block = jnp.concatenate([incoming, notes], axis=1)
-    swapped_saved = swapped(saved)
-    held, swapped_saved = lax.optimization_barrier((mine, swapped_saved))
-    other = swapped(held)
-    block, swapped_saved = lax.optimization_barrier((block, swapped_saved))
+    block, swapped_saved = lax.optimization_barrier((block, swapped(saved)))
 
     blocks = [block] + [plane_shift(block, step, True) for step in shifts]
     factors, hidden, kept = saved_factors(saved, swapped_saved, mine)
-    blocks[1], other, kept, factors, hidden = lax.optimization_barrier(
-        (blocks[1], other, kept, factors, hidden)
+    blocks[2], kept, factors, hidden = lax.optimization_barrier(
+        (blocks[2], kept, factors, hidden)
     )
     pieces = select_rows(blocks, slots)
     pieces = [pieces[0]] + [
         plane_shift(piece, step, False) for piece, step in zip(pieces[1:], shifts, strict=True)
     ]
-    values, lines = first_grads(pieces[:2], kept, other, factors)
-    pieces[2], values, lines = lax.optimization_barrier((pieces[2], values, lines))
+    mine0, other0, lines = first_grads(pieces[:2], kept, other, factors)
+    pieces[2], mine0, other0, lines = lax.optimization_barrier(
+        (pieces[2], mine0, other0, lines)
+    )
     rows = jnp.zeros((16 * slots, pieces[0].shape[1]), bf16)
     for index, piece in enumerate(pieces):
         rows = lax.dynamic_update_slice(rows, piece, (index * 4 * slots, 0))
-    g_mine, g_other, dots = last_grads(pieces[2:], kept, other, factors, values, lines)
+    mine1, other1, dots = last_grads(pieces[2:], kept, other, factors, lines)
     returned = lax.all_to_all(dots, ("expert", "dp"), split_axis=0, concat_axis=0, tiled=True)
     pair_grads, weight_grad, experts, places, scores = finished(
-        rows, swapped(rows), hidden, g_mine, swapped(g_other), (experts, places, scores)
+        rows,
+        swapped(rows),
+        hidden,
+        (mine0, mine1, swapped(other0), swapped(other1)),
+        (experts, places, scores),
     )
     returned, pair_grads, weight_grad = lax.optimization_barrier(
         (returned, pair_grads, weight_grad)

time: 55.1 us -> 55.7 us (1.011)
  starting transfers between devices: 24.5 us -> 26.1 us
  waiting for transfers between devices: 15.2 us -> 14.2 us
    ppermute x1, starting transfers between devices: 1.82 us -> 4.38 us  [local(): lax.ppermute(sent_up[0], ('pipe', 'dp'), [(2 * z + 1, 2 * z + 3) for z in...]
    ppermute x4 -> x5, starting transfers between devices: 6.72 us -> 5.55 us  [swapped(): return lax.ppermute(value, 'dp', [(0, 1), (1, 0)])]
    ppermute x6, starting transfers between devices: 9.68 us -> 10.3 us  [plane_shift(): return lax.ppermute(value, ('expert', 'dp'), pairs)]
  transfers between devices with their start and end apart: 13 -> 14, of which waited for: 7 -> 6; matrix products, arithmetic and copies ran while one was open for 1% -> 1% of each run, Pallas kernels for 14% -> 16%
where the time goes in v6:
time: 55.7 us; the launch traced here: 55 us
  starting transfers between devices  26.1 us (47%)
  waiting for transfers between devices  14.2 us (25%)
  Pallas kernels  9.57 us (17%)
  local copies, waits for them, and re-layouts  4.15 us (7%)
  between operations  0.77 us (1%)
    ppermute x6, starting transfers between devices, plane_shift(): return lax.ppermute(value, ('expert', 'dp'), pairs)  10.3 us
    ppermute x6, waiting for transfers between devices, plane_shift(): return lax.ppermute(value, ('expert', 'dp'), pairs)  10 us
    ppermute x5, starting transfers between devices, swapped(): return lax.ppermute(value, 'dp', [(0, 1), (1, 0)])  5.55 us
    all_to_all x1, starting transfers between devices, local(): lax.all_to_all(dots, ('expert', 'dp'), split_axis=0, concat_axis=0, tiled...  5.25 us
    ppermute x1, starting transfers between devices, local(): lax.ppermute(sent_up[0], ('pipe', 'dp'), [(2 * z + 1, 2 * z + 3) for z in...  4.38 us
    unnamed x8, local copies, waits for them, and re-layouts  3.9 us
    pallas_call x1, Pallas kernels, finished(): pl.pallas_call(finish_kernel, grid=(width // step,), out_shape=shapes, in...  3.71 us
    all_to_all x1, waiting for transfers between devices, local(): lax.all_to_all(dots, ('expert', 'dp'), split_axis=0, concat_axis=0, tiled...  3.2 us
  transfers between devices with their start and end apart: 14, of which 6 were waited for; matrix products, arithmetic and copies ran while one was open for 1% of the time, Pallas kernels for 16%

profile of v6, /device:TPU:1, one launch (start us, length us, event | category | flops | bytes accessed | tf_op | source)
XLA Modules:
  0.0 55.0 jit_solution(15861158490076029039)
XLA Ops:
  0.6 0.7 %collective-permute-start = (bf16[32,3584]{1,0:T(8,128)(2,1)}, bf16[32,3584]{1,0:T(8,128)(2,1)S(1)}, u32[]{:S(2)}, u32[]{:S(2)}) collective-permute-start(bf16[32,3584]{1,0:T(8,128)(2,1)} %bitcast.37), channel_id=1, source_target_pairs={{32,0},{64,32},{96,64},{128,96},{160,128},{192,160},{224,192},{34,... | collective-permute-start | bytes 688136 | tf_op jit(solution)/shard_map/ppermute | solution.py:380
  1.3 4.4 %collective-permute-start.1 = (bf16[32,3584]{1,0:T(8,128)(2,1)}, bf16[32,3584]{1,0:T(8,128)(2,1)S(1)}, u32[]{:S(2)}, u32[]{:S(2)}) collective-permute-start(bf16[32,3584]{1,0:T(8,128)(2,1)} %bitcast.38), channel_id=1, source_target_pairs={{1,33},{33,65},{65,97},{97,129},{129,161},{161,193},{193,225},{3,3... | collective-permute-start | bytes 688136 | tf_op jit(solution)/shard_map/ppermute | solution.py:383
  5.7 0.2 collective-permute-start.2
  5.9 0.0 copy-start.2
  5.9 0.7 %copy-done.2 = s32[2,1,32,2]{2,3,1,0:T(2,128)S(1)} copy-done((s32[2,1,32,2]{2,3,1,0:T(2,128)S(1)}, s32[2,1,32,2]{2,3,1,0:T(2,128)}, u32[]{:S(2)}) %copy-start.2) | copy-done | bytes 536
  6.6 0.0 copy-start.3
  6.6 0.7 %copy-done.3 = f32[2,1,32,2]{2,3,1,0:T(2,128)S(1)} copy-done((f32[2,1,32,2]{2,3,1,0:T(2,128)S(1)}, f32[2,1,32,2]{2,3,1,0:T(2,128)}, u32[]{:S(2)}) %copy-start.3) | copy-done | bytes 536
  7.3 0.2 slot_notes.1
  7.5 0.4 collective-permute-start.8
  7.9 0.1 compare_reduce_fusion
  8.0 0.0 collective-permute-done
  8.0 1.0 %collective-permute-done.1 = bf16[32,3584]{1,0:T(8,128)(2,1)S(1)} collective-permute-done((bf16[32,3584]{1,0:T(8,128)(2,1)}, bf16[32,3584]{1,0:T(8,128)(2,1)S(1)}, u32[]{:S(2)}, u32[]{:S(2)}) %collective-permute-start.1) | collective-permute-done | bytes 229408 | tf_op jit(solution)/shard_map/ppermute | solution.py:383
  9.0 0.1 broadcast_select_fusion
  9.1 0.0 collective-permute-done.2.swapped_saved
  9.1 1.4 %collective-permute-start.4 = (bf16[32,3712]{1,0:T(8,128)(2,1)S(1)}, bf16[32,3712]{1,0:T(8,128)(2,1)S(1)}, u32[]{:S(2)}, u32[]{:S(2)}) collective-permute-start(bf16[32,3712]{1,0:T(8,128)(2,1)S(1)} %pad_maximum_fusion.refs_0_), channel_id=1, source_target_pairs={{0,2},{1,9},{2,4},{3,11},{4,6},{5,13},{6,0},{7,15},{8,10},{9,17},{... | collective-permute-start | bytes 712712 | tf_op jit(solution)/shard_map/ppermute | solution.py:29
  10.5 2.6 %collective-permute-start.3 = (bf16[32,3712]{1,0:T(8,128)(2,1)S(1)}, bf16[32,3712]{1,0:T(8,128)(2,1)S(1)}, u32[]{:S(2)}, u32[]{:S(2)}) collective-permute-start(bf16[32,3712]{1,0:T(8,128)(2,1)S(1)} %pad_maximum_fusion.refs_0_), channel_id=1, source_target_pairs={{0,4},{1,17},{2,6},{3,19},{4,0},{5,21},{6,2},{7,23},{8,12},{9,25},... | collective-permute-start | bytes 712712 | tf_op jit(solution)/shard_map/ppermute | solution.py:29
  13.1 1.1 %collective-permute-start.5 = (bf16[32,3712]{1,0:T(8,128)(2,1)S(1)}, bf16[32,3712]{1,0:T(8,128)(2,1)S(1)}, u32[]{:S(2)}, u32[]{:S(2)}) collective-permute-start(bf16[32,3712]{1,0:T(8,128)(2,1)S(1)} %pad_maximum_fusion.refs_0_), channel_id=1, source_target_pairs={{0,6},{1,25},{2,0},{3,27},{4,2},{5,29},{6,4},{7,31},{8,14},{9,1},{... | collective-permute-start | bytes 712712 | tf_op jit(solution)/shard_map/ppermute | solution.py:29
  14.2 0.0 copy-start
  14.2 1.5 %copy-done = bf16[1,1,256,3584]{3,2,1,0:T(8,128)(2,1)S(1)} copy-done((bf16[1,1,256,3584]{3,2,1,0:T(8,128)(2,1)S(1)}, bf16[1,1,256,3584]{3,2,1,0:T(8,128)(2,1)}, u32[]{:S(2)}) %copy-start) | copy-done | bytes 1835032
  15.7 0.0 copy-start.1
  15.7 1.0 %copy-done.1 = bf16[2,1,1,2,256,256]{5,4,3,2,1,0:T(8,128)(2,1)S(1)} copy-done((bf16[2,1,1,2,256,256]{5,4,3,2,1,0:T(8,128)(2,1)S(1)}, bf16[2,1,1,2,256,256]{5,4,3,2,1,0:T(8,128)(2,1)}, u32[]{:S(2)}) %copy-start.1) | copy-done | bytes 524312
  16.7 0.4 saved_factors.1
  17.1 0.0 collective-permute-done.4.refs_2_
  17.1 2.3 %collective-permute-done.3.refs_1_ = bf16[32,3712]{1,0:T(8,128)(2,1)S(1)} collective-permute-done((bf16[32,3712]{1,0:T(8,128)(2,1)S(1)}, bf16[32,3712]{1,0:T(8,128)(2,1)S(1)}, u32[]{:S(2)}, u32[]{:S(2)}) %collective-permute-start.3) | collective-permute-done | bytes 237600 | tf_op jit(solution)/shard_map/ppermute | solution.py:29
  19.4 0.0 collective-permute-done.5.refs_3_
  19.4 0.8 %select_rows.1 = (bf16[64,3712]{1,0:T(8,128)(2,1)S(1)}, bf16[64,3712]{1,0:T(8,128)(2,1)S(1)}, bf16[64,3712]{1,0:T(8,128)(2,1)S(1)}, bf16[64,3712]{1,0:T(8,128)(2,1)S(1)}) custom-call(bf16[32,3712]{1,0:T(8,128)(2,1)S(1)} %pad_maximum_fusion.refs_0_, bf16[32,3712]{1,0:T(8,128)(2,1)S(1)} %collective-permute-done.3.refs_1_, ...), custom_call_target="tpu_custom_call" | custom-call | tf_op jit(solution)/shard_map/select_rows/pallas_call | solution.py:100
  20.3 2.5 %collective-permute-start.7 = (bf16[64,3712]{1,0:T(8,128)(2,1)S(1)}, bf16[64,3712]{1,0:T(8,128)(2,1)S(1)}, u32[]{:S(2)}, u32[]{:S(2)}) collective-permute-start(bf16[64,3712]{1,0:T(8,128)(2,1)S(1)} %get-tuple-element.52), channel_id=1, source_target_pairs={{0,16},{1,5},{2,18},{3,7},{4,20},{5,1},{6,22},{7,3},{8,24},{9,13},... | collective-permute-start | bytes 1425416 | tf_op jit(solution)/shard_map/ppermute | solution.py:29
  22.8 0.6 %collective-permute-start.6 = (bf16[64,3712]{1,0:T(8,128)(2,1)S(1)}, bf16[64,3712]{1,0:T(8,128)(2,1)S(1)}, u32[]{:S(2)}, u32[]{:S(2)}) collective-permute-start(bf16[64,3712]{1,0:T(8,128)(2,1)S(1)} %get-tuple-element.50), channel_id=1, source_target_pairs={{0,8},{1,3},{2,10},{3,5},{4,12},{5,7},{6,14},{7,1},{8,16},{9,11},{... | collective-permute-start | bytes 1425416 | tf_op jit(solution)/shard_map/ppermute | solution.py:29
  23.4 2.1 %collective-permute-start.9 = (bf16[64,3712]{1,0:T(8,128)(2,1)S(1)}, bf16[64,3712]{1,0:T(8,128)(2,1)S(1)}, u32[]{:S(2)}, u32[]{:S(2)}) collective-permute-start(bf16[64,3712]{1,0:T(8,128)(2,1)S(1)} %get-tuple-element.60), channel_id=1, source_target_pairs={{0,24},{1,7},{2,26},{3,1},{4,28},{5,3},{6,30},{7,5},{8,0},{9,15},{... | collective-permute-start | bytes 1425416 | tf_op jit(solution)/shard_map/ppermute | solution.py:29
  25.5 0.1 dynamic_update_slice.12
  25.6 4.1 %collective-permute-done.7.piece1 = bf16[64,3712]{1,0:T(8,128)(2,1)S(1)} collective-permute-done((bf16[64,3712]{1,0:T(8,128)(2,1)S(1)}, bf16[64,3712]{1,0:T(8,128)(2,1)S(1)}, u32[]{:S(2)}, u32[]{:S(2)}) %collective-permute-start.7) | collective-permute-done | bytes 475168 | tf_op jit(solution)/shard_map/ppermute | solution.py:29
  29.8 0.0 collective-permute-done.8.other
  29.8 1.4 %first_grads.1 = (bf16[2,128,256]{2,1,0:T(8,128)(2,1)S(1)}, bf16[2,128,256]{2,1,0:T(8,128)(2,1)S(1)}, f32[8,128]{1,0:T(8,128)S(1)}) custom-call(bf16[64,3712]{1,0:T(8,128)(2,1)S(1)} %get-tuple-element.51.piece0, bf16[64,3712]{1,0:T(8,128)(2,1)S(1)} %collective-permute-done.7.piece1, bf16[256,3584]{1,0:T(8,128)(2,1)S(1)} %get-tuple-element.53.mine, ...), custom_call_target="tpu_custom_call" | custom-call | tf_op jit(solution)/shard_map/first_grads/pallas_call | solution.py:194
  31.2 3.6 %collective-permute-done.6.piece0 = bf16[64,3712]{1,0:T(8,128)(2,1)S(1)} collective-permute-done((bf16[64,3712]{1,0:T(8,128)(2,1)S(1)}, bf16[64,3712]{1,0:T(8,128)(2,1)S(1)}, u32[]{:S(2)}, u32[]{:S(2)}) %collective-permute-start.6) | collective-permute-done | bytes 475168 | tf_op jit(solution)/shard_map/ppermute | solution.py:29
  34.8 0.1 collective-permute-done.9.piece1
  34.9 4.4 %collective-permute-start.10 = (bf16[256,3712]{1,0:T(8,128)(2,1)S(1)}, bf16[256,3712]{1,0:T(8,128)(2,1)}, u32[]{:S(2)}, u32[]{:S(2)}) collective-permute-start(bf16[256,3712]{1,0:T(8,128)(2,1)S(1)} %constant_dynamic-update-slice_fusion.rows.notes), channel_id=1, source_target_pairs={{0,1},{1,0},{2,3},{3,2},{4,5},{5,4},{6,7},{7,6},{8,9},{9,8},{10,11... | collective-permute-start | bytes 5701640 | tf_op jit(solution)/shard_map/ppermute | solution.py:33
  39.4 0.1 collective-permute-start.11
  39.5 2.0 %last_grads.1 = (bf16[2,128,256]{2,1,0:T(8,128)(2,1)S(1)}, bf16[2,128,256]{2,1,0:T(8,128)(2,1)S(1)}, f32[32,128]{1,0:T(8,128)}) custom-call(bf16[64,3712]{1,0:T(8,128)(2,1)S(1)} %collective-permute-done.6.piece0, bf16[64,3712]{1,0:T(8,128)(2,1)S(1)} %collective-permute-done.9.piece1, bf16[256,3584]{1,0:T(8,128)(2,1)S(1)} %get-tuple-element.53.mine, ...), custom_call_target="tpu_custom_call" | custom-call | tf_op jit(solution)/shard_map/last_grads/pallas_call | solution.py:221
  41.5 0.4 collective-permute-start.12
  41.9 5.2 %all-to-all-start = ((f32[32,1,128]{2,1,0:T(1,128)}), f32[32,1,128]{2,1,0:T(1,128)S(1)}, u32[]{:S(2)}, u32[]{:S(2)}) async-start(f32[32,1,128]{2,1,0:T(1,128)} %bitcast.11), calls=%async_computation | async-start | bytes 32768 | tf_op jit(solution)/shard_map/all_to_all | solution.py:412
  47.1 0.0 collective-permute-done.11.other0
  47.1 0.0 collective-permute-done.12.other1
  47.2 0.0 collective-permute-done.10.rows_other.notes_other
  47.2 3.7 %finished.1 = (bf16[2,2,256,256]{3,2,1,0:T(8,128)(2,1)}, bf16[256,3584]{1,0:T(8,128)(2,1)}, bf16[96,128]{1,0:T(8,128)(2,1)S(1)}, f32[16,128]{1,0:T(8,128)S(1)}, f32[4,32]{1,0:T(4,128)S(1)}) custom-call(bf16[256,3712]{1,0:T(8,128)(2,1)S(1)} %constant_dynamic-update-slice_fusion.rows.notes, bf16[256,3712]{1,0:T(8,128)(2,1)S(1)} %constant_dynamic-update-slice_fusion.rows.notes, ...), custom_call_target="tpu_custom_call" | custom-call | tf_op jit(solution)/shard_map/finished/pallas_call | solution.py:277
  50.9 3.2 %all-to-all-done = f32[32,1,128]{2,1,0:T(1,128)S(1)} async-done(((f32[32,1,128]{2,1,0:T(1,128)}), f32[32,1,128]{2,1,0:T(1,128)S(1)}, u32[]{:S(2)}, u32[]{:S(2)}) %all-to-all-start) | async-done | bytes 16416 | tf_op jit(solution)/shard_map/all_to_all | solution.py:412
  54.1 1.0 %logit_grads.1 = f32[4,32]{1,0:T(4,128)} custom-call(f32[32,128]{1,0:T(8,128)S(1)} %bitcast.31, bf16[96,128]{1,0:T(8,128)(2,1)S(1)} %get-tuple-element.76.experts, f32[16,128]{1,0:T(8,128)S(1)} %get-tuple-element.77.places, f32[4,32]{1,0:T(4,128)S(1)} %get-tuple-element.78.scores), custom_call_target="tpu_custom_call" | custom-call | tf_op jit(solution)/shard_map/logit_grads/pallas_call | solution.py:423
  (4 shorter events, 0.1 us)
Async XLA Ops:
  0.6 7.4 %collective-permute-start = (bf16[32,3584]{1,0:T(8,128)(2,1)}, bf16[32,3584]{1,0:T(8,128)(2,1)S(1)}, u32[]{:S(2)}, u32[]{:S(2)}) collective-permute-start(bf16[32,3584]{1,0:T(8,128)(2,1)} %bitcast.37), channel_id=1, source_target_pairs={{32,0},{64,32},{96,64},{128,96},{160,128},{192,160},{224,192},{34,... | collective-permute-start | bytes 688136 | tf_op jit(solution)/shard_map/ppermute | solution.py:380
  1.3 7.6 %collective-permute-start.1 = (bf16[32,3584]{1,0:T(8,128)(2,1)}, bf16[32,3584]{1,0:T(8,128)(2,1)S(1)}, u32[]{:S(2)}, u32[]{:S(2)}) collective-permute-start(bf16[32,3584]{1,0:T(8,128)(2,1)} %bitcast.38), channel_id=1, source_target_pairs={{1,33},{33,65},{65,97},{97,129},{129,161},{161,193},{193,225},{3,3... | collective-permute-start | bytes 688136 | tf_op jit(solution)/shard_map/ppermute | solution.py:383
  5.7 3.4 %collective-permute-start.2 = (bf16[2,2,256,256]{3,2,1,0:T(8,128)(2,1)}, bf16[2,2,256,256]{3,2,1,0:T(8,128)(2,1)S(1)}, u32[]{:S(2)}, u32[]{:S(2)}) collective-permute-start(bf16[2,2,256,256]{3,2,1,0:T(8,128)(2,1)} %bitcast.29), channel_id=1, source_target_pairs={{0,1},{1,0},{2,3},{3,2},{4,5},{5,4},{6,7},{7,6},{8,9},{9,8},{10,11... | collective-permute-start | bytes 1572872 | tf_op jit(solution)/shard_map/ppermute | solution.py:33
  5.9 0.7 %copy-start.2 = (s32[2,1,32,2]{2,3,1,0:T(2,128)S(1)}, s32[2,1,32,2]{2,3,1,0:T(2,128)}, u32[]{:S(2)}) copy-start(s32[2,1,32,2]{2,3,1,0:T(2,128)} %param.8) | copy-start | bytes 1540
  6.6 0.7 %copy-start.3 = (f32[2,1,32,2]{2,3,1,0:T(2,128)S(1)}, f32[2,1,32,2]{2,3,1,0:T(2,128)}, u32[]{:S(2)}) copy-start(f32[2,1,32,2]{2,3,1,0:T(2,128)} %param.9) | copy-start | bytes 1540
  7.5 22.3 %collective-permute-start.8 = (bf16[256,3584]{1,0:T(8,128)(2,1)}, bf16[256,3584]{1,0:T(8,128)(2,1)S(1)}, u32[]{:S(2)}, u32[]{:S(2)}) collective-permute-start(bf16[256,3584]{1,0:T(8,128)(2,1)} %bitcast.27), channel_id=1, source_target_pairs={{0,1},{1,0},{2,3},{3,2},{4,5},{5,4},{6,7},{7,6},{8,9},{9,8},{10,11... | collective-permute-start | bytes 5505032 | tf_op jit(solution)/shard_map/ppermute | solution.py:33
  9.1 8.0 %collective-permute-start.4 = (bf16[32,3712]{1,0:T(8,128)(2,1)S(1)}, bf16[32,3712]{1,0:T(8,128)(2,1)S(1)}, u32[]{:S(2)}, u32[]{:S(2)}) collective-permute-start(bf16[32,3712]{1,0:T(8,128)(2,1)S(1)} %pad_maximum_fusion.refs_0_), channel_id=1, source_target_pairs={{0,2},{1,9},{2,4},{3,11},{4,6},{5,13},{6,0},{7,15},{8,10},{9,17},{... | collective-permute-start | bytes 712712 | tf_op jit(solution)/shard_map/ppermute | solution.py:29
  10.5 9.0 %collective-permute-start.3 = (bf16[32,3712]{1,0:T(8,128)(2,1)S(1)}, bf16[32,3712]{1,0:T(8,128)(2,1)S(1)}, u32[]{:S(2)}, u32[]{:S(2)}) collective-permute-start(bf16[32,3712]{1,0:T(8,128)(2,1)S(1)} %pad_maximum_fusion.refs_0_), channel_id=1, source_target_pairs={{0,4},{1,17},{2,6},{3,19},{4,0},{5,21},{6,2},{7,23},{8,12},{9,25},... | collective-permute-start | bytes 712712 | tf_op jit(solution)/shard_map/ppermute | solution.py:29
  13.1 6.3 %collective-permute-start.5 = (bf16[32,3712]{1,0:T(8,128)(2,1)S(1)}, bf16[32,3712]{1,0:T(8,128)(2,1)S(1)}, u32[]{:S(2)}, u32[]{:S(2)}) collective-permute-start(bf16[32,3712]{1,0:T(8,128)(2,1)S(1)} %pad_maximum_fusion.refs_0_), channel_id=1, source_target_pairs={{0,6},{1,25},{2,0},{3,27},{4,2},{5,29},{6,4},{7,31},{8,14},{9,1},{... | collective-permute-start | bytes 712712 | tf_op jit(solution)/shard_map/ppermute | solution.py:29
  14.2 1.5 %copy-start = (bf16[1,1,256,3584]{3,2,1,0:T(8,128)(2,1)S(1)}, bf16[1,1,256,3584]{3,2,1,0:T(8,128)(2,1)}, u32[]{:S(2)}) copy-start(bf16[1,1,256,3584]{3,2,1,0:T(8,128)(2,1)} %param.11) | copy-start | bytes 5505028
  15.7 1.0 %copy-start.1 = (bf16[2,1,1,2,256,256]{5,4,3,2,1,0:T(8,128)(2,1)S(1)}, bf16[2,1,1,2,256,256]{5,4,3,2,1,0:T(8,128)(2,1)}, u32[]{:S(2)}) copy-start(bf16[2,1,1,2,256,256]{5,4,3,2,1,0:T(8,128)(2,1)} %param.10) | copy-start | bytes 1572868
  20.3 9.4 %collective-permute-start.7 = (bf16[64,3712]{1,0:T(8,128)(2,1)S(1)}, bf16[64,3712]{1,0:T(8,128)(2,1)S(1)}, u32[]{:S(2)}, u32[]{:S(2)}) collective-permute-start(bf16[64,3712]{1,0:T(8,128)(2,1)S(1)} %get-tuple-element.52), channel_id=1, source_target_pairs={{0,16},{1,5},{2,18},{3,7},{4,20},{5,1},{6,22},{7,3},{8,24},{9,13},... | collective-permute-start | bytes 1425416 | tf_op jit(solution)/shard_map/ppermute | solution.py:29
  22.8 11.9 %collective-permute-start.6 = (bf16[64,3712]{1,0:T(8,128)(2,1)S(1)}, bf16[64,3712]{1,0:T(8,128)(2,1)S(1)}, u32[]{:S(2)}, u32[]{:S(2)}) collective-permute-start(bf16[64,3712]{1,0:T(8,128)(2,1)S(1)} %get-tuple-element.50), channel_id=1, source_target_pairs={{0,8},{1,3},{2,10},{3,5},{4,12},{5,7},{6,14},{7,1},{8,16},{9,11},{... | collective-permute-start | bytes 1425416 | tf_op jit(solution)/shard_map/ppermute | solution.py:29
  23.4 11.5 %collective-permute-start.9 = (bf16[64,3712]{1,0:T(8,128)(2,1)S(1)}, bf16[64,3712]{1,0:T(8,128)(2,1)S(1)}, u32[]{:S(2)}, u32[]{:S(2)}) collective-permute-start(bf16[64,3712]{1,0:T(8,128)(2,1)S(1)} %get-tuple-element.60), channel_id=1, source_target_pairs={{0,24},{1,7},{2,26},{3,1},{4,28},{5,3},{6,30},{7,5},{8,0},{9,15},{... | collective-permute-start | bytes 1425416 | tf_op jit(solution)/shard_map/ppermute | solution.py:29
  34.9 12.2 %collective-permute-start.10 = (bf16[256,3712]{1,0:T(8,128)(2,1)S(1)}, bf16[256,3712]{1,0:T(8,128)(2,1)}, u32[]{:S(2)}, u32[]{:S(2)}) collective-permute-start(bf16[256,3712]{1,0:T(8,128)(2,1)S(1)} %constant_dynamic-update-slice_fusion.rows.notes), channel_id=1, source_target_pairs={{0,1},{1,0},{2,3},{3,2},{4,5},{5,4},{6,7},{7,6},{8,9},{9,8},{10,11... | collective-permute-start | bytes 5701640 | tf_op jit(solution)/shard_map/ppermute | solution.py:33
  39.4 7.8 %collective-permute-start.11 = (bf16[2,128,256]{2,1,0:T(8,128)(2,1)S(1)}, bf16[2,128,256]{2,1,0:T(8,128)(2,1)S(1)}, u32[]{:S(2)}, u32[]{:S(2)}) collective-permute-start(bf16[2,128,256]{2,1,0:T(8,128)(2,1)S(1)} %get-tuple-element.66), channel_id=1, source_target_pairs={{0,1},{1,0},{2,3},{3,2},{4,5},{5,4},{6,7},{7,6},{8,9},{9,8},{10,11... | collective-permute-start | bytes 393224 | tf_op jit(solution)/shard_map/ppermute | solution.py:33
  41.5 5.7 %collective-permute-start.12 = (bf16[2,128,256]{2,1,0:T(8,128)(2,1)S(1)}, bf16[2,128,256]{2,1,0:T(8,128)(2,1)S(1)}, u32[]{:S(2)}, u32[]{:S(2)}) collective-permute-start(bf16[2,128,256]{2,1,0:T(8,128)(2,1)S(1)} %get-tuple-element.67), channel_id=1, source_target_pairs={{0,1},{1,0},{2,3},{3,2},{4,5},{5,4},{6,7},{7,6},{8,9},{9,8},{10,11... | collective-permute-start | bytes 393224 | tf_op jit(solution)/shard_map/ppermute | solution.py:33
  41.9 12.2 %all-to-all-start = ((f32[32,1,128]{2,1,0:T(1,128)}), f32[32,1,128]{2,1,0:T(1,128)S(1)}, u32[]{:S(2)}, u32[]{:S(2)}) async-start(f32[32,1,128]{2,1,0:T(1,128)} %bitcast.11), calls=%async_computation | async-start | bytes 32768 | tf_op jit(solution)/shard_map/all_to_all | solution.py:412

commit v7 on v4

--- a/solution.py
+++ b/solution.py
@@ -12,7 +12,6 @@
 bf16, f32 = jnp.bfloat16, jnp.float32
 params = pltpu.CompilerParams(vmem_limit_bytes=16 * 2**20)
 whole = pl.BlockSpec(memory_space=pltpu.VMEM)
-in_hbm = pl.BlockSpec(memory_space=pltpu.HBM)
 
 
 def moved(place, step, along_x):
@@ -39,38 +38,40 @@
     return core, jnp.where(core == 0, x, y), jnp.where(core == 0, y, x)
 
 
-def token_blocks(core, far):
-    places = [(far + side - step) & 3 for step in (0,) + shifts]
+def token_blocks(core, near, far):
+    steps = (0,) + shifts
+    places = [(far + side - step) & 3 for step in steps]
+    holders = [(near + side - step) & 3 for step in steps]
     return [
-        jnp.where(core == 0, place * 4 + chunk, chunk * 4 + place)
+        jnp.where(core == 0, place * 4 + holder, holder * 4 + place)
         for place in places
-        for chunk in range(side)
+        for holder in holders
     ]
 
 
 def select_kernel(*refs):
-    blocks, outs = refs[:4], refs[4:]
+    blocks, outs = refs[:-4], refs[-4:]
     core, near, far = position()
-    held = [(near + side - step) & 3 for step in (0,) + shifts]
     targets = [(far + side + step) & 3 for step in (0,) + shifts]
     wanted = [jnp.where(core == 0, t * 2 + (near >> 1), near * 2 + (t >> 1)) for t in targets]
     tokens, width = blocks[0].shape
     width -= extra
-    slots = outs[0].shape[0] // 4
-    rows, columns = 4 * outs[0].shape[0], 4 * tokens
-
-    def pick(index, values):
-        return jnp.where(
-            index < 2,
-            jnp.where(index == 0, values[0], values[1]),
-            jnp.where(index == 2, values[2], values[3]),
-        )
-
-    notes = jnp.concatenate([ref[:, width:] for ref in blocks], axis=0).astype(f32).T
+    count, size = len(blocks), outs[0].shape[0]
+    rows, columns = 4 * size, 128
+    used = count * tokens
+
+    notes = [ref[:, width:] for ref in blocks]
+    if used < columns:
+        notes.append(jnp.zeros((columns - used, extra), bf16))
+    notes = jnp.concatenate(notes, axis=0).astype(f32).T
     row = lax.broadcasted_iota(jnp.int32, (rows, 1), 0)
     column = lax.broadcasted_iota(jnp.int32, (1, columns), 1)
-    expert = pick(row >> 6, wanted).astype(f32)
-    same = ((row >> 4) & 3) == pick(column >> 5, held)
+    later = [row >= size * target for target in range(1, 4)]
+    expert = jnp.where(later[0], wanted[1], wanted[0])
+    expert = jnp.where(later[1], wanted[2], expert)
+    expert = jnp.where(later[2], wanted[3], expert).astype(f32)
+    target = sum(passed.astype(jnp.int32) for passed in later)
+    same = ((row >> 4) - target * count) == (column >> 5)
     named0 = same & (notes[0:1] == expert)
     named = named0 | (same & (notes[1:2] == expert))
     i = lax.broadcasted_iota(jnp.int32, (columns, columns), 0)
@@ -82,11 +83,11 @@
     weight = jnp.sum(
         taken * jnp.where(named0, notes[2:3], notes[3:4]), axis=1, keepdims=True
     )
-    taken = taken.astype(bf16)
-
-    def put(start, size, value):
+    taken = taken[:, :used].astype(bf16)
+
+    def put(start, step, value):
         for index, out in enumerate(outs):
-            out[:, start : start + size] = value[index * 4 * slots : (index + 1) * 4 * slots]
+            out[:, start : start + step] = value[index * size : (index + 1) * size]
 
     put(width, extra, jnp.broadcast_to(weight, (rows, extra)).astype(bf16))
     step = 512 if width % 512 == 0 else width
@@ -96,23 +97,21 @@
 
 
 def select_rows(blocks, slots):
-    shape = jax.ShapeDtypeStruct((4 * slots, blocks[0].shape[1]), bf16)
+    shape = jax.ShapeDtypeStruct((len(blocks) * slots, blocks[0].shape[1]), bf16)
     return pl.pallas_call(
         select_kernel,
         out_shape=(shape,) * 4,
-        in_specs=[whole] * 4,
+        in_specs=[whole] * len(blocks),
         out_specs=(whole,) * 4,
         compiler_params=params,
         name="select_rows",
     )(*blocks)
 
 
-def factor_kernel(saved, swapped_saved, mine, factors, later, hidden, kept, arrived):
-    fetch = pltpu.make_async_copy(mine, kept, arrived)
-    fetch.start()
+def factor_kernel(saved, swapped_saved, factors, later, hidden):
     slots = saved.shape[2] // 16
     span, near, far = position()
-    order, order_other = token_blocks(span, far), token_blocks(1 - span, near)
+    order, order_other = token_blocks(span, near, far), token_blocks(1 - span, far, near)
 
     def loaded(ref, which, block):
         at = pl.ds(pl.multiple_of(block * slots, slots), slots)
@@ -132,10 +131,9 @@
         later[0, here, :], later[1, here, :], hidden[1, here, :] = loaded(
             saved, 1 - span, order_other[chunk]
         )
-    fetch.wait()
-
-
-def saved_factors(saved, swapped_saved, mine):
+
+
+def saved_factors(saved, swapped_saved):
     shape = saved.shape[2:]
     return pl.pallas_call(
         factor_kernel,
@@ -143,14 +141,12 @@
             jax.ShapeDtypeStruct((4,) + shape, f32),
             jax.ShapeDtypeStruct((2,) + shape, f32),
             jax.ShapeDtypeStruct((2,) + shape, bf16),
-            jax.ShapeDtypeStruct(mine.shape, bf16),
         ),
-        in_specs=[whole, whole, in_hbm],
-        out_specs=(whole,) * 4,
-        scratch_shapes=[pltpu.SemaphoreType.DMA],
+        in_specs=[whole] * 2,
+        out_specs=(whole,) * 3,
         compiler_params=params,
         name="saved_factors",
-    )(saved, swapped_saved, mine)
+    )(saved, swapped_saved)
 
 
 def slot_weights(notes, wide):
@@ -177,8 +173,7 @@
     count = rows.shape[0]
     width = rows.shape[1] - extra
     slots = count // 16
-    core, _, far = position()
-    order = token_blocks(core, far)
+    order = token_blocks(*position())
     raw_other = product_with(rows[:, :width], other[...])
     raw = product_with(rows[:, :width], mine[...])
     dot = jnp.sum(factors[0] * raw_other + factors[1] * raw, axis=1, keepdims=True)
@@ -214,7 +209,7 @@
     scaled, raw = refs[8:]
     count, wide = hidden.shape[1:]
     step = pl.program_id(0)
-    span, near, _ = position()
+    span, near, far = position()
 
     @pl.when(step == 0)
     def _():
@@ -241,7 +236,7 @@
             slot_weights(notes_other[...], wide),
             later[0],
             later[1],
-            token_blocks(1 - span, near),
+            token_blocks(1 - span, far, near),
         )
 
 
@@ -368,26 +363,32 @@
     notes, core, experts, places, scores = slot_notes(
         by_slot(expert_ids), by_slot(router_logits)
     )
+    notes, held = lax.optimization_barrier((notes, mine))
+    other = swapped(held)
     incoming = jnp.where(core == 0, from_above, from_below)
     block = jnp.concatenate([incoming, notes], axis=1)
-    swapped_saved = swapped(saved)
-    held, swapped_saved = lax.optimization_barrier((mine, swapped_saved))
-    other = swapped(held)
-    block, swapped_saved = lax.optimization_barrier((block, swapped_saved))
-
-    blocks = [block] + [plane_shift(block, step, True) for step in shifts]
-    factors, later, hidden, kept = saved_factors(saved, swapped_saved, mine)
-    blocks[1], other, kept, factors, later, hidden = lax.optimization_barrier(
-        (blocks[1], other, kept, factors, later, hidden)
-    )
-    pieces = select_rows(blocks, slots)
-    pieces = [pieces[0]] + [
-        plane_shift(piece, step, False) for piece, step in zip(pieces[1:], shifts, strict=True)
-    ]
-    rows = jnp.zeros((16 * slots, pieces[0].shape[1]), bf16)
-    for index, piece in enumerate(pieces):
-        rows = lax.dynamic_update_slice(rows, piece, (index * 4 * slots, 0))
-    grads, dots = raw_grads(rows, kept, other, factors)
+    block, swapped_saved = lax.optimization_barrier((block, swapped(saved)))
+
+    def sent(pieces):
+        return [pieces[0]] + [
+            plane_shift(piece, step, False)
+            for piece, step in zip(pieces[1:], shifts, strict=True)
+        ]
+
+    blocks = [plane_shift(block, step, True) for step in shifts]
+    block, other = lax.optimization_barrier((block, other))
+    picked = select_rows([block], slots)
+    own = sent(picked)
+    blocks[2], own[1] = lax.optimization_barrier((blocks[2], own[1]))
+    rest = sent(select_rows(blocks, slots))
+    own[1], saved, swapped_saved = lax.optimization_barrier((own[1], saved, swapped_saved))
+    factors, later, hidden = saved_factors(saved, swapped_saved)
+    rest[1], factors, later, hidden = lax.optimization_barrier((rest[1], factors, later, hidden))
+    rows = jnp.zeros((16 * slots, block.shape[1]), bf16)
+    for index in range(4):
+        rows = lax.dynamic_update_slice(rows, own[index], (index * 4 * slots, 0))
+        rows = lax.dynamic_update_slice(rows, rest[index], ((index * 4 + 1) * slots, 0))
+    grads, dots = raw_grads(rows, mine, other, factors)
     returned = lax.all_to_all(dots, ("expert", "dp"), split_axis=0, concat_axis=0, tiled=True)
     pair_grads, weight_grad, experts, places, scores = finished(
         rows, swapped(rows), mine, hidden, later, grads, (experts, places, scores)

time: 54.6 us -> 59.6 us (1.092)
  starting transfers between devices: 24.1 us -> 32.9 us
  local copies, waits for them, and re-layouts: 5.64 us -> 3.16 us
  waiting for transfers between devices: 14.4 us -> 12.4 us
    ppermute x6 -> x9, starting transfers between devices: 9.69 us -> 16.4 us  [plane_shift(): return lax.ppermute(value, ('expert', 'dp'), pairs)]
    ppermute x6 -> x9, waiting for transfers between devices: 12 us -> 8.33 us  [plane_shift(): return lax.ppermute(value, ('expert', 'dp'), pairs)]
    ppermute x3, starting transfers between devices: 6.7 us -> 9.9 us  [swapped(): return lax.ppermute(value, 'dp', [(0, 1), (1, 0)])]
    unnamed x10, local copies, waits for them, and re-layouts: 5.39 us -> 2.86 us
    ppermute x1, waiting for transfers between devices: 1.45 us -> 3.03 us  [local(): lax.ppermute(sent_up[0], ('pipe', 'dp'), [(2 * z + 1, 2 * z + 3) for z in...]
    all_to_all x1, starting transfers between devices: 5.23 us -> 4.12 us  [local(): lax.all_to_all(dots, ('expert', 'dp'), split_axis=0, concat_axis=0, tiled...]
  transfers between devices with their start and end apart: 12 -> 15, of which waited for: 7 -> 7; matrix products, arithmetic and copies ran while one was open for 1% -> 1% of each run, Pallas kernels for 13% -> 13%
where the time goes in v7:
time: 59.6 us; the launch traced here: 58.4 us
  starting transfers between devices  32.9 us (55%)
  waiting for transfers between devices  12.4 us (21%)
  Pallas kernels  8.93 us (15%)
  local copies, waits for them, and re-layouts  3.16 us (5%)
  between operations  0.81 us (1%)
    ppermute x9, starting transfers between devices, plane_shift(): return lax.ppermute(value, ('expert', 'dp'), pairs)  16.4 us
    ppermute x3, starting transfers between devices, swapped(): return lax.ppermute(value, 'dp', [(0, 1), (1, 0)])  9.9 us
    ppermute x9, waiting for transfers between devices, plane_shift(): return lax.ppermute(value, ('expert', 'dp'), pairs)  8.33 us
    pallas_call x1, Pallas kernels, finished(): pl.pallas_call(finish_kernel, grid=(width // step,), out_shape=shapes, in...  4.39 us
    all_to_all x1, starting transfers between devices, local(): lax.all_to_all(dots, ('expert', 'dp'), split_axis=0, concat_axis=0, tiled...  4.12 us
    ppermute x1, waiting for transfers between devices, local(): lax.ppermute(sent_up[0], ('pipe', 'dp'), [(2 * z + 1, 2 * z + 3) for z in...  3.03 us
    unnamed x10, local copies, waits for them, and re-layouts  2.86 us
    pallas_call x1, Pallas kernels, raw_grads(): pl.pallas_call(raw_kernel, out_shape=(jax.ShapeDtypeStruct((2,) + factors...  1.83 us
  transfers between devices with their start and end apart: 15, of which 7 were waited for; matrix products, arithmetic and copies ran while one was open for 1% of the time, Pallas kernels for 13%

profile of v7, /device:TPU:1, one launch (start us, length us, event | category | flops | bytes accessed | tf_op | source)
XLA Modules:
  0.0 58.4 jit_solution(6602598355564195053)
XLA Ops:
  0.6 0.0 copy-start.3
  0.6 0.7 %copy-done.3 = s32[2,1,32,2]{2,3,1,0:T(2,128)S(1)} copy-done((s32[2,1,32,2]{2,3,1,0:T(2,128)S(1)}, s32[2,1,32,2]{2,3,1,0:T(2,128)}, u32[]{:S(2)}) %copy-start.3) | copy-done | bytes 536
  1.3 0.0 copy-start.4
  1.3 0.7 %copy-done.4 = f32[2,1,32,2]{2,3,1,0:T(2,128)S(1)} copy-done((f32[2,1,32,2]{2,3,1,0:T(2,128)S(1)}, f32[2,1,32,2]{2,3,1,0:T(2,128)}, u32[]{:S(2)}) %copy-start.4) | copy-done | bytes 536
  2.0 0.2 slot_notes.1
  2.2 3.3 %collective-permute-start.3 = (bf16[256,3584]{1,0:T(8,128)(2,1)}, bf16[256,3584]{1,0:T(8,128)(2,1)S(1)}, u32[]{:S(2)}, u32[]{:S(2)}) collective-permute-start(bf16[256,3584]{1,0:T(8,128)(2,1)} %bitcast.27), channel_id=1, source_target_pairs={{0,1},{1,0},{2,3},{3,2},{4,5},{5,4},{6,7},{7,6},{8,9},{9,8},{10,11... | collective-permute-start | bytes 5505032 | tf_op jit(solution)/shard_map/ppermute | solution.py:32
  5.5 0.7 %collective-permute-start = (bf16[32,3584]{1,0:T(8,128)(2,1)}, bf16[32,3584]{1,0:T(8,128)(2,1)S(1)}, u32[]{:S(2)}, u32[]{:S(2)}) collective-permute-start(bf16[32,3584]{1,0:T(8,128)(2,1)} %bitcast.38), channel_id=1, source_target_pairs={{32,0},{64,32},{96,64},{128,96},{160,128},{192,160},{224,192},{34,... | collective-permute-start | bytes 688136 | tf_op jit(solution)/shard_map/ppermute | solution.py:357
  6.2 1.8 %collective-permute-start.1 = (bf16[32,3584]{1,0:T(8,128)(2,1)}, bf16[32,3584]{1,0:T(8,128)(2,1)S(1)}, u32[]{:S(2)}, u32[]{:S(2)}) collective-permute-start(bf16[32,3584]{1,0:T(8,128)(2,1)} %bitcast.39), channel_id=1, source_target_pairs={{1,33},{33,65},{65,97},{97,129},{129,161},{161,193},{193,225},{3,3... | collective-permute-start | bytes 688136 | tf_op jit(solution)/shard_map/ppermute | solution.py:360
  8.0 0.1 collective-permute-start.2
  8.1 0.1 compare_reduce_fusion
  8.2 0.0 collective-permute-done
  8.3 3.0 %collective-permute-done.1 = bf16[32,3584]{1,0:T(8,128)(2,1)S(1)} collective-permute-done((bf16[32,3584]{1,0:T(8,128)(2,1)}, bf16[32,3584]{1,0:T(8,128)(2,1)S(1)}, u32[]{:S(2)}, u32[]{:S(2)}) %collective-permute-start.1) | collective-permute-done | bytes 229408 | tf_op jit(solution)/shard_map/ppermute | solution.py:360
  11.3 0.1 broadcast_select_fusion
  11.4 0.0 copy-start.2
  11.4 0.0 collective-permute-done.2.swapped_saved
  11.4 2.8 %collective-permute-start.6 = (bf16[32,3712]{1,0:T(8,128)(2,1)S(1)}, bf16[32,3712]{1,0:T(8,128)(2,1)S(1)}, u32[]{:S(2)}, u32[]{:S(2)}) collective-permute-start(bf16[32,3712]{1,0:T(8,128)(2,1)S(1)} %pad_maximum_fusion.refs_0_), channel_id=1, source_target_pairs={{0,6},{1,25},{2,0},{3,27},{4,2},{5,29},{6,4},{7,31},{8,14},{9,1},{... | collective-permute-start | bytes 712712 | tf_op jit(solution)/shard_map/ppermute | solution.py:28
  14.2 0.0 collective-permute-start.5
  14.2 1.6 %collective-permute-start.4 = (bf16[32,3712]{1,0:T(8,128)(2,1)S(1)}, bf16[32,3712]{1,0:T(8,128)(2,1)S(1)}, u32[]{:S(2)}, u32[]{:S(2)}) collective-permute-start(bf16[32,3712]{1,0:T(8,128)(2,1)S(1)} %pad_maximum_fusion.refs_0_), channel_id=1, source_target_pairs={{0,4},{1,17},{2,6},{3,19},{4,0},{5,21},{6,2},{7,23},{8,12},{9,25},... | collective-permute-start | bytes 712712 | tf_op jit(solution)/shard_map/ppermute | solution.py:28
  15.9 0.0 collective-permute-done.3.other
  15.9 0.5 select_rows.2
  16.3 2.8 %collective-permute-start.7 = (bf16[16,3712]{1,0:T(8,128)(2,1)S(1)}, bf16[16,3712]{1,0:T(8,128)(2,1)S(1)}, u32[]{:S(2)}, u32[]{:S(2)}) collective-permute-start(bf16[16,3712]{1,0:T(8,128)(2,1)S(1)} %get-tuple-element.51), channel_id=1, source_target_pairs={{0,16},{1,5},{2,18},{3,7},{4,20},{5,1},{6,22},{7,3},{8,24},{9,13},... | collective-permute-start | bytes 356360 | tf_op jit(solution)/shard_map/ppermute | solution.py:28
  19.2 0.3 collective-permute-start.9
  19.5 0.1 dynamic_update_slice.24
  19.6 0.0 collective-permute-done.6.refs_2_
  19.6 2.5 %collective-permute-start.11 = (bf16[16,3712]{1,0:T(8,128)(2,1)S(1)}, bf16[16,3712]{1,0:T(8,128)(2,1)S(1)}, u32[]{:S(2)}, u32[]{:S(2)}) collective-permute-start(bf16[16,3712]{1,0:T(8,128)(2,1)S(1)} %get-tuple-element.66), channel_id=1, source_target_pairs={{0,24},{1,7},{2,26},{3,1},{4,28},{5,3},{6,30},{7,5},{8,0},{9,15},{... | collective-permute-start | bytes 356360 | tf_op jit(solution)/shard_map/ppermute | solution.py:28
  22.1 1.2 %collective-permute-done.7 = bf16[16,3712]{1,0:T(8,128)(2,1)S(1)} collective-permute-done((bf16[16,3712]{1,0:T(8,128)(2,1)S(1)}, bf16[16,3712]{1,0:T(8,128)(2,1)S(1)}, u32[]{:S(2)}, u32[]{:S(2)}) %collective-permute-start.7) | collective-permute-done | bytes 118816 | tf_op jit(solution)/shard_map/ppermute | solution.py:28
  23.3 1.2 %collective-permute-done.5.refs_1_ = bf16[32,3712]{1,0:T(8,128)(2,1)S(1)} collective-permute-done((bf16[32,3712]{1,0:T(8,128)(2,1)S(1)}, bf16[32,3712]{1,0:T(8,128)(2,1)S(1)}, u32[]{:S(2)}, u32[]{:S(2)}) %collective-permute-start.5) | collective-permute-done | bytes 237600 | tf_op jit(solution)/shard_map/ppermute | solution.py:28
  24.5 0.0 collective-permute-done.4.refs_0_
  24.5 0.7 %select_rows.3 = (bf16[48,3712]{1,0:T(8,128)(2,1)S(1)}, bf16[48,3712]{1,0:T(8,128)(2,1)S(1)}, bf16[48,3712]{1,0:T(8,128)(2,1)S(1)}, bf16[48,3712]{1,0:T(8,128)(2,1)S(1)}) custom-call(bf16[32,3712]{1,0:T(8,128)(2,1)S(1)} %collective-permute-done.4.refs_0_, bf16[32,3712]{1,0:T(8,128)(2,1)S(1)} %collective-permute-done.5.refs_1_, ...), custom_call_target="tpu_custom_call" | custom-call | tf_op jit(solution)/shard_map/select_rows/pallas_call | solution.py:101
  25.2 3.7 %collective-permute-start.8 = (bf16[48,3712]{1,0:T(8,128)(2,1)S(1)}, bf16[48,3712]{1,0:T(8,128)(2,1)S(1)}, u32[]{:S(2)}, u32[]{:S(2)}) collective-permute-start(bf16[48,3712]{1,0:T(8,128)(2,1)S(1)} %get-tuple-element.57), channel_id=1, source_target_pairs={{0,16},{1,5},{2,18},{3,7},{4,20},{5,1},{6,22},{7,3},{8,24},{9,13},... | collective-permute-start | bytes 1069064 | tf_op jit(solution)/shard_map/ppermute | solution.py:28
  28.9 0.2 collective-permute-start.10
  29.1 2.5 %collective-permute-start.12 = (bf16[48,3712]{1,0:T(8,128)(2,1)S(1)}, bf16[48,3712]{1,0:T(8,128)(2,1)S(1)}, u32[]{:S(2)}, u32[]{:S(2)}) collective-permute-start(bf16[48,3712]{1,0:T(8,128)(2,1)S(1)} %get-tuple-element.67), channel_id=1, source_target_pairs={{0,24},{1,7},{2,26},{3,1},{4,28},{5,3},{6,30},{7,5},{8,0},{9,15},{... | collective-permute-start | bytes 1069064 | tf_op jit(solution)/shard_map/ppermute | solution.py:28
  31.6 0.0 copy-done.2
  31.6 0.0 copy-start
  31.6 0.3 saved_factors.1
  32.0 1.8 %collective-permute-done.8 = bf16[48,3712]{1,0:T(8,128)(2,1)S(1)} collective-permute-done((bf16[48,3712]{1,0:T(8,128)(2,1)S(1)}, bf16[48,3712]{1,0:T(8,128)(2,1)S(1)}, u32[]{:S(2)}, u32[]{:S(2)}) %collective-permute-start.8) | collective-permute-done | bytes 356384 | tf_op jit(solution)/shard_map/ppermute | solution.py:28
  33.8 0.0 collective-permute-done.9
  33.8 3.9 %collective-permute-done.10 = bf16[48,3712]{1,0:T(8,128)(2,1)S(1)} collective-permute-done((bf16[48,3712]{1,0:T(8,128)(2,1)S(1)}, bf16[48,3712]{1,0:T(8,128)(2,1)S(1)}, u32[]{:S(2)}, u32[]{:S(2)}) %collective-permute-start.10) | collective-permute-done | bytes 356384 | tf_op jit(solution)/shard_map/ppermute | solution.py:28
  37.8 0.0 collective-permute-done.11
  37.9 0.1 collective-permute-done.12
  38.0 6.5 %collective-permute-start.13 = (bf16[256,3712]{1,0:T(8,128)(2,1)S(1)}, bf16[256,3712]{1,0:T(8,128)(2,1)}, u32[]{:S(2)}, u32[]{:S(2)}) collective-permute-start(bf16[256,3712]{1,0:T(8,128)(2,1)S(1)} %constant_dynamic-update-slice_fusion.rows.notes), channel_id=1, source_target_pairs={{0,1},{1,0},{2,3},{3,2},{4,5},{5,4},{6,7},{7,6},{8,9},{9,8},{10,11... | collective-permute-start | bytes 5701640 | tf_op jit(solution)/shard_map/ppermute | solution.py:32
  44.5 0.0 copy-done
  44.5 1.8 %raw_grads.1 = (bf16[2,256,256]{2,1,0:T(8,128)(2,1)S(1)}, f32[32,128]{1,0:T(8,128)}) custom-call(bf16[256,3712]{1,0:T(8,128)(2,1)S(1)} %constant_dynamic-update-slice_fusion.rows.notes, bf16[256,3584]{1,0:T(8,128)(2,1)S(1)} %bitcast.28, bf16[256,3584]{1,0:T(8,128)(2,1)S(1)} %collective-permute-done.3.other, f32[4,256,256]{2,1,0:T(8,128)S(1)} %get-tuple-element.69.factors), custom_call_target="tpu_custom_call" | custom-call | tf_op jit(solution)/shard_map/raw_grads/pallas_call | solution.py:192
  46.3 4.1 %all-to-all-start = ((f32[32,1,128]{2,1,0:T(1,128)}), f32[32,1,128]{2,1,0:T(1,128)S(1)}, u32[]{:S(2)}, u32[]{:S(2)}) async-start(f32[32,1,128]{2,1,0:T(1,128)} %bitcast.11), calls=%async_computation | async-start | bytes 32768 | tf_op jit(solution)/shard_map/all_to_all | solution.py:392
  50.4 0.0 collective-permute-done.13.rows_other.notes_other
  50.4 0.0 copy-start.1
  50.5 1.5 %copy-done.1 = bf16[1,1,256,3584]{3,2,1,0:T(8,128)(2,1)S(1)} copy-done((bf16[1,1,256,3584]{3,2,1,0:T(8,128)(2,1)S(1)}, bf16[1,1,256,3584]{3,2,1,0:T(8,128)(2,1)}, u32[]{:S(2)}) %copy-start.1) | copy-done | bytes 1835032
  51.9 4.4 %finished.1 = (bf16[2,2,256,256]{3,2,1,0:T(8,128)(2,1)}, bf16[256,3584]{1,0:T(8,128)(2,1)}, f32[32,128]{1,0:T(8,128)S(1)}, f32[128,128]{1,0:T(8,128)S(1)}, f32[4,32]{1,0:T(4,128)S(1)}) custom-call(bf16[256,3712]{1,0:T(8,128)(2,1)S(1)} %constant_dynamic-update-slice_fusion.rows.notes, bf16[256,3712]{1,0:T(8,128)(2,1)S(1)} %constant_dynamic-update-slice_fusion.rows.notes, ...), custom_call_target="tpu_custom_call" | custom-call | tf_op jit(solution)/shard_map/finished/pallas_call | solution.py:260
  56.3 1.0 %all-to-all-done = f32[32,1,128]{2,1,0:T(1,128)S(1)} async-done(((f32[32,1,128]{2,1,0:T(1,128)}), f32[32,1,128]{2,1,0:T(1,128)S(1)}, u32[]{:S(2)}, u32[]{:S(2)}) %all-to-all-start) | async-done | bytes 16416 | tf_op jit(solution)/shard_map/all_to_all | solution.py:392
  57.4 1.1 %logit_grads.1 = f32[4,32]{1,0:T(4,128)} custom-call(f32[32,128]{1,0:T(8,128)S(1)} %bitcast.32, f32[32,128]{1,0:T(8,128)S(1)} %get-tuple-element.82.experts, f32[128,128]{1,0:T(8,128)S(1)} %get-tuple-element.83.places, f32[4,32]{1,0:T(4,128)S(1)} %get-tuple-element.84.scores), custom_call_target="tpu_custom_call" | custom-call | tf_op jit(solution)/shard_map/logit_grads/pallas_call | solution.py:399
  (8 shorter events, 0.2 us)
Async XLA Ops:
  0.6 0.7 %copy-start.3 = (s32[2,1,32,2]{2,3,1,0:T(2,128)S(1)}, s32[2,1,32,2]{2,3,1,0:T(2,128)}, u32[]{:S(2)}) copy-start(s32[2,1,32,2]{2,3,1,0:T(2,128)} %param.8) | copy-start | bytes 1540
  1.3 0.7 %copy-start.4 = (f32[2,1,32,2]{2,3,1,0:T(2,128)S(1)}, f32[2,1,32,2]{2,3,1,0:T(2,128)}, u32[]{:S(2)}) copy-start(f32[2,1,32,2]{2,3,1,0:T(2,128)} %param.9) | copy-start | bytes 1540
  2.2 13.7 %collective-permute-start.3 = (bf16[256,3584]{1,0:T(8,128)(2,1)}, bf16[256,3584]{1,0:T(8,128)(2,1)S(1)}, u32[]{:S(2)}, u32[]{:S(2)}) collective-permute-start(bf16[256,3584]{1,0:T(8,128)(2,1)} %bitcast.27), channel_id=1, source_target_pairs={{0,1},{1,0},{2,3},{3,2},{4,5},{5,4},{6,7},{7,6},{8,9},{9,8},{10,11... | collective-permute-start | bytes 5505032 | tf_op jit(solution)/shard_map/ppermute | solution.py:32
  5.5 2.7 %collective-permute-start = (bf16[32,3584]{1,0:T(8,128)(2,1)}, bf16[32,3584]{1,0:T(8,128)(2,1)S(1)}, u32[]{:S(2)}, u32[]{:S(2)}) collective-permute-start(bf16[32,3584]{1,0:T(8,128)(2,1)} %bitcast.38), channel_id=1, source_target_pairs={{32,0},{64,32},{96,64},{128,96},{160,128},{192,160},{224,192},{34,... | collective-permute-start | bytes 688136 | tf_op jit(solution)/shard_map/ppermute | solution.py:357
  6.2 5.1 %collective-permute-start.1 = (bf16[32,3584]{1,0:T(8,128)(2,1)}, bf16[32,3584]{1,0:T(8,128)(2,1)S(1)}, u32[]{:S(2)}, u32[]{:S(2)}) collective-permute-start(bf16[32,3584]{1,0:T(8,128)(2,1)} %bitcast.39), channel_id=1, source_target_pairs={{1,33},{33,65},{65,97},{97,129},{129,161},{161,193},{193,225},{3,3... | collective-permute-start | bytes 688136 | tf_op jit(solution)/shard_map/ppermute | solution.py:360
  8.0 3.4 %collective-permute-start.2 = (bf16[2,2,256,256]{3,2,1,0:T(8,128)(2,1)}, bf16[2,2,256,256]{3,2,1,0:T(8,128)(2,1)S(1)}, u32[]{:S(2)}, u32[]{:S(2)}) collective-permute-start(bf16[2,2,256,256]{3,2,1,0:T(8,128)(2,1)} %bitcast.30), channel_id=1, source_target_pairs={{0,1},{1,0},{2,3},{3,2},{4,5},{5,4},{6,7},{7,6},{8,9},{9,8},{10,11... | collective-permute-start | bytes 1572872 | tf_op jit(solution)/shard_map/ppermute | solution.py:32
  11.4 20.2 %copy-start.2 = (bf16[2,1,1,2,256,256]{5,4,3,2,1,0:T(8,128)(2,1)S(1)}, bf16[2,1,1,2,256,256]{5,4,3,2,1,0:T(8,128)(2,1)}, u32[]{:S(2)}) copy-start(bf16[2,1,1,2,256,256]{5,4,3,2,1,0:T(8,128)(2,1)} %param.10) | copy-start | bytes 1572868
  11.4 8.2 %collective-permute-start.6 = (bf16[32,3712]{1,0:T(8,128)(2,1)S(1)}, bf16[32,3712]{1,0:T(8,128)(2,1)S(1)}, u32[]{:S(2)}, u32[]{:S(2)}) collective-permute-start(bf16[32,3712]{1,0:T(8,128)(2,1)S(1)} %pad_maximum_fusion.refs_0_), channel_id=1, source_target_pairs={{0,6},{1,25},{2,0},{3,27},{4,2},{5,29},{6,4},{7,31},{8,14},{9,1},{... | collective-permute-start | bytes 712712 | tf_op jit(solution)/shard_map/ppermute | solution.py:28
  14.2 10.3 %collective-permute-start.5 = (bf16[32,3712]{1,0:T(8,128)(2,1)S(1)}, bf16[32,3712]{1,0:T(8,128)(2,1)S(1)}, u32[]{:S(2)}, u32[]{:S(2)}) collective-permute-start(bf16[32,3712]{1,0:T(8,128)(2,1)S(1)} %pad_maximum_fusion.refs_0_), channel_id=1, source_target_pairs={{0,2},{1,9},{2,4},{3,11},{4,6},{5,13},{6,0},{7,15},{8,10},{9,17},{... | collective-permute-start | bytes 712712 | tf_op jit(solution)/shard_map/ppermute | solution.py:28
  14.2 10.3 %collective-permute-start.4 = (bf16[32,3712]{1,0:T(8,128)(2,1)S(1)}, bf16[32,3712]{1,0:T(8,128)(2,1)S(1)}, u32[]{:S(2)}, u32[]{:S(2)}) collective-permute-start(bf16[32,3712]{1,0:T(8,128)(2,1)S(1)} %pad_maximum_fusion.refs_0_), channel_id=1, source_target_pairs={{0,4},{1,17},{2,6},{3,19},{4,0},{5,21},{6,2},{7,23},{8,12},{9,25},... | collective-permute-start | bytes 712712 | tf_op jit(solution)/shard_map/ppermute | solution.py:28
  16.3 7.0 %collective-permute-start.7 = (bf16[16,3712]{1,0:T(8,128)(2,1)S(1)}, bf16[16,3712]{1,0:T(8,128)(2,1)S(1)}, u32[]{:S(2)}, u32[]{:S(2)}) collective-permute-start(bf16[16,3712]{1,0:T(8,128)(2,1)S(1)} %get-tuple-element.51), channel_id=1, source_target_pairs={{0,16},{1,5},{2,18},{3,7},{4,20},{5,1},{6,22},{7,3},{8,24},{9,13},... | collective-permute-start | bytes 356360 | tf_op jit(solution)/shard_map/ppermute | solution.py:28
  19.2 14.6 %collective-permute-start.9 = (bf16[16,3712]{1,0:T(8,128)(2,1)S(1)}, bf16[16,3712]{1,0:T(8,128)(2,1)S(1)}, u32[]{:S(2)}, u32[]{:S(2)}) collective-permute-start(bf16[16,3712]{1,0:T(8,128)(2,1)S(1)} %get-tuple-element.64), channel_id=1, source_target_pairs={{0,8},{1,3},{2,10},{3,5},{4,12},{5,7},{6,14},{7,1},{8,16},{9,11},{... | collective-permute-start | bytes 356360 | tf_op jit(solution)/shard_map/ppermute | solution.py:28
  19.6 18.2 %collective-permute-start.11 = (bf16[16,3712]{1,0:T(8,128)(2,1)S(1)}, bf16[16,3712]{1,0:T(8,128)(2,1)S(1)}, u32[]{:S(2)}, u32[]{:S(2)}) collective-permute-start(bf16[16,3712]{1,0:T(8,128)(2,1)S(1)} %get-tuple-element.66), channel_id=1, source_target_pairs={{0,24},{1,7},{2,26},{3,1},{4,28},{5,3},{6,30},{7,5},{8,0},{9,15},{... | collective-permute-start | bytes 356360 | tf_op jit(solution)/shard_map/ppermute | solution.py:28
  25.2 8.6 %collective-permute-start.8 = (bf16[48,3712]{1,0:T(8,128)(2,1)S(1)}, bf16[48,3712]{1,0:T(8,128)(2,1)S(1)}, u32[]{:S(2)}, u32[]{:S(2)}) collective-permute-start(bf16[48,3712]{1,0:T(8,128)(2,1)S(1)} %get-tuple-element.57), channel_id=1, source_target_pairs={{0,16},{1,5},{2,18},{3,7},{4,20},{5,1},{6,22},{7,3},{8,24},{9,13},... | collective-permute-start | bytes 1069064 | tf_op jit(solution)/shard_map/ppermute | solution.py:28
  28.9 8.9 %collective-permute-start.10 = (bf16[48,3712]{1,0:T(8,128)(2,1)S(1)}, bf16[48,3712]{1,0:T(8,128)(2,1)S(1)}, u32[]{:S(2)}, u32[]{:S(2)}) collective-permute-start(bf16[48,3712]{1,0:T(8,128)(2,1)S(1)} %get-tuple-element.65), channel_id=1, source_target_pairs={{0,8},{1,3},{2,10},{3,5},{4,12},{5,7},{6,14},{7,1},{8,16},{9,11},{... | collective-permute-start | bytes 1069064 | tf_op jit(solution)/shard_map/ppermute | solution.py:28
  29.1 8.9 %collective-permute-start.12 = (bf16[48,3712]{1,0:T(8,128)(2,1)S(1)}, bf16[48,3712]{1,0:T(8,128)(2,1)S(1)}, u32[]{:S(2)}, u32[]{:S(2)}) collective-permute-start(bf16[48,3712]{1,0:T(8,128)(2,1)S(1)} %get-tuple-element.67), channel_id=1, source_target_pairs={{0,24},{1,7},{2,26},{3,1},{4,28},{5,3},{6,30},{7,5},{8,0},{9,15},{... | collective-permute-start | bytes 1069064 | tf_op jit(solution)/shard_map/ppermute | solution.py:28
  31.6 12.9 %copy-start = (bf16[1,1,256,3584]{3,2,1,0:T(8,128)(2,1)S(1)}, bf16[1,1,256,3584]{3,2,1,0:T(8,128)(2,1)}, u32[]{:S(2)}) copy-start(bf16[1,1,256,3584]{3,2,1,0:T(8,128)(2,1)} %param.11) | copy-start | bytes 5505028
  38.0 12.4 %collective-permute-start.13 = (bf16[256,3712]{1,0:T(8,128)(2,1)S(1)}, bf16[256,3712]{1,0:T(8,128)(2,1)}, u32[]{:S(2)}, u32[]{:S(2)}) collective-permute-start(bf16[256,3712]{1,0:T(8,128)(2,1)S(1)} %constant_dynamic-update-slice_fusion.rows.notes), channel_id=1, source_target_pairs={{0,1},{1,0},{2,3},{3,2},{4,5},{5,4},{6,7},{7,6},{8,9},{9,8},{10,11... | collective-permute-start | bytes 5701640 | tf_op jit(solution)/shard_map/ppermute | solution.py:32
  46.3 11.1 %all-to-all-start = ((f32[32,1,128]{2,1,0:T(1,128)}), f32[32,1,128]{2,1,0:T(1,128)S(1)}, u32[]{:S(2)}, u32[]{:S(2)}) async-start(f32[32,1,128]{2,1,0:T(1,128)} %bitcast.11), calls=%async_computation | async-start | bytes 32768 | tf_op jit(solution)/shard_map/all_to_all | solution.py:392
  50.4 1.5 %copy-start.1 = (bf16[1,1,256,3584]{3,2,1,0:T(8,128)(2,1)S(1)}, bf16[1,1,256,3584]{3,2,1,0:T(8,128)(2,1)}, u32[]{:S(2)}) copy-start(bf16[1,1,256,3584]{3,2,1,0:T(8,128)(2,1)} %param.11) | copy-start | bytes 5505028

commit v8 on v4

--- a/solution.py
+++ b/solution.py
@@ -7,17 +7,16 @@
 
 route_scale = 2.5
 side = 4
-shifts = (2, 1, -1)
+gather_steps, exchange_steps = (2, 1, 3), (2, 3, 1)
 extra = 128
 bf16, f32 = jnp.bfloat16, jnp.float32
 params = pltpu.CompilerParams(vmem_limit_bytes=16 * 2**20)
 whole = pl.BlockSpec(memory_space=pltpu.VMEM)
-in_hbm = pl.BlockSpec(memory_space=pltpu.HBM)
 
 
 def moved(place, step, along_x):
     y, x = place // side, place % side
-    return y * side + (x + step) % side if along_x else (y + step) % side * side + x
+    return y * side + (x ^ step) if along_x else (y ^ step) * side + x
 
 
 def plane_shift(value, step, first_along_x):
@@ -40,7 +39,7 @@
 
 
 def token_blocks(core, far):
-    places = [(far + side - step) & 3 for step in (0,) + shifts]
+    places = [far ^ step for step in (0,) + exchange_steps]
     return [
         jnp.where(core == 0, place * 4 + chunk, chunk * 4 + place)
         for place in places
@@ -51,8 +50,8 @@
 def select_kernel(*refs):
     blocks, outs = refs[:4], refs[4:]
     core, near, far = position()
-    held = [(near + side - step) & 3 for step in (0,) + shifts]
-    targets = [(far + side + step) & 3 for step in (0,) + shifts]
+    held = [near ^ step for step in (0,) + gather_steps]
+    targets = [far ^ step for step in (0,) + exchange_steps]
     wanted = [jnp.where(core == 0, t * 2 + (near >> 1), near * 2 + (t >> 1)) for t in targets]
     tokens, width = blocks[0].shape
     width -= extra
@@ -107,9 +106,7 @@
     )(*blocks)
 
 
-def factor_kernel(saved, swapped_saved, mine, factors, later, hidden, kept, arrived):
-    fetch = pltpu.make_async_copy(mine, kept, arrived)
-    fetch.start()
+def factor_kernel(saved, swapped_saved, factors, later, hidden):
     slots = saved.shape[2] // 16
     span, near, far = position()
     order, order_other = token_blocks(span, far), token_blocks(1 - span, near)
@@ -132,10 +129,9 @@
         later[0, here, :], later[1, here, :], hidden[1, here, :] = loaded(
             saved, 1 - span, order_other[chunk]
         )
-    fetch.wait()
-
-
-def saved_factors(saved, swapped_saved, mine):
+
+
+def saved_factors(saved, swapped_saved):
     shape = saved.shape[2:]
     return pl.pallas_call(
         factor_kernel,
@@ -143,14 +139,12 @@
             jax.ShapeDtypeStruct((4,) + shape, f32),
             jax.ShapeDtypeStruct((2,) + shape, f32),
             jax.ShapeDtypeStruct((2,) + shape, bf16),
-            jax.ShapeDtypeStruct(mine.shape, bf16),
         ),
-        in_specs=[whole, whole, in_hbm],
-        out_specs=(whole,) * 4,
-        scratch_shapes=[pltpu.SemaphoreType.DMA],
+        in_specs=[whole] * 2,
+        out_specs=(whole,) * 3,
         compiler_params=params,
         name="saved_factors",
-    )(saved, swapped_saved, mine)
+    )(saved, swapped_saved)
 
 
 def slot_weights(notes, wide):
@@ -279,14 +273,18 @@
 
 def logit_kernel(returned, experts, places, scores, out):
     tokens = scores.shape[1]
+    left, parts = returned[...], []
+    for _ in range(3):
+        parts.append(left.astype(bf16))
+        left = left - parts[-1].astype(f32)
     spread = lax.dot_general(
-        returned[...],
+        jnp.concatenate(parts, axis=0),
         experts[...],
         (((0,), (0,)), ((), ())),
         preferred_element_type=f32,
-        precision=lax.Precision.HIGHEST,
-    )
-    route = jnp.sum(spread * places[...], axis=0, keepdims=True)
+    )
+    slots = places.shape[0]
+    route = jnp.sum(spread[:slots] * places[...], axis=0, keepdims=True)
     for span in range(2):
         first, second = 2 * span, 2 * span + 1
         route0 = route[:, first * tokens : (first + 1) * tokens]
@@ -308,7 +306,8 @@
     lane = lax.broadcasted_iota(jnp.int32, (1, 4 * tokens), 1)
     source = lax.broadcasted_iota(jnp.int32, (32, 4 * tokens), 0)
     span = lane >> 6
-    experts[...] = jnp.where(((source >> 2) == line) & ((source & 1) == span), 1.0, 0.0)
+    table = jnp.where(((source >> 2) == line) & ((source & 1) == span), 1.0, 0.0)
+    experts[...] = jnp.concatenate([table] * 3, axis=0).astype(bf16)
     expert = lax.broadcasted_iota(jnp.int32, (8, 4 * tokens), 0)
     marked = jnp.where(expert == line, 1.0, 0.0)
     i = lax.broadcasted_iota(jnp.int32, (4 * tokens, 4 * tokens), 0)
@@ -316,7 +315,7 @@
     earlier = jnp.where(((i >> 6) == (j >> 6)) & ((i & 31) < (j & 31)), 1.0, 0.0)
     before = jnp.dot(marked.astype(bf16), earlier.astype(bf16), preferred_element_type=f32)
     place = jnp.sum(before * marked, axis=0, keepdims=True)
-    slot = lax.broadcasted_iota(jnp.int32, (128, 4 * tokens), 0).astype(f32)
+    slot = lax.broadcasted_iota(jnp.int32, places.shape, 0).astype(f32)
     places[...] = jnp.where(slot == place, 1.0, 0.0)
     core[...] = jnp.broadcast_to(lax.axis_index("dp"), core.shape)
     first = lax.axis_index("dp") == 0
@@ -338,8 +337,8 @@
         out_shape=(
             jax.ShapeDtypeStruct((tokens, extra), bf16),
             jax.ShapeDtypeStruct((tokens, 1), jnp.int32),
-            jax.ShapeDtypeStruct((32, 4 * tokens), f32),
-            jax.ShapeDtypeStruct((128, 4 * tokens), f32),
+            jax.ShapeDtypeStruct((96, 4 * tokens), bf16),
+            jax.ShapeDtypeStruct((16, 4 * tokens), f32),
             jax.ShapeDtypeStruct((4, tokens), f32),
         ),
         in_specs=[whole] * 2,
@@ -368,26 +367,27 @@
     notes, core, experts, places, scores = slot_notes(
         by_slot(expert_ids), by_slot(router_logits)
     )
+    notes, held = lax.optimization_barrier((notes, mine))
+    other = swapped(held)
     incoming = jnp.where(core == 0, from_above, from_below)
     block = jnp.concatenate([incoming, notes], axis=1)
-    swapped_saved = swapped(saved)
-    held, swapped_saved = lax.optimization_barrier((mine, swapped_saved))
-    other = swapped(held)
-    block, swapped_saved = lax.optimization_barrier((block, swapped_saved))
-
-    blocks = [block] + [plane_shift(block, step, True) for step in shifts]
-    factors, later, hidden, kept = saved_factors(saved, swapped_saved, mine)
-    blocks[1], other, kept, factors, later, hidden = lax.optimization_barrier(
-        (blocks[1], other, kept, factors, later, hidden)
+    block, swapped_saved = lax.optimization_barrier((block, swapped(saved)))
+
+    blocks = [block] + [plane_shift(block, step, True) for step in gather_steps]
+    factors, later, hidden = saved_factors(saved, swapped_saved)
+    blocks[1], factors, later, hidden = lax.optimization_barrier(
+        (blocks[1], factors, later, hidden)
     )
     pieces = select_rows(blocks, slots)
     pieces = [pieces[0]] + [
-        plane_shift(piece, step, False) for piece, step in zip(pieces[1:], shifts, strict=True)
+        plane_shift(piece, step, False)
+        for piece, step in zip(pieces[1:], exchange_steps, strict=True)
     ]
+    pieces[1], other = lax.optimization_barrier((pieces[1], other))
     rows = jnp.zeros((16 * slots, pieces[0].shape[1]), bf16)
     for index, piece in enumerate(pieces):
         rows = lax.dynamic_update_slice(rows, piece, (index * 4 * slots, 0))
-    grads, dots = raw_grads(rows, kept, other, factors)
+    grads, dots = raw_grads(rows, mine, other, factors)
     returned = lax.all_to_all(dots, ("expert", "dp"), split_axis=0, concat_axis=0, tiled=True)
     pair_grads, weight_grad, experts, places, scores = finished(
         rows, swapped(rows), mine, hidden, later, grads, (experts, places, scores)

time: 54.6 us -> 54.2 us (level)
  waiting for transfers between devices: 14.4 us -> 17.3 us
  starting transfers between devices: 24.1 us -> 22.6 us
  local copies, waits for them, and re-layouts: 5.64 us -> 4.15 us
    ppermute x6, waiting for transfers between devices: 12 us -> 15.3 us  [plane_shift(): return lax.ppermute(value, ('expert', 'dp'), pairs)]
    ppermute x1, starting transfers between devices: 1.82 us -> 4.38 us  [local(): lax.ppermute(sent_up[0], ('pipe', 'dp'), [(2 * z + 1, 2 * z + 3) for z in...]
    ppermute x6, starting transfers between devices: 9.69 us -> 7.48 us  [plane_shift(): return lax.ppermute(value, ('expert', 'dp'), pairs)]
    ppermute x3, starting transfers between devices: 6.7 us -> 5 us  [swapped(): return lax.ppermute(value, 'dp', [(0, 1), (1, 0)])]
    unnamed x10, local copies, waits for them, and re-layouts: 5.39 us -> 3.9 us
  transfers between devices with their start and end apart: 12 -> 12, of which waited for: 7 -> 8; matrix products, arithmetic and copies ran while one was open for 1% -> 1% of each run, Pallas kernels for 13% -> 14%
where the time goes in v8:
time: 54.2 us; the launch traced here: 53.5 us
  starting transfers between devices  22.6 us (42%)
  waiting for transfers between devices  17.3 us (32%)
  Pallas kernels  8.49 us (16%)
  local copies, waits for them, and re-layouts  4.15 us (8%)
  between operations  0.74 us (1%)
    ppermute x6, waiting for transfers between devices, plane_shift(): return lax.ppermute(value, ('expert', 'dp'), pairs)  15.3 us
    ppermute x6, starting transfers between devices, plane_shift(): return lax.ppermute(value, ('expert', 'dp'), pairs)  7.48 us
    all_to_all x1, starting transfers between devices, local(): lax.all_to_all(dots, ('expert', 'dp'), split_axis=0, concat_axis=0, tiled...  5.02 us
    ppermute x3, starting transfers between devices, swapped(): return lax.ppermute(value, 'dp', [(0, 1), (1, 0)])  5 us
    pallas_call x1, Pallas kernels, finished(): pl.pallas_call(finish_kernel, grid=(width // step,), out_shape=shapes, in...  4.39 us
    ppermute x1, starting transfers between devices, local(): lax.ppermute(sent_up[0], ('pipe', 'dp'), [(2 * z + 1, 2 * z + 3) for z in...  4.38 us
    unnamed x10, local copies, waits for them, and re-layouts  3.9 us
    pallas_call x1, Pallas kernels, raw_grads(): pl.pallas_call(raw_kernel, out_shape=(jax.ShapeDtypeStruct((2,) + factors...  1.83 us
  transfers between devices with their start and end apart: 12, of which 8 were waited for; matrix products, arithmetic and copies ran while one was open for 1% of the time, Pallas kernels for 14%

profile of v8, /device:TPU:1, one launch (start us, length us, event | category | flops | bytes accessed | tf_op | source)
XLA Modules:
  0.0 53.5 jit_solution(3681807344447474754)
XLA Ops:
  0.6 0.7 %collective-permute-start = (bf16[32,3584]{1,0:T(8,128)(2,1)}, bf16[32,3584]{1,0:T(8,128)(2,1)S(1)}, u32[]{:S(2)}, u32[]{:S(2)}) collective-permute-start(bf16[32,3584]{1,0:T(8,128)(2,1)} %bitcast.38), channel_id=1, source_target_pairs={{32,0},{64,32},{96,64},{128,96},{160,128},{192,160},{224,192},{34,... | collective-permute-start | bytes 688136 | tf_op jit(solution)/shard_map/ppermute | solution.py:361
  1.3 4.4 %collective-permute-start.1 = (bf16[32,3584]{1,0:T(8,128)(2,1)}, bf16[32,3584]{1,0:T(8,128)(2,1)S(1)}, u32[]{:S(2)}, u32[]{:S(2)}) collective-permute-start(bf16[32,3584]{1,0:T(8,128)(2,1)} %bitcast.39), channel_id=1, source_target_pairs={{1,33},{33,65},{65,97},{97,129},{129,161},{161,193},{193,225},{3,3... | collective-permute-start | bytes 688136 | tf_op jit(solution)/shard_map/ppermute | solution.py:364
  5.7 0.2 collective-permute-start.2
  5.9 0.0 copy-start.3
  5.9 0.7 %copy-done.3 = s32[2,1,32,2]{2,3,1,0:T(2,128)S(1)} copy-done((s32[2,1,32,2]{2,3,1,0:T(2,128)S(1)}, s32[2,1,32,2]{2,3,1,0:T(2,128)}, u32[]{:S(2)}) %copy-start.3) | copy-done | bytes 536
  6.6 0.0 copy-start.4
  6.6 0.7 %copy-done.4 = f32[2,1,32,2]{2,3,1,0:T(2,128)S(1)} copy-done((f32[2,1,32,2]{2,3,1,0:T(2,128)S(1)}, f32[2,1,32,2]{2,3,1,0:T(2,128)}, u32[]{:S(2)}) %copy-start.4) | copy-done | bytes 536
  7.3 0.2 slot_notes.1
  7.5 0.4 collective-permute-start.7
  7.9 0.1 compare_reduce_fusion
  8.0 0.0 collective-permute-done
  8.0 1.0 %collective-permute-done.1 = bf16[32,3584]{1,0:T(8,128)(2,1)S(1)} collective-permute-done((bf16[32,3584]{1,0:T(8,128)(2,1)}, bf16[32,3584]{1,0:T(8,128)(2,1)S(1)}, u32[]{:S(2)}, u32[]{:S(2)}) %collective-permute-start.1) | collective-permute-done | bytes 229408 | tf_op jit(solution)/shard_map/ppermute | solution.py:364
  9.0 0.1 broadcast_select_fusion
  9.1 0.0 collective-permute-done.2.swapped_saved
  9.1 3.0 %collective-permute-start.3 = (bf16[32,3712]{1,0:T(8,128)(2,1)S(1)}, bf16[32,3712]{1,0:T(8,128)(2,1)S(1)}, u32[]{:S(2)}, u32[]{:S(2)}) collective-permute-start(bf16[32,3712]{1,0:T(8,128)(2,1)S(1)} %pad_maximum_fusion.refs_0_), channel_id=1, source_target_pairs={{0,4},{1,17},{2,6},{3,19},{4,0},{5,21},{6,2},{7,23},{8,12},{9,25},... | collective-permute-start | bytes 712712 | tf_op jit(solution)/shard_map/ppermute | solution.py:28
  12.1 0.8 %collective-permute-start.5 = (bf16[32,3712]{1,0:T(8,128)(2,1)S(1)}, bf16[32,3712]{1,0:T(8,128)(2,1)S(1)}, u32[]{:S(2)}, u32[]{:S(2)}) collective-permute-start(bf16[32,3712]{1,0:T(8,128)(2,1)S(1)} %pad_maximum_fusion.refs_0_), channel_id=1, source_target_pairs={{0,6},{1,25},{2,4},{3,27},{4,2},{5,29},{6,0},{7,31},{8,14},{9,17},... | collective-permute-start | bytes 712712 | tf_op jit(solution)/shard_map/ppermute | solution.py:28
  12.9 0.0 collective-permute-start.4
  12.9 0.0 copy-start.2
  12.9 1.0 %copy-done.2 = bf16[2,1,1,2,256,256]{5,4,3,2,1,0:T(8,128)(2,1)S(1)} copy-done((bf16[2,1,1,2,256,256]{5,4,3,2,1,0:T(8,128)(2,1)S(1)}, bf16[2,1,1,2,256,256]{5,4,3,2,1,0:T(8,128)(2,1)}, u32[]{:S(2)}) %copy-start.2) | copy-done | bytes 524312
  13.9 0.3 saved_factors.1
  14.2 1.4 %collective-permute-done.3.refs_1_ = bf16[32,3712]{1,0:T(8,128)(2,1)S(1)} collective-permute-done((bf16[32,3712]{1,0:T(8,128)(2,1)S(1)}, bf16[32,3712]{1,0:T(8,128)(2,1)S(1)}, u32[]{:S(2)}, u32[]{:S(2)}) %collective-permute-start.3) | collective-permute-done | bytes 237600 | tf_op jit(solution)/shard_map/ppermute | solution.py:28
  15.6 2.9 %collective-permute-done.5.refs_3_ = bf16[32,3712]{1,0:T(8,128)(2,1)S(1)} collective-permute-done((bf16[32,3712]{1,0:T(8,128)(2,1)S(1)}, bf16[32,3712]{1,0:T(8,128)(2,1)S(1)}, u32[]{:S(2)}, u32[]{:S(2)}) %collective-permute-start.5) | collective-permute-done | bytes 237600 | tf_op jit(solution)/shard_map/ppermute | solution.py:28
  18.6 0.3 collective-permute-done.4.refs_2_
  18.9 0.8 %select_rows.1 = (bf16[64,3712]{1,0:T(8,128)(2,1)S(1)}, bf16[64,3712]{1,0:T(8,128)(2,1)S(1)}, bf16[64,3712]{1,0:T(8,128)(2,1)S(1)}, bf16[64,3712]{1,0:T(8,128)(2,1)S(1)}) custom-call(bf16[32,3712]{1,0:T(8,128)(2,1)S(1)} %pad_maximum_fusion.refs_0_, bf16[32,3712]{1,0:T(8,128)(2,1)S(1)} %collective-permute-done.3.refs_1_, ...), custom_call_target="tpu_custom_call" | custom-call | tf_op jit(solution)/shard_map/select_rows/pallas_call | solution.py:99
  19.7 2.8 %collective-permute-start.6 = (bf16[64,3712]{1,0:T(8,128)(2,1)S(1)}, bf16[64,3712]{1,0:T(8,128)(2,1)S(1)}, u32[]{:S(2)}, u32[]{:S(2)}) collective-permute-start(bf16[64,3712]{1,0:T(8,128)(2,1)S(1)} %get-tuple-element.45), channel_id=1, source_target_pairs={{0,16},{1,5},{2,18},{3,7},{4,20},{5,1},{6,22},{7,3},{8,24},{9,13},... | collective-permute-start | bytes 1425416 | tf_op jit(solution)/shard_map/ppermute | solution.py:28
  22.5 0.9 %collective-permute-start.8 = (bf16[64,3712]{1,0:T(8,128)(2,1)S(1)}, bf16[64,3712]{1,0:T(8,128)(2,1)S(1)}, u32[]{:S(2)}, u32[]{:S(2)}) collective-permute-start(bf16[64,3712]{1,0:T(8,128)(2,1)S(1)} %get-tuple-element.48), channel_id=1, source_target_pairs={{0,24},{1,7},{2,26},{3,5},{4,28},{5,3},{6,30},{7,1},{8,16},{9,15},... | collective-permute-start | bytes 1425416 | tf_op jit(solution)/shard_map/ppermute | solution.py:28
  23.4 0.0 collective-permute-start.9
  23.4 0.1 dynamic_update_slice.12
  23.5 0.0 copy-start
  23.6 5.6 %collective-permute-done.6 = bf16[64,3712]{1,0:T(8,128)(2,1)S(1)} collective-permute-done((bf16[64,3712]{1,0:T(8,128)(2,1)S(1)}, bf16[64,3712]{1,0:T(8,128)(2,1)S(1)}, u32[]{:S(2)}, u32[]{:S(2)}) %collective-permute-start.6) | collective-permute-done | bytes 475168 | tf_op jit(solution)/shard_map/ppermute | solution.py:28
  29.1 0.0 collective-permute-done.7.other
  29.2 5.0 %collective-permute-done.8 = bf16[64,3712]{1,0:T(8,128)(2,1)S(1)} collective-permute-done((bf16[64,3712]{1,0:T(8,128)(2,1)S(1)}, bf16[64,3712]{1,0:T(8,128)(2,1)S(1)}, u32[]{:S(2)}, u32[]{:S(2)}) %collective-permute-start.8) | collective-permute-done | bytes 475168 | tf_op jit(solution)/shard_map/ppermute | solution.py:28
  34.2 0.1 collective-permute-done.9
  34.4 4.4 %collective-permute-start.10 = (bf16[256,3712]{1,0:T(8,128)(2,1)S(1)}, bf16[256,3712]{1,0:T(8,128)(2,1)}, u32[]{:S(2)}, u32[]{:S(2)}) collective-permute-start(bf16[256,3712]{1,0:T(8,128)(2,1)S(1)} %constant_dynamic-update-slice_fusion.rows.notes), channel_id=1, source_target_pairs={{0,1},{1,0},{2,3},{3,2},{4,5},{5,4},{6,7},{7,6},{8,9},{9,8},{10,11... | collective-permute-start | bytes 5701640 | tf_op jit(solution)/shard_map/ppermute | solution.py:32
  38.7 0.0 copy-done
  38.7 1.8 %raw_grads.1 = (bf16[2,256,256]{2,1,0:T(8,128)(2,1)S(1)}, f32[32,128]{1,0:T(8,128)}) custom-call(bf16[256,3712]{1,0:T(8,128)(2,1)S(1)} %constant_dynamic-update-slice_fusion.rows.notes, bf16[256,3584]{1,0:T(8,128)(2,1)S(1)} %bitcast.28, bf16[256,3584]{1,0:T(8,128)(2,1)S(1)} %collective-permute-done.7.other, f32[4,256,256]{2,1,0:T(8,128)S(1)} %get-tuple-element.51.factors), custom_call_target="tpu_custom_call" | custom-call | tf_op jit(solution)/shard_map/raw_grads/pallas_call | solution.py:191
  40.6 5.0 %all-to-all-start = ((f32[32,1,128]{2,1,0:T(1,128)}), f32[32,1,128]{2,1,0:T(1,128)S(1)}, u32[]{:S(2)}, u32[]{:S(2)}) async-start(f32[32,1,128]{2,1,0:T(1,128)} %bitcast.11), calls=%async_computation | async-start | bytes 32768 | tf_op jit(solution)/shard_map/all_to_all | solution.py:391
  45.6 0.0 collective-permute-done.10.rows_other.notes_other
  45.6 0.0 copy-start.1
  45.6 1.5 %copy-done.1 = bf16[1,1,256,3584]{3,2,1,0:T(8,128)(2,1)S(1)} copy-done((bf16[1,1,256,3584]{3,2,1,0:T(8,128)(2,1)S(1)}, bf16[1,1,256,3584]{3,2,1,0:T(8,128)(2,1)}, u32[]{:S(2)}) %copy-start.1) | copy-done | bytes 1835032
  47.1 4.4 %finished.1 = (bf16[2,2,256,256]{3,2,1,0:T(8,128)(2,1)}, bf16[256,3584]{1,0:T(8,128)(2,1)}, bf16[96,128]{1,0:T(8,128)(2,1)S(1)}, f32[16,128]{1,0:T(8,128)S(1)}, f32[4,32]{1,0:T(4,128)S(1)}) custom-call(bf16[256,3712]{1,0:T(8,128)(2,1)S(1)} %constant_dynamic-update-slice_fusion.rows.notes, bf16[256,3712]{1,0:T(8,128)(2,1)S(1)} %constant_dynamic-update-slice_fusion.rows.notes, ...), custom_call_target="tpu_custom_call" | custom-call | tf_op jit(solution)/shard_map/finished/pallas_call | solution.py:259
  51.5 1.0 %all-to-all-done = f32[32,1,128]{2,1,0:T(1,128)S(1)} async-done(((f32[32,1,128]{2,1,0:T(1,128)}), f32[32,1,128]{2,1,0:T(1,128)S(1)}, u32[]{:S(2)}, u32[]{:S(2)}) %all-to-all-start) | async-done | bytes 16416 | tf_op jit(solution)/shard_map/all_to_all | solution.py:391
  52.5 1.0 %logit_grads.1 = f32[4,32]{1,0:T(4,128)} custom-call(f32[32,128]{1,0:T(8,128)S(1)} %bitcast.32, bf16[96,128]{1,0:T(8,128)(2,1)S(1)} %get-tuple-element.64.experts, f32[16,128]{1,0:T(8,128)S(1)} %get-tuple-element.65.places, f32[4,32]{1,0:T(4,128)S(1)} %get-tuple-element.66.scores), custom_call_target="tpu_custom_call" | custom-call | tf_op jit(solution)/shard_map/logit_grads/pallas_call | solution.py:398
  (4 shorter events, 0.1 us)
Async XLA Ops:
  0.6 7.4 %collective-permute-start = (bf16[32,3584]{1,0:T(8,128)(2,1)}, bf16[32,3584]{1,0:T(8,128)(2,1)S(1)}, u32[]{:S(2)}, u32[]{:S(2)}) collective-permute-start(bf16[32,3584]{1,0:T(8,128)(2,1)} %bitcast.38), channel_id=1, source_target_pairs={{32,0},{64,32},{96,64},{128,96},{160,128},{192,160},{224,192},{34,... | collective-permute-start | bytes 688136 | tf_op jit(solution)/shard_map/ppermute | solution.py:361
  1.3 7.6 %collective-permute-start.1 = (bf16[32,3584]{1,0:T(8,128)(2,1)}, bf16[32,3584]{1,0:T(8,128)(2,1)S(1)}, u32[]{:S(2)}, u32[]{:S(2)}) collective-permute-start(bf16[32,3584]{1,0:T(8,128)(2,1)} %bitcast.39), channel_id=1, source_target_pairs={{1,33},{33,65},{65,97},{97,129},{129,161},{161,193},{193,225},{3,3... | collective-permute-start | bytes 688136 | tf_op jit(solution)/shard_map/ppermute | solution.py:364
  5.7 3.4 %collective-permute-start.2 = (bf16[2,2,256,256]{3,2,1,0:T(8,128)(2,1)}, bf16[2,2,256,256]{3,2,1,0:T(8,128)(2,1)S(1)}, u32[]{:S(2)}, u32[]{:S(2)}) collective-permute-start(bf16[2,2,256,256]{3,2,1,0:T(8,128)(2,1)} %bitcast.30), channel_id=1, source_target_pairs={{0,1},{1,0},{2,3},{3,2},{4,5},{5,4},{6,7},{7,6},{8,9},{9,8},{10,11... | collective-permute-start | bytes 1572872 | tf_op jit(solution)/shard_map/ppermute | solution.py:32
  5.9 0.7 %copy-start.3 = (s32[2,1,32,2]{2,3,1,0:T(2,128)S(1)}, s32[2,1,32,2]{2,3,1,0:T(2,128)}, u32[]{:S(2)}) copy-start(s32[2,1,32,2]{2,3,1,0:T(2,128)} %param.8) | copy-start | bytes 1540
  6.6 0.7 %copy-start.4 = (f32[2,1,32,2]{2,3,1,0:T(2,128)S(1)}, f32[2,1,32,2]{2,3,1,0:T(2,128)}, u32[]{:S(2)}) copy-start(f32[2,1,32,2]{2,3,1,0:T(2,128)} %param.9) | copy-start | bytes 1540
  7.5 21.6 %collective-permute-start.7 = (bf16[256,3584]{1,0:T(8,128)(2,1)}, bf16[256,3584]{1,0:T(8,128)(2,1)S(1)}, u32[]{:S(2)}, u32[]{:S(2)}) collective-permute-start(bf16[256,3584]{1,0:T(8,128)(2,1)} %bitcast.27), channel_id=1, source_target_pairs={{0,1},{1,0},{2,3},{3,2},{4,5},{5,4},{6,7},{7,6},{8,9},{9,8},{10,11... | collective-permute-start | bytes 5505032 | tf_op jit(solution)/shard_map/ppermute | solution.py:32
  9.1 6.6 %collective-permute-start.3 = (bf16[32,3712]{1,0:T(8,128)(2,1)S(1)}, bf16[32,3712]{1,0:T(8,128)(2,1)S(1)}, u32[]{:S(2)}, u32[]{:S(2)}) collective-permute-start(bf16[32,3712]{1,0:T(8,128)(2,1)S(1)} %pad_maximum_fusion.refs_0_), channel_id=1, source_target_pairs={{0,4},{1,17},{2,6},{3,19},{4,0},{5,21},{6,2},{7,23},{8,12},{9,25},... | collective-permute-start | bytes 712712 | tf_op jit(solution)/shard_map/ppermute | solution.py:28
  12.1 6.5 %collective-permute-start.5 = (bf16[32,3712]{1,0:T(8,128)(2,1)S(1)}, bf16[32,3712]{1,0:T(8,128)(2,1)S(1)}, u32[]{:S(2)}, u32[]{:S(2)}) collective-permute-start(bf16[32,3712]{1,0:T(8,128)(2,1)S(1)} %pad_maximum_fusion.refs_0_), channel_id=1, source_target_pairs={{0,6},{1,25},{2,4},{3,27},{4,2},{5,29},{6,0},{7,31},{8,14},{9,17},... | collective-permute-start | bytes 712712 | tf_op jit(solution)/shard_map/ppermute | solution.py:28
  12.9 6.0 %collective-permute-start.4 = (bf16[32,3712]{1,0:T(8,128)(2,1)S(1)}, bf16[32,3712]{1,0:T(8,128)(2,1)S(1)}, u32[]{:S(2)}, u32[]{:S(2)}) collective-permute-start(bf16[32,3712]{1,0:T(8,128)(2,1)S(1)} %pad_maximum_fusion.refs_0_), channel_id=1, source_target_pairs={{0,2},{1,9},{2,0},{3,11},{4,6},{5,13},{6,4},{7,15},{8,10},{9,1},{1... | collective-permute-start | bytes 712712 | tf_op jit(solution)/shard_map/ppermute | solution.py:28
  12.9 1.0 %copy-start.2 = (bf16[2,1,1,2,256,256]{5,4,3,2,1,0:T(8,128)(2,1)S(1)}, bf16[2,1,1,2,256,256]{5,4,3,2,1,0:T(8,128)(2,1)}, u32[]{:S(2)}) copy-start(bf16[2,1,1,2,256,256]{5,4,3,2,1,0:T(8,128)(2,1)} %param.10) | copy-start | bytes 1572868
  19.7 9.4 %collective-permute-start.6 = (bf16[64,3712]{1,0:T(8,128)(2,1)S(1)}, bf16[64,3712]{1,0:T(8,128)(2,1)S(1)}, u32[]{:S(2)}, u32[]{:S(2)}) collective-permute-start(bf16[64,3712]{1,0:T(8,128)(2,1)S(1)} %get-tuple-element.45), channel_id=1, source_target_pairs={{0,16},{1,5},{2,18},{3,7},{4,20},{5,1},{6,22},{7,3},{8,24},{9,13},... | collective-permute-start | bytes 1425416 | tf_op jit(solution)/shard_map/ppermute | solution.py:28
  22.5 11.6 %collective-permute-start.8 = (bf16[64,3712]{1,0:T(8,128)(2,1)S(1)}, bf16[64,3712]{1,0:T(8,128)(2,1)S(1)}, u32[]{:S(2)}, u32[]{:S(2)}) collective-permute-start(bf16[64,3712]{1,0:T(8,128)(2,1)S(1)} %get-tuple-element.48), channel_id=1, source_target_pairs={{0,24},{1,7},{2,26},{3,5},{4,28},{5,3},{6,30},{7,1},{8,16},{9,15},... | collective-permute-start | bytes 1425416 | tf_op jit(solution)/shard_map/ppermute | solution.py:28
  23.4 10.9 %collective-permute-start.9 = (bf16[64,3712]{1,0:T(8,128)(2,1)S(1)}, bf16[64,3712]{1,0:T(8,128)(2,1)S(1)}, u32[]{:S(2)}, u32[]{:S(2)}) collective-permute-start(bf16[64,3712]{1,0:T(8,128)(2,1)S(1)} %get-tuple-element.49), channel_id=1, source_target_pairs={{0,8},{1,3},{2,10},{3,1},{4,12},{5,7},{6,14},{7,5},{8,0},{9,11},{1... | collective-permute-start | bytes 1425416 | tf_op jit(solution)/shard_map/ppermute | solution.py:28
  23.5 15.2 %copy-start = (bf16[1,1,256,3584]{3,2,1,0:T(8,128)(2,1)S(1)}, bf16[1,1,256,3584]{3,2,1,0:T(8,128)(2,1)}, u32[]{:S(2)}) copy-start(bf16[1,1,256,3584]{3,2,1,0:T(8,128)(2,1)} %param.11) | copy-start | bytes 5505028
  34.4 11.3 %collective-permute-start.10 = (bf16[256,3712]{1,0:T(8,128)(2,1)S(1)}, bf16[256,3712]{1,0:T(8,128)(2,1)}, u32[]{:S(2)}, u32[]{:S(2)}) collective-permute-start(bf16[256,3712]{1,0:T(8,128)(2,1)S(1)} %constant_dynamic-update-slice_fusion.rows.notes), channel_id=1, source_target_pairs={{0,1},{1,0},{2,3},{3,2},{4,5},{5,4},{6,7},{7,6},{8,9},{9,8},{10,11... | collective-permute-start | bytes 5701640 | tf_op jit(solution)/shard_map/ppermute | solution.py:32
  40.6 12.0 %all-to-all-start = ((f32[32,1,128]{2,1,0:T(1,128)}), f32[32,1,128]{2,1,0:T(1,128)S(1)}, u32[]{:S(2)}, u32[]{:S(2)}) async-start(f32[32,1,128]{2,1,0:T(1,128)} %bitcast.11), calls=%async_computation | async-start | bytes 32768 | tf_op jit(solution)/shard_map/all_to_all | solution.py:391
  45.6 1.5 %copy-start.1 = (bf16[1,1,256,3584]{3,2,1,0:T(8,128)(2,1)S(1)}, bf16[1,1,256,3584]{3,2,1,0:T(8,128)(2,1)}, u32[]{:S(2)}) copy-start(bf16[1,1,256,3584]{3,2,1,0:T(8,128)(2,1)} %param.11) | copy-start | bytes 5505028

commit v9 on v8

--- a/solution.py
+++ b/solution.py
@@ -106,7 +106,7 @@
     )(*blocks)
 
 
-def factor_kernel(saved, swapped_saved, factors, later, hidden):
+def factor_kernel(saved, swapped_saved, factors, hidden):
     slots = saved.shape[2] // 16
     span, near, far = position()
     order, order_other = token_blocks(span, far), token_blocks(1 - span, near)
@@ -116,19 +116,17 @@
         gate, up = ref[which, 0, at, :].astype(f32), ref[which, 1, at, :].astype(f32)
         sigma = jax.nn.sigmoid(gate)
         silu = gate * sigma
-        return up * sigma * (1.0 + gate * (1.0 - sigma)), silu, (silu * up).astype(bf16)
+        return (silu * up).astype(bf16), up * sigma * (1.0 + gate * (1.0 - sigma)), silu
 
     for chunk in range(16):
         here = slice(chunk * slots, (chunk + 1) * slots)
-        factors[0, here, :] = loaded(swapped_saved, span, order[chunk])[2].astype(f32)
-        gate, up, product = loaded(saved, span, order[chunk])
-        factors[1, here, :] = product.astype(f32)
-        factors[2, here, :] = gate
-        factors[3, here, :] = up
+        for base, ref in ((0, swapped_saved), (3, saved)):
+            product, gate, up = loaded(ref, span, order[chunk])
+            factors[base, here, :] = product.astype(f32)
+            factors[base + 1, here, :] = gate
+            factors[base + 2, here, :] = up
         hidden[0, here, :] = product
-        later[0, here, :], later[1, here, :], hidden[1, here, :] = loaded(
-            saved, 1 - span, order_other[chunk]
-        )
+        hidden[1, here, :] = loaded(saved, 1 - span, order_other[chunk])[0]
 
 
 def saved_factors(saved, swapped_saved):
@@ -136,12 +134,11 @@
     return pl.pallas_call(
         factor_kernel,
         out_shape=(
-            jax.ShapeDtypeStruct((4,) + shape, f32),
-            jax.ShapeDtypeStruct((2,) + shape, f32),
+            jax.ShapeDtypeStruct((6,) + shape, f32),
             jax.ShapeDtypeStruct((2,) + shape, bf16),
         ),
         in_specs=[whole] * 2,
-        out_specs=(whole,) * 3,
+        out_specs=(whole,) * 2,
         compiler_params=params,
         name="saved_factors",
     )(saved, swapped_saved)
@@ -167,7 +164,7 @@
             out[part, at, :] = value[chunk * slots : (chunk + 1) * slots]
 
 
-def raw_kernel(rows, mine, other, factors, grads, dots):
+def raw_kernel(rows, mine, other, factors, g_mine, g_other, dots):
     count = rows.shape[0]
     width = rows.shape[1] - extra
     slots = count // 16
@@ -175,7 +172,7 @@
     order = token_blocks(core, far)
     raw_other = product_with(rows[:, :width], other[...])
     raw = product_with(rows[:, :width], mine[...])
-    dot = jnp.sum(factors[0] * raw_other + factors[1] * raw, axis=1, keepdims=True)
+    dot = jnp.sum(factors[0] * raw_other + factors[3] * raw, axis=1, keepdims=True)
     lane = lax.broadcasted_iota(jnp.int32, (count, 128), 1)
     row = lax.broadcasted_iota(jnp.int32, (count, 128), 0)
     spread = jnp.where(lane == (row & 15), dot, 0.0)
@@ -184,62 +181,45 @@
         for target in range(2):
             dots[pl.ds(order[chunk] * 2 + target, 1), :] = line
     weights = slot_weights(rows[:, width:], raw.shape[1])
-    store_grads(grads, raw, weights, factors[2], factors[3], order)
+    store_grads(g_other, raw_other, weights, factors[1], factors[2], order)
+    store_grads(g_mine, raw, weights, factors[4], factors[5], order)
 
 
 def raw_grads(rows, mine, other, factors):
+    grads = jax.ShapeDtypeStruct((2,) + factors.shape[1:], bf16)
     return pl.pallas_call(
         raw_kernel,
-        out_shape=(
-            jax.ShapeDtypeStruct((2,) + factors.shape[1:], bf16),
-            jax.ShapeDtypeStruct((32, 128), f32),
-        ),
+        out_shape=(grads, grads, jax.ShapeDtypeStruct((32, 128), f32)),
         in_specs=[whole] * 4,
-        out_specs=(whole,) * 2,
+        out_specs=(whole,) * 3,
         compiler_params=params,
         name="raw_grads",
     )(rows, mine, other, factors)
 
 
 def finish_kernel(
-    rows, notes, rows_other, notes_other, mine, hidden, later, grads, *refs
+    rows, notes, rows_other, notes_other, hidden, g_mine, g_other, *refs
 ):
-    tables, (pair_grads, weight_grad), passed = refs[:3], refs[3:5], refs[5:8]
-    scaled, raw = refs[8:]
+    tables, (pair_grads, weight_grad), passed, scaled = refs[:3], refs[3:5], refs[5:8], refs[8]
     count, wide = hidden.shape[1:]
-    step = pl.program_id(0)
-    span, near, _ = position()
-
-    @pl.when(step == 0)
+
+    @pl.when(pl.program_id(0) == 0)
     def _():
-        pair_grads[span] = grads[...]
+        span = lax.axis_index("dp")
+        pair_grads[span] = g_mine[...]
+        pair_grads[1 - span] = g_other[...]
         for table, out in zip(tables, passed, strict=True):
             out[...] = table[...]
         for index, ref in enumerate((notes, notes_other)):
             value = slot_weights(ref[...], wide) * hidden[index].astype(f32)
             scaled[:, index * count : (index + 1) * count] = value.T.astype(bf16)
-        raw[...] = jnp.zeros_like(raw)
 
     total = jnp.dot(scaled[:, :count], rows[...], preferred_element_type=f32)
     total = total + jnp.dot(scaled[:, count:], rows_other[...], preferred_element_type=f32)
     weight_grad[...] = total.astype(bf16)
-    columns = rows.shape[1]
-    here = pl.ds(pl.multiple_of(step * columns, 128), columns)
-    raw[...] += product_with(rows_other[...], mine[:, here])
-
-    @pl.when(step == pl.num_programs(0) - 1)
-    def _():
-        store_grads(
-            pair_grads.at[1 - span],
-            raw[...],
-            slot_weights(notes_other[...], wide),
-            later[0],
-            later[1],
-            token_blocks(1 - span, near),
-        )
-
-
-def finished(rows, rows_other, mine, hidden, later, grads, tables):
+
+
+def finished(rows, rows_other, hidden, g_mine, g_other, tables):
     count, wide = hidden.shape[1:]
     width = rows.shape[1] - extra
     step = width // 2 if width % 256 == 0 else width
@@ -249,26 +229,26 @@
 
     block = pl.BlockSpec((count, step), lambda i: (0, i))
     note = pl.BlockSpec((count, extra), lambda i: (0, width // extra))
-    weight = pl.BlockSpec((wide, step), lambda i: (0, i))
     shapes = (
-        jax.ShapeDtypeStruct((2,) + grads.shape, bf16),
+        jax.ShapeDtypeStruct((2,) + g_mine.shape, bf16),
         jax.ShapeDtypeStruct((wide, width), bf16),
         *(jax.ShapeDtypeStruct(table.shape, table.dtype) for table in tables),
     )
-    inputs = (hidden, later, grads, *tables)
+    inputs = (hidden, g_mine, g_other, *tables)
     return pl.pallas_call(
         finish_kernel,
         grid=(width // step,),
         out_shape=shapes,
-        in_specs=[block, note, block, note, whole, *(kept(value) for value in inputs)],
-        out_specs=(kept(shapes[0]), weight, *(kept(value) for value in shapes[2:])),
-        scratch_shapes=[
-            pltpu.VMEM((wide, 2 * count), bf16),
-            pltpu.VMEM((count, wide), f32),
-        ],
+        in_specs=[block, note, block, note, *(kept(value) for value in inputs)],
+        out_specs=(
+            kept(shapes[0]),
+            pl.BlockSpec((wide, step), lambda i: (0, i)),
+            *(kept(value) for value in shapes[2:]),
+        ),
+        scratch_shapes=[pltpu.VMEM((wide, 2 * count), bf16)],
         compiler_params=params,
         name="finished",
-    )(rows, rows, rows_other, rows_other, mine, *inputs)
+    )(rows, rows, rows_other, rows_other, *inputs)
 
 
 def logit_kernel(returned, experts, places, scores, out):
@@ -374,10 +354,8 @@
     block, swapped_saved = lax.optimization_barrier((block, swapped(saved)))
 
     blocks = [block] + [plane_shift(block, step, True) for step in gather_steps]
-    factors, later, hidden = saved_factors(saved, swapped_saved)
-    blocks[1], factors, later, hidden = lax.optimization_barrier(
-        (blocks[1], factors, later, hidden)
-    )
+    factors, hidden = saved_factors(saved, swapped_saved)
+    blocks[1], factors, hidden = lax.optimization_barrier((blocks[1], factors, hidden))
     pieces = select_rows(blocks, slots)
     pieces = [pieces[0]] + [
         plane_shift(piece, step, False)
@@ -387,10 +365,11 @@
     rows = jnp.zeros((16 * slots, pieces[0].shape[1]), bf16)
     for index, piece in enumerate(pieces):
         rows = lax.dynamic_update_slice(rows, piece, (index * 4 * slots, 0))
-    grads, dots = raw_grads(rows, mine, other, factors)
+    g_mine, g_other, dots = raw_grads(rows, mine, other, factors)
+    rows, g_other = lax.optimization_barrier((rows, g_other))
     returned = lax.all_to_all(dots, ("expert", "dp"), split_axis=0, concat_axis=0, tiled=True)
     pair_grads, weight_grad, experts, places, scores = finished(
-        rows, swapped(rows), mine, hidden, later, grads, (experts, places, scores)
+        rows, swapped(rows), hidden, g_mine, swapped(g_other), (experts, places, scores)
     )
     returned, pair_grads, weight_grad = lax.optimization_barrier(
         (returned, pair_grads, weight_grad)

time: 54.2 us -> 54.5 us (level)
  waiting for transfers between devices: 17.3 us -> 19.5 us
  local copies, waits for them, and re-layouts: 4.15 us -> 2.66 us
  Pallas kernels: 8.49 us -> 7.82 us
    all_to_all x1, waiting for transfers between devices: 1.03 us -> 3.22 us  [local(): lax.all_to_all(dots, ('expert', 'dp'), split_axis=0, concat_axis=0, tiled...]
    unnamed x10 -> x8, local copies, waits for them, and re-layouts: 3.9 us -> 2.41 us
    pallas_call x1, Pallas kernels: 4.39 us -> 3.69 us  [finished(): pl.pallas_call(finish_kernel, grid=(width // step,), out_shape=shapes, in...]
    ppermute x3 -> x4, starting transfers between devices: 5 us -> 4.92 us  [swapped(): return lax.ppermute(value, 'dp', [(0, 1), (1, 0)])]
  transfers between devices with their start and end apart: 12 -> 13, of which waited for: 8 -> 8; matrix products, arithmetic and copies ran while one was open for 1% -> 1% of each run, Pallas kernels for 14% -> 9%
where the time goes in v9:
time: 54.5 us; the launch traced here: 53.9 us
  starting transfers between devices  22.9 us (42%)
  waiting for transfers between devices  19.5 us (36%)
  Pallas kernels  7.82 us (14%)
  local copies, waits for them, and re-layouts  2.66 us (5%)
  between operations  0.75 us (1%)
    ppermute x6, waiting for transfers between devices, plane_shift(): return lax.ppermute(value, ('expert', 'dp'), pairs)  15.3 us
    ppermute x6, starting transfers between devices, plane_shift(): return lax.ppermute(value, ('expert', 'dp'), pairs)  7.48 us
    all_to_all x1, starting transfers between devices, local(): lax.all_to_all(dots, ('expert', 'dp'), split_axis=0, concat_axis=0, tiled...  5.42 us
    ppermute x4, starting transfers between devices, swapped(): return lax.ppermute(value, 'dp', [(0, 1), (1, 0)])  4.92 us
    ppermute x1, starting transfers between devices, local(): lax.ppermute(sent_up[0], ('pipe', 'dp'), [(2 * z + 1, 2 * z + 3) for z in...  4.38 us
    pallas_call x1, Pallas kernels, finished(): pl.pallas_call(finish_kernel, grid=(width // step,), out_shape=shapes, in...  3.69 us
    all_to_all x1, waiting for transfers between devices, local(): lax.all_to_all(dots, ('expert', 'dp'), split_axis=0, concat_axis=0, tiled...  3.22 us
    unnamed x8, local copies, waits for them, and re-layouts  2.41 us
  transfers between devices with their start and end apart: 13, of which 8 were waited for; matrix products, arithmetic and copies ran while one was open for 1% of the time, Pallas kernels for 9%

profile of v9, /device:TPU:1, one launch (start us, length us, event | category | flops | bytes accessed | tf_op | source)
XLA Modules:
  0.0 53.9 jit_solution(6432080432394636099)
XLA Ops:
  0.6 0.7 %collective-permute-start = (bf16[32,3584]{1,0:T(8,128)(2,1)}, bf16[32,3584]{1,0:T(8,128)(2,1)S(1)}, u32[]{:S(2)}, u32[]{:S(2)}) collective-permute-start(bf16[32,3584]{1,0:T(8,128)(2,1)} %bitcast.37), channel_id=1, source_target_pairs={{32,0},{64,32},{96,64},{128,96},{160,128},{192,160},{224,192},{34,... | collective-permute-start | bytes 688136 | tf_op jit(solution)/shard_map/ppermute | solution.py:341
  1.3 4.4 %collective-permute-start.1 = (bf16[32,3584]{1,0:T(8,128)(2,1)}, bf16[32,3584]{1,0:T(8,128)(2,1)S(1)}, u32[]{:S(2)}, u32[]{:S(2)}) collective-permute-start(bf16[32,3584]{1,0:T(8,128)(2,1)} %bitcast.38), channel_id=1, source_target_pairs={{1,33},{33,65},{65,97},{97,129},{129,161},{161,193},{193,225},{3,3... | collective-permute-start | bytes 688136 | tf_op jit(solution)/shard_map/ppermute | solution.py:344
  5.7 0.2 collective-permute-start.2
  5.9 0.0 copy-start.2
  5.9 0.7 %copy-done.2 = s32[2,1,32,2]{2,3,1,0:T(2,128)S(1)} copy-done((s32[2,1,32,2]{2,3,1,0:T(2,128)S(1)}, s32[2,1,32,2]{2,3,1,0:T(2,128)}, u32[]{:S(2)}) %copy-start.2) | copy-done | bytes 536
  6.6 0.0 copy-start.3
  6.6 0.7 %copy-done.3 = f32[2,1,32,2]{2,3,1,0:T(2,128)S(1)} copy-done((f32[2,1,32,2]{2,3,1,0:T(2,128)S(1)}, f32[2,1,32,2]{2,3,1,0:T(2,128)}, u32[]{:S(2)}) %copy-start.3) | copy-done | bytes 536
  7.3 0.2 slot_notes.1
  7.5 0.4 collective-permute-start.7
  7.9 0.1 compare_reduce_fusion
  8.0 0.0 collective-permute-done
  8.0 1.0 %collective-permute-done.1 = bf16[32,3584]{1,0:T(8,128)(2,1)S(1)} collective-permute-done((bf16[32,3584]{1,0:T(8,128)(2,1)}, bf16[32,3584]{1,0:T(8,128)(2,1)S(1)}, u32[]{:S(2)}, u32[]{:S(2)}) %collective-permute-start.1) | collective-permute-done | bytes 229408 | tf_op jit(solution)/shard_map/ppermute | solution.py:344
  9.0 0.1 broadcast_select_fusion
  9.1 0.0 collective-permute-done.2.swapped_saved
  9.1 3.0 %collective-permute-start.3 = (bf16[32,3712]{1,0:T(8,128)(2,1)S(1)}, bf16[32,3712]{1,0:T(8,128)(2,1)S(1)}, u32[]{:S(2)}, u32[]{:S(2)}) collective-permute-start(bf16[32,3712]{1,0:T(8,128)(2,1)S(1)} %pad_maximum_fusion.refs_0_), channel_id=1, source_target_pairs={{0,4},{1,17},{2,6},{3,19},{4,0},{5,21},{6,2},{7,23},{8,12},{9,25},... | collective-permute-start | bytes 712712 | tf_op jit(solution)/shard_map/ppermute | solution.py:28
  12.1 0.8 %collective-permute-start.5 = (bf16[32,3712]{1,0:T(8,128)(2,1)S(1)}, bf16[32,3712]{1,0:T(8,128)(2,1)S(1)}, u32[]{:S(2)}, u32[]{:S(2)}) collective-permute-start(bf16[32,3712]{1,0:T(8,128)(2,1)S(1)} %pad_maximum_fusion.refs_0_), channel_id=1, source_target_pairs={{0,6},{1,25},{2,4},{3,27},{4,2},{5,29},{6,0},{7,31},{8,14},{9,17},... | collective-permute-start | bytes 712712 | tf_op jit(solution)/shard_map/ppermute | solution.py:28
  12.9 0.0 collective-permute-start.4
  12.9 0.0 copy-start.1
  12.9 1.0 %copy-done.1 = bf16[2,1,1,2,256,256]{5,4,3,2,1,0:T(8,128)(2,1)S(1)} copy-done((bf16[2,1,1,2,256,256]{5,4,3,2,1,0:T(8,128)(2,1)S(1)}, bf16[2,1,1,2,256,256]{5,4,3,2,1,0:T(8,128)(2,1)}, u32[]{:S(2)}) %copy-start.1) | copy-done | bytes 524312
  13.9 0.3 saved_factors.1
  14.2 1.4 %collective-permute-done.3.refs_1_ = bf16[32,3712]{1,0:T(8,128)(2,1)S(1)} collective-permute-done((bf16[32,3712]{1,0:T(8,128)(2,1)S(1)}, bf16[32,3712]{1,0:T(8,128)(2,1)S(1)}, u32[]{:S(2)}, u32[]{:S(2)}) %collective-permute-start.3) | collective-permute-done | bytes 237600 | tf_op jit(solution)/shard_map/ppermute | solution.py:28
  15.6 2.9 %collective-permute-done.5.refs_3_ = bf16[32,3712]{1,0:T(8,128)(2,1)S(1)} collective-permute-done((bf16[32,3712]{1,0:T(8,128)(2,1)S(1)}, bf16[32,3712]{1,0:T(8,128)(2,1)S(1)}, u32[]{:S(2)}, u32[]{:S(2)}) %collective-permute-start.5) | collective-permute-done | bytes 237600 | tf_op jit(solution)/shard_map/ppermute | solution.py:28
  18.6 0.3 collective-permute-done.4.refs_2_
  18.9 0.8 %select_rows.1 = (bf16[64,3712]{1,0:T(8,128)(2,1)S(1)}, bf16[64,3712]{1,0:T(8,128)(2,1)S(1)}, bf16[64,3712]{1,0:T(8,128)(2,1)S(1)}, bf16[64,3712]{1,0:T(8,128)(2,1)S(1)}) custom-call(bf16[32,3712]{1,0:T(8,128)(2,1)S(1)} %pad_maximum_fusion.refs_0_, bf16[32,3712]{1,0:T(8,128)(2,1)S(1)} %collective-permute-done.3.refs_1_, ...), custom_call_target="tpu_custom_call" | custom-call | tf_op jit(solution)/shard_map/select_rows/pallas_call | solution.py:99
  19.7 2.8 %collective-permute-start.6 = (bf16[64,3712]{1,0:T(8,128)(2,1)S(1)}, bf16[64,3712]{1,0:T(8,128)(2,1)S(1)}, u32[]{:S(2)}, u32[]{:S(2)}) collective-permute-start(bf16[64,3712]{1,0:T(8,128)(2,1)S(1)} %get-tuple-element.45), channel_id=1, source_target_pairs={{0,16},{1,5},{2,18},{3,7},{4,20},{5,1},{6,22},{7,3},{8,24},{9,13},... | collective-permute-start | bytes 1425416 | tf_op jit(solution)/shard_map/ppermute | solution.py:28
  22.5 0.9 %collective-permute-start.8 = (bf16[64,3712]{1,0:T(8,128)(2,1)S(1)}, bf16[64,3712]{1,0:T(8,128)(2,1)S(1)}, u32[]{:S(2)}, u32[]{:S(2)}) collective-permute-start(bf16[64,3712]{1,0:T(8,128)(2,1)S(1)} %get-tuple-element.48), channel_id=1, source_target_pairs={{0,24},{1,7},{2,26},{3,5},{4,28},{5,3},{6,30},{7,1},{8,16},{9,15},... | collective-permute-start | bytes 1425416 | tf_op jit(solution)/shard_map/ppermute | solution.py:28
  23.4 0.0 collective-permute-start.9
  23.4 0.1 dynamic_update_slice.12
  23.5 0.0 copy-start
  23.5 5.6 %collective-permute-done.6 = bf16[64,3712]{1,0:T(8,128)(2,1)S(1)} collective-permute-done((bf16[64,3712]{1,0:T(8,128)(2,1)S(1)}, bf16[64,3712]{1,0:T(8,128)(2,1)S(1)}, u32[]{:S(2)}, u32[]{:S(2)}) %collective-permute-start.6) | collective-permute-done | bytes 475168 | tf_op jit(solution)/shard_map/ppermute | solution.py:28
  29.1 0.0 collective-permute-done.7.other
  29.2 5.0 %collective-permute-done.8 = bf16[64,3712]{1,0:T(8,128)(2,1)S(1)} collective-permute-done((bf16[64,3712]{1,0:T(8,128)(2,1)S(1)}, bf16[64,3712]{1,0:T(8,128)(2,1)S(1)}, u32[]{:S(2)}, u32[]{:S(2)}) %collective-permute-start.8) | collective-permute-done | bytes 475168 | tf_op jit(solution)/shard_map/ppermute | solution.py:28
  34.2 0.1 collective-permute-done.9
  34.4 0.0 copy-done
  34.4 1.9 %raw_grads.1 = (bf16[2,256,256]{2,1,0:T(8,128)(2,1)S(1)}, bf16[2,256,256]{2,1,0:T(8,128)(2,1)S(1)}, f32[32,128]{1,0:T(8,128)}) custom-call(bf16[256,3712]{1,0:T(8,128)(2,1)S(1)} %constant_dynamic-update-slice_fusion.rows.notes, bf16[256,3584]{1,0:T(8,128)(2,1)S(1)} %bitcast.28, bf16[256,3584]{1,0:T(8,128)(2,1)S(1)} %collective-permute-done.7.other, ...), custom_call_target="tpu_custom_call" | custom-call | tf_op jit(solution)/shard_map/raw_grads/pallas_call | solution.py:190
  36.2 4.3 %collective-permute-start.10 = (bf16[256,3712]{1,0:T(8,128)(2,1)S(1)}, bf16[256,3712]{1,0:T(8,128)(2,1)}, u32[]{:S(2)}, u32[]{:S(2)}) collective-permute-start(bf16[256,3712]{1,0:T(8,128)(2,1)S(1)} %constant_dynamic-update-slice_fusion.rows.notes), channel_id=1, source_target_pairs={{0,1},{1,0},{2,3},{3,2},{4,5},{5,4},{6,7},{7,6},{8,9},{9,8},{10,11... | collective-permute-start | bytes 5701640 | tf_op jit(solution)/shard_map/ppermute | solution.py:32
  40.5 0.0 collective-permute-start.11
  40.5 5.4 %all-to-all-start = ((f32[32,1,128]{2,1,0:T(1,128)}), f32[32,1,128]{2,1,0:T(1,128)S(1)}, u32[]{:S(2)}, u32[]{:S(2)}) async-start(f32[32,1,128]{2,1,0:T(1,128)} %bitcast.11), calls=%async_computation | async-start | bytes 32768 | tf_op jit(solution)/shard_map/all_to_all | solution.py:370
  46.0 0.0 collective-permute-done.11.g_other
  46.0 0.0 collective-permute-done.10.rows_other.notes_other
  46.0 3.7 %finished.1 = (bf16[2,2,256,256]{3,2,1,0:T(8,128)(2,1)}, bf16[256,3584]{1,0:T(8,128)(2,1)}, bf16[96,128]{1,0:T(8,128)(2,1)S(1)}, f32[16,128]{1,0:T(8,128)S(1)}, f32[4,32]{1,0:T(4,128)S(1)}) custom-call(bf16[256,3712]{1,0:T(8,128)(2,1)S(1)} %constant_dynamic-update-slice_fusion.rows.notes, bf16[256,3712]{1,0:T(8,128)(2,1)S(1)} %constant_dynamic-update-slice_fusion.rows.notes, ...), custom_call_target="tpu_custom_call" | custom-call | tf_op jit(solution)/shard_map/finished/pallas_call | solution.py:238
  49.7 3.2 %all-to-all-done = f32[32,1,128]{2,1,0:T(1,128)S(1)} async-done(((f32[32,1,128]{2,1,0:T(1,128)}), f32[32,1,128]{2,1,0:T(1,128)S(1)}, u32[]{:S(2)}, u32[]{:S(2)}) %all-to-all-start) | async-done | bytes 16416 | tf_op jit(solution)/shard_map/all_to_all | solution.py:370
  52.9 1.0 %logit_grads.1 = f32[4,32]{1,0:T(4,128)} custom-call(f32[32,128]{1,0:T(8,128)S(1)} %bitcast.31, bf16[96,128]{1,0:T(8,128)(2,1)S(1)} %get-tuple-element.66.experts, f32[16,128]{1,0:T(8,128)S(1)} %get-tuple-element.67.places, f32[4,32]{1,0:T(4,128)S(1)} %get-tuple-element.68.scores), custom_call_target="tpu_custom_call" | custom-call | tf_op jit(solution)/shard_map/logit_grads/pallas_call | solution.py:377
  (4 shorter events, 0.1 us)
Async XLA Ops:
  0.6 7.4 %collective-permute-start = (bf16[32,3584]{1,0:T(8,128)(2,1)}, bf16[32,3584]{1,0:T(8,128)(2,1)S(1)}, u32[]{:S(2)}, u32[]{:S(2)}) collective-permute-start(bf16[32,3584]{1,0:T(8,128)(2,1)} %bitcast.37), channel_id=1, source_target_pairs={{32,0},{64,32},{96,64},{128,96},{160,128},{192,160},{224,192},{34,... | collective-permute-start | bytes 688136 | tf_op jit(solution)/shard_map/ppermute | solution.py:341
  1.3 7.6 %collective-permute-start.1 = (bf16[32,3584]{1,0:T(8,128)(2,1)}, bf16[32,3584]{1,0:T(8,128)(2,1)S(1)}, u32[]{:S(2)}, u32[]{:S(2)}) collective-permute-start(bf16[32,3584]{1,0:T(8,128)(2,1)} %bitcast.38), channel_id=1, source_target_pairs={{1,33},{33,65},{65,97},{97,129},{129,161},{161,193},{193,225},{3,3... | collective-permute-start | bytes 688136 | tf_op jit(solution)/shard_map/ppermute | solution.py:344
  5.7 3.4 %collective-permute-start.2 = (bf16[2,2,256,256]{3,2,1,0:T(8,128)(2,1)}, bf16[2,2,256,256]{3,2,1,0:T(8,128)(2,1)S(1)}, u32[]{:S(2)}, u32[]{:S(2)}) collective-permute-start(bf16[2,2,256,256]{3,2,1,0:T(8,128)(2,1)} %bitcast.29), channel_id=1, source_target_pairs={{0,1},{1,0},{2,3},{3,2},{4,5},{5,4},{6,7},{7,6},{8,9},{9,8},{10,11... | collective-permute-start | bytes 1572872 | tf_op jit(solution)/shard_map/ppermute | solution.py:32
  5.9 0.7 %copy-start.2 = (s32[2,1,32,2]{2,3,1,0:T(2,128)S(1)}, s32[2,1,32,2]{2,3,1,0:T(2,128)}, u32[]{:S(2)}) copy-start(s32[2,1,32,2]{2,3,1,0:T(2,128)} %param.8) | copy-start | bytes 1540
  6.6 0.7 %copy-start.3 = (f32[2,1,32,2]{2,3,1,0:T(2,128)S(1)}, f32[2,1,32,2]{2,3,1,0:T(2,128)}, u32[]{:S(2)}) copy-start(f32[2,1,32,2]{2,3,1,0:T(2,128)} %param.9) | copy-start | bytes 1540
  7.5 21.6 %collective-permute-start.7 = (bf16[256,3584]{1,0:T(8,128)(2,1)}, bf16[256,3584]{1,0:T(8,128)(2,1)S(1)}, u32[]{:S(2)}, u32[]{:S(2)}) collective-permute-start(bf16[256,3584]{1,0:T(8,128)(2,1)} %bitcast.27), channel_id=1, source_target_pairs={{0,1},{1,0},{2,3},{3,2},{4,5},{5,4},{6,7},{7,6},{8,9},{9,8},{10,11... | collective-permute-start | bytes 5505032 | tf_op jit(solution)/shard_map/ppermute | solution.py:32
  9.1 6.6 %collective-permute-start.3 = (bf16[32,3712]{1,0:T(8,128)(2,1)S(1)}, bf16[32,3712]{1,0:T(8,128)(2,1)S(1)}, u32[]{:S(2)}, u32[]{:S(2)}) collective-permute-start(bf16[32,3712]{1,0:T(8,128)(2,1)S(1)} %pad_maximum_fusion.refs_0_), channel_id=1, source_target_pairs={{0,4},{1,17},{2,6},{3,19},{4,0},{5,21},{6,2},{7,23},{8,12},{9,25},... | collective-permute-start | bytes 712712 | tf_op jit(solution)/shard_map/ppermute | solution.py:28
  12.1 6.5 %collective-permute-start.5 = (bf16[32,3712]{1,0:T(8,128)(2,1)S(1)}, bf16[32,3712]{1,0:T(8,128)(2,1)S(1)}, u32[]{:S(2)}, u32[]{:S(2)}) collective-permute-start(bf16[32,3712]{1,0:T(8,128)(2,1)S(1)} %pad_maximum_fusion.refs_0_), channel_id=1, source_target_pairs={{0,6},{1,25},{2,4},{3,27},{4,2},{5,29},{6,0},{7,31},{8,14},{9,17},... | collective-permute-start | bytes 712712 | tf_op jit(solution)/shard_map/ppermute | solution.py:28
  12.9 6.0 %collective-permute-start.4 = (bf16[32,3712]{1,0:T(8,128)(2,1)S(1)}, bf16[32,3712]{1,0:T(8,128)(2,1)S(1)}, u32[]{:S(2)}, u32[]{:S(2)}) collective-permute-start(bf16[32,3712]{1,0:T(8,128)(2,1)S(1)} %pad_maximum_fusion.refs_0_), channel_id=1, source_target_pairs={{0,2},{1,9},{2,0},{3,11},{4,6},{5,13},{6,4},{7,15},{8,10},{9,1},{1... | collective-permute-start | bytes 712712 | tf_op jit(solution)/shard_map/ppermute | solution.py:28
  12.9 1.0 %copy-start.1 = (bf16[2,1,1,2,256,256]{5,4,3,2,1,0:T(8,128)(2,1)S(1)}, bf16[2,1,1,2,256,256]{5,4,3,2,1,0:T(8,128)(2,1)}, u32[]{:S(2)}) copy-start(bf16[2,1,1,2,256,256]{5,4,3,2,1,0:T(8,128)(2,1)} %param.10) | copy-start | bytes 1572868
  19.7 9.4 %collective-permute-start.6 = (bf16[64,3712]{1,0:T(8,128)(2,1)S(1)}, bf16[64,3712]{1,0:T(8,128)(2,1)S(1)}, u32[]{:S(2)}, u32[]{:S(2)}) collective-permute-start(bf16[64,3712]{1,0:T(8,128)(2,1)S(1)} %get-tuple-element.45), channel_id=1, source_target_pairs={{0,16},{1,5},{2,18},{3,7},{4,20},{5,1},{6,22},{7,3},{8,24},{9,13},... | collective-permute-start | bytes 1425416 | tf_op jit(solution)/shard_map/ppermute | solution.py:28
  22.5 11.6 %collective-permute-start.8 = (bf16[64,3712]{1,0:T(8,128)(2,1)S(1)}, bf16[64,3712]{1,0:T(8,128)(2,1)S(1)}, u32[]{:S(2)}, u32[]{:S(2)}) collective-permute-start(bf16[64,3712]{1,0:T(8,128)(2,1)S(1)} %get-tuple-element.48), channel_id=1, source_target_pairs={{0,24},{1,7},{2,26},{3,5},{4,28},{5,3},{6,30},{7,1},{8,16},{9,15},... | collective-permute-start | bytes 1425416 | tf_op jit(solution)/shard_map/ppermute | solution.py:28
  23.4 10.9 %collective-permute-start.9 = (bf16[64,3712]{1,0:T(8,128)(2,1)S(1)}, bf16[64,3712]{1,0:T(8,128)(2,1)S(1)}, u32[]{:S(2)}, u32[]{:S(2)}) collective-permute-start(bf16[64,3712]{1,0:T(8,128)(2,1)S(1)} %get-tuple-element.49), channel_id=1, source_target_pairs={{0,8},{1,3},{2,10},{3,1},{4,12},{5,7},{6,14},{7,5},{8,0},{9,11},{1... | collective-permute-start | bytes 1425416 | tf_op jit(solution)/shard_map/ppermute | solution.py:28
  23.5 10.8 %copy-start = (bf16[1,1,256,3584]{3,2,1,0:T(8,128)(2,1)S(1)}, bf16[1,1,256,3584]{3,2,1,0:T(8,128)(2,1)}, u32[]{:S(2)}) copy-start(bf16[1,1,256,3584]{3,2,1,0:T(8,128)(2,1)} %param.11) | copy-start | bytes 5505028
  36.2 9.7 %collective-permute-start.10 = (bf16[256,3712]{1,0:T(8,128)(2,1)S(1)}, bf16[256,3712]{1,0:T(8,128)(2,1)}, u32[]{:S(2)}, u32[]{:S(2)}) collective-permute-start(bf16[256,3712]{1,0:T(8,128)(2,1)S(1)} %constant_dynamic-update-slice_fusion.rows.notes), channel_id=1, source_target_pairs={{0,1},{1,0},{2,3},{3,2},{4,5},{5,4},{6,7},{7,6},{8,9},{9,8},{10,11... | collective-permute-start | bytes 5701640 | tf_op jit(solution)/shard_map/ppermute | solution.py:32
  40.5 5.4 %collective-permute-start.11 = (bf16[2,256,256]{2,1,0:T(8,128)(2,1)S(1)}, bf16[2,256,256]{2,1,0:T(8,128)(2,1)S(1)}, u32[]{:S(2)}, u32[]{:S(2)}) collective-permute-start(bf16[2,256,256]{2,1,0:T(8,128)(2,1)S(1)} %get-tuple-element.57), channel_id=1, source_target_pairs={{0,1},{1,0},{2,3},{3,2},{4,5},{5,4},{6,7},{7,6},{8,9},{9,8},{10,11... | collective-permute-start | bytes 786440 | tf_op jit(solution)/shard_map/ppermute | solution.py:32
  40.5 12.4 %all-to-all-start = ((f32[32,1,128]{2,1,0:T(1,128)}), f32[32,1,128]{2,1,0:T(1,128)S(1)}, u32[]{:S(2)}, u32[]{:S(2)}) async-start(f32[32,1,128]{2,1,0:T(1,128)} %bitcast.11), calls=%async_computation | async-start | bytes 32768 | tf_op jit(solution)/shard_map/all_to_all | solution.py:370

commit v10 on v8

--- a/solution.py
+++ b/solution.py
@@ -167,7 +167,7 @@
             out[part, at, :] = value[chunk * slots : (chunk + 1) * slots]
 
 
-def raw_kernel(rows, mine, other, factors, grads, dots):
+def raw_kernel(rows, mine, other, factors, grads, dots, table, left):
     count = rows.shape[0]
     width = rows.shape[1] - extra
     slots = count // 16
@@ -182,9 +182,12 @@
     for chunk in range(16):
         line = jnp.sum(spread[chunk * slots : (chunk + 1) * slots], axis=0, keepdims=True)
         for target in range(2):
-            dots[pl.ds(order[chunk] * 2 + target, 1), :] = line
+            table[pl.ds(order[chunk] * 2 + target, 1), :] = line
+    leaving = pltpu.make_async_copy(table, dots, left)
+    leaving.start()
     weights = slot_weights(rows[:, width:], raw.shape[1])
     store_grads(grads, raw, weights, factors[2], factors[3], order)
+    leaving.wait()
 
 
 def raw_grads(rows, mine, other, factors):
@@ -195,7 +198,8 @@
             jax.ShapeDtypeStruct((32, 128), f32),
         ),
         in_specs=[whole] * 4,
-        out_specs=(whole,) * 2,
+        out_specs=(whole, pl.BlockSpec(memory_space=pl.ANY)),
+        scratch_shapes=[pltpu.VMEM((32, 128), f32), pltpu.SemaphoreType.DMA],
         compiler_params=params,
         name="raw_grads",
     )(rows, mine, other, factors)

time: 54.2 us -> 54.2 us (level)
  no operation moved by 1% of the time
where the time goes in v10:
time: 54.2 us; the launch traced here: 53.5 us
  starting transfers between devices  22.6 us (42%)
  waiting for transfers between devices  17.3 us (32%)
  Pallas kernels  8.49 us (16%)
  local copies, waits for them, and re-layouts  4.15 us (8%)
  between operations  0.75 us (1%)
    ppermute x6, waiting for transfers between devices, plane_shift(): return lax.ppermute(value, ('expert', 'dp'), pairs)  15.3 us
    ppermute x6, starting transfers between devices, plane_shift(): return lax.ppermute(value, ('expert', 'dp'), pairs)  7.48 us
    all_to_all x1, starting transfers between devices, local(): lax.all_to_all(dots, ('expert', 'dp'), split_axis=0, concat_axis=0, tiled...  5.03 us
    ppermute x3, starting transfers between devices, swapped(): return lax.ppermute(value, 'dp', [(0, 1), (1, 0)])  5 us
    pallas_call x1, Pallas kernels, finished(): pl.pallas_call(finish_kernel, grid=(width // step,), out_shape=shapes, in...  4.39 us
    ppermute x1, starting transfers between devices, local(): lax.ppermute(sent_up[0], ('pipe', 'dp'), [(2 * z + 1, 2 * z + 3) for z in...  4.38 us
    unnamed x10, local copies, waits for them, and re-layouts  3.9 us
    pallas_call x1, Pallas kernels, raw_grads(): pl.pallas_call(raw_kernel, out_shape=(jax.ShapeDtypeStruct((2,) + factors...  1.84 us
  transfers between devices with their start and end apart: 12, of which 8 were waited for; matrix products, arithmetic and copies ran while one was open for 1% of the time, Pallas kernels for 14%

profile of v10, /device:TPU:1, one launch (start us, length us, event | category | flops | bytes accessed | tf_op | source)
XLA Modules:
  0.0 53.5 jit_solution(14103642847925813197)
XLA Ops:
  0.6 0.7 %collective-permute-start = (bf16[32,3584]{1,0:T(8,128)(2,1)}, bf16[32,3584]{1,0:T(8,128)(2,1)S(1)}, u32[]{:S(2)}, u32[]{:S(2)}) collective-permute-start(bf16[32,3584]{1,0:T(8,128)(2,1)} %bitcast.38), channel_id=1, source_target_pairs={{32,0},{64,32},{96,64},{128,96},{160,128},{192,160},{224,192},{34,... | collective-permute-start | bytes 688136 | tf_op jit(solution)/shard_map/ppermute | solution.py:365
  1.3 4.4 %collective-permute-start.1 = (bf16[32,3584]{1,0:T(8,128)(2,1)}, bf16[32,3584]{1,0:T(8,128)(2,1)S(1)}, u32[]{:S(2)}, u32[]{:S(2)}) collective-permute-start(bf16[32,3584]{1,0:T(8,128)(2,1)} %bitcast.39), channel_id=1, source_target_pairs={{1,33},{33,65},{65,97},{97,129},{129,161},{161,193},{193,225},{3,3... | collective-permute-start | bytes 688136 | tf_op jit(solution)/shard_map/ppermute | solution.py:368
  5.7 0.2 collective-permute-start.2
  5.9 0.0 copy-start.3
  5.9 0.7 %copy-done.3 = s32[2,1,32,2]{2,3,1,0:T(2,128)S(1)} copy-done((s32[2,1,32,2]{2,3,1,0:T(2,128)S(1)}, s32[2,1,32,2]{2,3,1,0:T(2,128)}, u32[]{:S(2)}) %copy-start.3) | copy-done | bytes 536
  6.6 0.0 copy-start.4
  6.6 0.7 %copy-done.4 = f32[2,1,32,2]{2,3,1,0:T(2,128)S(1)} copy-done((f32[2,1,32,2]{2,3,1,0:T(2,128)S(1)}, f32[2,1,32,2]{2,3,1,0:T(2,128)}, u32[]{:S(2)}) %copy-start.4) | copy-done | bytes 536
  7.3 0.2 slot_notes.1
  7.5 0.4 collective-permute-start.7
  7.9 0.1 compare_reduce_fusion
  8.0 0.0 collective-permute-done
  8.0 1.0 %collective-permute-done.1 = bf16[32,3584]{1,0:T(8,128)(2,1)S(1)} collective-permute-done((bf16[32,3584]{1,0:T(8,128)(2,1)}, bf16[32,3584]{1,0:T(8,128)(2,1)S(1)}, u32[]{:S(2)}, u32[]{:S(2)}) %collective-permute-start.1) | collective-permute-done | bytes 229408 | tf_op jit(solution)/shard_map/ppermute | solution.py:368
  9.0 0.1 broadcast_select_fusion
  9.1 0.0 collective-permute-done.2.swapped_saved
  9.1 3.0 %collective-permute-start.3 = (bf16[32,3712]{1,0:T(8,128)(2,1)S(1)}, bf16[32,3712]{1,0:T(8,128)(2,1)S(1)}, u32[]{:S(2)}, u32[]{:S(2)}) collective-permute-start(bf16[32,3712]{1,0:T(8,128)(2,1)S(1)} %pad_maximum_fusion.refs_0_), channel_id=1, source_target_pairs={{0,4},{1,17},{2,6},{3,19},{4,0},{5,21},{6,2},{7,23},{8,12},{9,25},... | collective-permute-start | bytes 712712 | tf_op jit(solution)/shard_map/ppermute | solution.py:28
  12.1 0.8 %collective-permute-start.5 = (bf16[32,3712]{1,0:T(8,128)(2,1)S(1)}, bf16[32,3712]{1,0:T(8,128)(2,1)S(1)}, u32[]{:S(2)}, u32[]{:S(2)}) collective-permute-start(bf16[32,3712]{1,0:T(8,128)(2,1)S(1)} %pad_maximum_fusion.refs_0_), channel_id=1, source_target_pairs={{0,6},{1,25},{2,4},{3,27},{4,2},{5,29},{6,0},{7,31},{8,14},{9,17},... | collective-permute-start | bytes 712712 | tf_op jit(solution)/shard_map/ppermute | solution.py:28
  12.9 0.0 collective-permute-start.4
  12.9 0.0 copy-start.2
  12.9 1.0 %copy-done.2 = bf16[2,1,1,2,256,256]{5,4,3,2,1,0:T(8,128)(2,1)S(1)} copy-done((bf16[2,1,1,2,256,256]{5,4,3,2,1,0:T(8,128)(2,1)S(1)}, bf16[2,1,1,2,256,256]{5,4,3,2,1,0:T(8,128)(2,1)}, u32[]{:S(2)}) %copy-start.2) | copy-done | bytes 524312
  13.9 0.3 saved_factors.1
  14.2 1.4 %collective-permute-done.3.refs_1_ = bf16[32,3712]{1,0:T(8,128)(2,1)S(1)} collective-permute-done((bf16[32,3712]{1,0:T(8,128)(2,1)S(1)}, bf16[32,3712]{1,0:T(8,128)(2,1)S(1)}, u32[]{:S(2)}, u32[]{:S(2)}) %collective-permute-start.3) | collective-permute-done | bytes 237600 | tf_op jit(solution)/shard_map/ppermute | solution.py:28
  15.6 2.9 %collective-permute-done.5.refs_3_ = bf16[32,3712]{1,0:T(8,128)(2,1)S(1)} collective-permute-done((bf16[32,3712]{1,0:T(8,128)(2,1)S(1)}, bf16[32,3712]{1,0:T(8,128)(2,1)S(1)}, u32[]{:S(2)}, u32[]{:S(2)}) %collective-permute-start.5) | collective-permute-done | bytes 237600 | tf_op jit(solution)/shard_map/ppermute | solution.py:28
  18.6 0.3 collective-permute-done.4.refs_2_
  18.9 0.8 %select_rows.1 = (bf16[64,3712]{1,0:T(8,128)(2,1)S(1)}, bf16[64,3712]{1,0:T(8,128)(2,1)S(1)}, bf16[64,3712]{1,0:T(8,128)(2,1)S(1)}, bf16[64,3712]{1,0:T(8,128)(2,1)S(1)}) custom-call(bf16[32,3712]{1,0:T(8,128)(2,1)S(1)} %pad_maximum_fusion.refs_0_, bf16[32,3712]{1,0:T(8,128)(2,1)S(1)} %collective-permute-done.3.refs_1_, ...), custom_call_target="tpu_custom_call" | custom-call | tf_op jit(solution)/shard_map/select_rows/pallas_call | solution.py:99
  19.7 2.8 %collective-permute-start.6 = (bf16[64,3712]{1,0:T(8,128)(2,1)S(1)}, bf16[64,3712]{1,0:T(8,128)(2,1)S(1)}, u32[]{:S(2)}, u32[]{:S(2)}) collective-permute-start(bf16[64,3712]{1,0:T(8,128)(2,1)S(1)} %get-tuple-element.45), channel_id=1, source_target_pairs={{0,16},{1,5},{2,18},{3,7},{4,20},{5,1},{6,22},{7,3},{8,24},{9,13},... | collective-permute-start | bytes 1425416 | tf_op jit(solution)/shard_map/ppermute | solution.py:28
  22.5 0.9 %collective-permute-start.8 = (bf16[64,3712]{1,0:T(8,128)(2,1)S(1)}, bf16[64,3712]{1,0:T(8,128)(2,1)S(1)}, u32[]{:S(2)}, u32[]{:S(2)}) collective-permute-start(bf16[64,3712]{1,0:T(8,128)(2,1)S(1)} %get-tuple-element.48), channel_id=1, source_target_pairs={{0,24},{1,7},{2,26},{3,5},{4,28},{5,3},{6,30},{7,1},{8,16},{9,15},... | collective-permute-start | bytes 1425416 | tf_op jit(solution)/shard_map/ppermute | solution.py:28
  23.4 0.0 collective-permute-start.9
  23.4 0.1 dynamic_update_slice.12
  23.5 0.0 copy-start
  23.6 5.6 %collective-permute-done.6 = bf16[64,3712]{1,0:T(8,128)(2,1)S(1)} collective-permute-done((bf16[64,3712]{1,0:T(8,128)(2,1)S(1)}, bf16[64,3712]{1,0:T(8,128)(2,1)S(1)}, u32[]{:S(2)}, u32[]{:S(2)}) %collective-permute-start.6) | collective-permute-done | bytes 475168 | tf_op jit(solution)/shard_map/ppermute | solution.py:28
  29.1 0.0 collective-permute-done.7.other
  29.2 5.0 %collective-permute-done.8 = bf16[64,3712]{1,0:T(8,128)(2,1)S(1)} collective-permute-done((bf16[64,3712]{1,0:T(8,128)(2,1)S(1)}, bf16[64,3712]{1,0:T(8,128)(2,1)S(1)}, u32[]{:S(2)}, u32[]{:S(2)}) %collective-permute-start.8) | collective-permute-done | bytes 475168 | tf_op jit(solution)/shard_map/ppermute | solution.py:28
  34.2 0.1 collective-permute-done.9
  34.4 4.4 %collective-permute-start.10 = (bf16[256,3712]{1,0:T(8,128)(2,1)S(1)}, bf16[256,3712]{1,0:T(8,128)(2,1)}, u32[]{:S(2)}, u32[]{:S(2)}) collective-permute-start(bf16[256,3712]{1,0:T(8,128)(2,1)S(1)} %constant_dynamic-update-slice_fusion.rows.notes), channel_id=1, source_target_pairs={{0,1},{1,0},{2,3},{3,2},{4,5},{5,4},{6,7},{7,6},{8,9},{9,8},{10,11... | collective-permute-start | bytes 5701640 | tf_op jit(solution)/shard_map/ppermute | solution.py:32
  38.7 0.0 copy-done
  38.7 1.8 %raw_grads.1 = (bf16[2,256,256]{2,1,0:T(8,128)(2,1)S(1)}, f32[32,128]{1,0:T(8,128)}) custom-call(bf16[256,3712]{1,0:T(8,128)(2,1)S(1)} %constant_dynamic-update-slice_fusion.rows.notes, bf16[256,3584]{1,0:T(8,128)(2,1)S(1)} %bitcast.28, bf16[256,3584]{1,0:T(8,128)(2,1)S(1)} %collective-permute-done.7.other, f32[4,256,256]{2,1,0:T(8,128)S(1)} %get-tuple-element.51.factors), custom_call_target="tpu_custom_call" | custom-call | tf_op jit(solution)/shard_map/raw_grads/pallas_call | solution.py:194
  40.6 5.0 %all-to-all-start = ((f32[32,1,128]{2,1,0:T(1,128)}), f32[32,1,128]{2,1,0:T(1,128)S(1)}, u32[]{:S(2)}, u32[]{:S(2)}) async-start(f32[32,1,128]{2,1,0:T(1,128)} %bitcast.11), calls=%async_computation | async-start | bytes 32768 | tf_op jit(solution)/shard_map/all_to_all | solution.py:395
  45.6 0.0 collective-permute-done.10.rows_other.notes_other
  45.6 0.0 copy-start.1
  45.7 1.5 %copy-done.1 = bf16[1,1,256,3584]{3,2,1,0:T(8,128)(2,1)S(1)} copy-done((bf16[1,1,256,3584]{3,2,1,0:T(8,128)(2,1)S(1)}, bf16[1,1,256,3584]{3,2,1,0:T(8,128)(2,1)}, u32[]{:S(2)}) %copy-start.1) | copy-done | bytes 1835032
  47.1 4.4 %finished.1 = (bf16[2,2,256,256]{3,2,1,0:T(8,128)(2,1)}, bf16[256,3584]{1,0:T(8,128)(2,1)}, bf16[96,128]{1,0:T(8,128)(2,1)S(1)}, f32[16,128]{1,0:T(8,128)S(1)}, f32[4,32]{1,0:T(4,128)S(1)}) custom-call(bf16[256,3712]{1,0:T(8,128)(2,1)S(1)} %constant_dynamic-update-slice_fusion.rows.notes, bf16[256,3712]{1,0:T(8,128)(2,1)S(1)} %constant_dynamic-update-slice_fusion.rows.notes, ...), custom_call_target="tpu_custom_call" | custom-call | tf_op jit(solution)/shard_map/finished/pallas_call | solution.py:263
  51.5 1.0 %all-to-all-done = f32[32,1,128]{2,1,0:T(1,128)S(1)} async-done(((f32[32,1,128]{2,1,0:T(1,128)}), f32[32,1,128]{2,1,0:T(1,128)S(1)}, u32[]{:S(2)}, u32[]{:S(2)}) %all-to-all-start) | async-done | bytes 16416 | tf_op jit(solution)/shard_map/all_to_all | solution.py:395
  52.6 1.0 %logit_grads.1 = f32[4,32]{1,0:T(4,128)} custom-call(f32[32,128]{1,0:T(8,128)S(1)} %bitcast.32, bf16[96,128]{1,0:T(8,128)(2,1)S(1)} %get-tuple-element.64.experts, f32[16,128]{1,0:T(8,128)S(1)} %get-tuple-element.65.places, f32[4,32]{1,0:T(4,128)S(1)} %get-tuple-element.66.scores), custom_call_target="tpu_custom_call" | custom-call | tf_op jit(solution)/shard_map/logit_grads/pallas_call | solution.py:402
  (4 shorter events, 0.1 us)
Async XLA Ops:
  0.6 7.4 %collective-permute-start = (bf16[32,3584]{1,0:T(8,128)(2,1)}, bf16[32,3584]{1,0:T(8,128)(2,1)S(1)}, u32[]{:S(2)}, u32[]{:S(2)}) collective-permute-start(bf16[32,3584]{1,0:T(8,128)(2,1)} %bitcast.38), channel_id=1, source_target_pairs={{32,0},{64,32},{96,64},{128,96},{160,128},{192,160},{224,192},{34,... | collective-permute-start | bytes 688136 | tf_op jit(solution)/shard_map/ppermute | solution.py:365
  1.3 7.6 %collective-permute-start.1 = (bf16[32,3584]{1,0:T(8,128)(2,1)}, bf16[32,3584]{1,0:T(8,128)(2,1)S(1)}, u32[]{:S(2)}, u32[]{:S(2)}) collective-permute-start(bf16[32,3584]{1,0:T(8,128)(2,1)} %bitcast.39), channel_id=1, source_target_pairs={{1,33},{33,65},{65,97},{97,129},{129,161},{161,193},{193,225},{3,3... | collective-permute-start | bytes 688136 | tf_op jit(solution)/shard_map/ppermute | solution.py:368
  5.7 3.4 %collective-permute-start.2 = (bf16[2,2,256,256]{3,2,1,0:T(8,128)(2,1)}, bf16[2,2,256,256]{3,2,1,0:T(8,128)(2,1)S(1)}, u32[]{:S(2)}, u32[]{:S(2)}) collective-permute-start(bf16[2,2,256,256]{3,2,1,0:T(8,128)(2,1)} %bitcast.30), channel_id=1, source_target_pairs={{0,1},{1,0},{2,3},{3,2},{4,5},{5,4},{6,7},{7,6},{8,9},{9,8},{10,11... | collective-permute-start | bytes 1572872 | tf_op jit(solution)/shard_map/ppermute | solution.py:32
  5.9 0.7 %copy-start.3 = (s32[2,1,32,2]{2,3,1,0:T(2,128)S(1)}, s32[2,1,32,2]{2,3,1,0:T(2,128)}, u32[]{:S(2)}) copy-start(s32[2,1,32,2]{2,3,1,0:T(2,128)} %param.8) | copy-start | bytes 1540
  6.6 0.7 %copy-start.4 = (f32[2,1,32,2]{2,3,1,0:T(2,128)S(1)}, f32[2,1,32,2]{2,3,1,0:T(2,128)}, u32[]{:S(2)}) copy-start(f32[2,1,32,2]{2,3,1,0:T(2,128)} %param.9) | copy-start | bytes 1540
  7.5 21.6 %collective-permute-start.7 = (bf16[256,3584]{1,0:T(8,128)(2,1)}, bf16[256,3584]{1,0:T(8,128)(2,1)S(1)}, u32[]{:S(2)}, u32[]{:S(2)}) collective-permute-start(bf16[256,3584]{1,0:T(8,128)(2,1)} %bitcast.27), channel_id=1, source_target_pairs={{0,1},{1,0},{2,3},{3,2},{4,5},{5,4},{6,7},{7,6},{8,9},{9,8},{10,11... | collective-permute-start | bytes 5505032 | tf_op jit(solution)/shard_map/ppermute | solution.py:32
  9.1 6.6 %collective-permute-start.3 = (bf16[32,3712]{1,0:T(8,128)(2,1)S(1)}, bf16[32,3712]{1,0:T(8,128)(2,1)S(1)}, u32[]{:S(2)}, u32[]{:S(2)}) collective-permute-start(bf16[32,3712]{1,0:T(8,128)(2,1)S(1)} %pad_maximum_fusion.refs_0_), channel_id=1, source_target_pairs={{0,4},{1,17},{2,6},{3,19},{4,0},{5,21},{6,2},{7,23},{8,12},{9,25},... | collective-permute-start | bytes 712712 | tf_op jit(solution)/shard_map/ppermute | solution.py:28
  12.1 6.5 %collective-permute-start.5 = (bf16[32,3712]{1,0:T(8,128)(2,1)S(1)}, bf16[32,3712]{1,0:T(8,128)(2,1)S(1)}, u32[]{:S(2)}, u32[]{:S(2)}) collective-permute-start(bf16[32,3712]{1,0:T(8,128)(2,1)S(1)} %pad_maximum_fusion.refs_0_), channel_id=1, source_target_pairs={{0,6},{1,25},{2,4},{3,27},{4,2},{5,29},{6,0},{7,31},{8,14},{9,17},... | collective-permute-start | bytes 712712 | tf_op jit(solution)/shard_map/ppermute | solution.py:28
  12.9 6.0 %collective-permute-start.4 = (bf16[32,3712]{1,0:T(8,128)(2,1)S(1)}, bf16[32,3712]{1,0:T(8,128)(2,1)S(1)}, u32[]{:S(2)}, u32[]{:S(2)}) collective-permute-start(bf16[32,3712]{1,0:T(8,128)(2,1)S(1)} %pad_maximum_fusion.refs_0_), channel_id=1, source_target_pairs={{0,2},{1,9},{2,0},{3,11},{4,6},{5,13},{6,4},{7,15},{8,10},{9,1},{1... | collective-permute-start | bytes 712712 | tf_op jit(solution)/shard_map/ppermute | solution.py:28
  12.9 1.0 %copy-start.2 = (bf16[2,1,1,2,256,256]{5,4,3,2,1,0:T(8,128)(2,1)S(1)}, bf16[2,1,1,2,256,256]{5,4,3,2,1,0:T(8,128)(2,1)}, u32[]{:S(2)}) copy-start(bf16[2,1,1,2,256,256]{5,4,3,2,1,0:T(8,128)(2,1)} %param.10) | copy-start | bytes 1572868
  19.7 9.4 %collective-permute-start.6 = (bf16[64,3712]{1,0:T(8,128)(2,1)S(1)}, bf16[64,3712]{1,0:T(8,128)(2,1)S(1)}, u32[]{:S(2)}, u32[]{:S(2)}) collective-permute-start(bf16[64,3712]{1,0:T(8,128)(2,1)S(1)} %get-tuple-element.45), channel_id=1, source_target_pairs={{0,16},{1,5},{2,18},{3,7},{4,20},{5,1},{6,22},{7,3},{8,24},{9,13},... | collective-permute-start | bytes 1425416 | tf_op jit(solution)/shard_map/ppermute | solution.py:28
  22.5 11.6 %collective-permute-start.8 = (bf16[64,3712]{1,0:T(8,128)(2,1)S(1)}, bf16[64,3712]{1,0:T(8,128)(2,1)S(1)}, u32[]{:S(2)}, u32[]{:S(2)}) collective-permute-start(bf16[64,3712]{1,0:T(8,128)(2,1)S(1)} %get-tuple-element.48), channel_id=1, source_target_pairs={{0,24},{1,7},{2,26},{3,5},{4,28},{5,3},{6,30},{7,1},{8,16},{9,15},... | collective-permute-start | bytes 1425416 | tf_op jit(solution)/shard_map/ppermute | solution.py:28
  23.4 10.9 %collective-permute-start.9 = (bf16[64,3712]{1,0:T(8,128)(2,1)S(1)}, bf16[64,3712]{1,0:T(8,128)(2,1)S(1)}, u32[]{:S(2)}, u32[]{:S(2)}) collective-permute-start(bf16[64,3712]{1,0:T(8,128)(2,1)S(1)} %get-tuple-element.49), channel_id=1, source_target_pairs={{0,8},{1,3},{2,10},{3,1},{4,12},{5,7},{6,14},{7,5},{8,0},{9,11},{1... | collective-permute-start | bytes 1425416 | tf_op jit(solution)/shard_map/ppermute | solution.py:28
  23.5 15.2 %copy-start = (bf16[1,1,256,3584]{3,2,1,0:T(8,128)(2,1)S(1)}, bf16[1,1,256,3584]{3,2,1,0:T(8,128)(2,1)}, u32[]{:S(2)}) copy-start(bf16[1,1,256,3584]{3,2,1,0:T(8,128)(2,1)} %param.11) | copy-start | bytes 5505028
  34.4 11.3 %collective-permute-start.10 = (bf16[256,3712]{1,0:T(8,128)(2,1)S(1)}, bf16[256,3712]{1,0:T(8,128)(2,1)}, u32[]{:S(2)}, u32[]{:S(2)}) collective-permute-start(bf16[256,3712]{1,0:T(8,128)(2,1)S(1)} %constant_dynamic-update-slice_fusion.rows.notes), channel_id=1, source_target_pairs={{0,1},{1,0},{2,3},{3,2},{4,5},{5,4},{6,7},{7,6},{8,9},{9,8},{10,11... | collective-permute-start | bytes 5701640 | tf_op jit(solution)/shard_map/ppermute | solution.py:32
  40.6 12.0 %all-to-all-start = ((f32[32,1,128]{2,1,0:T(1,128)}), f32[32,1,128]{2,1,0:T(1,128)S(1)}, u32[]{:S(2)}, u32[]{:S(2)}) async-start(f32[32,1,128]{2,1,0:T(1,128)} %bitcast.11), calls=%async_computation | async-start | bytes 32768 | tf_op jit(solution)/shard_map/all_to_all | solution.py:395
  45.6 1.5 %copy-start.1 = (bf16[1,1,256,3584]{3,2,1,0:T(8,128)(2,1)S(1)}, bf16[1,1,256,3584]{3,2,1,0:T(8,128)(2,1)}, u32[]{:S(2)}) copy-start(bf16[1,1,256,3584]{3,2,1,0:T(8,128)(2,1)} %param.11) | copy-start | bytes 5505028

commit v11 on v8

--- a/solution.py
+++ b/solution.py
@@ -388,6 +388,7 @@
     for index, piece in enumerate(pieces):
         rows = lax.dynamic_update_slice(rows, piece, (index * 4 * slots, 0))
     grads, dots = raw_grads(rows, mine, other, factors)
+    rows, grads = lax.optimization_barrier((rows, grads))
     returned = lax.all_to_all(dots, ("expert", "dp"), split_axis=0, concat_axis=0, tiled=True)
     pair_grads, weight_grad, experts, places, scores = finished(
         rows, swapped(rows), mine, hidden, later, grads, (experts, places, scores)

time: 54.2 us -> 54.1 us (level)
  transfers between devices with their start and end apart: 12 -> 12, of which waited for: 8 -> 8; matrix products, arithmetic and copies ran while one was open for 1% -> 1% of each run, Pallas kernels for 14% -> 11%
where the time goes in v11:
time: 54.1 us; the launch traced here: 53.4 us
  starting transfers between devices  22.5 us (42%)
  waiting for transfers between devices  17.3 us (32%)
  Pallas kernels  8.49 us (16%)
  local copies, waits for them, and re-layouts  4.15 us (8%)
  between operations  0.75 us (1%)
    ppermute x6, waiting for transfers between devices, plane_shift(): return lax.ppermute(value, ('expert', 'dp'), pairs)  15.3 us
    ppermute x6, starting transfers between devices, plane_shift(): return lax.ppermute(value, ('expert', 'dp'), pairs)  7.48 us
    all_to_all x1, starting transfers between devices, local(): lax.all_to_all(dots, ('expert', 'dp'), split_axis=0, concat_axis=0, tiled...  5.02 us
    ppermute x3, starting transfers between devices, swapped(): return lax.ppermute(value, 'dp', [(0, 1), (1, 0)])  4.92 us
    pallas_call x1, Pallas kernels, finished(): pl.pallas_call(finish_kernel, grid=(width // step,), out_shape=shapes, in...  4.39 us
    ppermute x1, starting transfers between devices, local(): lax.ppermute(sent_up[0], ('pipe', 'dp'), [(2 * z + 1, 2 * z + 3) for z in...  4.38 us
    unnamed x10, local copies, waits for them, and re-layouts  3.9 us
    pallas_call x1, Pallas kernels, raw_grads(): pl.pallas_call(raw_kernel, out_shape=(jax.ShapeDtypeStruct((2,) + factors...  1.83 us
  transfers between devices with their start and end apart: 12, of which 8 were waited for; matrix products, arithmetic and copies ran while one was open for 1% of the time, Pallas kernels for 11%

profile of v11, /device:TPU:1, one launch (start us, length us, event | category | flops | bytes accessed | tf_op | source)
XLA Modules:
  0.0 53.4 jit_solution(6458033467259056422)
XLA Ops:
  0.6 0.7 %collective-permute-start = (bf16[32,3584]{1,0:T(8,128)(2,1)}, bf16[32,3584]{1,0:T(8,128)(2,1)S(1)}, u32[]{:S(2)}, u32[]{:S(2)}) collective-permute-start(bf16[32,3584]{1,0:T(8,128)(2,1)} %bitcast.38), channel_id=1, source_target_pairs={{32,0},{64,32},{96,64},{128,96},{160,128},{192,160},{224,192},{34,... | collective-permute-start | bytes 688136 | tf_op jit(solution)/shard_map/ppermute | solution.py:361
  1.3 4.4 %collective-permute-start.1 = (bf16[32,3584]{1,0:T(8,128)(2,1)}, bf16[32,3584]{1,0:T(8,128)(2,1)S(1)}, u32[]{:S(2)}, u32[]{:S(2)}) collective-permute-start(bf16[32,3584]{1,0:T(8,128)(2,1)} %bitcast.39), channel_id=1, source_target_pairs={{1,33},{33,65},{65,97},{97,129},{129,161},{161,193},{193,225},{3,3... | collective-permute-start | bytes 688136 | tf_op jit(solution)/shard_map/ppermute | solution.py:364
  5.7 0.2 collective-permute-start.2
  5.9 0.0 copy-start.3
  5.9 0.7 %copy-done.3 = s32[2,1,32,2]{2,3,1,0:T(2,128)S(1)} copy-done((s32[2,1,32,2]{2,3,1,0:T(2,128)S(1)}, s32[2,1,32,2]{2,3,1,0:T(2,128)}, u32[]{:S(2)}) %copy-start.3) | copy-done | bytes 536
  6.6 0.0 copy-start.4
  6.6 0.7 %copy-done.4 = f32[2,1,32,2]{2,3,1,0:T(2,128)S(1)} copy-done((f32[2,1,32,2]{2,3,1,0:T(2,128)S(1)}, f32[2,1,32,2]{2,3,1,0:T(2,128)}, u32[]{:S(2)}) %copy-start.4) | copy-done | bytes 536
  7.3 0.2 slot_notes.1
  7.5 0.4 collective-permute-start.7
  7.9 0.1 compare_reduce_fusion
  8.0 0.0 collective-permute-done
  8.0 1.0 %collective-permute-done.1 = bf16[32,3584]{1,0:T(8,128)(2,1)S(1)} collective-permute-done((bf16[32,3584]{1,0:T(8,128)(2,1)}, bf16[32,3584]{1,0:T(8,128)(2,1)S(1)}, u32[]{:S(2)}, u32[]{:S(2)}) %collective-permute-start.1) | collective-permute-done | bytes 229408 | tf_op jit(solution)/shard_map/ppermute | solution.py:364
  9.0 0.1 broadcast_select_fusion
  9.1 0.0 collective-permute-done.2.swapped_saved
  9.1 3.0 %collective-permute-start.3 = (bf16[32,3712]{1,0:T(8,128)(2,1)S(1)}, bf16[32,3712]{1,0:T(8,128)(2,1)S(1)}, u32[]{:S(2)}, u32[]{:S(2)}) collective-permute-start(bf16[32,3712]{1,0:T(8,128)(2,1)S(1)} %pad_maximum_fusion.refs_0_), channel_id=1, source_target_pairs={{0,4},{1,17},{2,6},{3,19},{4,0},{5,21},{6,2},{7,23},{8,12},{9,25},... | collective-permute-start | bytes 712712 | tf_op jit(solution)/shard_map/ppermute | solution.py:28
  12.1 0.8 %collective-permute-start.5 = (bf16[32,3712]{1,0:T(8,128)(2,1)S(1)}, bf16[32,3712]{1,0:T(8,128)(2,1)S(1)}, u32[]{:S(2)}, u32[]{:S(2)}) collective-permute-start(bf16[32,3712]{1,0:T(8,128)(2,1)S(1)} %pad_maximum_fusion.refs_0_), channel_id=1, source_target_pairs={{0,6},{1,25},{2,4},{3,27},{4,2},{5,29},{6,0},{7,31},{8,14},{9,17},... | collective-permute-start | bytes 712712 | tf_op jit(solution)/shard_map/ppermute | solution.py:28
  12.9 0.0 collective-permute-start.4
  12.9 0.0 copy-start.2
  12.9 1.0 %copy-done.2 = bf16[2,1,1,2,256,256]{5,4,3,2,1,0:T(8,128)(2,1)S(1)} copy-done((bf16[2,1,1,2,256,256]{5,4,3,2,1,0:T(8,128)(2,1)S(1)}, bf16[2,1,1,2,256,256]{5,4,3,2,1,0:T(8,128)(2,1)}, u32[]{:S(2)}) %copy-start.2) | copy-done | bytes 524312
  13.9 0.3 saved_factors.1
  14.2 1.4 %collective-permute-done.3.refs_1_ = bf16[32,3712]{1,0:T(8,128)(2,1)S(1)} collective-permute-done((bf16[32,3712]{1,0:T(8,128)(2,1)S(1)}, bf16[32,3712]{1,0:T(8,128)(2,1)S(1)}, u32[]{:S(2)}, u32[]{:S(2)}) %collective-permute-start.3) | collective-permute-done | bytes 237600 | tf_op jit(solution)/shard_map/ppermute | solution.py:28
  15.6 2.9 %collective-permute-done.5.refs_3_ = bf16[32,3712]{1,0:T(8,128)(2,1)S(1)} collective-permute-done((bf16[32,3712]{1,0:T(8,128)(2,1)S(1)}, bf16[32,3712]{1,0:T(8,128)(2,1)S(1)}, u32[]{:S(2)}, u32[]{:S(2)}) %collective-permute-start.5) | collective-permute-done | bytes 237600 | tf_op jit(solution)/shard_map/ppermute | solution.py:28
  18.6 0.3 collective-permute-done.4.refs_2_
  18.9 0.8 %select_rows.1 = (bf16[64,3712]{1,0:T(8,128)(2,1)S(1)}, bf16[64,3712]{1,0:T(8,128)(2,1)S(1)}, bf16[64,3712]{1,0:T(8,128)(2,1)S(1)}, bf16[64,3712]{1,0:T(8,128)(2,1)S(1)}) custom-call(bf16[32,3712]{1,0:T(8,128)(2,1)S(1)} %pad_maximum_fusion.refs_0_, bf16[32,3712]{1,0:T(8,128)(2,1)S(1)} %collective-permute-done.3.refs_1_, ...), custom_call_target="tpu_custom_call" | custom-call | tf_op jit(solution)/shard_map/select_rows/pallas_call | solution.py:99
  19.7 2.8 %collective-permute-start.6 = (bf16[64,3712]{1,0:T(8,128)(2,1)S(1)}, bf16[64,3712]{1,0:T(8,128)(2,1)S(1)}, u32[]{:S(2)}, u32[]{:S(2)}) collective-permute-start(bf16[64,3712]{1,0:T(8,128)(2,1)S(1)} %get-tuple-element.47), channel_id=1, source_target_pairs={{0,16},{1,5},{2,18},{3,7},{4,20},{5,1},{6,22},{7,3},{8,24},{9,13},... | collective-permute-start | bytes 1425416 | tf_op jit(solution)/shard_map/ppermute | solution.py:28
  22.5 0.9 %collective-permute-start.8 = (bf16[64,3712]{1,0:T(8,128)(2,1)S(1)}, bf16[64,3712]{1,0:T(8,128)(2,1)S(1)}, u32[]{:S(2)}, u32[]{:S(2)}) collective-permute-start(bf16[64,3712]{1,0:T(8,128)(2,1)S(1)} %get-tuple-element.50), channel_id=1, source_target_pairs={{0,24},{1,7},{2,26},{3,5},{4,28},{5,3},{6,30},{7,1},{8,16},{9,15},... | collective-permute-start | bytes 1425416 | tf_op jit(solution)/shard_map/ppermute | solution.py:28
  23.4 0.0 collective-permute-start.9
  23.4 0.1 dynamic_update_slice.12
  23.5 0.0 copy-start
  23.6 5.6 %collective-permute-done.6 = bf16[64,3712]{1,0:T(8,128)(2,1)S(1)} collective-permute-done((bf16[64,3712]{1,0:T(8,128)(2,1)S(1)}, bf16[64,3712]{1,0:T(8,128)(2,1)S(1)}, u32[]{:S(2)}, u32[]{:S(2)}) %collective-permute-start.6) | collective-permute-done | bytes 475168 | tf_op jit(solution)/shard_map/ppermute | solution.py:28
  29.1 0.0 collective-permute-done.7.other
  29.2 5.0 %collective-permute-done.8 = bf16[64,3712]{1,0:T(8,128)(2,1)S(1)} collective-permute-done((bf16[64,3712]{1,0:T(8,128)(2,1)S(1)}, bf16[64,3712]{1,0:T(8,128)(2,1)S(1)}, u32[]{:S(2)}, u32[]{:S(2)}) %collective-permute-start.8) | collective-permute-done | bytes 475168 | tf_op jit(solution)/shard_map/ppermute | solution.py:28
  34.2 0.1 collective-permute-done.9
  34.4 0.0 copy-done
  34.4 1.8 %raw_grads.1 = (bf16[2,256,256]{2,1,0:T(8,128)(2,1)S(1)}, f32[32,128]{1,0:T(8,128)}) custom-call(bf16[256,3712]{1,0:T(8,128)(2,1)S(1)} %constant_dynamic-update-slice_fusion.rows.notes, bf16[256,3584]{1,0:T(8,128)(2,1)S(1)} %bitcast.28, bf16[256,3584]{1,0:T(8,128)(2,1)S(1)} %collective-permute-done.7.other, f32[4,256,256]{2,1,0:T(8,128)S(1)} %get-tuple-element.53.factors), custom_call_target="tpu_custom_call" | custom-call | tf_op jit(solution)/shard_map/raw_grads/pallas_call | solution.py:191
  36.2 4.3 %collective-permute-start.10 = (bf16[256,3712]{1,0:T(8,128)(2,1)S(1)}, bf16[256,3712]{1,0:T(8,128)(2,1)}, u32[]{:S(2)}, u32[]{:S(2)}) collective-permute-start(bf16[256,3712]{1,0:T(8,128)(2,1)S(1)} %constant_dynamic-update-slice_fusion.rows.notes), channel_id=1, source_target_pairs={{0,1},{1,0},{2,3},{3,2},{4,5},{5,4},{6,7},{7,6},{8,9},{9,8},{10,11... | collective-permute-start | bytes 5701640 | tf_op jit(solution)/shard_map/ppermute | solution.py:32
  40.5 5.0 %all-to-all-start = ((f32[32,1,128]{2,1,0:T(1,128)}), f32[32,1,128]{2,1,0:T(1,128)S(1)}, u32[]{:S(2)}, u32[]{:S(2)}) async-start(f32[32,1,128]{2,1,0:T(1,128)} %bitcast.11), calls=%async_computation | async-start | bytes 32768 | tf_op jit(solution)/shard_map/all_to_all | solution.py:392
  45.5 0.0 collective-permute-done.10.rows_other.notes_other
  45.5 0.0 copy-start.1
  45.6 1.5 %copy-done.1 = bf16[1,1,256,3584]{3,2,1,0:T(8,128)(2,1)S(1)} copy-done((bf16[1,1,256,3584]{3,2,1,0:T(8,128)(2,1)S(1)}, bf16[1,1,256,3584]{3,2,1,0:T(8,128)(2,1)}, u32[]{:S(2)}) %copy-start.1) | copy-done | bytes 1835032
  47.0 4.4 %finished.1 = (bf16[2,2,256,256]{3,2,1,0:T(8,128)(2,1)}, bf16[256,3584]{1,0:T(8,128)(2,1)}, bf16[96,128]{1,0:T(8,128)(2,1)S(1)}, f32[16,128]{1,0:T(8,128)S(1)}, f32[4,32]{1,0:T(4,128)S(1)}) custom-call(bf16[256,3712]{1,0:T(8,128)(2,1)S(1)} %constant_dynamic-update-slice_fusion.rows.notes, bf16[256,3712]{1,0:T(8,128)(2,1)S(1)} %constant_dynamic-update-slice_fusion.rows.notes, ...), custom_call_target="tpu_custom_call" | custom-call | tf_op jit(solution)/shard_map/finished/pallas_call | solution.py:259
  51.4 1.0 %all-to-all-done = f32[32,1,128]{2,1,0:T(1,128)S(1)} async-done(((f32[32,1,128]{2,1,0:T(1,128)}), f32[32,1,128]{2,1,0:T(1,128)S(1)}, u32[]{:S(2)}, u32[]{:S(2)}) %all-to-all-start) | async-done | bytes 16416 | tf_op jit(solution)/shard_map/all_to_all | solution.py:392
  52.5 1.0 %logit_grads.1 = f32[4,32]{1,0:T(4,128)} custom-call(f32[32,128]{1,0:T(8,128)S(1)} %bitcast.32, bf16[96,128]{1,0:T(8,128)(2,1)S(1)} %get-tuple-element.68.experts, f32[16,128]{1,0:T(8,128)S(1)} %get-tuple-element.69.places, f32[4,32]{1,0:T(4,128)S(1)} %get-tuple-element.70.scores), custom_call_target="tpu_custom_call" | custom-call | tf_op jit(solution)/shard_map/logit_grads/pallas_call | solution.py:399
  (4 shorter events, 0.1 us)
Async XLA Ops:
  0.6 7.4 %collective-permute-start = (bf16[32,3584]{1,0:T(8,128)(2,1)}, bf16[32,3584]{1,0:T(8,128)(2,1)S(1)}, u32[]{:S(2)}, u32[]{:S(2)}) collective-permute-start(bf16[32,3584]{1,0:T(8,128)(2,1)} %bitcast.38), channel_id=1, source_target_pairs={{32,0},{64,32},{96,64},{128,96},{160,128},{192,160},{224,192},{34,... | collective-permute-start | bytes 688136 | tf_op jit(solution)/shard_map/ppermute | solution.py:361
  1.3 7.6 %collective-permute-start.1 = (bf16[32,3584]{1,0:T(8,128)(2,1)}, bf16[32,3584]{1,0:T(8,128)(2,1)S(1)}, u32[]{:S(2)}, u32[]{:S(2)}) collective-permute-start(bf16[32,3584]{1,0:T(8,128)(2,1)} %bitcast.39), channel_id=1, source_target_pairs={{1,33},{33,65},{65,97},{97,129},{129,161},{161,193},{193,225},{3,3... | collective-permute-start | bytes 688136 | tf_op jit(solution)/shard_map/ppermute | solution.py:364
  5.7 3.4 %collective-permute-start.2 = (bf16[2,2,256,256]{3,2,1,0:T(8,128)(2,1)}, bf16[2,2,256,256]{3,2,1,0:T(8,128)(2,1)S(1)}, u32[]{:S(2)}, u32[]{:S(2)}) collective-permute-start(bf16[2,2,256,256]{3,2,1,0:T(8,128)(2,1)} %bitcast.30), channel_id=1, source_target_pairs={{0,1},{1,0},{2,3},{3,2},{4,5},{5,4},{6,7},{7,6},{8,9},{9,8},{10,11... | collective-permute-start | bytes 1572872 | tf_op jit(solution)/shard_map/ppermute | solution.py:32
  5.9 0.7 %copy-start.3 = (s32[2,1,32,2]{2,3,1,0:T(2,128)S(1)}, s32[2,1,32,2]{2,3,1,0:T(2,128)}, u32[]{:S(2)}) copy-start(s32[2,1,32,2]{2,3,1,0:T(2,128)} %param.8) | copy-start | bytes 1540
  6.6 0.7 %copy-start.4 = (f32[2,1,32,2]{2,3,1,0:T(2,128)S(1)}, f32[2,1,32,2]{2,3,1,0:T(2,128)}, u32[]{:S(2)}) copy-start(f32[2,1,32,2]{2,3,1,0:T(2,128)} %param.9) | copy-start | bytes 1540
  7.5 21.6 %collective-permute-start.7 = (bf16[256,3584]{1,0:T(8,128)(2,1)}, bf16[256,3584]{1,0:T(8,128)(2,1)S(1)}, u32[]{:S(2)}, u32[]{:S(2)}) collective-permute-start(bf16[256,3584]{1,0:T(8,128)(2,1)} %bitcast.27), channel_id=1, source_target_pairs={{0,1},{1,0},{2,3},{3,2},{4,5},{5,4},{6,7},{7,6},{8,9},{9,8},{10,11... | collective-permute-start | bytes 5505032 | tf_op jit(solution)/shard_map/ppermute | solution.py:32
  9.1 6.6 %collective-permute-start.3 = (bf16[32,3712]{1,0:T(8,128)(2,1)S(1)}, bf16[32,3712]{1,0:T(8,128)(2,1)S(1)}, u32[]{:S(2)}, u32[]{:S(2)}) collective-permute-start(bf16[32,3712]{1,0:T(8,128)(2,1)S(1)} %pad_maximum_fusion.refs_0_), channel_id=1, source_target_pairs={{0,4},{1,17},{2,6},{3,19},{4,0},{5,21},{6,2},{7,23},{8,12},{9,25},... | collective-permute-start | bytes 712712 | tf_op jit(solution)/shard_map/ppermute | solution.py:28
  12.1 6.5 %collective-permute-start.5 = (bf16[32,3712]{1,0:T(8,128)(2,1)S(1)}, bf16[32,3712]{1,0:T(8,128)(2,1)S(1)}, u32[]{:S(2)}, u32[]{:S(2)}) collective-permute-start(bf16[32,3712]{1,0:T(8,128)(2,1)S(1)} %pad_maximum_fusion.refs_0_), channel_id=1, source_target_pairs={{0,6},{1,25},{2,4},{3,27},{4,2},{5,29},{6,0},{7,31},{8,14},{9,17},... | collective-permute-start | bytes 712712 | tf_op jit(solution)/shard_map/ppermute | solution.py:28
  12.9 6.0 %collective-permute-start.4 = (bf16[32,3712]{1,0:T(8,128)(2,1)S(1)}, bf16[32,3712]{1,0:T(8,128)(2,1)S(1)}, u32[]{:S(2)}, u32[]{:S(2)}) collective-permute-start(bf16[32,3712]{1,0:T(8,128)(2,1)S(1)} %pad_maximum_fusion.refs_0_), channel_id=1, source_target_pairs={{0,2},{1,9},{2,0},{3,11},{4,6},{5,13},{6,4},{7,15},{8,10},{9,1},{1... | collective-permute-start | bytes 712712 | tf_op jit(solution)/shard_map/ppermute | solution.py:28
  12.9 1.0 %copy-start.2 = (bf16[2,1,1,2,256,256]{5,4,3,2,1,0:T(8,128)(2,1)S(1)}, bf16[2,1,1,2,256,256]{5,4,3,2,1,0:T(8,128)(2,1)}, u32[]{:S(2)}) copy-start(bf16[2,1,1,2,256,256]{5,4,3,2,1,0:T(8,128)(2,1)} %param.10) | copy-start | bytes 1572868
  19.7 9.4 %collective-permute-start.6 = (bf16[64,3712]{1,0:T(8,128)(2,1)S(1)}, bf16[64,3712]{1,0:T(8,128)(2,1)S(1)}, u32[]{:S(2)}, u32[]{:S(2)}) collective-permute-start(bf16[64,3712]{1,0:T(8,128)(2,1)S(1)} %get-tuple-element.47), channel_id=1, source_target_pairs={{0,16},{1,5},{2,18},{3,7},{4,20},{5,1},{6,22},{7,3},{8,24},{9,13},... | collective-permute-start | bytes 1425416 | tf_op jit(solution)/shard_map/ppermute | solution.py:28
  22.5 11.6 %collective-permute-start.8 = (bf16[64,3712]{1,0:T(8,128)(2,1)S(1)}, bf16[64,3712]{1,0:T(8,128)(2,1)S(1)}, u32[]{:S(2)}, u32[]{:S(2)}) collective-permute-start(bf16[64,3712]{1,0:T(8,128)(2,1)S(1)} %get-tuple-element.50), channel_id=1, source_target_pairs={{0,24},{1,7},{2,26},{3,5},{4,28},{5,3},{6,30},{7,1},{8,16},{9,15},... | collective-permute-start | bytes 1425416 | tf_op jit(solution)/shard_map/ppermute | solution.py:28
  23.4 10.9 %collective-permute-start.9 = (bf16[64,3712]{1,0:T(8,128)(2,1)S(1)}, bf16[64,3712]{1,0:T(8,128)(2,1)S(1)}, u32[]{:S(2)}, u32[]{:S(2)}) collective-permute-start(bf16[64,3712]{1,0:T(8,128)(2,1)S(1)} %get-tuple-element.51), channel_id=1, source_target_pairs={{0,8},{1,3},{2,10},{3,1},{4,12},{5,7},{6,14},{7,5},{8,0},{9,11},{1... | collective-permute-start | bytes 1425416 | tf_op jit(solution)/shard_map/ppermute | solution.py:28
  23.5 10.8 %copy-start = (bf16[1,1,256,3584]{3,2,1,0:T(8,128)(2,1)S(1)}, bf16[1,1,256,3584]{3,2,1,0:T(8,128)(2,1)}, u32[]{:S(2)}) copy-start(bf16[1,1,256,3584]{3,2,1,0:T(8,128)(2,1)} %param.11) | copy-start | bytes 5505028
  36.2 9.3 %collective-permute-start.10 = (bf16[256,3712]{1,0:T(8,128)(2,1)S(1)}, bf16[256,3712]{1,0:T(8,128)(2,1)}, u32[]{:S(2)}, u32[]{:S(2)}) collective-permute-start(bf16[256,3712]{1,0:T(8,128)(2,1)S(1)} %constant_dynamic-update-slice_fusion.rows.notes), channel_id=1, source_target_pairs={{0,1},{1,0},{2,3},{3,2},{4,5},{5,4},{6,7},{7,6},{8,9},{9,8},{10,11... | collective-permute-start | bytes 5701640 | tf_op jit(solution)/shard_map/ppermute | solution.py:32
  40.5 12.0 %all-to-all-start = ((f32[32,1,128]{2,1,0:T(1,128)}), f32[32,1,128]{2,1,0:T(1,128)S(1)}, u32[]{:S(2)}, u32[]{:S(2)}) async-start(f32[32,1,128]{2,1,0:T(1,128)} %bitcast.11), calls=%async_computation | async-start | bytes 32768 | tf_op jit(solution)/shard_map/all_to_all | solution.py:392
  45.5 1.5 %copy-start.1 = (bf16[1,1,256,3584]{3,2,1,0:T(8,128)(2,1)S(1)}, bf16[1,1,256,3584]{3,2,1,0:T(8,128)(2,1)}, u32[]{:S(2)}) copy-start(bf16[1,1,256,3584]{3,2,1,0:T(8,128)(2,1)} %param.11) | copy-start | bytes 5505028

commit v12 on v8

--- a/solution.py
+++ b/solution.py
@@ -7,7 +7,7 @@
 
 route_scale = 2.5
 side = 4
-gather_steps, exchange_steps = (2, 1, 3), (2, 3, 1)
+gather_steps, exchange_steps = (3, 1, 2), (3, 2, 1)
 extra = 128
 bf16, f32 = jnp.bfloat16, jnp.float32
 params = pltpu.CompilerParams(vmem_limit_bytes=16 * 2**20)

time: 54.2 us -> 55.7 us (1.028)
  waiting for transfers between devices: 17.3 us -> 18.3 us
  starting transfers between devices: 22.6 us -> 23.2 us
    ppermute x6, waiting for transfers between devices: 15.3 us -> 16.3 us  [plane_shift(): return lax.ppermute(value, ('expert', 'dp'), pairs)]
    ppermute x3, starting transfers between devices: 5 us -> 5.82 us  [swapped(): return lax.ppermute(value, 'dp', [(0, 1), (1, 0)])]
    ppermute x6, starting transfers between devices: 7.48 us -> 6.84 us  [plane_shift(): return lax.ppermute(value, ('expert', 'dp'), pairs)]
  transfers between devices with their start and end apart: 12 -> 12, of which waited for: 8 -> 7; matrix products, arithmetic and copies ran while one was open for 1% -> 1% of each run, Pallas kernels for 14% -> 14%
where the time goes in v12:
time: 55.7 us; the launch traced here: 55.1 us
  starting transfers between devices  23.2 us (42%)
  waiting for transfers between devices  18.3 us (33%)
  Pallas kernels  8.48 us (15%)
  local copies, waits for them, and re-layouts  4.15 us (7%)
  between operations  0.75 us (1%)
    ppermute x6, waiting for transfers between devices, plane_shift(): return lax.ppermute(value, ('expert', 'dp'), pairs)  16.3 us
    ppermute x6, starting transfers between devices, plane_shift(): return lax.ppermute(value, ('expert', 'dp'), pairs)  6.84 us
    ppermute x3, starting transfers between devices, swapped(): return lax.ppermute(value, 'dp', [(0, 1), (1, 0)])  5.82 us
    all_to_all x1, starting transfers between devices, local(): lax.all_to_all(dots, ('expert', 'dp'), split_axis=0, concat_axis=0, tiled...  5.46 us
    pallas_call x1, Pallas kernels, finished(): pl.pallas_call(finish_kernel, grid=(width // step,), out_shape=shapes, in...  4.39 us
    ppermute x1, starting transfers between devices, local(): lax.ppermute(sent_up[0], ('pipe', 'dp'), [(2 * z + 1, 2 * z + 3) for z in...  4.38 us
    unnamed x10, local copies, waits for them, and re-layouts  3.9 us
    pallas_call x1, Pallas kernels, raw_grads(): pl.pallas_call(raw_kernel, out_shape=(jax.ShapeDtypeStruct((2,) + factors...  1.83 us
  transfers between devices with their start and end apart: 12, of which 7 were waited for; matrix products, arithmetic and copies ran while one was open for 1% of the time, Pallas kernels for 14%

profile of v12, /device:TPU:1, one launch (start us, length us, event | category | flops | bytes accessed | tf_op | source)
XLA Modules:
  0.0 55.1 jit_solution(5736413844996235634)
XLA Ops:
  0.6 0.7 %collective-permute-start = (bf16[32,3584]{1,0:T(8,128)(2,1)}, bf16[32,3584]{1,0:T(8,128)(2,1)S(1)}, u32[]{:S(2)}, u32[]{:S(2)}) collective-permute-start(bf16[32,3584]{1,0:T(8,128)(2,1)} %bitcast.38), channel_id=1, source_target_pairs={{32,0},{64,32},{96,64},{128,96},{160,128},{192,160},{224,192},{34,... | collective-permute-start | bytes 688136 | tf_op jit(solution)/shard_map/ppermute | solution.py:361
  1.3 4.4 %collective-permute-start.1 = (bf16[32,3584]{1,0:T(8,128)(2,1)}, bf16[32,3584]{1,0:T(8,128)(2,1)S(1)}, u32[]{:S(2)}, u32[]{:S(2)}) collective-permute-start(bf16[32,3584]{1,0:T(8,128)(2,1)} %bitcast.39), channel_id=1, source_target_pairs={{1,33},{33,65},{65,97},{97,129},{129,161},{161,193},{193,225},{3,3... | collective-permute-start | bytes 688136 | tf_op jit(solution)/shard_map/ppermute | solution.py:364
  5.7 0.2 collective-permute-start.2
  5.9 0.0 copy-start.3
  5.9 0.7 %copy-done.3 = s32[2,1,32,2]{2,3,1,0:T(2,128)S(1)} copy-done((s32[2,1,32,2]{2,3,1,0:T(2,128)S(1)}, s32[2,1,32,2]{2,3,1,0:T(2,128)}, u32[]{:S(2)}) %copy-start.3) | copy-done | bytes 536
  6.6 0.0 copy-start.4
  6.6 0.7 %copy-done.4 = f32[2,1,32,2]{2,3,1,0:T(2,128)S(1)} copy-done((f32[2,1,32,2]{2,3,1,0:T(2,128)S(1)}, f32[2,1,32,2]{2,3,1,0:T(2,128)}, u32[]{:S(2)}) %copy-start.4) | copy-done | bytes 536
  7.3 0.2 slot_notes.1
  7.5 0.4 collective-permute-start.7
  7.9 0.1 compare_reduce_fusion
  8.0 0.0 collective-permute-done
  8.0 1.0 %collective-permute-done.1 = bf16[32,3584]{1,0:T(8,128)(2,1)S(1)} collective-permute-done((bf16[32,3584]{1,0:T(8,128)(2,1)}, bf16[32,3584]{1,0:T(8,128)(2,1)S(1)}, u32[]{:S(2)}, u32[]{:S(2)}) %collective-permute-start.1) | collective-permute-done | bytes 229408 | tf_op jit(solution)/shard_map/ppermute | solution.py:364
  9.0 0.1 broadcast_select_fusion
  9.1 0.0 collective-permute-done.2.swapped_saved
  9.1 2.8 %collective-permute-start.3 = (bf16[32,3712]{1,0:T(8,128)(2,1)S(1)}, bf16[32,3712]{1,0:T(8,128)(2,1)S(1)}, u32[]{:S(2)}, u32[]{:S(2)}) collective-permute-start(bf16[32,3712]{1,0:T(8,128)(2,1)S(1)} %pad_maximum_fusion.refs_0_), channel_id=1, source_target_pairs={{0,6},{1,25},{2,4},{3,27},{4,2},{5,29},{6,0},{7,31},{8,14},{9,17},... | collective-permute-start | bytes 712712 | tf_op jit(solution)/shard_map/ppermute | solution.py:28
  11.9 0.3 collective-permute-start.5
  12.3 0.3 collective-permute-start.4
  12.6 0.0 copy-start.2
  12.6 1.0 %copy-done.2 = bf16[2,1,1,2,256,256]{5,4,3,2,1,0:T(8,128)(2,1)S(1)} copy-done((bf16[2,1,1,2,256,256]{5,4,3,2,1,0:T(8,128)(2,1)S(1)}, bf16[2,1,1,2,256,256]{5,4,3,2,1,0:T(8,128)(2,1)}, u32[]{:S(2)}) %copy-start.2) | copy-done | bytes 524312
  13.6 0.3 saved_factors.1
  13.9 3.6 %collective-permute-done.3.refs_1_ = bf16[32,3712]{1,0:T(8,128)(2,1)S(1)} collective-permute-done((bf16[32,3712]{1,0:T(8,128)(2,1)S(1)}, bf16[32,3712]{1,0:T(8,128)(2,1)S(1)}, u32[]{:S(2)}, u32[]{:S(2)}) %collective-permute-start.3) | collective-permute-done | bytes 237600 | tf_op jit(solution)/shard_map/ppermute | solution.py:28
  17.5 1.2 %collective-permute-done.5.refs_3_ = bf16[32,3712]{1,0:T(8,128)(2,1)S(1)} collective-permute-done((bf16[32,3712]{1,0:T(8,128)(2,1)S(1)}, bf16[32,3712]{1,0:T(8,128)(2,1)S(1)}, u32[]{:S(2)}, u32[]{:S(2)}) %collective-permute-start.5) | collective-permute-done | bytes 237600 | tf_op jit(solution)/shard_map/ppermute | solution.py:28
  18.7 0.3 collective-permute-done.4.refs_2_
  19.0 0.8 %select_rows.1 = (bf16[64,3712]{1,0:T(8,128)(2,1)S(1)}, bf16[64,3712]{1,0:T(8,128)(2,1)S(1)}, bf16[64,3712]{1,0:T(8,128)(2,1)S(1)}, bf16[64,3712]{1,0:T(8,128)(2,1)S(1)}) custom-call(bf16[32,3712]{1,0:T(8,128)(2,1)S(1)} %pad_maximum_fusion.refs_0_, bf16[32,3712]{1,0:T(8,128)(2,1)S(1)} %collective-permute-done.3.refs_1_, ...), custom_call_target="tpu_custom_call" | custom-call | tf_op jit(solution)/shard_map/select_rows/pallas_call | solution.py:99
  19.8 2.6 %collective-permute-start.6 = (bf16[64,3712]{1,0:T(8,128)(2,1)S(1)}, bf16[64,3712]{1,0:T(8,128)(2,1)S(1)}, u32[]{:S(2)}, u32[]{:S(2)}) collective-permute-start(bf16[64,3712]{1,0:T(8,128)(2,1)S(1)} %get-tuple-element.45), channel_id=1, source_target_pairs={{0,24},{1,7},{2,26},{3,5},{4,28},{5,3},{6,30},{7,1},{8,16},{9,15},... | collective-permute-start | bytes 1425416 | tf_op jit(solution)/shard_map/ppermute | solution.py:28
  22.4 0.5 collective-permute-start.8
  22.9 0.2 collective-permute-start.9
  23.1 0.1 dynamic_update_slice.12
  23.3 0.0 copy-start
  23.3 10.7 %collective-permute-done.6 = bf16[64,3712]{1,0:T(8,128)(2,1)S(1)} collective-permute-done((bf16[64,3712]{1,0:T(8,128)(2,1)S(1)}, bf16[64,3712]{1,0:T(8,128)(2,1)S(1)}, u32[]{:S(2)}, u32[]{:S(2)}) %collective-permute-start.6) | collective-permute-done | bytes 475168 | tf_op jit(solution)/shard_map/ppermute | solution.py:28
  34.0 0.0 collective-permute-done.7.other
  34.0 0.0 collective-permute-done.8
  34.1 0.5 collective-permute-done.9
  34.7 5.2 %collective-permute-start.10 = (bf16[256,3712]{1,0:T(8,128)(2,1)S(1)}, bf16[256,3712]{1,0:T(8,128)(2,1)}, u32[]{:S(2)}, u32[]{:S(2)}) collective-permute-start(bf16[256,3712]{1,0:T(8,128)(2,1)S(1)} %constant_dynamic-update-slice_fusion.rows.notes), channel_id=1, source_target_pairs={{0,1},{1,0},{2,3},{3,2},{4,5},{5,4},{6,7},{7,6},{8,9},{9,8},{10,11... | collective-permute-start | bytes 5701640 | tf_op jit(solution)/shard_map/ppermute | solution.py:32
  39.9 0.0 copy-done
  39.9 1.8 %raw_grads.1 = (bf16[2,256,256]{2,1,0:T(8,128)(2,1)S(1)}, f32[32,128]{1,0:T(8,128)}) custom-call(bf16[256,3712]{1,0:T(8,128)(2,1)S(1)} %constant_dynamic-update-slice_fusion.rows.notes, bf16[256,3584]{1,0:T(8,128)(2,1)S(1)} %bitcast.28, bf16[256,3584]{1,0:T(8,128)(2,1)S(1)} %collective-permute-done.7.other, f32[4,256,256]{2,1,0:T(8,128)S(1)} %get-tuple-element.51.factors), custom_call_target="tpu_custom_call" | custom-call | tf_op jit(solution)/shard_map/raw_grads/pallas_call | solution.py:191
  41.7 5.5 %all-to-all-start = ((f32[32,1,128]{2,1,0:T(1,128)}), f32[32,1,128]{2,1,0:T(1,128)S(1)}, u32[]{:S(2)}, u32[]{:S(2)}) async-start(f32[32,1,128]{2,1,0:T(1,128)} %bitcast.11), calls=%async_computation | async-start | bytes 32768 | tf_op jit(solution)/shard_map/all_to_all | solution.py:391
  47.2 0.0 collective-permute-done.10.rows_other.notes_other
  47.2 0.0 copy-start.1
  47.2 1.5 %copy-done.1 = bf16[1,1,256,3584]{3,2,1,0:T(8,128)(2,1)S(1)} copy-done((bf16[1,1,256,3584]{3,2,1,0:T(8,128)(2,1)S(1)}, bf16[1,1,256,3584]{3,2,1,0:T(8,128)(2,1)}, u32[]{:S(2)}) %copy-start.1) | copy-done | bytes 1835032
  48.7 4.4 %finished.1 = (bf16[2,2,256,256]{3,2,1,0:T(8,128)(2,1)}, bf16[256,3584]{1,0:T(8,128)(2,1)}, bf16[96,128]{1,0:T(8,128)(2,1)S(1)}, f32[16,128]{1,0:T(8,128)S(1)}, f32[4,32]{1,0:T(4,128)S(1)}) custom-call(bf16[256,3712]{1,0:T(8,128)(2,1)S(1)} %constant_dynamic-update-slice_fusion.rows.notes, bf16[256,3712]{1,0:T(8,128)(2,1)S(1)} %constant_dynamic-update-slice_fusion.rows.notes, ...), custom_call_target="tpu_custom_call" | custom-call | tf_op jit(solution)/shard_map/finished/pallas_call | solution.py:259
  53.1 1.0 %all-to-all-done = f32[32,1,128]{2,1,0:T(1,128)S(1)} async-done(((f32[32,1,128]{2,1,0:T(1,128)}), f32[32,1,128]{2,1,0:T(1,128)S(1)}, u32[]{:S(2)}, u32[]{:S(2)}) %all-to-all-start) | async-done | bytes 16416 | tf_op jit(solution)/shard_map/all_to_all | solution.py:391
  54.1 1.0 %logit_grads.1 = f32[4,32]{1,0:T(4,128)} custom-call(f32[32,128]{1,0:T(8,128)S(1)} %bitcast.32, bf16[96,128]{1,0:T(8,128)(2,1)S(1)} %get-tuple-element.64.experts, f32[16,128]{1,0:T(8,128)S(1)} %get-tuple-element.65.places, f32[4,32]{1,0:T(4,128)S(1)} %get-tuple-element.66.scores), custom_call_target="tpu_custom_call" | custom-call | tf_op jit(solution)/shard_map/logit_grads/pallas_call | solution.py:398
  (4 shorter events, 0.1 us)
Async XLA Ops:
  0.6 7.4 %collective-permute-start = (bf16[32,3584]{1,0:T(8,128)(2,1)}, bf16[32,3584]{1,0:T(8,128)(2,1)S(1)}, u32[]{:S(2)}, u32[]{:S(2)}) collective-permute-start(bf16[32,3584]{1,0:T(8,128)(2,1)} %bitcast.38), channel_id=1, source_target_pairs={{32,0},{64,32},{96,64},{128,96},{160,128},{192,160},{224,192},{34,... | collective-permute-start | bytes 688136 | tf_op jit(solution)/shard_map/ppermute | solution.py:361
  1.3 7.6 %collective-permute-start.1 = (bf16[32,3584]{1,0:T(8,128)(2,1)}, bf16[32,3584]{1,0:T(8,128)(2,1)S(1)}, u32[]{:S(2)}, u32[]{:S(2)}) collective-permute-start(bf16[32,3584]{1,0:T(8,128)(2,1)} %bitcast.39), channel_id=1, source_target_pairs={{1,33},{33,65},{65,97},{97,129},{129,161},{161,193},{193,225},{3,3... | collective-permute-start | bytes 688136 | tf_op jit(solution)/shard_map/ppermute | solution.py:364
  5.7 3.4 %collective-permute-start.2 = (bf16[2,2,256,256]{3,2,1,0:T(8,128)(2,1)}, bf16[2,2,256,256]{3,2,1,0:T(8,128)(2,1)S(1)}, u32[]{:S(2)}, u32[]{:S(2)}) collective-permute-start(bf16[2,2,256,256]{3,2,1,0:T(8,128)(2,1)} %bitcast.30), channel_id=1, source_target_pairs={{0,1},{1,0},{2,3},{3,2},{4,5},{5,4},{6,7},{7,6},{8,9},{9,8},{10,11... | collective-permute-start | bytes 1572872 | tf_op jit(solution)/shard_map/ppermute | solution.py:32
  5.9 0.7 %copy-start.3 = (s32[2,1,32,2]{2,3,1,0:T(2,128)S(1)}, s32[2,1,32,2]{2,3,1,0:T(2,128)}, u32[]{:S(2)}) copy-start(s32[2,1,32,2]{2,3,1,0:T(2,128)} %param.8) | copy-start | bytes 1540
  6.6 0.7 %copy-start.4 = (f32[2,1,32,2]{2,3,1,0:T(2,128)S(1)}, f32[2,1,32,2]{2,3,1,0:T(2,128)}, u32[]{:S(2)}) copy-start(f32[2,1,32,2]{2,3,1,0:T(2,128)} %param.9) | copy-start | bytes 1540
  7.5 26.5 %collective-permute-start.7 = (bf16[256,3584]{1,0:T(8,128)(2,1)}, bf16[256,3584]{1,0:T(8,128)(2,1)S(1)}, u32[]{:S(2)}, u32[]{:S(2)}) collective-permute-start(bf16[256,3584]{1,0:T(8,128)(2,1)} %bitcast.27), channel_id=1, source_target_pairs={{0,1},{1,0},{2,3},{3,2},{4,5},{5,4},{6,7},{7,6},{8,9},{9,8},{10,11... | collective-permute-start | bytes 5505032 | tf_op jit(solution)/shard_map/ppermute | solution.py:32
  9.1 8.4 %collective-permute-start.3 = (bf16[32,3712]{1,0:T(8,128)(2,1)S(1)}, bf16[32,3712]{1,0:T(8,128)(2,1)S(1)}, u32[]{:S(2)}, u32[]{:S(2)}) collective-permute-start(bf16[32,3712]{1,0:T(8,128)(2,1)S(1)} %pad_maximum_fusion.refs_0_), channel_id=1, source_target_pairs={{0,6},{1,25},{2,4},{3,27},{4,2},{5,29},{6,0},{7,31},{8,14},{9,17},... | collective-permute-start | bytes 712712 | tf_op jit(solution)/shard_map/ppermute | solution.py:28
  11.9 6.8 %collective-permute-start.5 = (bf16[32,3712]{1,0:T(8,128)(2,1)S(1)}, bf16[32,3712]{1,0:T(8,128)(2,1)S(1)}, u32[]{:S(2)}, u32[]{:S(2)}) collective-permute-start(bf16[32,3712]{1,0:T(8,128)(2,1)S(1)} %pad_maximum_fusion.refs_0_), channel_id=1, source_target_pairs={{0,4},{1,17},{2,6},{3,19},{4,0},{5,21},{6,2},{7,23},{8,12},{9,25},... | collective-permute-start | bytes 712712 | tf_op jit(solution)/shard_map/ppermute | solution.py:28
  12.3 6.7 %collective-permute-start.4 = (bf16[32,3712]{1,0:T(8,128)(2,1)S(1)}, bf16[32,3712]{1,0:T(8,128)(2,1)S(1)}, u32[]{:S(2)}, u32[]{:S(2)}) collective-permute-start(bf16[32,3712]{1,0:T(8,128)(2,1)S(1)} %pad_maximum_fusion.refs_0_), channel_id=1, source_target_pairs={{0,2},{1,9},{2,0},{3,11},{4,6},{5,13},{6,4},{7,15},{8,10},{9,1},{1... | collective-permute-start | bytes 712712 | tf_op jit(solution)/shard_map/ppermute | solution.py:28
  12.6 1.0 %copy-start.2 = (bf16[2,1,1,2,256,256]{5,4,3,2,1,0:T(8,128)(2,1)S(1)}, bf16[2,1,1,2,256,256]{5,4,3,2,1,0:T(8,128)(2,1)}, u32[]{:S(2)}) copy-start(bf16[2,1,1,2,256,256]{5,4,3,2,1,0:T(8,128)(2,1)} %param.10) | copy-start | bytes 1572868
  19.8 14.2 %collective-permute-start.6 = (bf16[64,3712]{1,0:T(8,128)(2,1)S(1)}, bf16[64,3712]{1,0:T(8,128)(2,1)S(1)}, u32[]{:S(2)}, u32[]{:S(2)}) collective-permute-start(bf16[64,3712]{1,0:T(8,128)(2,1)S(1)} %get-tuple-element.45), channel_id=1, source_target_pairs={{0,24},{1,7},{2,26},{3,5},{4,28},{5,3},{6,30},{7,1},{8,16},{9,15},... | collective-permute-start | bytes 1425416 | tf_op jit(solution)/shard_map/ppermute | solution.py:28
  22.4 11.7 %collective-permute-start.8 = (bf16[64,3712]{1,0:T(8,128)(2,1)S(1)}, bf16[64,3712]{1,0:T(8,128)(2,1)S(1)}, u32[]{:S(2)}, u32[]{:S(2)}) collective-permute-start(bf16[64,3712]{1,0:T(8,128)(2,1)S(1)} %get-tuple-element.48), channel_id=1, source_target_pairs={{0,16},{1,5},{2,18},{3,7},{4,20},{5,1},{6,22},{7,3},{8,24},{9,13},... | collective-permute-start | bytes 1425416 | tf_op jit(solution)/shard_map/ppermute | solution.py:28
  22.9 11.7 %collective-permute-start.9 = (bf16[64,3712]{1,0:T(8,128)(2,1)S(1)}, bf16[64,3712]{1,0:T(8,128)(2,1)S(1)}, u32[]{:S(2)}, u32[]{:S(2)}) collective-permute-start(bf16[64,3712]{1,0:T(8,128)(2,1)S(1)} %get-tuple-element.49), channel_id=1, source_target_pairs={{0,8},{1,3},{2,10},{3,1},{4,12},{5,7},{6,14},{7,5},{8,0},{9,11},{1... | collective-permute-start | bytes 1425416 | tf_op jit(solution)/shard_map/ppermute | solution.py:28
  23.3 16.6 %copy-start = (bf16[1,1,256,3584]{3,2,1,0:T(8,128)(2,1)S(1)}, bf16[1,1,256,3584]{3,2,1,0:T(8,128)(2,1)}, u32[]{:S(2)}) copy-start(bf16[1,1,256,3584]{3,2,1,0:T(8,128)(2,1)} %param.11) | copy-start | bytes 5505028
  34.7 12.5 %collective-permute-start.10 = (bf16[256,3712]{1,0:T(8,128)(2,1)S(1)}, bf16[256,3712]{1,0:T(8,128)(2,1)}, u32[]{:S(2)}, u32[]{:S(2)}) collective-permute-start(bf16[256,3712]{1,0:T(8,128)(2,1)S(1)} %constant_dynamic-update-slice_fusion.rows.notes), channel_id=1, source_target_pairs={{0,1},{1,0},{2,3},{3,2},{4,5},{5,4},{6,7},{7,6},{8,9},{9,8},{10,11... | collective-permute-start | bytes 5701640 | tf_op jit(solution)/shard_map/ppermute | solution.py:32
  41.7 12.4 %all-to-all-start = ((f32[32,1,128]{2,1,0:T(1,128)}), f32[32,1,128]{2,1,0:T(1,128)S(1)}, u32[]{:S(2)}, u32[]{:S(2)}) async-start(f32[32,1,128]{2,1,0:T(1,128)} %bitcast.11), calls=%async_computation | async-start | bytes 32768 | tf_op jit(solution)/shard_map/all_to_all | solution.py:391
  47.2 1.5 %copy-start.1 = (bf16[1,1,256,3584]{3,2,1,0:T(8,128)(2,1)S(1)}, bf16[1,1,256,3584]{3,2,1,0:T(8,128)(2,1)}, u32[]{:S(2)}) copy-start(bf16[1,1,256,3584]{3,2,1,0:T(8,128)(2,1)} %param.11) | copy-start | bytes 5505028

commit v13 on v12

--- a/solution.py
+++ b/solution.py
@@ -7,7 +7,7 @@
 
 route_scale = 2.5
 side = 4
-gather_steps, exchange_steps = (3, 1, 2), (3, 2, 1)
+gather_steps, exchange_steps = (2, 3, 1), (2, 3, 1)
 extra = 128
 bf16, f32 = jnp.bfloat16, jnp.float32
 params = pltpu.CompilerParams(vmem_limit_bytes=16 * 2**20)

time: 55.7 us -> 54.5 us (0.978)
  waiting for transfers between devices: 18.3 us -> 17.5 us
  starting transfers between devices: 23.2 us -> 22.6 us
    ppermute x3, starting transfers between devices: 5.82 us -> 4.91 us  [swapped(): return lax.ppermute(value, 'dp', [(0, 1), (1, 0)])]
    ppermute x6, waiting for transfers between devices: 16.3 us -> 15.5 us  [plane_shift(): return lax.ppermute(value, ('expert', 'dp'), pairs)]
  transfers between devices with their start and end apart: 12 -> 12, of which waited for: 7 -> 8; matrix products, arithmetic and copies ran while one was open for 1% -> 1% of each run, Pallas kernels for 14% -> 14%
where the time goes in v13:
time: 54.5 us; the launch traced here: 53.8 us
  starting transfers between devices  22.6 us (41%)
  waiting for transfers between devices  17.5 us (32%)
  Pallas kernels  8.49 us (16%)
  local copies, waits for them, and re-layouts  4.15 us (8%)
  between operations  0.74 us (1%)
    ppermute x6, waiting for transfers between devices, plane_shift(): return lax.ppermute(value, ('expert', 'dp'), pairs)  15.5 us
    ppermute x6, starting transfers between devices, plane_shift(): return lax.ppermute(value, ('expert', 'dp'), pairs)  7.39 us
    all_to_all x1, starting transfers between devices, local(): lax.all_to_all(dots, ('expert', 'dp'), split_axis=0, concat_axis=0, tiled...  5.28 us
    ppermute x3, starting transfers between devices, swapped(): return lax.ppermute(value, 'dp', [(0, 1), (1, 0)])  4.91 us
    pallas_call x1, Pallas kernels, finished(): pl.pallas_call(finish_kernel, grid=(width // step,), out_shape=shapes, in...  4.39 us
    ppermute x1, starting transfers between devices, local(): lax.ppermute(sent_up[0], ('pipe', 'dp'), [(2 * z + 1, 2 * z + 3) for z in...  4.38 us
    unnamed x10, local copies, waits for them, and re-layouts  3.9 us
    pallas_call x1, Pallas kernels, raw_grads(): pl.pallas_call(raw_kernel, out_shape=(jax.ShapeDtypeStruct((2,) + factors...  1.83 us
  transfers between devices with their start and end apart: 12, of which 8 were waited for; matrix products, arithmetic and copies ran while one was open for 1% of the time, Pallas kernels for 14%

profile of v13, /device:TPU:1, one launch (start us, length us, event | category | flops | bytes accessed | tf_op | source)
XLA Modules:
  0.0 53.8 jit_solution(8746415383113975758)
XLA Ops:
  0.6 0.7 %collective-permute-start = (bf16[32,3584]{1,0:T(8,128)(2,1)}, bf16[32,3584]{1,0:T(8,128)(2,1)S(1)}, u32[]{:S(2)}, u32[]{:S(2)}) collective-permute-start(bf16[32,3584]{1,0:T(8,128)(2,1)} %bitcast.38), channel_id=1, source_target_pairs={{32,0},{64,32},{96,64},{128,96},{160,128},{192,160},{224,192},{34,... | collective-permute-start | bytes 688136 | tf_op jit(solution)/shard_map/ppermute | solution.py:361
  1.3 4.4 %collective-permute-start.1 = (bf16[32,3584]{1,0:T(8,128)(2,1)}, bf16[32,3584]{1,0:T(8,128)(2,1)S(1)}, u32[]{:S(2)}, u32[]{:S(2)}) collective-permute-start(bf16[32,3584]{1,0:T(8,128)(2,1)} %bitcast.39), channel_id=1, source_target_pairs={{1,33},{33,65},{65,97},{97,129},{129,161},{161,193},{193,225},{3,3... | collective-permute-start | bytes 688136 | tf_op jit(solution)/shard_map/ppermute | solution.py:364
  5.7 0.2 collective-permute-start.2
  5.9 0.0 copy-start.3
  5.9 0.7 %copy-done.3 = s32[2,1,32,2]{2,3,1,0:T(2,128)S(1)} copy-done((s32[2,1,32,2]{2,3,1,0:T(2,128)S(1)}, s32[2,1,32,2]{2,3,1,0:T(2,128)}, u32[]{:S(2)}) %copy-start.3) | copy-done | bytes 536
  6.6 0.0 copy-start.4
  6.6 0.7 %copy-done.4 = f32[2,1,32,2]{2,3,1,0:T(2,128)S(1)} copy-done((f32[2,1,32,2]{2,3,1,0:T(2,128)S(1)}, f32[2,1,32,2]{2,3,1,0:T(2,128)}, u32[]{:S(2)}) %copy-start.4) | copy-done | bytes 536
  7.3 0.2 slot_notes.1
  7.5 0.4 collective-permute-start.7
  7.9 0.1 compare_reduce_fusion
  8.0 0.0 collective-permute-done
  8.0 1.0 %collective-permute-done.1 = bf16[32,3584]{1,0:T(8,128)(2,1)S(1)} collective-permute-done((bf16[32,3584]{1,0:T(8,128)(2,1)}, bf16[32,3584]{1,0:T(8,128)(2,1)S(1)}, u32[]{:S(2)}, u32[]{:S(2)}) %collective-permute-start.1) | collective-permute-done | bytes 229408 | tf_op jit(solution)/shard_map/ppermute | solution.py:364
  9.0 0.1 broadcast_select_fusion
  9.1 0.0 collective-permute-done.2.swapped_saved
  9.1 3.0 %collective-permute-start.3 = (bf16[32,3712]{1,0:T(8,128)(2,1)S(1)}, bf16[32,3712]{1,0:T(8,128)(2,1)S(1)}, u32[]{:S(2)}, u32[]{:S(2)}) collective-permute-start(bf16[32,3712]{1,0:T(8,128)(2,1)S(1)} %pad_maximum_fusion.refs_0_), channel_id=1, source_target_pairs={{0,4},{1,17},{2,6},{3,19},{4,0},{5,21},{6,2},{7,23},{8,12},{9,25},... | collective-permute-start | bytes 712712 | tf_op jit(solution)/shard_map/ppermute | solution.py:28
  12.1 0.4 collective-permute-start.5
  12.5 0.4 collective-permute-start.4
  12.9 0.0 copy-start.2
  12.9 1.0 %copy-done.2 = bf16[2,1,1,2,256,256]{5,4,3,2,1,0:T(8,128)(2,1)S(1)} copy-done((bf16[2,1,1,2,256,256]{5,4,3,2,1,0:T(8,128)(2,1)S(1)}, bf16[2,1,1,2,256,256]{5,4,3,2,1,0:T(8,128)(2,1)}, u32[]{:S(2)}) %copy-start.2) | copy-done | bytes 524312
  13.9 0.3 saved_factors.1
  14.2 1.4 %collective-permute-done.3.refs_1_ = bf16[32,3712]{1,0:T(8,128)(2,1)S(1)} collective-permute-done((bf16[32,3712]{1,0:T(8,128)(2,1)S(1)}, bf16[32,3712]{1,0:T(8,128)(2,1)S(1)}, u32[]{:S(2)}, u32[]{:S(2)}) %collective-permute-start.3) | collective-permute-done | bytes 237600 | tf_op jit(solution)/shard_map/ppermute | solution.py:28
  15.6 3.2 %collective-permute-done.5.refs_3_ = bf16[32,3712]{1,0:T(8,128)(2,1)S(1)} collective-permute-done((bf16[32,3712]{1,0:T(8,128)(2,1)S(1)}, bf16[32,3712]{1,0:T(8,128)(2,1)S(1)}, u32[]{:S(2)}, u32[]{:S(2)}) %collective-permute-start.5) | collective-permute-done | bytes 237600 | tf_op jit(solution)/shard_map/ppermute | solution.py:28
  18.9 0.1 collective-permute-done.4.refs_2_
  19.0 0.8 %select_rows.1 = (bf16[64,3712]{1,0:T(8,128)(2,1)S(1)}, bf16[64,3712]{1,0:T(8,128)(2,1)S(1)}, bf16[64,3712]{1,0:T(8,128)(2,1)S(1)}, bf16[64,3712]{1,0:T(8,128)(2,1)S(1)}) custom-call(bf16[32,3712]{1,0:T(8,128)(2,1)S(1)} %pad_maximum_fusion.refs_0_, bf16[32,3712]{1,0:T(8,128)(2,1)S(1)} %collective-permute-done.3.refs_1_, ...), custom_call_target="tpu_custom_call" | custom-call | tf_op jit(solution)/shard_map/select_rows/pallas_call | solution.py:99
  19.8 2.7 %collective-permute-start.6 = (bf16[64,3712]{1,0:T(8,128)(2,1)S(1)}, bf16[64,3712]{1,0:T(8,128)(2,1)S(1)}, u32[]{:S(2)}, u32[]{:S(2)}) collective-permute-start(bf16[64,3712]{1,0:T(8,128)(2,1)S(1)} %get-tuple-element.45), channel_id=1, source_target_pairs={{0,16},{1,5},{2,18},{3,7},{4,20},{5,1},{6,22},{7,3},{8,24},{9,13},... | collective-permute-start | bytes 1425416 | tf_op jit(solution)/shard_map/ppermute | solution.py:28
  22.5 0.9 %collective-permute-start.8 = (bf16[64,3712]{1,0:T(8,128)(2,1)S(1)}, bf16[64,3712]{1,0:T(8,128)(2,1)S(1)}, u32[]{:S(2)}, u32[]{:S(2)}) collective-permute-start(bf16[64,3712]{1,0:T(8,128)(2,1)S(1)} %get-tuple-element.48), channel_id=1, source_target_pairs={{0,24},{1,7},{2,26},{3,5},{4,28},{5,3},{6,30},{7,1},{8,16},{9,15},... | collective-permute-start | bytes 1425416 | tf_op jit(solution)/shard_map/ppermute | solution.py:28
  23.4 0.0 collective-permute-start.9
  23.4 0.1 dynamic_update_slice.12
  23.5 0.0 copy-start
  23.5 5.7 %collective-permute-done.6 = bf16[64,3712]{1,0:T(8,128)(2,1)S(1)} collective-permute-done((bf16[64,3712]{1,0:T(8,128)(2,1)S(1)}, bf16[64,3712]{1,0:T(8,128)(2,1)S(1)}, u32[]{:S(2)}, u32[]{:S(2)}) %collective-permute-start.6) | collective-permute-done | bytes 475168 | tf_op jit(solution)/shard_map/ppermute | solution.py:28
  29.2 0.0 collective-permute-done.7.other
  29.3 5.0 %collective-permute-done.8 = bf16[64,3712]{1,0:T(8,128)(2,1)S(1)} collective-permute-done((bf16[64,3712]{1,0:T(8,128)(2,1)S(1)}, bf16[64,3712]{1,0:T(8,128)(2,1)S(1)}, u32[]{:S(2)}, u32[]{:S(2)}) %collective-permute-start.8) | collective-permute-done | bytes 475168 | tf_op jit(solution)/shard_map/ppermute | solution.py:28
  34.3 0.1 collective-permute-done.9
  34.5 4.3 %collective-permute-start.10 = (bf16[256,3712]{1,0:T(8,128)(2,1)S(1)}, bf16[256,3712]{1,0:T(8,128)(2,1)}, u32[]{:S(2)}, u32[]{:S(2)}) collective-permute-start(bf16[256,3712]{1,0:T(8,128)(2,1)S(1)} %constant_dynamic-update-slice_fusion.rows.notes), channel_id=1, source_target_pairs={{0,1},{1,0},{2,3},{3,2},{4,5},{5,4},{6,7},{7,6},{8,9},{9,8},{10,11... | collective-permute-start | bytes 5701640 | tf_op jit(solution)/shard_map/ppermute | solution.py:32
  38.7 0.0 copy-done
  38.8 1.8 %raw_grads.1 = (bf16[2,256,256]{2,1,0:T(8,128)(2,1)S(1)}, f32[32,128]{1,0:T(8,128)}) custom-call(bf16[256,3712]{1,0:T(8,128)(2,1)S(1)} %constant_dynamic-update-slice_fusion.rows.notes, bf16[256,3584]{1,0:T(8,128)(2,1)S(1)} %bitcast.28, bf16[256,3584]{1,0:T(8,128)(2,1)S(1)} %collective-permute-done.7.other, f32[4,256,256]{2,1,0:T(8,128)S(1)} %get-tuple-element.51.factors), custom_call_target="tpu_custom_call" | custom-call | tf_op jit(solution)/shard_map/raw_grads/pallas_call | solution.py:191
  40.6 5.3 %all-to-all-start = ((f32[32,1,128]{2,1,0:T(1,128)}), f32[32,1,128]{2,1,0:T(1,128)S(1)}, u32[]{:S(2)}, u32[]{:S(2)}) async-start(f32[32,1,128]{2,1,0:T(1,128)} %bitcast.11), calls=%async_computation | async-start | bytes 32768 | tf_op jit(solution)/shard_map/all_to_all | solution.py:391
  45.9 0.0 collective-permute-done.10.rows_other.notes_other
  45.9 0.0 copy-start.1
  45.9 1.5 %copy-done.1 = bf16[1,1,256,3584]{3,2,1,0:T(8,128)(2,1)S(1)} copy-done((bf16[1,1,256,3584]{3,2,1,0:T(8,128)(2,1)S(1)}, bf16[1,1,256,3584]{3,2,1,0:T(8,128)(2,1)}, u32[]{:S(2)}) %copy-start.1) | copy-done | bytes 1835032
  47.4 4.4 %finished.1 = (bf16[2,2,256,256]{3,2,1,0:T(8,128)(2,1)}, bf16[256,3584]{1,0:T(8,128)(2,1)}, bf16[96,128]{1,0:T(8,128)(2,1)S(1)}, f32[16,128]{1,0:T(8,128)S(1)}, f32[4,32]{1,0:T(4,128)S(1)}) custom-call(bf16[256,3712]{1,0:T(8,128)(2,1)S(1)} %constant_dynamic-update-slice_fusion.rows.notes, bf16[256,3712]{1,0:T(8,128)(2,1)S(1)} %constant_dynamic-update-slice_fusion.rows.notes, ...), custom_call_target="tpu_custom_call" | custom-call | tf_op jit(solution)/shard_map/finished/pallas_call | solution.py:259
  51.8 1.0 %all-to-all-done = f32[32,1,128]{2,1,0:T(1,128)S(1)} async-done(((f32[32,1,128]{2,1,0:T(1,128)}), f32[32,1,128]{2,1,0:T(1,128)S(1)}, u32[]{:S(2)}, u32[]{:S(2)}) %all-to-all-start) | async-done | bytes 16416 | tf_op jit(solution)/shard_map/all_to_all | solution.py:391
  52.8 1.0 %logit_grads.1 = f32[4,32]{1,0:T(4,128)} custom-call(f32[32,128]{1,0:T(8,128)S(1)} %bitcast.32, bf16[96,128]{1,0:T(8,128)(2,1)S(1)} %get-tuple-element.64.experts, f32[16,128]{1,0:T(8,128)S(1)} %get-tuple-element.65.places, f32[4,32]{1,0:T(4,128)S(1)} %get-tuple-element.66.scores), custom_call_target="tpu_custom_call" | custom-call | tf_op jit(solution)/shard_map/logit_grads/pallas_call | solution.py:398
  (4 shorter events, 0.1 us)
Async XLA Ops:
  0.6 7.4 %collective-permute-start = (bf16[32,3584]{1,0:T(8,128)(2,1)}, bf16[32,3584]{1,0:T(8,128)(2,1)S(1)}, u32[]{:S(2)}, u32[]{:S(2)}) collective-permute-start(bf16[32,3584]{1,0:T(8,128)(2,1)} %bitcast.38), channel_id=1, source_target_pairs={{32,0},{64,32},{96,64},{128,96},{160,128},{192,160},{224,192},{34,... | collective-permute-start | bytes 688136 | tf_op jit(solution)/shard_map/ppermute | solution.py:361
  1.3 7.6 %collective-permute-start.1 = (bf16[32,3584]{1,0:T(8,128)(2,1)}, bf16[32,3584]{1,0:T(8,128)(2,1)S(1)}, u32[]{:S(2)}, u32[]{:S(2)}) collective-permute-start(bf16[32,3584]{1,0:T(8,128)(2,1)} %bitcast.39), channel_id=1, source_target_pairs={{1,33},{33,65},{65,97},{97,129},{129,161},{161,193},{193,225},{3,3... | collective-permute-start | bytes 688136 | tf_op jit(solution)/shard_map/ppermute | solution.py:364
  5.7 3.4 %collective-permute-start.2 = (bf16[2,2,256,256]{3,2,1,0:T(8,128)(2,1)}, bf16[2,2,256,256]{3,2,1,0:T(8,128)(2,1)S(1)}, u32[]{:S(2)}, u32[]{:S(2)}) collective-permute-start(bf16[2,2,256,256]{3,2,1,0:T(8,128)(2,1)} %bitcast.30), channel_id=1, source_target_pairs={{0,1},{1,0},{2,3},{3,2},{4,5},{5,4},{6,7},{7,6},{8,9},{9,8},{10,11... | collective-permute-start | bytes 1572872 | tf_op jit(solution)/shard_map/ppermute | solution.py:32
  5.9 0.7 %copy-start.3 = (s32[2,1,32,2]{2,3,1,0:T(2,128)S(1)}, s32[2,1,32,2]{2,3,1,0:T(2,128)}, u32[]{:S(2)}) copy-start(s32[2,1,32,2]{2,3,1,0:T(2,128)} %param.8) | copy-start | bytes 1540
  6.6 0.7 %copy-start.4 = (f32[2,1,32,2]{2,3,1,0:T(2,128)S(1)}, f32[2,1,32,2]{2,3,1,0:T(2,128)}, u32[]{:S(2)}) copy-start(f32[2,1,32,2]{2,3,1,0:T(2,128)} %param.9) | copy-start | bytes 1540
  7.5 21.7 %collective-permute-start.7 = (bf16[256,3584]{1,0:T(8,128)(2,1)}, bf16[256,3584]{1,0:T(8,128)(2,1)S(1)}, u32[]{:S(2)}, u32[]{:S(2)}) collective-permute-start(bf16[256,3584]{1,0:T(8,128)(2,1)} %bitcast.27), channel_id=1, source_target_pairs={{0,1},{1,0},{2,3},{3,2},{4,5},{5,4},{6,7},{7,6},{8,9},{9,8},{10,11... | collective-permute-start | bytes 5505032 | tf_op jit(solution)/shard_map/ppermute | solution.py:32
  9.1 6.6 %collective-permute-start.3 = (bf16[32,3712]{1,0:T(8,128)(2,1)S(1)}, bf16[32,3712]{1,0:T(8,128)(2,1)S(1)}, u32[]{:S(2)}, u32[]{:S(2)}) collective-permute-start(bf16[32,3712]{1,0:T(8,128)(2,1)S(1)} %pad_maximum_fusion.refs_0_), channel_id=1, source_target_pairs={{0,4},{1,17},{2,6},{3,19},{4,0},{5,21},{6,2},{7,23},{8,12},{9,25},... | collective-permute-start | bytes 712712 | tf_op jit(solution)/shard_map/ppermute | solution.py:28
  12.1 6.8 %collective-permute-start.5 = (bf16[32,3712]{1,0:T(8,128)(2,1)S(1)}, bf16[32,3712]{1,0:T(8,128)(2,1)S(1)}, u32[]{:S(2)}, u32[]{:S(2)}) collective-permute-start(bf16[32,3712]{1,0:T(8,128)(2,1)S(1)} %pad_maximum_fusion.refs_0_), channel_id=1, source_target_pairs={{0,2},{1,9},{2,0},{3,11},{4,6},{5,13},{6,4},{7,15},{8,10},{9,1},{1... | collective-permute-start | bytes 712712 | tf_op jit(solution)/shard_map/ppermute | solution.py:28
  12.5 6.5 %collective-permute-start.4 = (bf16[32,3712]{1,0:T(8,128)(2,1)S(1)}, bf16[32,3712]{1,0:T(8,128)(2,1)S(1)}, u32[]{:S(2)}, u32[]{:S(2)}) collective-permute-start(bf16[32,3712]{1,0:T(8,128)(2,1)S(1)} %pad_maximum_fusion.refs_0_), channel_id=1, source_target_pairs={{0,6},{1,25},{2,4},{3,27},{4,2},{5,29},{6,0},{7,31},{8,14},{9,17},... | collective-permute-start | bytes 712712 | tf_op jit(solution)/shard_map/ppermute | solution.py:28
  12.9 1.0 %copy-start.2 = (bf16[2,1,1,2,256,256]{5,4,3,2,1,0:T(8,128)(2,1)S(1)}, bf16[2,1,1,2,256,256]{5,4,3,2,1,0:T(8,128)(2,1)}, u32[]{:S(2)}) copy-start(bf16[2,1,1,2,256,256]{5,4,3,2,1,0:T(8,128)(2,1)} %param.10) | copy-start | bytes 1572868
  19.8 9.4 %collective-permute-start.6 = (bf16[64,3712]{1,0:T(8,128)(2,1)S(1)}, bf16[64,3712]{1,0:T(8,128)(2,1)S(1)}, u32[]{:S(2)}, u32[]{:S(2)}) collective-permute-start(bf16[64,3712]{1,0:T(8,128)(2,1)S(1)} %get-tuple-element.45), channel_id=1, source_target_pairs={{0,16},{1,5},{2,18},{3,7},{4,20},{5,1},{6,22},{7,3},{8,24},{9,13},... | collective-permute-start | bytes 1425416 | tf_op jit(solution)/shard_map/ppermute | solution.py:28
  22.5 11.7 %collective-permute-start.8 = (bf16[64,3712]{1,0:T(8,128)(2,1)S(1)}, bf16[64,3712]{1,0:T(8,128)(2,1)S(1)}, u32[]{:S(2)}, u32[]{:S(2)}) collective-permute-start(bf16[64,3712]{1,0:T(8,128)(2,1)S(1)} %get-tuple-element.48), channel_id=1, source_target_pairs={{0,24},{1,7},{2,26},{3,5},{4,28},{5,3},{6,30},{7,1},{8,16},{9,15},... | collective-permute-start | bytes 1425416 | tf_op jit(solution)/shard_map/ppermute | solution.py:28
  23.4 11.0 %collective-permute-start.9 = (bf16[64,3712]{1,0:T(8,128)(2,1)S(1)}, bf16[64,3712]{1,0:T(8,128)(2,1)S(1)}, u32[]{:S(2)}, u32[]{:S(2)}) collective-permute-start(bf16[64,3712]{1,0:T(8,128)(2,1)S(1)} %get-tuple-element.49), channel_id=1, source_target_pairs={{0,8},{1,3},{2,10},{3,1},{4,12},{5,7},{6,14},{7,5},{8,0},{9,11},{1... | collective-permute-start | bytes 1425416 | tf_op jit(solution)/shard_map/ppermute | solution.py:28
  23.5 15.2 %copy-start = (bf16[1,1,256,3584]{3,2,1,0:T(8,128)(2,1)S(1)}, bf16[1,1,256,3584]{3,2,1,0:T(8,128)(2,1)}, u32[]{:S(2)}) copy-start(bf16[1,1,256,3584]{3,2,1,0:T(8,128)(2,1)} %param.11) | copy-start | bytes 5505028
  34.5 11.4 %collective-permute-start.10 = (bf16[256,3712]{1,0:T(8,128)(2,1)S(1)}, bf16[256,3712]{1,0:T(8,128)(2,1)}, u32[]{:S(2)}, u32[]{:S(2)}) collective-permute-start(bf16[256,3712]{1,0:T(8,128)(2,1)S(1)} %constant_dynamic-update-slice_fusion.rows.notes), channel_id=1, source_target_pairs={{0,1},{1,0},{2,3},{3,2},{4,5},{5,4},{6,7},{7,6},{8,9},{9,8},{10,11... | collective-permute-start | bytes 5701640 | tf_op jit(solution)/shard_map/ppermute | solution.py:32
  40.6 12.2 %all-to-all-start = ((f32[32,1,128]{2,1,0:T(1,128)}), f32[32,1,128]{2,1,0:T(1,128)S(1)}, u32[]{:S(2)}, u32[]{:S(2)}) async-start(f32[32,1,128]{2,1,0:T(1,128)} %bitcast.11), calls=%async_computation | async-start | bytes 32768 | tf_op jit(solution)/shard_map/all_to_all | solution.py:391
  45.9 1.5 %copy-start.1 = (bf16[1,1,256,3584]{3,2,1,0:T(8,128)(2,1)S(1)}, bf16[1,1,256,3584]{3,2,1,0:T(8,128)(2,1)}, u32[]{:S(2)}) copy-start(bf16[1,1,256,3584]{3,2,1,0:T(8,128)(2,1)} %param.11) | copy-start | bytes 5505028

commit v14 on v8

--- a/solution.py
+++ b/solution.py
@@ -1,3 +1,5 @@
+import functools
+
 import jax
 import jax.numpy as jnp
 from jax import lax
@@ -47,16 +49,16 @@
     ]
 
 
-def select_kernel(*refs):
+def select_kernel(steps, *refs):
     blocks, outs = refs[:4], refs[4:]
     core, near, far = position()
     held = [near ^ step for step in (0,) + gather_steps]
-    targets = [far ^ step for step in (0,) + exchange_steps]
+    targets = [far ^ step for step in (steps * 4)[:4]]
     wanted = [jnp.where(core == 0, t * 2 + (near >> 1), near * 2 + (t >> 1)) for t in targets]
     tokens, width = blocks[0].shape
     width -= extra
     slots = outs[0].shape[0] // 4
-    rows, columns = 4 * outs[0].shape[0], 4 * tokens
+    rows, columns = len(steps) * outs[0].shape[0], 4 * tokens
 
     def pick(index, values):
         return jnp.where(
@@ -94,13 +96,13 @@
         put(start, step, jnp.dot(taken, chunk, preferred_element_type=f32).astype(bf16))
 
 
-def select_rows(blocks, slots):
+def select_rows(blocks, slots, steps):
     shape = jax.ShapeDtypeStruct((4 * slots, blocks[0].shape[1]), bf16)
     return pl.pallas_call(
-        select_kernel,
-        out_shape=(shape,) * 4,
+        functools.partial(select_kernel, steps),
+        out_shape=(shape,) * len(steps),
         in_specs=[whole] * 4,
-        out_specs=(whole,) * 4,
+        out_specs=(whole,) * len(steps),
         compiler_params=params,
         name="select_rows",
     )(*blocks)
@@ -378,11 +380,14 @@
     blocks[1], factors, later, hidden = lax.optimization_barrier(
         (blocks[1], factors, later, hidden)
     )
-    pieces = select_rows(blocks, slots)
-    pieces = [pieces[0]] + [
+    pieces = [
         plane_shift(piece, step, False)
-        for piece, step in zip(pieces[1:], exchange_steps, strict=True)
+        for piece, step in zip(
+            select_rows(blocks, slots, exchange_steps), exchange_steps, strict=True
+        )
     ]
+    pieces[0], *blocks = lax.optimization_barrier((pieces[0], *blocks))
+    pieces = [*select_rows(blocks, slots, (0,)), *pieces]
     pieces[1], other = lax.optimization_barrier((pieces[1], other))
     rows = jnp.zeros((16 * slots, pieces[0].shape[1]), bf16)
     for index, piece in enumerate(pieces):

time: 54.2 us -> 54.1 us (level)
    pallas_call x1 -> x2, Pallas kernels: 0.83 us -> 1.18 us  [select_rows(): pl.pallas_call(functools.partial(select_kernel, steps), out_shape=(shape,...]
  transfers between devices with their start and end apart: 12 -> 12, of which waited for: 8 -> 8; matrix products, arithmetic and copies ran while one was open for 1% -> 1% of each run, Pallas kernels for 14% -> 15%
where the time goes in v14:
time: 54.1 us; the launch traced here: 53.4 us
  starting transfers between devices  22.6 us (42%)
  waiting for transfers between devices  16.9 us (31%)
  Pallas kernels  8.83 us (16%)
  local copies, waits for them, and re-layouts  4.15 us (8%)
  between operations  0.76 us (1%)
    ppermute x6, waiting for transfers between devices, plane_shift(): return lax.ppermute(value, ('expert', 'dp'), pairs)  14.9 us
    ppermute x6, starting transfers between devices, plane_shift(): return lax.ppermute(value, ('expert', 'dp'), pairs)  7.47 us
    all_to_all x1, starting transfers between devices, local(): lax.all_to_all(dots, ('expert', 'dp'), split_axis=0, concat_axis=0, tiled...  5.02 us
    ppermute x3, starting transfers between devices, swapped(): return lax.ppermute(value, 'dp', [(0, 1), (1, 0)])  5 us
    pallas_call x1, Pallas kernels, finished(): pl.pallas_call(finish_kernel, grid=(width // step,), out_shape=shapes, in...  4.39 us
    ppermute x1, starting transfers between devices, local(): lax.ppermute(sent_up[0], ('pipe', 'dp'), [(2 * z + 1, 2 * z + 3) for z in...  4.38 us
    unnamed x10, local copies, waits for them, and re-layouts  3.9 us
    pallas_call x1, Pallas kernels, raw_grads(): pl.pallas_call(raw_kernel, out_shape=(jax.ShapeDtypeStruct((2,) + factors...  1.83 us
  transfers between devices with their start and end apart: 12, of which 8 were waited for; matrix products, arithmetic and copies ran while one was open for 1% of the time, Pallas kernels for 15%

profile of v14, /device:TPU:1, one launch (start us, length us, event | category | flops | bytes accessed | tf_op | source)
XLA Modules:
  0.0 53.4 jit_solution(11599419642815154091)
XLA Ops:
  0.6 0.7 %collective-permute-start = (bf16[32,3584]{1,0:T(8,128)(2,1)}, bf16[32,3584]{1,0:T(8,128)(2,1)S(1)}, u32[]{:S(2)}, u32[]{:S(2)}) collective-permute-start(bf16[32,3584]{1,0:T(8,128)(2,1)} %bitcast.38), channel_id=1, source_target_pairs={{32,0},{64,32},{96,64},{128,96},{160,128},{192,160},{224,192},{34,... | collective-permute-start | bytes 688136 | tf_op jit(solution)/shard_map/ppermute | solution.py:363
  1.3 4.4 %collective-permute-start.1 = (bf16[32,3584]{1,0:T(8,128)(2,1)}, bf16[32,3584]{1,0:T(8,128)(2,1)S(1)}, u32[]{:S(2)}, u32[]{:S(2)}) collective-permute-start(bf16[32,3584]{1,0:T(8,128)(2,1)} %bitcast.39), channel_id=1, source_target_pairs={{1,33},{33,65},{65,97},{97,129},{129,161},{161,193},{193,225},{3,3... | collective-permute-start | bytes 688136 | tf_op jit(solution)/shard_map/ppermute | solution.py:366
  5.7 0.2 collective-permute-start.2
  5.9 0.0 copy-start.3
  5.9 0.7 %copy-done.3 = s32[2,1,32,2]{2,3,1,0:T(2,128)S(1)} copy-done((s32[2,1,32,2]{2,3,1,0:T(2,128)S(1)}, s32[2,1,32,2]{2,3,1,0:T(2,128)}, u32[]{:S(2)}) %copy-start.3) | copy-done | bytes 536
  6.6 0.0 copy-start.4
  6.6 0.7 %copy-done.4 = f32[2,1,32,2]{2,3,1,0:T(2,128)S(1)} copy-done((f32[2,1,32,2]{2,3,1,0:T(2,128)S(1)}, f32[2,1,32,2]{2,3,1,0:T(2,128)}, u32[]{:S(2)}) %copy-start.4) | copy-done | bytes 536
  7.3 0.2 slot_notes.1
  7.5 0.4 collective-permute-start.7
  7.9 0.1 compare_reduce_fusion
  8.0 0.0 collective-permute-done
  8.0 1.0 %collective-permute-done.1 = bf16[32,3584]{1,0:T(8,128)(2,1)S(1)} collective-permute-done((bf16[32,3584]{1,0:T(8,128)(2,1)}, bf16[32,3584]{1,0:T(8,128)(2,1)S(1)}, u32[]{:S(2)}, u32[]{:S(2)}) %collective-permute-start.1) | collective-permute-done | bytes 229408 | tf_op jit(solution)/shard_map/ppermute | solution.py:366
  9.0 0.1 broadcast_select_fusion
  9.1 0.0 collective-permute-done.2.swapped_saved
  9.1 3.0 %collective-permute-start.3 = (bf16[32,3712]{1,0:T(8,128)(2,1)S(1)}, bf16[32,3712]{1,0:T(8,128)(2,1)S(1)}, u32[]{:S(2)}, u32[]{:S(2)}) collective-permute-start(bf16[32,3712]{1,0:T(8,128)(2,1)S(1)} %pad_maximum_fusion.refs_0_), channel_id=1, source_target_pairs={{0,4},{1,17},{2,6},{3,19},{4,0},{5,21},{6,2},{7,23},{8,12},{9,25},... | collective-permute-start | bytes 712712 | tf_op jit(solution)/shard_map/ppermute | solution.py:30
  12.1 0.8 %collective-permute-start.5 = (bf16[32,3712]{1,0:T(8,128)(2,1)S(1)}, bf16[32,3712]{1,0:T(8,128)(2,1)S(1)}, u32[]{:S(2)}, u32[]{:S(2)}) collective-permute-start(bf16[32,3712]{1,0:T(8,128)(2,1)S(1)} %pad_maximum_fusion.refs_0_), channel_id=1, source_target_pairs={{0,6},{1,25},{2,4},{3,27},{4,2},{5,29},{6,0},{7,31},{8,14},{9,17},... | collective-permute-start | bytes 712712 | tf_op jit(solution)/shard_map/ppermute | solution.py:30
  12.9 0.0 collective-permute-start.4
  12.9 0.0 copy-start.2
  12.9 1.0 %copy-done.2 = bf16[2,1,1,2,256,256]{5,4,3,2,1,0:T(8,128)(2,1)S(1)} copy-done((bf16[2,1,1,2,256,256]{5,4,3,2,1,0:T(8,128)(2,1)S(1)}, bf16[2,1,1,2,256,256]{5,4,3,2,1,0:T(8,128)(2,1)}, u32[]{:S(2)}) %copy-start.2) | copy-done | bytes 524312
  13.9 0.3 saved_factors.1
  14.2 1.4 %collective-permute-done.3.refs_1_ = bf16[32,3712]{1,0:T(8,128)(2,1)S(1)} collective-permute-done((bf16[32,3712]{1,0:T(8,128)(2,1)S(1)}, bf16[32,3712]{1,0:T(8,128)(2,1)S(1)}, u32[]{:S(2)}, u32[]{:S(2)}) %collective-permute-start.3) | collective-permute-done | bytes 237600 | tf_op jit(solution)/shard_map/ppermute | solution.py:30
  15.6 2.9 %collective-permute-done.5.refs_3_ = bf16[32,3712]{1,0:T(8,128)(2,1)S(1)} collective-permute-done((bf16[32,3712]{1,0:T(8,128)(2,1)S(1)}, bf16[32,3712]{1,0:T(8,128)(2,1)S(1)}, u32[]{:S(2)}, u32[]{:S(2)}) %collective-permute-start.5) | collective-permute-done | bytes 237600 | tf_op jit(solution)/shard_map/ppermute | solution.py:30
  18.6 0.3 collective-permute-done.4.refs_2_
  18.9 0.7 %select_rows.2 = (bf16[64,3712]{1,0:T(8,128)(2,1)S(1)}, bf16[64,3712]{1,0:T(8,128)(2,1)S(1)}, bf16[64,3712]{1,0:T(8,128)(2,1)S(1)}) custom-call(bf16[32,3712]{1,0:T(8,128)(2,1)S(1)} %pad_maximum_fusion.refs_0_, bf16[32,3712]{1,0:T(8,128)(2,1)S(1)} %collective-permute-done.3.refs_1_, bf16[32,3712]{1,0:T(8,128)(2,1)S(1)} %collective-permute-done.4.refs_2_, ...), custom_call_target="tpu_custom_call" | custom-call | tf_op jit(solution)/shard_map/select_rows/pallas_call | solution.py:101
  19.6 2.8 %collective-permute-start.6 = (bf16[64,3712]{1,0:T(8,128)(2,1)S(1)}, bf16[64,3712]{1,0:T(8,128)(2,1)S(1)}, u32[]{:S(2)}, u32[]{:S(2)}) collective-permute-start(bf16[64,3712]{1,0:T(8,128)(2,1)S(1)} %get-tuple-element.48), channel_id=1, source_target_pairs={{0,16},{1,5},{2,18},{3,7},{4,20},{5,1},{6,22},{7,3},{8,24},{9,13},... | collective-permute-start | bytes 1425416 | tf_op jit(solution)/shard_map/ppermute | solution.py:30
  22.4 0.9 %collective-permute-start.8 = (bf16[64,3712]{1,0:T(8,128)(2,1)S(1)}, bf16[64,3712]{1,0:T(8,128)(2,1)S(1)}, u32[]{:S(2)}, u32[]{:S(2)}) collective-permute-start(bf16[64,3712]{1,0:T(8,128)(2,1)S(1)} %get-tuple-element.56), channel_id=1, source_target_pairs={{0,24},{1,7},{2,26},{3,5},{4,28},{5,3},{6,30},{7,1},{8,16},{9,15},... | collective-permute-start | bytes 1425416 | tf_op jit(solution)/shard_map/ppermute | solution.py:30
  23.3 0.0 collective-permute-start.9
  23.3 5.7 %collective-permute-done.6 = bf16[64,3712]{1,0:T(8,128)(2,1)S(1)} collective-permute-done((bf16[64,3712]{1,0:T(8,128)(2,1)S(1)}, bf16[64,3712]{1,0:T(8,128)(2,1)S(1)}, u32[]{:S(2)}, u32[]{:S(2)}) %collective-permute-start.6) | collective-permute-done | bytes 475168 | tf_op jit(solution)/shard_map/ppermute | solution.py:30
  29.0 0.5 select_rows.3
  29.5 0.1 dynamic_update_slice.12
  29.6 0.0 copy-start
  29.6 0.0 collective-permute-done.7.other
  29.7 4.4 %collective-permute-done.8 = bf16[64,3712]{1,0:T(8,128)(2,1)S(1)} collective-permute-done((bf16[64,3712]{1,0:T(8,128)(2,1)S(1)}, bf16[64,3712]{1,0:T(8,128)(2,1)S(1)}, u32[]{:S(2)}, u32[]{:S(2)}) %collective-permute-start.8) | collective-permute-done | bytes 475168 | tf_op jit(solution)/shard_map/ppermute | solution.py:30
  34.1 0.1 collective-permute-done.9
  34.2 4.4 %collective-permute-start.10 = (bf16[256,3712]{1,0:T(8,128)(2,1)S(1)}, bf16[256,3712]{1,0:T(8,128)(2,1)}, u32[]{:S(2)}, u32[]{:S(2)}) collective-permute-start(bf16[256,3712]{1,0:T(8,128)(2,1)S(1)} %constant_dynamic-update-slice_fusion.rows.notes), channel_id=1, source_target_pairs={{0,1},{1,0},{2,3},{3,2},{4,5},{5,4},{6,7},{7,6},{8,9},{9,8},{10,11... | collective-permute-start | bytes 5701640 | tf_op jit(solution)/shard_map/ppermute | solution.py:34
  38.6 0.0 copy-done
  38.6 1.8 %raw_grads.1 = (bf16[2,256,256]{2,1,0:T(8,128)(2,1)S(1)}, f32[32,128]{1,0:T(8,128)}) custom-call(bf16[256,3712]{1,0:T(8,128)(2,1)S(1)} %constant_dynamic-update-slice_fusion.rows.notes, bf16[256,3584]{1,0:T(8,128)(2,1)S(1)} %bitcast.28, bf16[256,3584]{1,0:T(8,128)(2,1)S(1)} %collective-permute-done.7.other, f32[4,256,256]{2,1,0:T(8,128)S(1)} %get-tuple-element.59.factors), custom_call_target="tpu_custom_call" | custom-call | tf_op jit(solution)/shard_map/raw_grads/pallas_call | solution.py:193
  40.5 5.0 %all-to-all-start = ((f32[32,1,128]{2,1,0:T(1,128)}), f32[32,1,128]{2,1,0:T(1,128)S(1)}, u32[]{:S(2)}, u32[]{:S(2)}) async-start(f32[32,1,128]{2,1,0:T(1,128)} %bitcast.11), calls=%async_computation | async-start | bytes 32768 | tf_op jit(solution)/shard_map/all_to_all | solution.py:396
  45.5 0.0 collective-permute-done.10.rows_other.notes_other
  45.5 0.0 copy-start.1
  45.5 1.5 %copy-done.1 = bf16[1,1,256,3584]{3,2,1,0:T(8,128)(2,1)S(1)} copy-done((bf16[1,1,256,3584]{3,2,1,0:T(8,128)(2,1)S(1)}, bf16[1,1,256,3584]{3,2,1,0:T(8,128)(2,1)}, u32[]{:S(2)}) %copy-start.1) | copy-done | bytes 1835032
  47.0 4.4 %finished.1 = (bf16[2,2,256,256]{3,2,1,0:T(8,128)(2,1)}, bf16[256,3584]{1,0:T(8,128)(2,1)}, bf16[96,128]{1,0:T(8,128)(2,1)S(1)}, f32[16,128]{1,0:T(8,128)S(1)}, f32[4,32]{1,0:T(4,128)S(1)}) custom-call(bf16[256,3712]{1,0:T(8,128)(2,1)S(1)} %constant_dynamic-update-slice_fusion.rows.notes, bf16[256,3712]{1,0:T(8,128)(2,1)S(1)} %constant_dynamic-update-slice_fusion.rows.notes, ...), custom_call_target="tpu_custom_call" | custom-call | tf_op jit(solution)/shard_map/finished/pallas_call | solution.py:261
  51.4 1.0 %all-to-all-done = f32[32,1,128]{2,1,0:T(1,128)S(1)} async-done(((f32[32,1,128]{2,1,0:T(1,128)}), f32[32,1,128]{2,1,0:T(1,128)S(1)}, u32[]{:S(2)}, u32[]{:S(2)}) %all-to-all-start) | async-done | bytes 16416 | tf_op jit(solution)/shard_map/all_to_all | solution.py:396
  52.4 1.0 %logit_grads.1 = f32[4,32]{1,0:T(4,128)} custom-call(f32[32,128]{1,0:T(8,128)S(1)} %bitcast.32, bf16[96,128]{1,0:T(8,128)(2,1)S(1)} %get-tuple-element.72.experts, f32[16,128]{1,0:T(8,128)S(1)} %get-tuple-element.73.places, f32[4,32]{1,0:T(4,128)S(1)} %get-tuple-element.74.scores), custom_call_target="tpu_custom_call" | custom-call | tf_op jit(solution)/shard_map/logit_grads/pallas_call | solution.py:403
  (4 shorter events, 0.1 us)
Async XLA Ops:
  0.6 7.4 %collective-permute-start = (bf16[32,3584]{1,0:T(8,128)(2,1)}, bf16[32,3584]{1,0:T(8,128)(2,1)S(1)}, u32[]{:S(2)}, u32[]{:S(2)}) collective-permute-start(bf16[32,3584]{1,0:T(8,128)(2,1)} %bitcast.38), channel_id=1, source_target_pairs={{32,0},{64,32},{96,64},{128,96},{160,128},{192,160},{224,192},{34,... | collective-permute-start | bytes 688136 | tf_op jit(solution)/shard_map/ppermute | solution.py:363
  1.3 7.6 %collective-permute-start.1 = (bf16[32,3584]{1,0:T(8,128)(2,1)}, bf16[32,3584]{1,0:T(8,128)(2,1)S(1)}, u32[]{:S(2)}, u32[]{:S(2)}) collective-permute-start(bf16[32,3584]{1,0:T(8,128)(2,1)} %bitcast.39), channel_id=1, source_target_pairs={{1,33},{33,65},{65,97},{97,129},{129,161},{161,193},{193,225},{3,3... | collective-permute-start | bytes 688136 | tf_op jit(solution)/shard_map/ppermute | solution.py:366
  5.7 3.4 %collective-permute-start.2 = (bf16[2,2,256,256]{3,2,1,0:T(8,128)(2,1)}, bf16[2,2,256,256]{3,2,1,0:T(8,128)(2,1)S(1)}, u32[]{:S(2)}, u32[]{:S(2)}) collective-permute-start(bf16[2,2,256,256]{3,2,1,0:T(8,128)(2,1)} %bitcast.30), channel_id=1, source_target_pairs={{0,1},{1,0},{2,3},{3,2},{4,5},{5,4},{6,7},{7,6},{8,9},{9,8},{10,11... | collective-permute-start | bytes 1572872 | tf_op jit(solution)/shard_map/ppermute | solution.py:34
  5.9 0.7 %copy-start.3 = (s32[2,1,32,2]{2,3,1,0:T(2,128)S(1)}, s32[2,1,32,2]{2,3,1,0:T(2,128)}, u32[]{:S(2)}) copy-start(s32[2,1,32,2]{2,3,1,0:T(2,128)} %param.8) | copy-start | bytes 1540
  6.6 0.7 %copy-start.4 = (f32[2,1,32,2]{2,3,1,0:T(2,128)S(1)}, f32[2,1,32,2]{2,3,1,0:T(2,128)}, u32[]{:S(2)}) copy-start(f32[2,1,32,2]{2,3,1,0:T(2,128)} %param.9) | copy-start | bytes 1540
  7.5 22.1 %collective-permute-start.7 = (bf16[256,3584]{1,0:T(8,128)(2,1)}, bf16[256,3584]{1,0:T(8,128)(2,1)S(1)}, u32[]{:S(2)}, u32[]{:S(2)}) collective-permute-start(bf16[256,3584]{1,0:T(8,128)(2,1)} %bitcast.27), channel_id=1, source_target_pairs={{0,1},{1,0},{2,3},{3,2},{4,5},{5,4},{6,7},{7,6},{8,9},{9,8},{10,11... | collective-permute-start | bytes 5505032 | tf_op jit(solution)/shard_map/ppermute | solution.py:34
  9.1 6.6 %collective-permute-start.3 = (bf16[32,3712]{1,0:T(8,128)(2,1)S(1)}, bf16[32,3712]{1,0:T(8,128)(2,1)S(1)}, u32[]{:S(2)}, u32[]{:S(2)}) collective-permute-start(bf16[32,3712]{1,0:T(8,128)(2,1)S(1)} %pad_maximum_fusion.refs_0_), channel_id=1, source_target_pairs={{0,4},{1,17},{2,6},{3,19},{4,0},{5,21},{6,2},{7,23},{8,12},{9,25},... | collective-permute-start | bytes 712712 | tf_op jit(solution)/shard_map/ppermute | solution.py:30
  12.1 6.5 %collective-permute-start.5 = (bf16[32,3712]{1,0:T(8,128)(2,1)S(1)}, bf16[32,3712]{1,0:T(8,128)(2,1)S(1)}, u32[]{:S(2)}, u32[]{:S(2)}) collective-permute-start(bf16[32,3712]{1,0:T(8,128)(2,1)S(1)} %pad_maximum_fusion.refs_0_), channel_id=1, source_target_pairs={{0,6},{1,25},{2,4},{3,27},{4,2},{5,29},{6,0},{7,31},{8,14},{9,17},... | collective-permute-start | bytes 712712 | tf_op jit(solution)/shard_map/ppermute | solution.py:30
  12.9 6.0 %collective-permute-start.4 = (bf16[32,3712]{1,0:T(8,128)(2,1)S(1)}, bf16[32,3712]{1,0:T(8,128)(2,1)S(1)}, u32[]{:S(2)}, u32[]{:S(2)}) collective-permute-start(bf16[32,3712]{1,0:T(8,128)(2,1)S(1)} %pad_maximum_fusion.refs_0_), channel_id=1, source_target_pairs={{0,2},{1,9},{2,0},{3,11},{4,6},{5,13},{6,4},{7,15},{8,10},{9,1},{1... | collective-permute-start | bytes 712712 | tf_op jit(solution)/shard_map/ppermute | solution.py:30
  12.9 1.0 %copy-start.2 = (bf16[2,1,1,2,256,256]{5,4,3,2,1,0:T(8,128)(2,1)S(1)}, bf16[2,1,1,2,256,256]{5,4,3,2,1,0:T(8,128)(2,1)}, u32[]{:S(2)}) copy-start(bf16[2,1,1,2,256,256]{5,4,3,2,1,0:T(8,128)(2,1)} %param.10) | copy-start | bytes 1572868
  19.6 9.4 %collective-permute-start.6 = (bf16[64,3712]{1,0:T(8,128)(2,1)S(1)}, bf16[64,3712]{1,0:T(8,128)(2,1)S(1)}, u32[]{:S(2)}, u32[]{:S(2)}) collective-permute-start(bf16[64,3712]{1,0:T(8,128)(2,1)S(1)} %get-tuple-element.48), channel_id=1, source_target_pairs={{0,16},{1,5},{2,18},{3,7},{4,20},{5,1},{6,22},{7,3},{8,24},{9,13},... | collective-permute-start | bytes 1425416 | tf_op jit(solution)/shard_map/ppermute | solution.py:30
  22.4 11.6 %collective-permute-start.8 = (bf16[64,3712]{1,0:T(8,128)(2,1)S(1)}, bf16[64,3712]{1,0:T(8,128)(2,1)S(1)}, u32[]{:S(2)}, u32[]{:S(2)}) collective-permute-start(bf16[64,3712]{1,0:T(8,128)(2,1)S(1)} %get-tuple-element.56), channel_id=1, source_target_pairs={{0,24},{1,7},{2,26},{3,5},{4,28},{5,3},{6,30},{7,1},{8,16},{9,15},... | collective-permute-start | bytes 1425416 | tf_op jit(solution)/shard_map/ppermute | solution.py:30
  23.3 10.9 %collective-permute-start.9 = (bf16[64,3712]{1,0:T(8,128)(2,1)S(1)}, bf16[64,3712]{1,0:T(8,128)(2,1)S(1)}, u32[]{:S(2)}, u32[]{:S(2)}) collective-permute-start(bf16[64,3712]{1,0:T(8,128)(2,1)S(1)} %get-tuple-element.57), channel_id=1, source_target_pairs={{0,8},{1,3},{2,10},{3,1},{4,12},{5,7},{6,14},{7,5},{8,0},{9,11},{1... | collective-permute-start | bytes 1425416 | tf_op jit(solution)/shard_map/ppermute | solution.py:30
  29.6 9.0 %copy-start = (bf16[1,1,256,3584]{3,2,1,0:T(8,128)(2,1)S(1)}, bf16[1,1,256,3584]{3,2,1,0:T(8,128)(2,1)}, u32[]{:S(2)}) copy-start(bf16[1,1,256,3584]{3,2,1,0:T(8,128)(2,1)} %param.11) | copy-start | bytes 5505028
  34.2 11.3 %collective-permute-start.10 = (bf16[256,3712]{1,0:T(8,128)(2,1)S(1)}, bf16[256,3712]{1,0:T(8,128)(2,1)}, u32[]{:S(2)}, u32[]{:S(2)}) collective-permute-start(bf16[256,3712]{1,0:T(8,128)(2,1)S(1)} %constant_dynamic-update-slice_fusion.rows.notes), channel_id=1, source_target_pairs={{0,1},{1,0},{2,3},{3,2},{4,5},{5,4},{6,7},{7,6},{8,9},{9,8},{10,11... | collective-permute-start | bytes 5701640 | tf_op jit(solution)/shard_map/ppermute | solution.py:34
  40.5 12.0 %all-to-all-start = ((f32[32,1,128]{2,1,0:T(1,128)}), f32[32,1,128]{2,1,0:T(1,128)S(1)}, u32[]{:S(2)}, u32[]{:S(2)}) async-start(f32[32,1,128]{2,1,0:T(1,128)} %bitcast.11), calls=%async_computation | async-start | bytes 32768 | tf_op jit(solution)/shard_map/all_to_all | solution.py:396
  45.5 1.5 %copy-start.1 = (bf16[1,1,256,3584]{3,2,1,0:T(8,128)(2,1)S(1)}, bf16[1,1,256,3584]{3,2,1,0:T(8,128)(2,1)}, u32[]{:S(2)}) copy-start(bf16[1,1,256,3584]{3,2,1,0:T(8,128)(2,1)} %param.11) | copy-start | bytes 5505028

commit v15 on v14

--- a/solution.py
+++ b/solution.py
@@ -9,7 +9,7 @@
 
 route_scale = 2.5
 side = 4
-gather_steps, exchange_steps = (2, 1, 3), (2, 3, 1)
+gather_steps, exchange_steps = (2, 1, 3), (2, 1, 3)
 extra = 128
 bf16, f32 = jnp.bfloat16, jnp.float32
 params = pltpu.CompilerParams(vmem_limit_bytes=16 * 2**20)

time: 54.1 us -> 54.2 us (level)
  transfers between devices with their start and end apart: 12 -> 12, of which waited for: 8 -> 7; matrix products, arithmetic and copies ran while one was open for 1% -> 1% of each run, Pallas kernels for 15% -> 15%
where the time goes in v15:
time: 54.2 us; the launch traced here: 53.5 us
  starting transfers between devices  22.6 us (42%)
  waiting for transfers between devices  16.9 us (31%)
  Pallas kernels  8.84 us (16%)
  local copies, waits for them, and re-layouts  4.16 us (8%)
  between operations  0.78 us (1%)
    ppermute x6, waiting for transfers between devices, plane_shift(): return lax.ppermute(value, ('expert', 'dp'), pairs)  14.9 us
    ppermute x6, starting transfers between devices, plane_shift(): return lax.ppermute(value, ('expert', 'dp'), pairs)  7.47 us
    all_to_all x1, starting transfers between devices, local(): lax.all_to_all(dots, ('expert', 'dp'), split_axis=0, concat_axis=0, tiled...  5.2 us
    ppermute x3, starting transfers between devices, swapped(): return lax.ppermute(value, 'dp', [(0, 1), (1, 0)])  4.88 us
    pallas_call x1, Pallas kernels, finished(): pl.pallas_call(finish_kernel, grid=(width // step,), out_shape=shapes, in...  4.39 us
    ppermute x1, starting transfers between devices, local(): lax.ppermute(sent_up[0], ('pipe', 'dp'), [(2 * z + 1, 2 * z + 3) for z in...  4.38 us
    unnamed x10, local copies, waits for them, and re-layouts  3.9 us
    pallas_call x1, Pallas kernels, raw_grads(): pl.pallas_call(raw_kernel, out_shape=(jax.ShapeDtypeStruct((2,) + factors...  1.83 us
  transfers between devices with their start and end apart: 12, of which 7 were waited for; matrix products, arithmetic and copies ran while one was open for 1% of the time, Pallas kernels for 15%

profile of v15, /device:TPU:1, one launch (start us, length us, event | category | flops | bytes accessed | tf_op | source)
XLA Modules:
  0.0 53.5 jit_solution(12276223467142704155)
XLA Ops:
  0.6 0.7 %collective-permute-start = (bf16[32,3584]{1,0:T(8,128)(2,1)}, bf16[32,3584]{1,0:T(8,128)(2,1)S(1)}, u32[]{:S(2)}, u32[]{:S(2)}) collective-permute-start(bf16[32,3584]{1,0:T(8,128)(2,1)} %bitcast.38), channel_id=1, source_target_pairs={{32,0},{64,32},{96,64},{128,96},{160,128},{192,160},{224,192},{34,... | collective-permute-start | bytes 688136 | tf_op jit(solution)/shard_map/ppermute | solution.py:363
  1.3 4.4 %collective-permute-start.1 = (bf16[32,3584]{1,0:T(8,128)(2,1)}, bf16[32,3584]{1,0:T(8,128)(2,1)S(1)}, u32[]{:S(2)}, u32[]{:S(2)}) collective-permute-start(bf16[32,3584]{1,0:T(8,128)(2,1)} %bitcast.39), channel_id=1, source_target_pairs={{1,33},{33,65},{65,97},{97,129},{129,161},{161,193},{193,225},{3,3... | collective-permute-start | bytes 688136 | tf_op jit(solution)/shard_map/ppermute | solution.py:366
  5.7 0.2 collective-permute-start.2
  5.9 0.0 copy-start.3
  5.9 0.7 %copy-done.3 = s32[2,1,32,2]{2,3,1,0:T(2,128)S(1)} copy-done((s32[2,1,32,2]{2,3,1,0:T(2,128)S(1)}, s32[2,1,32,2]{2,3,1,0:T(2,128)}, u32[]{:S(2)}) %copy-start.3) | copy-done | bytes 536
  6.6 0.0 copy-start.4
  6.6 0.7 %copy-done.4 = f32[2,1,32,2]{2,3,1,0:T(2,128)S(1)} copy-done((f32[2,1,32,2]{2,3,1,0:T(2,128)S(1)}, f32[2,1,32,2]{2,3,1,0:T(2,128)}, u32[]{:S(2)}) %copy-start.4) | copy-done | bytes 536
  7.3 0.2 slot_notes.1
  7.5 0.4 collective-permute-start.7
  7.9 0.1 compare_reduce_fusion
  8.0 0.0 collective-permute-done
  8.0 1.0 %collective-permute-done.1 = bf16[32,3584]{1,0:T(8,128)(2,1)S(1)} collective-permute-done((bf16[32,3584]{1,0:T(8,128)(2,1)}, bf16[32,3584]{1,0:T(8,128)(2,1)S(1)}, u32[]{:S(2)}, u32[]{:S(2)}) %collective-permute-start.1) | collective-permute-done | bytes 229408 | tf_op jit(solution)/shard_map/ppermute | solution.py:366
  9.0 0.1 broadcast_select_fusion
  9.1 0.0 collective-permute-done.2.swapped_saved
  9.1 3.0 %collective-permute-start.3 = (bf16[32,3712]{1,0:T(8,128)(2,1)S(1)}, bf16[32,3712]{1,0:T(8,128)(2,1)S(1)}, u32[]{:S(2)}, u32[]{:S(2)}) collective-permute-start(bf16[32,3712]{1,0:T(8,128)(2,1)S(1)} %pad_maximum_fusion.refs_0_), channel_id=1, source_target_pairs={{0,4},{1,17},{2,6},{3,19},{4,0},{5,21},{6,2},{7,23},{8,12},{9,25},... | collective-permute-start | bytes 712712 | tf_op jit(solution)/shard_map/ppermute | solution.py:30
  12.1 0.8 %collective-permute-start.5 = (bf16[32,3712]{1,0:T(8,128)(2,1)S(1)}, bf16[32,3712]{1,0:T(8,128)(2,1)S(1)}, u32[]{:S(2)}, u32[]{:S(2)}) collective-permute-start(bf16[32,3712]{1,0:T(8,128)(2,1)S(1)} %pad_maximum_fusion.refs_0_), channel_id=1, source_target_pairs={{0,6},{1,25},{2,4},{3,27},{4,2},{5,29},{6,0},{7,31},{8,14},{9,17},... | collective-permute-start | bytes 712712 | tf_op jit(solution)/shard_map/ppermute | solution.py:30
  12.9 0.0 collective-permute-start.4
  12.9 0.0 copy-start.2
  12.9 1.0 %copy-done.2 = bf16[2,1,1,2,256,256]{5,4,3,2,1,0:T(8,128)(2,1)S(1)} copy-done((bf16[2,1,1,2,256,256]{5,4,3,2,1,0:T(8,128)(2,1)S(1)}, bf16[2,1,1,2,256,256]{5,4,3,2,1,0:T(8,128)(2,1)}, u32[]{:S(2)}) %copy-start.2) | copy-done | bytes 524312
  13.9 0.3 saved_factors.1
  14.2 1.4 %collective-permute-done.3.refs_1_ = bf16[32,3712]{1,0:T(8,128)(2,1)S(1)} collective-permute-done((bf16[32,3712]{1,0:T(8,128)(2,1)S(1)}, bf16[32,3712]{1,0:T(8,128)(2,1)S(1)}, u32[]{:S(2)}, u32[]{:S(2)}) %collective-permute-start.3) | collective-permute-done | bytes 237600 | tf_op jit(solution)/shard_map/ppermute | solution.py:30
  15.6 2.9 %collective-permute-done.5.refs_3_ = bf16[32,3712]{1,0:T(8,128)(2,1)S(1)} collective-permute-done((bf16[32,3712]{1,0:T(8,128)(2,1)S(1)}, bf16[32,3712]{1,0:T(8,128)(2,1)S(1)}, u32[]{:S(2)}, u32[]{:S(2)}) %collective-permute-start.5) | collective-permute-done | bytes 237600 | tf_op jit(solution)/shard_map/ppermute | solution.py:30
  18.6 0.3 collective-permute-done.4.refs_2_
  18.9 0.7 %select_rows.2 = (bf16[64,3712]{1,0:T(8,128)(2,1)S(1)}, bf16[64,3712]{1,0:T(8,128)(2,1)S(1)}, bf16[64,3712]{1,0:T(8,128)(2,1)S(1)}) custom-call(bf16[32,3712]{1,0:T(8,128)(2,1)S(1)} %pad_maximum_fusion.refs_0_, bf16[32,3712]{1,0:T(8,128)(2,1)S(1)} %collective-permute-done.3.refs_1_, bf16[32,3712]{1,0:T(8,128)(2,1)S(1)} %collective-permute-done.4.refs_2_, ...), custom_call_target="tpu_custom_call" | custom-call | tf_op jit(solution)/shard_map/select_rows/pallas_call | solution.py:101
  19.6 2.8 %collective-permute-start.6 = (bf16[64,3712]{1,0:T(8,128)(2,1)S(1)}, bf16[64,3712]{1,0:T(8,128)(2,1)S(1)}, u32[]{:S(2)}, u32[]{:S(2)}) collective-permute-start(bf16[64,3712]{1,0:T(8,128)(2,1)S(1)} %get-tuple-element.48), channel_id=1, source_target_pairs={{0,16},{1,5},{2,18},{3,7},{4,20},{5,1},{6,22},{7,3},{8,24},{9,13},... | collective-permute-start | bytes 1425416 | tf_op jit(solution)/shard_map/ppermute | solution.py:30
  22.4 0.3 collective-permute-start.8
  22.7 0.6 %collective-permute-start.9 = (bf16[64,3712]{1,0:T(8,128)(2,1)S(1)}, bf16[64,3712]{1,0:T(8,128)(2,1)S(1)}, u32[]{:S(2)}, u32[]{:S(2)}) collective-permute-start(bf16[64,3712]{1,0:T(8,128)(2,1)S(1)} %get-tuple-element.57), channel_id=1, source_target_pairs={{0,24},{1,7},{2,26},{3,5},{4,28},{5,3},{6,30},{7,1},{8,16},{9,15},... | collective-permute-start | bytes 1425416 | tf_op jit(solution)/shard_map/ppermute | solution.py:30
  23.3 5.7 %collective-permute-done.6 = bf16[64,3712]{1,0:T(8,128)(2,1)S(1)} collective-permute-done((bf16[64,3712]{1,0:T(8,128)(2,1)S(1)}, bf16[64,3712]{1,0:T(8,128)(2,1)S(1)}, u32[]{:S(2)}, u32[]{:S(2)}) %collective-permute-start.6) | collective-permute-done | bytes 475168 | tf_op jit(solution)/shard_map/ppermute | solution.py:30
  29.0 0.5 select_rows.3
  29.5 0.1 dynamic_update_slice.12
  29.6 0.0 copy-start
  29.6 0.0 collective-permute-done.7.other
  29.7 4.5 %collective-permute-done.8 = bf16[64,3712]{1,0:T(8,128)(2,1)S(1)} collective-permute-done((bf16[64,3712]{1,0:T(8,128)(2,1)S(1)}, bf16[64,3712]{1,0:T(8,128)(2,1)S(1)}, u32[]{:S(2)}, u32[]{:S(2)}) %collective-permute-start.8) | collective-permute-done | bytes 475168 | tf_op jit(solution)/shard_map/ppermute | solution.py:30
  34.2 0.0 collective-permute-done.9
  34.3 4.3 %collective-permute-start.10 = (bf16[256,3712]{1,0:T(8,128)(2,1)S(1)}, bf16[256,3712]{1,0:T(8,128)(2,1)}, u32[]{:S(2)}, u32[]{:S(2)}) collective-permute-start(bf16[256,3712]{1,0:T(8,128)(2,1)S(1)} %constant_dynamic-update-slice_fusion.rows.notes), channel_id=1, source_target_pairs={{0,1},{1,0},{2,3},{3,2},{4,5},{5,4},{6,7},{7,6},{8,9},{9,8},{10,11... | collective-permute-start | bytes 5701640 | tf_op jit(solution)/shard_map/ppermute | solution.py:34
  38.6 0.0 copy-done
  38.6 1.8 %raw_grads.1 = (bf16[2,256,256]{2,1,0:T(8,128)(2,1)S(1)}, f32[32,128]{1,0:T(8,128)}) custom-call(bf16[256,3712]{1,0:T(8,128)(2,1)S(1)} %constant_dynamic-update-slice_fusion.rows.notes, bf16[256,3584]{1,0:T(8,128)(2,1)S(1)} %bitcast.28, bf16[256,3584]{1,0:T(8,128)(2,1)S(1)} %collective-permute-done.7.other, f32[4,256,256]{2,1,0:T(8,128)S(1)} %get-tuple-element.59.factors), custom_call_target="tpu_custom_call" | custom-call | tf_op jit(solution)/shard_map/raw_grads/pallas_call | solution.py:193
  40.4 5.2 %all-to-all-start = ((f32[32,1,128]{2,1,0:T(1,128)}), f32[32,1,128]{2,1,0:T(1,128)S(1)}, u32[]{:S(2)}, u32[]{:S(2)}) async-start(f32[32,1,128]{2,1,0:T(1,128)} %bitcast.11), calls=%async_computation | async-start | bytes 32768 | tf_op jit(solution)/shard_map/all_to_all | solution.py:396
  45.6 0.0 collective-permute-done.10.rows_other.notes_other
  45.6 0.0 copy-start.1
  45.6 1.5 %copy-done.1 = bf16[1,1,256,3584]{3,2,1,0:T(8,128)(2,1)S(1)} copy-done((bf16[1,1,256,3584]{3,2,1,0:T(8,128)(2,1)S(1)}, bf16[1,1,256,3584]{3,2,1,0:T(8,128)(2,1)}, u32[]{:S(2)}) %copy-start.1) | copy-done | bytes 1835032
  47.1 4.4 %finished.1 = (bf16[2,2,256,256]{3,2,1,0:T(8,128)(2,1)}, bf16[256,3584]{1,0:T(8,128)(2,1)}, bf16[96,128]{1,0:T(8,128)(2,1)S(1)}, f32[16,128]{1,0:T(8,128)S(1)}, f32[4,32]{1,0:T(4,128)S(1)}) custom-call(bf16[256,3712]{1,0:T(8,128)(2,1)S(1)} %constant_dynamic-update-slice_fusion.rows.notes, bf16[256,3712]{1,0:T(8,128)(2,1)S(1)} %constant_dynamic-update-slice_fusion.rows.notes, ...), custom_call_target="tpu_custom_call" | custom-call | tf_op jit(solution)/shard_map/finished/pallas_call | solution.py:261
  51.5 1.0 %all-to-all-done = f32[32,1,128]{2,1,0:T(1,128)S(1)} async-done(((f32[32,1,128]{2,1,0:T(1,128)}), f32[32,1,128]{2,1,0:T(1,128)S(1)}, u32[]{:S(2)}, u32[]{:S(2)}) %all-to-all-start) | async-done | bytes 16416 | tf_op jit(solution)/shard_map/all_to_all | solution.py:396
  52.5 1.0 %logit_grads.1 = f32[4,32]{1,0:T(4,128)} custom-call(f32[32,128]{1,0:T(8,128)S(1)} %bitcast.32, bf16[96,128]{1,0:T(8,128)(2,1)S(1)} %get-tuple-element.72.experts, f32[16,128]{1,0:T(8,128)S(1)} %get-tuple-element.73.places, f32[4,32]{1,0:T(4,128)S(1)} %get-tuple-element.74.scores), custom_call_target="tpu_custom_call" | custom-call | tf_op jit(solution)/shard_map/logit_grads/pallas_call | solution.py:403
  (4 shorter events, 0.1 us)
Async XLA Ops:
  0.6 7.4 %collective-permute-start = (bf16[32,3584]{1,0:T(8,128)(2,1)}, bf16[32,3584]{1,0:T(8,128)(2,1)S(1)}, u32[]{:S(2)}, u32[]{:S(2)}) collective-permute-start(bf16[32,3584]{1,0:T(8,128)(2,1)} %bitcast.38), channel_id=1, source_target_pairs={{32,0},{64,32},{96,64},{128,96},{160,128},{192,160},{224,192},{34,... | collective-permute-start | bytes 688136 | tf_op jit(solution)/shard_map/ppermute | solution.py:363
  1.3 7.6 %collective-permute-start.1 = (bf16[32,3584]{1,0:T(8,128)(2,1)}, bf16[32,3584]{1,0:T(8,128)(2,1)S(1)}, u32[]{:S(2)}, u32[]{:S(2)}) collective-permute-start(bf16[32,3584]{1,0:T(8,128)(2,1)} %bitcast.39), channel_id=1, source_target_pairs={{1,33},{33,65},{65,97},{97,129},{129,161},{161,193},{193,225},{3,3... | collective-permute-start | bytes 688136 | tf_op jit(solution)/shard_map/ppermute | solution.py:366
  5.7 3.4 %collective-permute-start.2 = (bf16[2,2,256,256]{3,2,1,0:T(8,128)(2,1)}, bf16[2,2,256,256]{3,2,1,0:T(8,128)(2,1)S(1)}, u32[]{:S(2)}, u32[]{:S(2)}) collective-permute-start(bf16[2,2,256,256]{3,2,1,0:T(8,128)(2,1)} %bitcast.30), channel_id=1, source_target_pairs={{0,1},{1,0},{2,3},{3,2},{4,5},{5,4},{6,7},{7,6},{8,9},{9,8},{10,11... | collective-permute-start | bytes 1572872 | tf_op jit(solution)/shard_map/ppermute | solution.py:34
  5.9 0.7 %copy-start.3 = (s32[2,1,32,2]{2,3,1,0:T(2,128)S(1)}, s32[2,1,32,2]{2,3,1,0:T(2,128)}, u32[]{:S(2)}) copy-start(s32[2,1,32,2]{2,3,1,0:T(2,128)} %param.8) | copy-start | bytes 1540
  6.6 0.7 %copy-start.4 = (f32[2,1,32,2]{2,3,1,0:T(2,128)S(1)}, f32[2,1,32,2]{2,3,1,0:T(2,128)}, u32[]{:S(2)}) copy-start(f32[2,1,32,2]{2,3,1,0:T(2,128)} %param.9) | copy-start | bytes 1540
  7.5 22.1 %collective-permute-start.7 = (bf16[256,3584]{1,0:T(8,128)(2,1)}, bf16[256,3584]{1,0:T(8,128)(2,1)S(1)}, u32[]{:S(2)}, u32[]{:S(2)}) collective-permute-start(bf16[256,3584]{1,0:T(8,128)(2,1)} %bitcast.27), channel_id=1, source_target_pairs={{0,1},{1,0},{2,3},{3,2},{4,5},{5,4},{6,7},{7,6},{8,9},{9,8},{10,11... | collective-permute-start | bytes 5505032 | tf_op jit(solution)/shard_map/ppermute | solution.py:34
  9.1 6.6 %collective-permute-start.3 = (bf16[32,3712]{1,0:T(8,128)(2,1)S(1)}, bf16[32,3712]{1,0:T(8,128)(2,1)S(1)}, u32[]{:S(2)}, u32[]{:S(2)}) collective-permute-start(bf16[32,3712]{1,0:T(8,128)(2,1)S(1)} %pad_maximum_fusion.refs_0_), channel_id=1, source_target_pairs={{0,4},{1,17},{2,6},{3,19},{4,0},{5,21},{6,2},{7,23},{8,12},{9,25},... | collective-permute-start | bytes 712712 | tf_op jit(solution)/shard_map/ppermute | solution.py:30
  12.1 6.5 %collective-permute-start.5 = (bf16[32,3712]{1,0:T(8,128)(2,1)S(1)}, bf16[32,3712]{1,0:T(8,128)(2,1)S(1)}, u32[]{:S(2)}, u32[]{:S(2)}) collective-permute-start(bf16[32,3712]{1,0:T(8,128)(2,1)S(1)} %pad_maximum_fusion.refs_0_), channel_id=1, source_target_pairs={{0,6},{1,25},{2,4},{3,27},{4,2},{5,29},{6,0},{7,31},{8,14},{9,17},... | collective-permute-start | bytes 712712 | tf_op jit(solution)/shard_map/ppermute | solution.py:30
  12.9 6.0 %collective-permute-start.4 = (bf16[32,3712]{1,0:T(8,128)(2,1)S(1)}, bf16[32,3712]{1,0:T(8,128)(2,1)S(1)}, u32[]{:S(2)}, u32[]{:S(2)}) collective-permute-start(bf16[32,3712]{1,0:T(8,128)(2,1)S(1)} %pad_maximum_fusion.refs_0_), channel_id=1, source_target_pairs={{0,2},{1,9},{2,0},{3,11},{4,6},{5,13},{6,4},{7,15},{8,10},{9,1},{1... | collective-permute-start | bytes 712712 | tf_op jit(solution)/shard_map/ppermute | solution.py:30
  12.9 1.0 %copy-start.2 = (bf16[2,1,1,2,256,256]{5,4,3,2,1,0:T(8,128)(2,1)S(1)}, bf16[2,1,1,2,256,256]{5,4,3,2,1,0:T(8,128)(2,1)}, u32[]{:S(2)}) copy-start(bf16[2,1,1,2,256,256]{5,4,3,2,1,0:T(8,128)(2,1)} %param.10) | copy-start | bytes 1572868
  19.6 9.4 %collective-permute-start.6 = (bf16[64,3712]{1,0:T(8,128)(2,1)S(1)}, bf16[64,3712]{1,0:T(8,128)(2,1)S(1)}, u32[]{:S(2)}, u32[]{:S(2)}) collective-permute-start(bf16[64,3712]{1,0:T(8,128)(2,1)S(1)} %get-tuple-element.48), channel_id=1, source_target_pairs={{0,16},{1,5},{2,18},{3,7},{4,20},{5,1},{6,22},{7,3},{8,24},{9,13},... | collective-permute-start | bytes 1425416 | tf_op jit(solution)/shard_map/ppermute | solution.py:30
  22.4 11.8 %collective-permute-start.8 = (bf16[64,3712]{1,0:T(8,128)(2,1)S(1)}, bf16[64,3712]{1,0:T(8,128)(2,1)S(1)}, u32[]{:S(2)}, u32[]{:S(2)}) collective-permute-start(bf16[64,3712]{1,0:T(8,128)(2,1)S(1)} %get-tuple-element.56), channel_id=1, source_target_pairs={{0,8},{1,3},{2,10},{3,1},{4,12},{5,7},{6,14},{7,5},{8,0},{9,11},{1... | collective-permute-start | bytes 1425416 | tf_op jit(solution)/shard_map/ppermute | solution.py:30
  22.7 11.5 %collective-permute-start.9 = (bf16[64,3712]{1,0:T(8,128)(2,1)S(1)}, bf16[64,3712]{1,0:T(8,128)(2,1)S(1)}, u32[]{:S(2)}, u32[]{:S(2)}) collective-permute-start(bf16[64,3712]{1,0:T(8,128)(2,1)S(1)} %get-tuple-element.57), channel_id=1, source_target_pairs={{0,24},{1,7},{2,26},{3,5},{4,28},{5,3},{6,30},{7,1},{8,16},{9,15},... | collective-permute-start | bytes 1425416 | tf_op jit(solution)/shard_map/ppermute | solution.py:30
  29.6 8.9 %copy-start = (bf16[1,1,256,3584]{3,2,1,0:T(8,128)(2,1)S(1)}, bf16[1,1,256,3584]{3,2,1,0:T(8,128)(2,1)}, u32[]{:S(2)}) copy-start(bf16[1,1,256,3584]{3,2,1,0:T(8,128)(2,1)} %param.11) | copy-start | bytes 5505028
  34.3 11.3 %collective-permute-start.10 = (bf16[256,3712]{1,0:T(8,128)(2,1)S(1)}, bf16[256,3712]{1,0:T(8,128)(2,1)}, u32[]{:S(2)}, u32[]{:S(2)}) collective-permute-start(bf16[256,3712]{1,0:T(8,128)(2,1)S(1)} %constant_dynamic-update-slice_fusion.rows.notes), channel_id=1, source_target_pairs={{0,1},{1,0},{2,3},{3,2},{4,5},{5,4},{6,7},{7,6},{8,9},{9,8},{10,11... | collective-permute-start | bytes 5701640 | tf_op jit(solution)/shard_map/ppermute | solution.py:34
  40.4 12.1 %all-to-all-start = ((f32[32,1,128]{2,1,0:T(1,128)}), f32[32,1,128]{2,1,0:T(1,128)S(1)}, u32[]{:S(2)}, u32[]{:S(2)}) async-start(f32[32,1,128]{2,1,0:T(1,128)} %bitcast.11), calls=%async_computation | async-start | bytes 32768 | tf_op jit(solution)/shard_map/all_to_all | solution.py:396
  45.6 1.5 %copy-start.1 = (bf16[1,1,256,3584]{3,2,1,0:T(8,128)(2,1)S(1)}, bf16[1,1,256,3584]{3,2,1,0:T(8,128)(2,1)}, u32[]{:S(2)}) copy-start(bf16[1,1,256,3584]{3,2,1,0:T(8,128)(2,1)} %param.11) | copy-start | bytes 5505028
